TPU v7x, 32 devices: a whole 2x2x4 slice. The times are simulated.
32 devices in a mesh: head: 4 (over y, core), tail: 8 (over z, x).
Axes of the slice: x: 2, y: 2, z: 4, core: 2. Of those that a mesh axis runs over, the one named last changes fastest.
Arguments:
- head_table: float32 [16384, 512], P(('head', 'tail')), may hold values from -2.5 to 2.5
- head_state: float32 [16384], P(('head', 'tail')), may hold values from 0.01 to 0.1
- tail_table: float32 [16384, 512], P(('head', 'tail')), may hold values from -2.5 to 2.5
- tail_state: float32 [16384], P(('head', 'tail')), may hold values from 0.01 to 0.1
- relations: float32 [1024, 512], P(('head', 'tail')), may hold values from -0.25 to 0.25
- relation_state: float32 [1024, 512], P(('head', 'tail')), may hold values from 10 to 100
- head_rows: int32 [2, 16384], P(None, ('head', 'tail')), may hold values from 0 to 511
- tail_rows: int32 [2, 16384], P(None, ('head', 'tail')), may hold values from 0 to 511
- negatives: int32 [2, 128, 128], P(None, ('head', 'tail')), may hold values from 0 to 511
- relation_ids: int32 [2, 128], P(None, ('head', 'tail')), may hold values from 0 to 1
- block_counts: int32 [2, 32], P(None, ('head', 'tail')), may hold values from 1 to 4, 64 in all within a row
Outputs:
- heads_out: float32 [16384, 512], P(('head', 'tail'))
- tails_out: float32 [16384, 512], P(('head', 'tail'))
- relations_out: float32 [1024, 512], P(('head', 'tail'))
Inputs may be any that keep to these rules, and one draw needn't show every extreme that they name: `block_counts`: in each bucket the counts over all devices sum to 4 // 2 times the number of devices, and some device has 4.
All inputs are finite; a program needn't handle non-finite values.
Results may differ from a plain program's by a relative error of at most 0.01.
Values may be sent and summed in bfloat16 or wider, within the bound.
No kernel may reach another device: no remote copies, remote signals or barrier semaphores. Data moves between devices by JAX's collectives and lax.ppermute only.
A program may use at most 64 MiB of HBM per device.

v0:
```python
import jax
import jax.numpy as jnp
from jax import lax
from jax.sharding import PartitionSpec as P

RATE_ROWS = 0.2
RATE_RELATIONS = 0.05
EPSILON = 1e-06


def passed_along(x, axis, by):
    peers = lax.axis_size(axis)
    return lax.ppermute(x, axis, [(i, (i + by) % peers) for i in range(peers)])


def row_adagrad(emb_table, row_state, gradient):
    state_new = row_state + jnp.mean(gradient * gradient, axis=1)
    table_new = emb_table - RATE_ROWS * gradient / (jnp.sqrt(state_new) + EPSILON)[:, None]
    return (table_new, state_new)


def relation_adagrad(rel_table, rel_state, gradient):
    state_new = rel_state + gradient * gradient
    return (rel_table - RATE_RELATIONS * gradient / (jnp.sqrt(state_new) + EPSILON), state_new)


def score_bucket(
    head_table,
    head_state,
    tail_table,
    tail_state,
    rel_bf,
    head_index,
    tail_index,
    neg_index,
    rel_index,
    live_blocks,
):
    model_width = head_table.shape[1]
    block_total = rel_index.shape[0]
    per_block = head_index.shape[0] // block_total
    neg_total = neg_index.shape[1]
    rel_total = rel_bf.shape[0] // model_width
    head_vecs = (
        head_table[head_index].astype(jnp.bfloat16).reshape(block_total, per_block, model_width)
    )
    tail_vecs = (
        tail_table[tail_index].astype(jnp.bfloat16).reshape(block_total, per_block, model_width)
    )
    neg_vecs = tail_table[neg_index].astype(jnp.bfloat16)
    chosen = rel_bf.reshape(rel_total, model_width, model_width)[rel_index]
    live_mask = (jnp.arange(block_total, dtype=jnp.int32) < live_blocks).astype(jnp.float32)
    projected = jnp.einsum(
        "bed,bdk->bek", head_vecs, chosen, preferred_element_type=jnp.float32
    ).astype(jnp.bfloat16)
    pos_score = jnp.einsum("bek,bek->be", projected, tail_vecs, preferred_element_type=jnp.float32)
    neg_score = jnp.einsum("bek,bnk->ben", projected, neg_vecs, preferred_element_type=jnp.float32)
    pos_weight = -jax.nn.sigmoid(-pos_score) * live_mask[:, None]
    neg_weight = (jax.nn.sigmoid(neg_score) * live_mask[:, None, None] / neg_total).astype(
        jnp.bfloat16
    )
    edge_grad = (
        pos_weight[:, :, None] * tail_vecs.astype(jnp.float32)
        + jnp.einsum("ben,bnk->bek", neg_weight, neg_vecs, preferred_element_type=jnp.float32)
    ).astype(jnp.bfloat16)
    head_terms = jnp.einsum(
        "bek,bdk->bed", edge_grad, chosen, preferred_element_type=jnp.float32
    ).reshape(-1, model_width)
    head_grad = jnp.zeros(head_table.shape, jnp.float32).at[head_index].add(head_terms)
    pos_terms = (pos_weight[:, :, None] * projected.astype(jnp.float32)).reshape(-1, model_width)
    neg_terms = jnp.einsum(
        "ben,bek->bnk", neg_weight, projected, preferred_element_type=jnp.float32
    ).reshape(-1, model_width)
    tail_grad = jnp.zeros(tail_table.shape, jnp.float32).at[tail_index].add(pos_terms)
    tail_grad = tail_grad.at[neg_index.reshape(-1)].add(neg_terms)
    head_new, head_state_new = row_adagrad(head_table, head_state, head_grad)
    tail_new, tail_state_new = row_adagrad(tail_table, tail_state, tail_grad)
    return (head_new, head_state_new, tail_new, tail_state_new, head_vecs, edge_grad)


def relation_term(head_vecs, edge_grad, rel_index, row_count):
    model_width = head_vecs.shape[2]
    row_ids = jnp.arange(row_count, dtype=jnp.int32)
    columns = jnp.take(head_vecs, row_ids % model_width, axis=2)
    per_block = jnp.einsum("bek,bej->kbj", columns, edge_grad, preferred_element_type=jnp.float32)
    select = (row_ids[:, None] // model_width == rel_index[None, :]).astype(jnp.float32)
    return jnp.einsum("kb,kbj->kj", select, per_block)


def shards(
    head_table,
    head_state,
    tail_table,
    tail_state,
    relations,
    relation_state,
    head_rows,
    tail_rows,
    negatives,
    relation_ids,
    block_counts,
):
    own_rows = relations.shape[0]
    full_table, full_state = (
        lax.all_gather(relations, ("head", "tail"), axis=0, tiled=True),
        lax.all_gather(relation_state, ("head", "tail"), axis=0, tiled=True),
    )
    for bucket in range(2):
        if bucket == 1:
            tail_table, tail_state = passed_along((tail_table, tail_state), "tail", 1)
        rel_bf = full_table.astype(jnp.bfloat16)
        rel_index = relation_ids[bucket]
        head_table, head_state, tail_table, tail_state, head_vecs, edge_grad = score_bucket(
            head_table,
            head_state,
            tail_table,
            tail_state,
            rel_bf,
            head_rows[bucket],
            tail_rows[bucket],
            negatives[bucket],
            rel_index,
            block_counts[bucket, 0],
        )
        grad_total = lax.psum(
            relation_term(head_vecs, edge_grad, rel_index, rel_bf.shape[0]), ("head", "tail")
        )
        full_table, full_state = relation_adagrad(full_table, full_state, grad_total)
    relations = lax.dynamic_slice_in_dim(
        full_table, lax.axis_index(("head", "tail")) * own_rows, own_rows, 0
    )
    return (head_table, tail_table, relations)


def solution(mesh):
    in_specs = (
        P(("head", "tail"), None),
        P(("head", "tail")),
        P(("head", "tail"), None),
        P(("head", "tail")),
        P(("head", "tail"), None),
        P(("head", "tail"), None),
        P(None, ("head", "tail")),
        P(None, ("head", "tail")),
        P(None, ("head", "tail"), None),
        P(None, ("head", "tail")),
        P(None, ("head", "tail")),
    )
    out_specs = (P(("head", "tail"), None), P(("head", "tail"), None), P(("head", "tail"), None))
    return jax.shard_map(shards, mesh=mesh, in_specs=in_specs, out_specs=out_specs, check_vma=False)
```

profile of v0, /device:TPU:0, one launch (start us, length us, event | category | flops | bytes accessed | tf_op | source)
XLA Modules:
  0.0 470.0 jit_solution(6722956914980398611)
XLA Ops:
  7.2 0.7 all-gather.3.cloned.1.call-update
  7.9 0.7 all-gather.5.cloned.1.call-update
  8.7 0.6 compare_and_fusion
  9.3 0.8 fusion.45
  10.1 0.8 slice_bitcast_fusion
  10.8 0.7 fusion.43
  11.5 1.3 fusion.47
  12.8 0.8 compare_select_fusion.3
  13.6 0.8 compare_select_fusion.1
  15.0 4.0 gather_fusion.2
  19.0 2.2 gather_fusion.3
  21.8 0.6 compare_convert_fusion.1
  22.4 0.6 pad_clamp_fusion.3
  23.1 1.6 gather_fusion
  25.5 0.6 pad_clamp_fusion.1
  26.1 7.6 %gather_fusion.8 = bf16[1024,4,128]{2,1,0:T(4,128)(2,1)} fusion(bf16[4,128,512]{1,0,2:T(4,128)(2,1)S(1)} %copy.16, s32[1024]{0:T(1024)S(1)} %fusion.41), kind=kCustom, calls=%fused_computation.clone | custom fusion | bytes 2101248 | tf_op jit(solution)/shard_map/jit(_take)/gather | solution.py:84
  33.7 1.1 compare_convert_fusion
  35.7 34.6 %all-gather.3.cloned.1.call-done = f32[1024,512]{1,0:T(8,128)} async-done(((f32[32,512]{1,0:T(8,128)}), f32[1024,512]{1,0:T(8,128)}) %all-gather.3.cloned.1.call-update) | async-done | bytes 2097168 | tf_op jit(solution)/shard_map/all_gather | solution.py:105
  70.3 1.7 convert_element_type.96
  72.0 2.0 gather_fusion.1
  74.0 2.5 fusion.19
  76.5 1.2 fusion.15
  78.2 1.8 fusion.49
  80.0 4.7 scatter_custom_fusion
  84.9 0.8 copy-done.5
  85.7 0.7 sqrt_add_fusion.3
  86.4 1.4 divide_subtract_fusion.4
  87.8 1.7 gather_fusion.4
  89.9 7.6 %gather_fusion.9 = bf16[1024,4,128]{2,1,0:T(4,128)(2,1)} fusion(bf16[4,128,512]{1,0,2:T(4,128)(2,1)S(1)} %copy.19, s32[1024]{0:T(1024)S(1)} %fusion.41), kind=kCustom, calls=%fused_computation.1.clone | custom fusion | bytes 2101248 | tf_op jit(solution)/shard_map/jit(_take)/gather | solution.py:84
  97.5 6.1 %select_bitcast_fusion = (bf16[4,128,1024]{1,0,2:T(4,128)(2,1)}, bf16[4,128,1024]{1,0,2:T(4,128)(2,1)S(1)}) fusion(bf16[1024,4,128]{2,1,0:T(4,128)(2,1)} %gather_fusion.9, pred[1024]{0:T(1024)(128)(4,1)} %compare_and_fusion, bf16[1024,4,128]{2,1,0:T(4,128)(2,1)} %gather_fusion.8), kind=kLoop, calls=%fused_computation.56 | loop fusion | flops 1048576 | bytes 4195328 | tf_op jit(solution)/shard_map/jit(_take)/select_n | solution.py:84
  103.6 3.2 convolution_bitcast_fusion.1
  106.9 7.9 %copy.26 = bf16[1024,4,512]{2,1,0:T(4,128)(2,1)} copy(bf16[1024,4,512]{0,2,1:T(8,128)(2,1)} %convolution_bitcast_fusion.1) | data formatting | bytes 8388608 | tf_op jit(solution)/shard_map/bek,bej->kbj/transpose | solution.py:85
  114.8 4.5 fusion.2
  119.3 1.5 copy.51
  120.8 1.1 convert_multiply_fusion.2
  121.9 4.5 scatter_custom_fusion.1
  126.5 2.4 fusion.50
  128.8 4.9 %scatter_fusion = f32[512,512]{1,0:T(8,128)S(1)} fusion(f32[512,512]{1,0:T(8,128)S(1)} %scatter_custom_fusion.1, s32[512]{0:T(512)S(1)} %bitcast.116, f32[512,512]{1,0:T(8,128)} %bitcast.107), kind=kCustom, calls=%fused_computation.12 | custom fusion | flops 262144 | bytes 3147776 | tf_op jit(solution)/shard_map/scatter-add | solution.py:75
  133.9 1.2 divide_subtract_fusion.3
  135.1 1.4 collective-permute-start
  136.5 0.7 collective-permute-start.1
  137.2 134.6 %all-reduce.3.cloned.1.call-done = f32[1024,512]{1,0:T(8,128)} async-done(((f32[1024,512]{1,0:T(8,128)}), f32[1024,512]{1,0:T(8,128)}) %all-reduce.3.cloned.1.call-update) | async-done | bytes 2097168 | tf_op jit(solution)/shard_map/psum | solution.py:125
  271.9 5.8 %fusion.46 = (bf16[1024,512]{1,0:T(8,128)(2,1)S(1)}, f32[1024,512]{1,0:T(8,128)}, f32[1024,512]{1,0:T(8,128)}) fusion(f32[1024,512]{1,0:T(8,128)} %all-gather.3.cloned.1.call-done, f32[1024,512]{1,0:T(8,128)} %all-reduce.3.cloned.1.call-done, f32[1024,512]{1,0:T(8,128)} %all-gather.5.cloned.1.call-done), kind=kLoop, calls=%fused_computation.129 | loop fusion | flops 3670016 | bytes 11534336 | tf_op jit(solution)/shard_map/convert_element_type | solution.py:111
  277.7 2.1 gather_fusion.5
  279.8 2.2 convolution_convert_fusion
  282.1 1.6 gather_fusion.6
  283.9 2.2 gather_fusion.7
  286.2 1.4 fusion.16
  287.6 1.4 fusion.52
  289.0 1.3 convert_multiply_fusion
  290.3 1.8 fusion.51
  292.1 4.5 scatter_custom_fusion.3
  296.8 0.8 copy-done.4
  297.6 4.8 %scatter_custom_fusion.4 = f32[512,512]{1,0:T(8,128)S(1)} fusion(s32[512]{0:T(512)} %bitcast.119, f32[512,512]{1,0:T(8,128)} %bitcast.115, f32[]{:T(128)} %constant.72.clone.1), kind=kCustom, calls=%fused_computation.66 | custom fusion | flops 262144 | bytes 1049088 | tf_op jit(solution)/shard_map/scatter-add | solution.py:74
  302.3 4.6 convolution_bitcast_fusion
  307.0 7.9 %copy.36 = bf16[1024,4,512]{2,1,0:T(4,128)(2,1)} copy(bf16[1024,4,512]{0,2,1:T(8,128)(2,1)} %convolution_bitcast_fusion) | data formatting | bytes 8388608 | tf_op jit(solution)/shard_map/bek,bej->kbj/transpose | solution.py:85
  314.9 5.8 %fusion = f32[1024,1,512]{2,1,0:T(1,128)} fusion(bf16[1024,4,512]{2,1,0:T(4,128)(2,1)} %copy.36, pred[1024,4,1]{1,0,2:T(32,128)(4,1)S(1)} %get-tuple-element.9), kind=kOutput, calls=%fused_computation.22 | convolution fusion | flops 4194304 | bytes 6295552 | tf_op jit(solution)/shard_map/kb,kbj->kj/dot_general | solution.py:87
  320.7 4.6 scatter_fusion.1
  325.5 3.1 copy.50
  328.6 0.6 copy-done.18
  329.3 2.4 divide_subtract_fusion.2
  331.7 1.2 divide_subtract_fusion.1
  332.9 128.5 %all-reduce.5.cloned.1.call-done = f32[1024,512]{1,0:T(8,128)} async-done(((f32[1024,512]{1,0:T(8,128)}), f32[1024,512]{1,0:T(8,128)}) %all-reduce.5.cloned.1.call-update) | async-done | bytes 2097168 | tf_op jit(solution)/shard_map/psum | solution.py:125
  461.4 1.6 dynamic-slice_subtract_fusion
  (87 shorter events, 4.9 us)
Async XLA Ops:
  7.2 63.1 %all-gather.3.cloned.1.call-start = ((), (), s32[]{:S(2)}) async-start(), calls=%async_computation | async-start | bytes 2162688 | tf_op jit(solution)/shard_map/all_gather | solution.py:105
  7.9 129.3 %all-gather.5.cloned.1.call-start = ((), (), s32[]{:S(2)}) async-start(), calls=%async_computation.2 | async-start | bytes 2162688 | tf_op jit(solution)/shard_map/all_gather | solution.py:106
  8.6 263.2 %all-reduce.3.cloned.1.call-start = ((), (), s32[]{:S(2)}) async-start(), calls=%async_computation.1 | async-start | bytes 4194304 | tf_op jit(solution)/shard_map/psum | solution.py:125
  13.6 1.4 copy-start.22
  13.6 8.9 %copy-start.20 = (s32[512,1]{0,1:T(1,128)}, s32[512,1]{0,1:T(1,128)S(1)}, u32[]{:S(2)}) copy-start(s32[512,1]{0,1:T(1,128)S(1)} %get-tuple-element.17) | copy-start | bytes 6148
  14.4 0.6 copy-start.21
  14.4 11.2 %copy-start.19 = (s32[512,1]{0,1:T(1,128)}, s32[512,1]{0,1:T(1,128)S(1)}, u32[]{:S(2)}) copy-start(s32[512,1]{0,1:T(1,128)S(1)} %get-tuple-element.13) | copy-start | bytes 6148
  15.0 4.0 copy-start
  19.0 2.2 copy-start.24
  19.0 4.1 copy-start.1
  22.4 54.0 %copy-start.27 = (f32[4]{0:T(128)}, f32[4]{0:T(128)S(1)}, u32[]{:S(2)}) copy-start(f32[4]{0:T(128)S(1)} %compare_convert_fusion.1) | copy-start | bytes 52
  24.6 11.0 %copy-start.6 = (bf16[512,512]{1,0:T(8,128)(2,1)}, bf16[512,512]{1,0:T(8,128)(2,1)S(1)}, u32[]{:S(2)}) copy-start(bf16[512,512]{1,0:T(8,128)(2,1)S(1)} %gather_fusion) | copy-start | bytes 1572868
  74.0 2.5 copy-start.14
  74.0 3.8 copy-start.7
  76.5 3.6 copy-start.8
  76.5 1.8 copy-start.3
  78.2 1.8 copy-start.11
  84.7 1.0 copy-start.5
  89.6 14.1 %copy-start.10 = (bf16[512,512]{1,0:T(8,128)(2,1)}, bf16[512,512]{1,0:T(8,128)(2,1)S(1)}, u32[]{:S(2)}) copy-start(bf16[512,512]{1,0:T(8,128)(2,1)S(1)} %gather_fusion.4) | copy-start | bytes 1572868
  97.5 6.2 %copy-start.12 = (bf16[4,128,512]{2,1,0:T(8,128)(2,1)S(1)}, bf16[4,128,512]{2,1,0:T(8,128)(2,1)}, u32[]{:S(2)}) copy-start(bf16[4,128,512]{2,1,0:T(8,128)(2,1)} %copy-done.11) | copy-start | bytes 1572868
  119.3 1.5 copy-start.9
  126.4 2.4 copy-start.17
  126.4 335.0 %all-reduce.5.cloned.1.call-start = ((), (), s32[]{:S(2)}) async-start(), calls=%async_computation.3 | async-start | bytes 4194304 | tf_op jit(solution)/shard_map/psum | solution.py:125
  128.8 5.0 %copy-start.25 = (f32[512]{0:T(512)S(1)}, f32[512]{0:T(512)}, u32[]{:S(2)}) copy-start(f32[512]{0:T(512)} %param.16) | copy-start | bytes 6148
  133.7 2.8 copy-start.23
  135.1 147.0 %collective-permute-start = (f32[512,512]{1,0:T(8,128)}, f32[512,512]{1,0:T(8,128)S(1)}, u32[]{:S(2)}, u32[]{:S(2)}) collective-permute-start(f32[512,512]{1,0:T(8,128)} %divide_subtract_fusion.3), channel_id=1, source_target_pairs={{0,1},{1,2},{2,3},{3,4},{4,5},{5,6},{6,7},{7,0},{8,9},{9,10},{10,1... | collective-permute-start | bytes 3145736 | tf_op jit(solution)/shard_map/ppermute | solution.py:13
  136.5 192.1 %collective-permute-start.1 = (f32[512]{0:T(512)S(1)}, f32[512]{0:T(512)S(1)}, u32[]{:S(2)}, u32[]{:S(2)}) collective-permute-start(f32[512]{0:T(512)S(1)} %get-tuple-element.5), channel_id=1, source_target_pairs={{0,1},{1,2},{2,3},{3,4},{4,5},{5,6},{6,7},{7,0},{8,9},{9,10},{10,1... | collective-permute-start | bytes 6152 | tf_op jit(solution)/shard_map/ppermute | solution.py:13
  279.8 2.2 copy-start.16
  282.0 1.8 copy-start.26
  286.2 2.9 copy-start.15
  287.6 2.7 copy-start.2
  290.3 1.8 copy-start.13
  296.6 1.0 copy-start.4
  328.6 0.7 copy-start.18
Sparse Core Ops, SparseCore 0:
  11.0 59.2 all-gather.2
  73.2 55.3 all-gather.4
  134.0 137.8 all-reduce.2
  328.7 132.6 all-reduce.4
where the time goes:
time: 479 us; the launch traced here: 470 us
  waiting for transfers between devices  299 us (62%)
  other arithmetic  60.2 us (13%)
  local copies, waits for them, and re-layouts  59.2 us (12%)
  matrix products  34.4 us (7%)
  between operations  14.6 us (3%)
    psum x2, waiting for transfers between devices, shards(): lax.psum(relation_term(head_vecs, edge_grad, rel_index, rel_bf.shape[0]),...  263 us
    all_gather x1, waiting for transfers between devices, shards(): lax.all_gather(relations, ('head', 'tail'), axis=0, tiled=True)  34.6 us
    transpose x2, local copies, waits for them, and re-layouts, relation_term(): jnp.einsum('bek,bej->kbj', columns, edge_grad, preferred_element_type=jnp...  15.7 us
    gather x2, local copies, waits for them, and re-layouts, relation_term(): columns = jnp.take(head_vecs, row_ids % model_width, axis=2)  15.2 us
    dot_general x2, matrix products, relation_term(): return jnp.einsum('kb,kbj->kj', select, per_block)  10.3 us
  transfers between devices with their start and end apart: 6, of which 3 were waited for; matrix products, arithmetic and copies ran while one was open for 32% of the time, Pallas kernels for 0%

commit v1 on v0

v1 whole, which is shorter than its diff:
```python
import functools

import jax
import jax.numpy as jnp
import numpy as np
from jax import lax
from jax.experimental import pallas as pl
from jax.experimental.pallas import tpu as pltpu
from jax.sharding import PartitionSpec as P

RATE_ROWS = 0.2
RATE_RELATIONS = 0.05
EPSILON = 1e-06
AXES = ("head", "tail")
F32, BF16 = jnp.float32, jnp.bfloat16
ROWS, COLS = 0, 1
PACK_ROWS = 16
VMEM_LIMIT = 24 * 1024 * 1024
VMEM = pl.BlockSpec(memory_space=pltpu.VMEM)
SMEM = pl.BlockSpec(memory_space=pltpu.SMEM)


def dot(a, b, contract_a, contract_b):
    return lax.dot_general(
        a, b, (((contract_a,), (contract_b,)), ((), ())), preferred_element_type=F32
    )


def to_column(row):
    return jnp.broadcast_to(row, (128, row.shape[1])).T


def spread(column, width):
    return jnp.concatenate([column] * (width // column.shape[1]), axis=1)


def adagrad_rows(table, state_row, gradient):
    width = gradient.shape[1]
    mean = jnp.sum(gradient * gradient, axis=1, keepdims=True) * (1.0 / width)
    state = to_column(state_row) + mean
    factor = RATE_ROWS / (jnp.sqrt(state) + EPSILON)
    return table - gradient * spread(factor, width), state


def one_hot_rows(index_row, rows):
    n = index_row.shape[1]
    return (lax.broadcasted_iota(jnp.int32, (rows, n), 0) == index_row).astype(F32).astype(BF16)


def by_relation(x, rel_ref, k, blocks, relation):
    size = x.shape[0] // blocks
    parts = []
    for b in range(blocks):
        part = x[b * size : (b + 1) * size]
        parts.append(jnp.where(rel_ref[k, b] == relation, part, jnp.zeros_like(part)))
    return jnp.concatenate(parts, axis=0)


def restore_relations(nat_ref, lo_ref, hi_ref, rel_s):
    half = lo_ref.shape[0]
    own = 2 * half // nat_ref.shape[0]
    if own % PACK_ROWS:
        rel_s[:half] = lo_ref[...]
        rel_s[half:] = hi_ref[...]
        return
    for part, ref in enumerate((lo_ref, hi_ref)):
        for j in range(half // own):
            block = nat_ref[part * (half // own) + j]
            rel_s[pl.ds(pl.multiple_of(block * own, own), own)] = ref[j * own : (j + 1) * own]


def prepare_kernel(
    head_ref, tail_ref, hrows_ref, trows_ref, neg_ref, h_ref, t_ref, tcol_ref, cnt_ref
):
    buckets = hrows_ref.shape[0]
    blocks, nneg = neg_ref.shape[1:]
    pick = one_hot_rows(hrows_ref[0:1, :], head_ref.shape[0])
    h_ref[...] = dot(pick, head_ref[...].astype(BF16), ROWS, ROWS).astype(BF16)
    t_ref[...] = tail_ref[...].astype(BF16)
    ones = jnp.ones((8, nneg), BF16)
    for k in range(buckets):
        tcol_ref[k] = to_column(trows_ref[k : k + 1, :].astype(F32))
        for b in range(blocks):
            hot = one_hot_rows(neg_ref[k, b : b + 1, :], tail_ref.shape[0])
            cnt_ref[k, b : b + 1, :] = dot(ones, hot, COLS, COLS)[0:1, :]


def score_kernel(
    k, nneg, nat_ref, live_ref, rel_ref, lo_ref, hi_ref, h_ref, t_ref, tcol_ref, cnt_ref,
    keep_ref, send_ref, w_ref, u_ref, gu_ref, rel_s, grad_s,
):
    edges, width = h_ref.shape
    blocks, rows = cnt_ref.shape[1:]
    size = edges // blocks
    relations = rel_s.shape[0] // width
    restore_relations(nat_ref, lo_ref, hi_ref, rel_s)
    masked = [by_relation(h_ref[...], rel_ref, k, blocks, r) for r in range(relations)]
    u = dot(masked[0], rel_s[0:width], COLS, ROWS)
    for r in range(1, relations):
        u = u + dot(masked[r], rel_s[r * width : (r + 1) * width], COLS, ROWS)
    u = u.astype(BF16)
    u_ref[...] = u
    tails = t_ref[0:rows]
    score = dot(u, tails, COLS, COLS)
    row_id = lax.broadcasted_iota(jnp.int32, (size, rows), 1).astype(F32)
    for b in range(blocks):
        part = slice(b * size, (b + 1) * size)
        live = jnp.where(live_ref[k, 0] > b, 1.0, 0.0)
        half_tanh = 0.5 * jnp.tanh(0.5 * score[part])
        negative = ((0.5 + half_tanh) * (live / nneg)).astype(BF16).astype(F32)
        positive = (0.5 - half_tanh) * live
        is_tail = spread(tcol_ref[k, part], rows) == row_id
        weight = cnt_ref[k, b : b + 1, :] * negative - jnp.where(is_tail, positive, 0.0)
        w_ref[part] = weight.astype(BF16)
    gu = dot(w_ref[...], tails, COLS, ROWS).astype(BF16)
    gu_ref[...] = gu
    for r in range(relations):
        grad_s[r * width : (r + 1) * width] = dot(masked[r], gu, ROWS, ROWS)
    half = keep_ref.shape[0]
    own = 2 * half // nat_ref.shape[0]
    if own % PACK_ROWS:
        keep_ref[...] = grad_s[:half].astype(BF16)
        send_ref[...] = grad_s[half:].astype(BF16)
        return
    for part, ref in enumerate((keep_ref, send_ref)):
        for j in range(half // own):
            block = nat_ref[part * (half // own) + j]
            rows_of = pl.ds(pl.multiple_of(block * own, own), own)
            ref[j * own : (j + 1) * own] = grad_s[rows_of].astype(BF16)


def tail_kernel(w_ref, u_ref, table_ref, state_ref, out_ref):
    rows, width = table_ref.shape
    gradient = dot(w_ref[...], u_ref[...], ROWS, ROWS)
    table, state = adagrad_rows(table_ref[...], state_ref[...], gradient)
    out_ref[0:rows] = table.astype(BF16)
    state_row = state.T[0:1, :]
    high = state_row.astype(BF16).astype(F32)
    row_id = lax.broadcasted_iota(jnp.int32, (PACK_ROWS, width), 0)
    packed = jnp.where(row_id == 0, high, jnp.where(row_id == 1, state_row - high, 0.0))
    out_ref[rows : rows + PACK_ROWS] = packed.astype(BF16)


def last_tail_kernel(w_ref, u_ref, packed_ref, out_ref):
    rows = out_ref.shape[0]
    gradient = dot(w_ref[...], u_ref[...], ROWS, ROWS)
    packed = packed_ref[rows : rows + PACK_ROWS].astype(F32)
    state_row = packed[0:1, :] + packed[1:2, :]
    out_ref[...] = adagrad_rows(packed_ref[0:rows].astype(F32), state_row, gradient)[0]


def head_kernel(
    k, blocks, nat_ref, rel_ref, lo_ref, hi_ref, gu_ref, hrows_ref, table_ref, state_ref, *rest
):
    out_ref, rel_s = rest[0], rest[-1]
    rows, width = table_ref.shape
    relations = rel_s.shape[0] // width
    restore_relations(nat_ref, lo_ref, hi_ref, rel_s)
    gu = gu_ref[...]
    terms = None
    for r in range(relations):
        part = by_relation(gu, rel_ref, k, blocks, r)
        term = dot(part, rel_s[r * width : (r + 1) * width], COLS, COLS)
        terms = term if terms is None else terms + term
    hot = one_hot_rows(hrows_ref[k : k + 1, :], rows)
    gradient = dot(hot, terms.astype(BF16), COLS, ROWS)
    table, state = adagrad_rows(table_ref[...], state_ref[...], gradient)
    out_ref[...] = table
    if len(rest) > 2:
        state_out_ref, h_ref = rest[1:3]
        state_out_ref[...] = state.T[0:1, :]
        pick = one_hot_rows(hrows_ref[k + 1 : k + 2, :], rows)
        h_ref[...] = dot(pick, table.astype(BF16), ROWS, ROWS).astype(BF16)


def call(kernel, outs, smem, scratch, flops, *args):
    outs = [jax.ShapeDtypeStruct(shape, kind) for shape, kind in outs]
    moved = sum(a.size * a.dtype.itemsize for a in (*args, *outs))
    return pl.pallas_call(
        kernel,
        out_shape=outs,
        in_specs=[SMEM] * smem + [VMEM] * (len(args) - smem),
        out_specs=[VMEM] * len(outs),
        scratch_shapes=scratch,
        compiler_params=pltpu.CompilerParams(vmem_limit_bytes=VMEM_LIMIT),
        cost_estimate=pl.CostEstimate(flops=flops, bytes_accessed=moved, transcendentals=0),
    )(*args)


class Exchange:
    def __init__(self, heads, tails):
        self.devices = heads * tails
        cores = [tails] if heads > 1 else []
        heads_left = [tails << i for i in range(1, heads.bit_length() - 1)]
        self.masks = cores + heads_left + [1 << i for i in range(tails.bit_length() - 1)]
        bits = len(self.masks)
        places = [
            sum(m for i, m in enumerate(self.masks) if j >> (bits - 1 - i) & 1)
            for j in range(self.devices)
        ]
        slots = np.zeros(self.devices, np.int32)
        slots[places] = np.arange(self.devices)
        me = lax.axis_index(AXES)
        self.block_of_slot = jnp.asarray(places, jnp.int32) ^ me
        self.slot_of_block = jnp.asarray(slots)[jnp.arange(self.devices, dtype=jnp.int32) ^ me]

    def swap(self, x, mask):
        return lax.ppermute(x, AXES, [(i, i ^ mask) for i in range(self.devices)])

    def reduce_scatter(self, keep, send):
        if (2 * keep.shape[0] // self.devices) % PACK_ROWS:
            both = jnp.concatenate([keep, send])
            both = both.reshape(self.devices, -1, both.shape[1])[self.block_of_slot]
            keep, send = jnp.split(both.reshape(-1, both.shape[2]), 2)
        for i, mask in enumerate(self.masks):
            got = self.swap(send, mask)
            half = keep.shape[0] // 2
            if i + 1 == len(self.masks):
                return keep.astype(F32) + got.astype(F32)
            send = (keep[half:].astype(F32) + got[half:].astype(F32)).astype(BF16)
            keep = (keep[:half].astype(F32) + got[:half].astype(F32)).astype(BF16)

    def all_gather(self, own):
        rows = own.shape[0]
        for mask in self.masks[:0:-1]:
            own = jnp.concatenate([own, self.swap(own, mask)])
        lo, hi = own, self.swap(own, self.masks[0])
        if rows % PACK_ROWS:
            both = jnp.concatenate([lo, hi]).reshape(self.devices, rows, -1)[self.slot_of_block]
            lo, hi = jnp.split(both.reshape(self.devices * rows, -1), 2)
        return lo, hi


def shards(
    head_table,
    head_state,
    tail_table,
    tail_state,
    relations,
    relation_state,
    head_rows,
    tail_rows,
    negatives,
    relation_ids,
    block_counts,
):
    heads, tails = lax.axis_size("head"), lax.axis_size("tail")
    exchange = Exchange(heads, tails)
    nat = exchange.block_of_slot
    rows, width = tail_table.shape
    edges = head_rows.shape[1]
    blocks, nneg = negatives.shape[1:]
    all_rows = relations.shape[0] * exchange.devices
    half = all_rows // 2
    square = 2 * rows * edges * width

    own_bf = relations.astype(BF16)
    head_vecs, tail_vecs, tail_col, counts = call(
        prepare_kernel,
        [
            ((edges, width), BF16),
            ((rows, width), BF16),
            ((2, edges, 128), F32),
            ((2, blocks, rows), F32),
        ],
        0, [], square,
        head_table, tail_table, head_rows, tail_rows, negatives,
    )
    head_state = head_state.reshape(1, -1)
    tail_state = tail_state.reshape(1, -1)
    for k in range(2):
        lo, hi = exchange.all_gather(own_bf)
        keep, send, weights, projected, edge_grad = call(
            functools.partial(score_kernel, k, float(nneg)),
            [
                ((half, width), BF16),
                ((half, width), BF16),
                ((edges, rows), BF16),
                ((edges, width), BF16),
                ((edges, width), BF16),
            ],
            3, [pltpu.VMEM((all_rows, width), BF16), pltpu.VMEM((all_rows, width), F32)], 6 * square,
            nat, block_counts, relation_ids, lo, hi, head_vecs, tail_vecs, tail_col, counts,
        )
        rel_scratch = [pltpu.VMEM((all_rows, width), BF16)]
        head_args = (nat, relation_ids, lo, hi, edge_grad, head_rows, head_table, head_state)
        if k == 0:
            (packed,) = call(
                tail_kernel, [((rows + PACK_ROWS, width), BF16)], 0, [], square,
                weights, projected, tail_table, tail_state,
            )
            tail_vecs = lax.ppermute(packed, "tail", [(i, (i + 1) % tails) for i in range(tails)])
            head_table, head_state, head_vecs = call(
                functools.partial(head_kernel, k, blocks),
                [(head_table.shape, F32), (head_state.shape, F32), ((edges, width), BF16)],
                2, rel_scratch, 4 * square, *head_args,
            )
        else:
            (tail_table,) = call(
                last_tail_kernel, [((rows, width), F32)], 0, [], square,
                weights, projected, tail_vecs,
            )
            (head_table,) = call(
                functools.partial(head_kernel, k, blocks), [(head_table.shape, F32)],
                2, rel_scratch, 3 * square, *head_args,
            )
        grad = exchange.reduce_scatter(keep, send)
        relation_state = relation_state + grad * grad
        relations = relations - RATE_RELATIONS * grad / (jnp.sqrt(relation_state) + EPSILON)
        own_bf = relations.astype(BF16)
    return (head_table, tail_table, relations)


def solution(mesh):
    both = P(AXES, None)
    in_specs = (
        both,
        P(AXES),
        both,
        P(AXES),
        both,
        both,
        P(None, AXES),
        P(None, AXES),
        P(None, AXES, None),
        P(None, AXES),
        P(None, AXES),
    )
    return jax.shard_map(
        shards, mesh=mesh, in_specs=in_specs, out_specs=(both, both, both), check_vma=False
    )
```

time: 479 us -> 119 us (0.25); the launches traced: 470 us -> 119 us
  waiting for transfers between devices: 299 us -> 68.9 us
  other arithmetic: 60.2 us -> 2.29 us
  local copies, waits for them, and re-layouts: 59.2 us -> 3.96 us
  matrix products: 34.4 us -> 0 us
  starting transfers between devices: 2.27 us -> 28.4 us
  Pallas kernels: 0 us -> 14.3 us
  between operations: 14.6 us -> 0.91 us
    psum x2 -> x0, waiting for transfers between devices: 263 us -> none  [shards(): lax.psum(relation_term(head_vecs, edge_grad, rel_index, rel_bf.shape[0]),...]
    ppermute x2 -> x21, waiting for transfers between devices: 0.01 us -> 68.9 us  [the longest x20 68.9 us: swap(): return lax.ppermute(x, AXES, [(i, i ^ mask) for i in range(self.devices)])]
    all_gather x2 -> x0, waiting for transfers between devices: 34.6 us -> none  [the longest x1 34.6 us: shards(): lax.all_gather(relations, ('head', 'tail'), axis=0, tiled=True)]
    dot_general x14 -> x0, matrix products: 34.4 us -> none  [the longest x2 10.3 us: relation_term(): return jnp.einsum('kb,kbj->kj', select, per_block)]
    gather x10 -> x0, local copies, waits for them, and re-layouts: 32.6 us -> none  [the longest x2 15.2 us: relation_term(): columns = jnp.take(head_vecs, row_ids % model_width, axis=2)]
    scatter-add x6 -> x0, other arithmetic: 28 us -> none  [the longest x2 9.52 us: score_bucket(): tail_grad = tail_grad.at[neg_index.reshape(-1)].add(neg_terms)]
    ppermute x2 -> x21, starting transfers between devices: 2.12 us -> 28.4 us  [the longest x20 28 us: swap(): return lax.ppermute(x, AXES, [(i, i ^ mask) for i in range(self.devices)])]
    transpose x2 -> x0, local copies, waits for them, and re-layouts: 15.7 us -> none  [relation_term(): jnp.einsum('bek,bej->kbj', columns, edge_grad, preferred_element_type=jnp...]
  transfers between devices with their start and end apart: 6 -> 21, of which waited for: 3 -> 18; matrix products, arithmetic and copies ran while one was open for 32% -> 0% of each run, Pallas kernels for 0% -> 7%
where the time goes in v1:
time: 119 us
  waiting for transfers between devices  68.9 us (58%)
  starting transfers between devices  28.4 us (24%)
  Pallas kernels  14.3 us (12%)
  local copies, waits for them, and re-layouts  3.96 us (3%)
  other arithmetic  2.29 us (2%)
    ppermute x20, waiting for transfers between devices, swap(): return lax.ppermute(x, AXES, [(i, i ^ mask) for i in range(self.devices)])  68.9 us
    ppermute x20, starting transfers between devices, swap(): return lax.ppermute(x, AXES, [(i, i ^ mask) for i in range(self.devices)])  28 us
    pallas_call x7, Pallas kernels, call(): pl.pallas_call(kernel, out_shape=outs, in_specs=[SMEM] * smem + [VMEM] *...  14.3 us
    unnamed x33, local copies, waits for them, and re-layouts  3.92 us
  transfers between devices with their start and end apart: 21, of which 18 were waited for; matrix products, arithmetic and copies ran while one was open for 0% of the time, Pallas kernels for 7%

profile of v1, /device:TPU:0, one launch (start us, length us, event | category | flops | bytes accessed | tf_op | source)
XLA Modules:
  0.0 118.7 jit_solution(524737537626138546)
XLA Ops:
  0.6 0.9 constant_dynamic-update-slice_fusion.4
  1.6 4.0 %collective-permute-start = (bf16[32,512]{1,0:T(8,128)(2,1)S(1)}, bf16[32,512]{1,0:T(8,128)(2,1)S(1)}, u32[]{:S(2)}, u32[]{:S(2)}) collective-permute-start(bf16[32,512]{1,0:T(8,128)(2,1)S(1)} %get-tuple-element.40), channel_id=1, source_target_pairs={{0,4},{1,5},{2,6},{3,7},{4,0},{5,1},{6,2},{7,3},{8,12},{9,13},{10,... | collective-permute-start | bytes 98312 | tf_op jit(solution)/shard_map/ppermute | solution.py:208
  5.6 2.2 %collective-permute-done = bf16[32,512]{1,0:T(8,128)(2,1)S(1)} collective-permute-done((bf16[32,512]{1,0:T(8,128)(2,1)S(1)}, bf16[32,512]{1,0:T(8,128)(2,1)S(1)}, u32[]{:S(2)}, u32[]{:S(2)}) %collective-permute-start) | collective-permute-done | bytes 32800 | tf_op jit(solution)/shard_map/ppermute | solution.py:208
  7.9 1.6 %collective-permute-start.1 = (bf16[64,512]{1,0:T(8,128)(2,1)S(1)}, bf16[64,512]{1,0:T(8,128)(2,1)S(1)}, u32[]{:S(2)}, u32[]{:S(2)}) collective-permute-start(bf16[64,512]{1,0:T(8,128)(2,1)S(1)} %pad_maximum_fusion.4), channel_id=1, source_target_pairs={{0,2},{1,3},{2,0},{3,1},{4,6},{5,7},{6,4},{7,5},{8,10},{9,11},{10,... | collective-permute-start | bytes 196616 | tf_op jit(solution)/shard_map/ppermute | solution.py:208
  9.4 2.7 %collective-permute-done.1 = bf16[64,512]{1,0:T(8,128)(2,1)S(1)} collective-permute-done((bf16[64,512]{1,0:T(8,128)(2,1)S(1)}, bf16[64,512]{1,0:T(8,128)(2,1)S(1)}, u32[]{:S(2)}, u32[]{:S(2)}) %collective-permute-start.1) | collective-permute-done | bytes 65568 | tf_op jit(solution)/shard_map/ppermute | solution.py:208
  12.1 1.8 %collective-permute-start.2 = (bf16[128,512]{1,0:T(8,128)(2,1)S(1)}, bf16[128,512]{1,0:T(8,128)(2,1)S(1)}, u32[]{:S(2)}, u32[]{:S(2)}) collective-permute-start(bf16[128,512]{1,0:T(8,128)(2,1)S(1)} %pad_maximum_fusion.2), channel_id=1, source_target_pairs={{0,1},{1,0},{2,3},{3,2},{4,5},{5,4},{6,7},{7,6},{8,9},{9,8},{10,11... | collective-permute-start | bytes 393224 | tf_op jit(solution)/shard_map/ppermute | solution.py:208
  13.9 3.3 %collective-permute-done.2 = bf16[128,512]{1,0:T(8,128)(2,1)S(1)} collective-permute-done((bf16[128,512]{1,0:T(8,128)(2,1)S(1)}, bf16[128,512]{1,0:T(8,128)(2,1)S(1)}, u32[]{:S(2)}, u32[]{:S(2)}) %collective-permute-start.2) | collective-permute-done | bytes 131104 | tf_op jit(solution)/shard_map/ppermute | solution.py:208
  17.2 1.8 %collective-permute-start.3 = (bf16[256,512]{1,0:T(8,128)(2,1)S(1)}, bf16[256,512]{1,0:T(8,128)(2,1)S(1)}, u32[]{:S(2)}, u32[]{:S(2)}) collective-permute-start(bf16[256,512]{1,0:T(8,128)(2,1)S(1)} %pad_maximum_fusion), channel_id=1, source_target_pairs={{0,16},{1,17},{2,18},{3,19},{4,20},{5,21},{6,22},{7,23},{8,24},{9,... | collective-permute-start | bytes 786440 | tf_op jit(solution)/shard_map/ppermute | solution.py:208
  19.0 4.6 %collective-permute-done.3 = bf16[256,512]{1,0:T(8,128)(2,1)S(1)} collective-permute-done((bf16[256,512]{1,0:T(8,128)(2,1)S(1)}, bf16[256,512]{1,0:T(8,128)(2,1)S(1)}, u32[]{:S(2)}, u32[]{:S(2)}) %collective-permute-start.3) | collective-permute-done | bytes 262176 | tf_op jit(solution)/shard_map/ppermute | solution.py:208
  23.7 0.1 collective-permute-start.4
  23.7 0.0 copy-start.5
  23.8 0.0 copy-start.4
  23.8 0.5 copy-done.11
  24.3 0.1 copy.15.live_ref
  24.4 0.0 copy-done.5
  24.4 0.0 copy-done.4
  24.4 0.0 copy-done.3
  24.5 1.2 %copy-done.1 = f32[512,512]{1,0:T(8,128)S(1)} copy-done((f32[512,512]{1,0:T(8,128)S(1)}, f32[512,512]{1,0:T(8,128)}, u32[]{:S(2)}) %copy-start.1) | copy-done | bytes 1048600
  25.7 0.7 shard_map.139
  26.4 0.7 copy-done.7
  27.1 3.0 %shard_map.140 = (bf16[512,512]{1,0:T(8,128)(2,1)S(1)}, bf16[512,512]{1,0:T(8,128)(2,1)S(1)}, bf16[512,512]{1,0:T(8,128)(2,1)S(1)}, bf16[512,512]{1,0:T(8,128)(2,1)S(1)}, bf16[512,512]{1,0:T(8,128)(2,1)S(1)}) custom-call(s32[32]{0:T(128)S(1)} %broadcast_xor_fusion.nat_ref, s32[2,1]{1,0:T(2,128)S(1)} %copy.15.live_ref, s32[2,4]{1,0:T(2,128)S(1)} %copy-done.7, ...), custom_call_target="tpu_custom_call" | custom-call | flops 1610612736 | bytes 5259432 | tf_op jit(solution)/shard_map/pallas_call | solution.py:179
  30.1 0.5 collective-permute-start.5
  30.7 1.5 %collective-permute-done.5 = bf16[512,512]{1,0:T(8,128)(2,1)S(1)} collective-permute-done((bf16[512,512]{1,0:T(8,128)(2,1)S(1)}, bf16[512,512]{1,0:T(8,128)(2,1)S(1)}, u32[]{:S(2)}, u32[]{:S(2)}) %collective-permute-start.5) | collective-permute-done | bytes 524320 | tf_op jit(solution)/shard_map/ppermute | solution.py:208
  32.2 0.1 add_convert_fusion.3
  32.4 1.8 %collective-permute-start.6 = (bf16[256,512]{1,0:T(8,128)(2,1)S(1)}, bf16[256,512]{1,0:T(8,128)(2,1)S(1)}, u32[]{:S(2)}, u32[]{:S(2)}) collective-permute-start(bf16[256,512]{1,0:T(8,128)(2,1)S(1)} %get-tuple-element.44), channel_id=1, source_target_pairs={{0,16},{1,17},{2,18},{3,19},{4,20},{5,21},{6,22},{7,23},{8,24},{9,... | collective-permute-start | bytes 786440 | tf_op jit(solution)/shard_map/ppermute | solution.py:208
  34.2 6.8 %collective-permute-done.6 = bf16[256,512]{1,0:T(8,128)(2,1)S(1)} collective-permute-done((bf16[256,512]{1,0:T(8,128)(2,1)S(1)}, bf16[256,512]{1,0:T(8,128)(2,1)S(1)}, u32[]{:S(2)}, u32[]{:S(2)}) %collective-permute-start.6) | collective-permute-done | bytes 262176 | tf_op jit(solution)/shard_map/ppermute | solution.py:208
  41.0 0.1 add_convert_fusion.7
  41.1 1.8 %collective-permute-start.7 = (bf16[128,512]{1,0:T(8,128)(2,1)S(1)}, bf16[128,512]{1,0:T(8,128)(2,1)S(1)}, u32[]{:S(2)}, u32[]{:S(2)}) collective-permute-start(bf16[128,512]{1,0:T(8,128)(2,1)S(1)} %get-tuple-element.48), channel_id=1, source_target_pairs={{0,1},{1,0},{2,3},{3,2},{4,5},{5,4},{6,7},{7,6},{8,9},{9,8},{10,11... | collective-permute-start | bytes 393224 | tf_op jit(solution)/shard_map/ppermute | solution.py:208
  42.9 3.3 %collective-permute-done.7 = bf16[128,512]{1,0:T(8,128)(2,1)S(1)} collective-permute-done((bf16[128,512]{1,0:T(8,128)(2,1)S(1)}, bf16[128,512]{1,0:T(8,128)(2,1)S(1)}, u32[]{:S(2)}, u32[]{:S(2)}) %collective-permute-start.7) | collective-permute-done | bytes 131104 | tf_op jit(solution)/shard_map/ppermute | solution.py:208
  46.2 1.6 %collective-permute-start.8 = (bf16[64,512]{1,0:T(8,128)(2,1)S(1)}, bf16[64,512]{1,0:T(8,128)(2,1)S(1)}, u32[]{:S(2)}, u32[]{:S(2)}) collective-permute-start(bf16[64,512]{1,0:T(8,128)(2,1)S(1)} %get-tuple-element.52), channel_id=1, source_target_pairs={{0,2},{1,3},{2,0},{3,1},{4,6},{5,7},{6,4},{7,5},{8,10},{9,11},{10,... | collective-permute-start | bytes 196616 | tf_op jit(solution)/shard_map/ppermute | solution.py:208
  47.8 2.7 %collective-permute-done.8 = bf16[64,512]{1,0:T(8,128)(2,1)S(1)} collective-permute-done((bf16[64,512]{1,0:T(8,128)(2,1)S(1)}, bf16[64,512]{1,0:T(8,128)(2,1)S(1)}, u32[]{:S(2)}, u32[]{:S(2)}) %collective-permute-start.8) | collective-permute-done | bytes 65568 | tf_op jit(solution)/shard_map/ppermute | solution.py:208
  50.5 2.7 %collective-permute-start.9 = (bf16[32,512]{1,0:T(8,128)(2,1)S(1)}, bf16[32,512]{1,0:T(8,128)(2,1)S(1)}, u32[]{:S(2)}, u32[]{:S(2)}) collective-permute-start(bf16[32,512]{1,0:T(8,128)(2,1)S(1)} %add_convert_fusion.14), channel_id=1, source_target_pairs={{0,4},{1,5},{2,6},{3,7},{4,0},{5,1},{6,2},{7,3},{8,12},{9,13},{10,... | collective-permute-start | bytes 98312 | tf_op jit(solution)/shard_map/ppermute | solution.py:208
  53.2 2.4 %collective-permute-done.9 = bf16[32,512]{1,0:T(8,128)(2,1)S(1)} collective-permute-done((bf16[32,512]{1,0:T(8,128)(2,1)S(1)}, bf16[32,512]{1,0:T(8,128)(2,1)S(1)}, u32[]{:S(2)}, u32[]{:S(2)}) %collective-permute-start.9) | collective-permute-done | bytes 32800 | tf_op jit(solution)/shard_map/ppermute | solution.py:208
  55.6 0.1 constant_dynamic-update-slice_fusion.9
  55.7 2.8 %collective-permute-start.10 = (bf16[32,512]{1,0:T(8,128)(2,1)S(1)}, bf16[32,512]{1,0:T(8,128)(2,1)S(1)}, u32[]{:S(2)}, u32[]{:S(2)}) collective-permute-start(bf16[32,512]{1,0:T(8,128)(2,1)S(1)} %get-tuple-element.38), channel_id=1, source_target_pairs={{0,4},{1,5},{2,6},{3,7},{4,0},{5,1},{6,2},{7,3},{8,12},{9,13},{10,... | collective-permute-start | bytes 98312 | tf_op jit(solution)/shard_map/ppermute | solution.py:208
  58.5 2.1 %collective-permute-done.10 = bf16[32,512]{1,0:T(8,128)(2,1)S(1)} collective-permute-done((bf16[32,512]{1,0:T(8,128)(2,1)S(1)}, bf16[32,512]{1,0:T(8,128)(2,1)S(1)}, u32[]{:S(2)}, u32[]{:S(2)}) %collective-permute-start.10) | collective-permute-done | bytes 32800 | tf_op jit(solution)/shard_map/ppermute | solution.py:208
  60.6 2.0 %collective-permute-start.11 = (bf16[64,512]{1,0:T(8,128)(2,1)S(1)}, bf16[64,512]{1,0:T(8,128)(2,1)S(1)}, u32[]{:S(2)}, u32[]{:S(2)}) collective-permute-start(bf16[64,512]{1,0:T(8,128)(2,1)S(1)} %pad_maximum_fusion.5), channel_id=1, source_target_pairs={{0,2},{1,3},{2,0},{3,1},{4,6},{5,7},{6,4},{7,5},{8,10},{9,11},{10,... | collective-permute-start | bytes 196616 | tf_op jit(solution)/shard_map/ppermute | solution.py:208
  62.6 2.3 %collective-permute-done.11 = bf16[64,512]{1,0:T(8,128)(2,1)S(1)} collective-permute-done((bf16[64,512]{1,0:T(8,128)(2,1)S(1)}, bf16[64,512]{1,0:T(8,128)(2,1)S(1)}, u32[]{:S(2)}, u32[]{:S(2)}) %collective-permute-start.11) | collective-permute-done | bytes 65568 | tf_op jit(solution)/shard_map/ppermute | solution.py:208
  64.9 1.8 %collective-permute-start.12 = (bf16[128,512]{1,0:T(8,128)(2,1)S(1)}, bf16[128,512]{1,0:T(8,128)(2,1)S(1)}, u32[]{:S(2)}, u32[]{:S(2)}) collective-permute-start(bf16[128,512]{1,0:T(8,128)(2,1)S(1)} %pad_maximum_fusion.3), channel_id=1, source_target_pairs={{0,1},{1,0},{2,3},{3,2},{4,5},{5,4},{6,7},{7,6},{8,9},{9,8},{10,11... | collective-permute-start | bytes 393224 | tf_op jit(solution)/shard_map/ppermute | solution.py:208
  66.7 0.7 copy-done.6
  67.3 0.7 shard_map.142
  68.0 0.3 collective-permute-start.15
  68.4 12.3 %collective-permute-done.12 = bf16[128,512]{1,0:T(8,128)(2,1)S(1)} collective-permute-done((bf16[128,512]{1,0:T(8,128)(2,1)S(1)}, bf16[128,512]{1,0:T(8,128)(2,1)S(1)}, u32[]{:S(2)}, u32[]{:S(2)}) %collective-permute-start.12) | collective-permute-done | bytes 131104 | tf_op jit(solution)/shard_map/ppermute | solution.py:208
  80.7 1.7 %collective-permute-start.13 = (bf16[256,512]{1,0:T(8,128)(2,1)S(1)}, bf16[256,512]{1,0:T(8,128)(2,1)S(1)}, u32[]{:S(2)}, u32[]{:S(2)}) collective-permute-start(bf16[256,512]{1,0:T(8,128)(2,1)S(1)} %pad_maximum_fusion.1), channel_id=1, source_target_pairs={{0,16},{1,17},{2,18},{3,19},{4,20},{5,21},{6,22},{7,23},{8,24},{9,... | collective-permute-start | bytes 786440 | tf_op jit(solution)/shard_map/ppermute | solution.py:208
  82.4 4.7 %collective-permute-done.13 = bf16[256,512]{1,0:T(8,128)(2,1)S(1)} collective-permute-done((bf16[256,512]{1,0:T(8,128)(2,1)S(1)}, bf16[256,512]{1,0:T(8,128)(2,1)S(1)}, u32[]{:S(2)}, u32[]{:S(2)}) %collective-permute-start.13) | collective-permute-done | bytes 262176 | tf_op jit(solution)/shard_map/ppermute | solution.py:208
  87.1 0.1 collective-permute-start.14
  87.2 0.6 copy-done.8
  87.8 2.2 %shard_map.141 = (f32[512,512]{1,0:T(8,128)S(1)}, f32[1,512]{1,0:T(1,128)S(1)}, bf16[512,512]{1,0:T(8,128)(2,1)S(1)}) custom-call(s32[32]{0:T(128)S(1)} %broadcast_xor_fusion.nat_ref, s32[2,4]{1,0:T(2,128)S(1)} %copy-done.7, bf16[512,512]{1,0:T(8,128)(2,1)S(1)} %constant_dynamic-update-slice_fusion.lo_ref, ...), custom_call_target="tpu_custom_call" | custom-call | flops 1073741824 | bytes 4202656 | tf_op jit(solution)/shard_map/pallas_call | solution.py:179
  90.1 3.0 %shard_map.143 = (bf16[512,512]{1,0:T(8,128)(2,1)S(1)}, bf16[512,512]{1,0:T(8,128)(2,1)S(1)}, bf16[512,512]{1,0:T(8,128)(2,1)S(1)}, bf16[512,512]{1,0:T(8,128)(2,1)S(1)}, bf16[512,512]{1,0:T(8,128)(2,1)S(1)}) custom-call(s32[32]{0:T(128)S(1)} %broadcast_xor_fusion.nat_ref, s32[2,1]{1,0:T(2,128)S(1)} %copy.15.live_ref, s32[2,4]{1,0:T(2,128)S(1)} %copy-done.7, ...), custom_call_target="tpu_custom_call" | custom-call | flops 1610612736 | bytes 5275816 | tf_op jit(solution)/shard_map/pallas_call | solution.py:179
  93.1 0.1 collective-permute-start.16
  93.2 1.9 %collective-permute-done.16 = bf16[512,512]{1,0:T(8,128)(2,1)S(1)} collective-permute-done((bf16[512,512]{1,0:T(8,128)(2,1)S(1)}, bf16[512,512]{1,0:T(8,128)(2,1)S(1)}, u32[]{:S(2)}, u32[]{:S(2)}) %collective-permute-start.16) | collective-permute-done | bytes 524320 | tf_op jit(solution)/shard_map/ppermute | solution.py:208
  95.1 0.1 add_convert_fusion.1
  95.2 1.7 %collective-permute-start.17 = (bf16[256,512]{1,0:T(8,128)(2,1)S(1)}, bf16[256,512]{1,0:T(8,128)(2,1)S(1)}, u32[]{:S(2)}, u32[]{:S(2)}) collective-permute-start(bf16[256,512]{1,0:T(8,128)(2,1)S(1)} %get-tuple-element.42), channel_id=1, source_target_pairs={{0,16},{1,17},{2,18},{3,19},{4,20},{5,21},{6,22},{7,23},{8,24},{9,... | collective-permute-start | bytes 786440 | tf_op jit(solution)/shard_map/ppermute | solution.py:208
  96.9 6.7 %collective-permute-done.17 = bf16[256,512]{1,0:T(8,128)(2,1)S(1)} collective-permute-done((bf16[256,512]{1,0:T(8,128)(2,1)S(1)}, bf16[256,512]{1,0:T(8,128)(2,1)S(1)}, u32[]{:S(2)}, u32[]{:S(2)}) %collective-permute-start.17) | collective-permute-done | bytes 262176 | tf_op jit(solution)/shard_map/ppermute | solution.py:208
  103.6 0.1 add_convert_fusion.5
  103.7 0.1 collective-permute-start.18
  103.8 5.0 %collective-permute-done.18 = bf16[128,512]{1,0:T(8,128)(2,1)S(1)} collective-permute-done((bf16[128,512]{1,0:T(8,128)(2,1)S(1)}, bf16[128,512]{1,0:T(8,128)(2,1)S(1)}, u32[]{:S(2)}, u32[]{:S(2)}) %collective-permute-start.18) | collective-permute-done | bytes 131104 | tf_op jit(solution)/shard_map/ppermute | solution.py:208
  108.8 0.1 collective-permute-start.19
  108.9 4.3 %collective-permute-done.19 = bf16[64,512]{1,0:T(8,128)(2,1)S(1)} collective-permute-done((bf16[64,512]{1,0:T(8,128)(2,1)S(1)}, bf16[64,512]{1,0:T(8,128)(2,1)S(1)}, u32[]{:S(2)}, u32[]{:S(2)}) %collective-permute-start.19) | collective-permute-done | bytes 65568 | tf_op jit(solution)/shard_map/ppermute | solution.py:208
  113.1 0.1 collective-permute-start.20
  113.2 2.9 %shard_map.144 = f32[512,512]{1,0:T(8,128)} custom-call(s32[32]{0:T(128)S(1)} %broadcast_xor_fusion.nat_ref, s32[2,4]{1,0:T(2,128)S(1)} %copy-done.7, bf16[512,512]{1,0:T(8,128)(2,1)S(1)} %constant_dynamic-update-slice_fusion.5.lo_ref, bf16[512,512]{1,0:T(8,128)(2,1)S(1)} %collective-permute-done.14.hi_ref, bf16[512,512]{1,0:T(8,128)(2,1)S(1)} %get-tuple-element.30.gu_ref, ...), custom_call_target="tpu_custom_call" | custom-call | flops 805306368 | bytes 3676320 | tf_op jit(solution)/shard_map/pallas_call | solution.py:179
  116.1 1.7 %shard_map.145 = f32[512,512]{1,0:T(8,128)} custom-call(bf16[512,512]{1,0:T(8,128)(2,1)S(1)} %get-tuple-element.33.w_ref, bf16[512,512]{1,0:T(8,128)(2,1)S(1)} %get-tuple-element.34.u_ref, bf16[528,512]{1,0:T(8,128)(2,1)S(1)} %collective-permute-done.15.t_ref.packed_ref), custom_call_target="tpu_custom_call" | custom-call | flops 268435456 | bytes 2637824 | tf_op jit(solution)/shard_map/pallas_call | solution.py:179
  117.8 0.2 collective-permute-done.20
  118.0 0.7 divide_subtract_fusion
  (38 shorter events, 0.3 us)
Async XLA Ops:
  0.6 23.8 %copy-start = (f32[512,512]{1,0:T(8,128)S(1)}, f32[512,512]{1,0:T(8,128)}, u32[]{:S(2)}) copy-start(f32[512,512]{1,0:T(8,128)} %table_ref.3) | copy-start | bytes 3145732
  1.6 6.3 %collective-permute-start = (bf16[32,512]{1,0:T(8,128)(2,1)S(1)}, bf16[32,512]{1,0:T(8,128)(2,1)S(1)}, u32[]{:S(2)}, u32[]{:S(2)}) collective-permute-start(bf16[32,512]{1,0:T(8,128)(2,1)S(1)} %get-tuple-element.40), channel_id=1, source_target_pairs={{0,4},{1,5},{2,6},{3,7},{4,0},{5,1},{6,2},{7,3},{8,12},{9,13},{10,... | collective-permute-start | bytes 98312 | tf_op jit(solution)/shard_map/ppermute | solution.py:208
  7.9 4.3 %collective-permute-start.1 = (bf16[64,512]{1,0:T(8,128)(2,1)S(1)}, bf16[64,512]{1,0:T(8,128)(2,1)S(1)}, u32[]{:S(2)}, u32[]{:S(2)}) collective-permute-start(bf16[64,512]{1,0:T(8,128)(2,1)S(1)} %pad_maximum_fusion.4), channel_id=1, source_target_pairs={{0,2},{1,3},{2,0},{3,1},{4,6},{5,7},{6,4},{7,5},{8,10},{9,11},{10,... | collective-permute-start | bytes 196616 | tf_op jit(solution)/shard_map/ppermute | solution.py:208
  12.1 5.0 %collective-permute-start.2 = (bf16[128,512]{1,0:T(8,128)(2,1)S(1)}, bf16[128,512]{1,0:T(8,128)(2,1)S(1)}, u32[]{:S(2)}, u32[]{:S(2)}) collective-permute-start(bf16[128,512]{1,0:T(8,128)(2,1)S(1)} %pad_maximum_fusion.2), channel_id=1, source_target_pairs={{0,1},{1,0},{2,3},{3,2},{4,5},{5,4},{6,7},{7,6},{8,9},{9,8},{10,11... | collective-permute-start | bytes 393224 | tf_op jit(solution)/shard_map/ppermute | solution.py:208
  17.2 6.4 %collective-permute-start.3 = (bf16[256,512]{1,0:T(8,128)(2,1)S(1)}, bf16[256,512]{1,0:T(8,128)(2,1)S(1)}, u32[]{:S(2)}, u32[]{:S(2)}) collective-permute-start(bf16[256,512]{1,0:T(8,128)(2,1)S(1)} %pad_maximum_fusion), channel_id=1, source_target_pairs={{0,16},{1,17},{2,18},{3,19},{4,20},{5,21},{6,22},{7,23},{8,24},{9,... | collective-permute-start | bytes 786440 | tf_op jit(solution)/shard_map/ppermute | solution.py:208
  23.6 0.7 copy-start.11
  23.7 2.8 %collective-permute-start.4 = (bf16[512,512]{1,0:T(8,128)(2,1)S(1)}, bf16[512,512]{1,0:T(8,128)(2,1)S(1)}, u32[]{:S(2)}, u32[]{:S(2)}) collective-permute-start(bf16[512,512]{1,0:T(8,128)(2,1)S(1)} %constant_dynamic-update-slice_fusion.lo_ref), channel_id=1, source_target_pairs={{0,8},{1,9},{2,10},{3,11},{4,12},{5,13},{6,14},{7,15},{8,0},{9,1},... | collective-permute-start | bytes 1572872 | tf_op jit(solution)/shard_map/ppermute | solution.py:208
  23.7 0.7 copy-start.5
  23.8 0.7 copy-start.4
  23.8 0.7 copy-start.3
  24.5 1.2 %copy-start.1 = (f32[512,512]{1,0:T(8,128)S(1)}, f32[512,512]{1,0:T(8,128)}, u32[]{:S(2)}) copy-start(f32[512,512]{1,0:T(8,128)} %table_ref.2) | copy-start | bytes 3145732
  25.7 0.7 copy-start.12
  26.4 0.7 copy-start.7
  30.1 2.1 %collective-permute-start.5 = (bf16[512,512]{1,0:T(8,128)(2,1)S(1)}, bf16[512,512]{1,0:T(8,128)(2,1)S(1)}, u32[]{:S(2)}, u32[]{:S(2)}) collective-permute-start(bf16[512,512]{1,0:T(8,128)(2,1)S(1)} %get-tuple-element.25), channel_id=1, source_target_pairs={{0,8},{1,9},{2,10},{3,11},{4,12},{5,13},{6,14},{7,15},{8,0},{9,1},... | collective-permute-start | bytes 1572872 | tf_op jit(solution)/shard_map/ppermute | solution.py:208
  32.4 8.7 %collective-permute-start.6 = (bf16[256,512]{1,0:T(8,128)(2,1)S(1)}, bf16[256,512]{1,0:T(8,128)(2,1)S(1)}, u32[]{:S(2)}, u32[]{:S(2)}) collective-permute-start(bf16[256,512]{1,0:T(8,128)(2,1)S(1)} %get-tuple-element.44), channel_id=1, source_target_pairs={{0,16},{1,17},{2,18},{3,19},{4,20},{5,21},{6,22},{7,23},{8,24},{9,... | collective-permute-start | bytes 786440 | tf_op jit(solution)/shard_map/ppermute | solution.py:208
  41.1 5.0 %collective-permute-start.7 = (bf16[128,512]{1,0:T(8,128)(2,1)S(1)}, bf16[128,512]{1,0:T(8,128)(2,1)S(1)}, u32[]{:S(2)}, u32[]{:S(2)}) collective-permute-start(bf16[128,512]{1,0:T(8,128)(2,1)S(1)} %get-tuple-element.48), channel_id=1, source_target_pairs={{0,1},{1,0},{2,3},{3,2},{4,5},{5,4},{6,7},{7,6},{8,9},{9,8},{10,11... | collective-permute-start | bytes 393224 | tf_op jit(solution)/shard_map/ppermute | solution.py:208
  46.1 9.5 %copy-start.10 = (f32[32,512]{1,0:T(8,128)S(1)}, f32[32,512]{1,0:T(8,128)}, u32[]{:S(2)}) copy-start(f32[32,512]{1,0:T(8,128)} %param.17) | copy-start | bytes 196612
  46.2 9.5 %copy-start.9 = (f32[32,512]{1,0:T(8,128)S(1)}, f32[32,512]{1,0:T(8,128)}, u32[]{:S(2)}) copy-start(f32[32,512]{1,0:T(8,128)} %param.16) | copy-start | bytes 196612
  46.2 4.3 %collective-permute-start.8 = (bf16[64,512]{1,0:T(8,128)(2,1)S(1)}, bf16[64,512]{1,0:T(8,128)(2,1)S(1)}, u32[]{:S(2)}, u32[]{:S(2)}) collective-permute-start(bf16[64,512]{1,0:T(8,128)(2,1)S(1)} %get-tuple-element.52), channel_id=1, source_target_pairs={{0,2},{1,3},{2,0},{3,1},{4,6},{5,7},{6,4},{7,5},{8,10},{9,11},{10,... | collective-permute-start | bytes 196616 | tf_op jit(solution)/shard_map/ppermute | solution.py:208
  50.5 5.1 %collective-permute-start.9 = (bf16[32,512]{1,0:T(8,128)(2,1)S(1)}, bf16[32,512]{1,0:T(8,128)(2,1)S(1)}, u32[]{:S(2)}, u32[]{:S(2)}) collective-permute-start(bf16[32,512]{1,0:T(8,128)(2,1)S(1)} %add_convert_fusion.14), channel_id=1, source_target_pairs={{0,4},{1,5},{2,6},{3,7},{4,0},{5,1},{6,2},{7,3},{8,12},{9,13},{10,... | collective-permute-start | bytes 98312 | tf_op jit(solution)/shard_map/ppermute | solution.py:208
  55.7 4.9 %collective-permute-start.10 = (bf16[32,512]{1,0:T(8,128)(2,1)S(1)}, bf16[32,512]{1,0:T(8,128)(2,1)S(1)}, u32[]{:S(2)}, u32[]{:S(2)}) collective-permute-start(bf16[32,512]{1,0:T(8,128)(2,1)S(1)} %get-tuple-element.38), channel_id=1, source_target_pairs={{0,4},{1,5},{2,6},{3,7},{4,0},{5,1},{6,2},{7,3},{8,12},{9,13},{10,... | collective-permute-start | bytes 98312 | tf_op jit(solution)/shard_map/ppermute | solution.py:208
  60.6 4.3 %collective-permute-start.11 = (bf16[64,512]{1,0:T(8,128)(2,1)S(1)}, bf16[64,512]{1,0:T(8,128)(2,1)S(1)}, u32[]{:S(2)}, u32[]{:S(2)}) collective-permute-start(bf16[64,512]{1,0:T(8,128)(2,1)S(1)} %pad_maximum_fusion.5), channel_id=1, source_target_pairs={{0,2},{1,3},{2,0},{3,1},{4,6},{5,7},{6,4},{7,5},{8,10},{9,11},{10,... | collective-permute-start | bytes 196616 | tf_op jit(solution)/shard_map/ppermute | solution.py:208
  64.9 15.8 %collective-permute-start.12 = (bf16[128,512]{1,0:T(8,128)(2,1)S(1)}, bf16[128,512]{1,0:T(8,128)(2,1)S(1)}, u32[]{:S(2)}, u32[]{:S(2)}) collective-permute-start(bf16[128,512]{1,0:T(8,128)(2,1)S(1)} %pad_maximum_fusion.3), channel_id=1, source_target_pairs={{0,1},{1,0},{2,3},{3,2},{4,5},{5,4},{6,7},{7,6},{8,9},{9,8},{10,11... | collective-permute-start | bytes 393224 | tf_op jit(solution)/shard_map/ppermute | solution.py:208
  66.7 0.7 copy-start.6
  68.0 19.2 %copy-start.2 = (f32[512,512]{1,0:T(8,128)S(1)}, f32[512,512]{1,0:T(8,128)}, u32[]{:S(2)}) copy-start(f32[512,512]{1,0:T(8,128)} %table_ref.2) | copy-start | bytes 3145732
  68.0 22.0 %collective-permute-start.15 = (bf16[528,512]{1,0:T(8,128)(2,1)S(1)}, bf16[528,512]{1,0:T(8,128)(2,1)S(1)}, u32[]{:S(2)}, u32[]{:S(2)}) collective-permute-start(bf16[528,512]{1,0:T(8,128)(2,1)S(1)} %shard_map.142), channel_id=1, source_target_pairs={{0,1},{1,2},{2,3},{3,4},{4,5},{5,6},{6,7},{7,0},{8,9},{9,10},{10,1... | collective-permute-start | bytes 1622024 | tf_op jit(solution)/shard_map/ppermute | solution.py:292
  80.7 6.4 %collective-permute-start.13 = (bf16[256,512]{1,0:T(8,128)(2,1)S(1)}, bf16[256,512]{1,0:T(8,128)(2,1)S(1)}, u32[]{:S(2)}, u32[]{:S(2)}) collective-permute-start(bf16[256,512]{1,0:T(8,128)(2,1)S(1)} %pad_maximum_fusion.1), channel_id=1, source_target_pairs={{0,16},{1,17},{2,18},{3,19},{4,20},{5,21},{6,22},{7,23},{8,24},{9,... | collective-permute-start | bytes 786440 | tf_op jit(solution)/shard_map/ppermute | solution.py:208
  87.1 0.7 copy-start.8
  87.1 2.9 %collective-permute-start.14 = (bf16[512,512]{1,0:T(8,128)(2,1)S(1)}, bf16[512,512]{1,0:T(8,128)(2,1)S(1)}, u32[]{:S(2)}, u32[]{:S(2)}) collective-permute-start(bf16[512,512]{1,0:T(8,128)(2,1)S(1)} %constant_dynamic-update-slice_fusion.5.lo_ref), channel_id=1, source_target_pairs={{0,8},{1,9},{2,10},{3,11},{4,12},{5,13},{6,14},{7,15},{8,0},{9,1},... | collective-permute-start | bytes 1572872 | tf_op jit(solution)/shard_map/ppermute | solution.py:208
  93.1 2.0 %collective-permute-start.16 = (bf16[512,512]{1,0:T(8,128)(2,1)S(1)}, bf16[512,512]{1,0:T(8,128)(2,1)S(1)}, u32[]{:S(2)}, u32[]{:S(2)}) collective-permute-start(bf16[512,512]{1,0:T(8,128)(2,1)S(1)} %get-tuple-element.36), channel_id=1, source_target_pairs={{0,8},{1,9},{2,10},{3,11},{4,12},{5,13},{6,14},{7,15},{8,0},{9,1},... | collective-permute-start | bytes 1572872 | tf_op jit(solution)/shard_map/ppermute | solution.py:208
  95.2 8.4 %collective-permute-start.17 = (bf16[256,512]{1,0:T(8,128)(2,1)S(1)}, bf16[256,512]{1,0:T(8,128)(2,1)S(1)}, u32[]{:S(2)}, u32[]{:S(2)}) collective-permute-start(bf16[256,512]{1,0:T(8,128)(2,1)S(1)} %get-tuple-element.42), channel_id=1, source_target_pairs={{0,16},{1,17},{2,18},{3,19},{4,20},{5,21},{6,22},{7,23},{8,24},{9,... | collective-permute-start | bytes 786440 | tf_op jit(solution)/shard_map/ppermute | solution.py:208
  103.7 5.0 %collective-permute-start.18 = (bf16[128,512]{1,0:T(8,128)(2,1)S(1)}, bf16[128,512]{1,0:T(8,128)(2,1)S(1)}, u32[]{:S(2)}, u32[]{:S(2)}) collective-permute-start(bf16[128,512]{1,0:T(8,128)(2,1)S(1)} %get-tuple-element.46), channel_id=1, source_target_pairs={{0,1},{1,0},{2,3},{3,2},{4,5},{5,4},{6,7},{7,6},{8,9},{9,8},{10,11... | collective-permute-start | bytes 393224 | tf_op jit(solution)/shard_map/ppermute | solution.py:208
  108.8 4.3 %collective-permute-start.19 = (bf16[64,512]{1,0:T(8,128)(2,1)S(1)}, bf16[64,512]{1,0:T(8,128)(2,1)S(1)}, u32[]{:S(2)}, u32[]{:S(2)}) collective-permute-start(bf16[64,512]{1,0:T(8,128)(2,1)S(1)} %get-tuple-element.50), channel_id=1, source_target_pairs={{0,2},{1,3},{2,0},{3,1},{4,6},{5,7},{6,4},{7,5},{8,10},{9,11},{10,... | collective-permute-start | bytes 196616 | tf_op jit(solution)/shard_map/ppermute | solution.py:208
  113.1 4.9 %collective-permute-start.20 = (bf16[32,512]{1,0:T(8,128)(2,1)S(1)}, bf16[32,512]{1,0:T(8,128)(2,1)S(1)}, u32[]{:S(2)}, u32[]{:S(2)}) collective-permute-start(bf16[32,512]{1,0:T(8,128)(2,1)S(1)} %add_convert_fusion.12), channel_id=1, source_target_pairs={{0,4},{1,5},{2,6},{3,7},{4,0},{5,1},{6,2},{7,3},{8,12},{9,13},{10,... | collective-permute-start | bytes 98312 | tf_op jit(solution)/shard_map/ppermute | solution.py:208

commit v2 on v1

--- a/solution.py
+++ b/solution.py
@@ -190,45 +190,59 @@
 class Exchange:
     def __init__(self, heads, tails):
         self.devices = heads * tails
-        cores = [tails] if heads > 1 else []
-        heads_left = [tails << i for i in range(1, heads.bit_length() - 1)]
-        self.masks = cores + heads_left + [1 << i for i in range(tails.bit_length() - 1)]
-        bits = len(self.masks)
-        places = [
-            sum(m for i, m in enumerate(self.masks) if j >> (bits - 1 - i) & 1)
-            for j in range(self.devices)
-        ]
+        head_bits = [tails << i for i in range(heads.bit_length() - 1)]
+        tail_bits = [1 << i for i in range(tails.bit_length() - 1)]
+        rest = head_bits[1:2] + tail_bits + head_bits[2:]
+        self.stages = [head_bits[:1]] + [rest[i : i + 2] for i in range(0, len(rest), 2)]
+        bits = [bit for stage in self.stages for bit in stage]
+        places = [self.others(bits, j) for j in range(self.devices)]
         slots = np.zeros(self.devices, np.int32)
         slots[places] = np.arange(self.devices)
         me = lax.axis_index(AXES)
         self.block_of_slot = jnp.asarray(places, jnp.int32) ^ me
         self.slot_of_block = jnp.asarray(slots)[jnp.arange(self.devices, dtype=jnp.int32) ^ me]
 
+    def others(self, bits, j):
+        return sum(bit for i, bit in enumerate(bits) if j >> (len(bits) - 1 - i) & 1)
+
+    def masks(self, stage):
+        return [self.others(stage, j) for j in range(1, 1 << len(stage))]
+
     def swap(self, x, mask):
         return lax.ppermute(x, AXES, [(i, i ^ mask) for i in range(self.devices)])
 
-    def reduce_scatter(self, keep, send):
+    def reduce_scatter(self, keep, send, beside):
         if (2 * keep.shape[0] // self.devices) % PACK_ROWS:
             both = jnp.concatenate([keep, send])
             both = both.reshape(self.devices, -1, both.shape[1])[self.block_of_slot]
             keep, send = jnp.split(both.reshape(-1, both.shape[2]), 2)
-        for i, mask in enumerate(self.masks):
-            got = self.swap(send, mask)
-            half = keep.shape[0] // 2
-            if i + 1 == len(self.masks):
-                return keep.astype(F32) + got.astype(F32)
-            send = (keep[half:].astype(F32) + got[half:].astype(F32)).astype(BF16)
-            keep = (keep[:half].astype(F32) + got[:half].astype(F32)).astype(BF16)
-
-    def all_gather(self, own):
+        parts = [keep, send]
+        for i, stage in enumerate(self.stages):
+            got = [self.swap(part, mask) for part, mask in zip(parts[1:], self.masks(stage))]
+            if i == 1:
+                got, beside = lax.optimization_barrier((got, beside))
+            pieces = parts[:1] + got
+            if i + 1 == len(self.stages):
+                return sum(piece.astype(F32) for piece in pieces), beside
+            count = 1 << len(self.stages[i + 1])
+            size = pieces[0].shape[0] // count
+            parts = [
+                sum(piece[j * size : (j + 1) * size].astype(F32) for piece in pieces).astype(BF16)
+                for j in range(count)
+            ]
+
+    def all_gather(self, own, beside=()):
         rows = own.shape[0]
-        for mask in self.masks[:0:-1]:
-            own = jnp.concatenate([own, self.swap(own, mask)])
-        lo, hi = own, self.swap(own, self.masks[0])
+        for i, stage in reversed(list(enumerate(self.stages))[1:]):
+            got = [self.swap(own, mask) for mask in self.masks(stage)]
+            if i == 1:
+                got, beside = lax.optimization_barrier((got, beside))
+            own = jnp.concatenate([own] + got)
+        lo, hi = own, self.swap(own, self.masks(self.stages[0])[0])
         if rows % PACK_ROWS:
             both = jnp.concatenate([lo, hi]).reshape(self.devices, rows, -1)[self.slot_of_block]
             lo, hi = jnp.split(both.reshape(self.devices * rows, -1), 2)
-        return lo, hi
+        return lo, hi, beside
 
 
 def shards(
@@ -254,8 +268,7 @@
     half = all_rows // 2
     square = 2 * rows * edges * width
 
-    own_bf = relations.astype(BF16)
-    head_vecs, tail_vecs, tail_col, counts = call(
+    beside = call(
         prepare_kernel,
         [
             ((edges, width), BF16),
@@ -269,7 +282,9 @@
     head_state = head_state.reshape(1, -1)
     tail_state = tail_state.reshape(1, -1)
     for k in range(2):
-        lo, hi = exchange.all_gather(own_bf)
+        lo, hi, beside = exchange.all_gather(relations.astype(BF16), beside)
+        if k == 0:
+            head_vecs, tail_vecs, tail_col, counts = beside
         keep, send, weights, projected, edge_grad = call(
             functools.partial(score_kernel, k, float(nneg)),
             [
@@ -282,33 +297,31 @@
             3, [pltpu.VMEM((all_rows, width), BF16), pltpu.VMEM((all_rows, width), F32)], 6 * square,
             nat, block_counts, relation_ids, lo, hi, head_vecs, tail_vecs, tail_col, counts,
         )
-        rel_scratch = [pltpu.VMEM((all_rows, width), BF16)]
-        head_args = (nat, relation_ids, lo, hi, edge_grad, head_rows, head_table, head_state)
+        head_outs = [(head_table.shape, F32)]
         if k == 0:
-            (packed,) = call(
+            tail_new = call(
                 tail_kernel, [((rows + PACK_ROWS, width), BF16)], 0, [], square,
                 weights, projected, tail_table, tail_state,
             )
-            tail_vecs = lax.ppermute(packed, "tail", [(i, (i + 1) % tails) for i in range(tails)])
-            head_table, head_state, head_vecs = call(
-                functools.partial(head_kernel, k, blocks),
-                [(head_table.shape, F32), (head_state.shape, F32), ((edges, width), BF16)],
-                2, rel_scratch, 4 * square, *head_args,
-            )
+            head_outs += [(head_state.shape, F32), ((edges, width), BF16)]
         else:
-            (tail_table,) = call(
+            tail_new = call(
                 last_tail_kernel, [((rows, width), F32)], 0, [], square,
                 weights, projected, tail_vecs,
             )
-            (head_table,) = call(
-                functools.partial(head_kernel, k, blocks), [(head_table.shape, F32)],
-                2, rel_scratch, 3 * square, *head_args,
-            )
-        grad = exchange.reduce_scatter(keep, send)
+        head_new = call(
+            functools.partial(head_kernel, k, blocks), head_outs,
+            2, [pltpu.VMEM((all_rows, width), BF16)], 4 * square,
+            nat, relation_ids, lo, hi, edge_grad, head_rows, head_table, head_state,
+        )
+        grad, ((tail_new,), head_new) = exchange.reduce_scatter(keep, send, (tail_new, head_new))
+        if k == 0:
+            head_table, head_state, head_vecs = head_new
+            tail_vecs = lax.ppermute(tail_new, "tail", [(i, (i + 1) % tails) for i in range(tails)])
         relation_state = relation_state + grad * grad
         relations = relations - RATE_RELATIONS * grad / (jnp.sqrt(relation_state) + EPSILON)
-        own_bf = relations.astype(BF16)
-    return (head_table, tail_table, relations)
+        beside = ()
+    return (head_new[0], tail_new, relations)
 
 
 def solution(mesh):

time: 119 us -> 93 us (0.78)
  waiting for transfers between devices: 68.9 us -> 35.6 us
  starting transfers between devices: 28.4 us -> 34.2 us
  local copies, waits for them, and re-layouts: 3.96 us -> 5.59 us
    ppermute x20 -> x28, waiting for transfers between devices: 68.9 us -> 35.6 us  [swap(): return lax.ppermute(x, AXES, [(i, i ^ mask) for i in range(self.devices)])]
    ppermute x20 -> x28, starting transfers between devices: 28 us -> 33.1 us  [swap(): return lax.ppermute(x, AXES, [(i, i ^ mask) for i in range(self.devices)])]
    unnamed x33 -> x39, local copies, waits for them, and re-layouts: 3.92 us -> 5.57 us
  transfers between devices with their start and end apart: 21 -> 29, of which waited for: 18 -> 21; matrix products, arithmetic and copies ran while one was open for 0% -> 0% of each run, Pallas kernels for 7% -> 9%
where the time goes in v2:
time: 93 us; the launch traced here: 92.6 us
  waiting for transfers between devices  35.6 us (38%)
  starting transfers between devices  34.2 us (37%)
  Pallas kernels  14.3 us (15%)
  local copies, waits for them, and re-layouts  5.59 us (6%)
  other arithmetic  2.08 us (2%)
    ppermute x28, waiting for transfers between devices, swap(): return lax.ppermute(x, AXES, [(i, i ^ mask) for i in range(self.devices)])  35.6 us
    ppermute x28, starting transfers between devices, swap(): return lax.ppermute(x, AXES, [(i, i ^ mask) for i in range(self.devices)])  33.1 us
    pallas_call x7, Pallas kernels, call(): pl.pallas_call(kernel, out_shape=outs, in_specs=[SMEM] * smem + [VMEM] *...  14.3 us
    unnamed x39, local copies, waits for them, and re-layouts  5.57 us
  transfers between devices with their start and end apart: 29, of which 21 were waited for; matrix products, arithmetic and copies ran while one was open for 0% of the time, Pallas kernels for 9%

profile of v2, /device:TPU:0, one launch (start us, length us, event | category | flops | bytes accessed | tf_op | source)
XLA Modules:
  0.0 92.6 jit_solution(1008779332044015409)
XLA Ops:
  0.7 0.9 constant_dynamic-update-slice_fusion.6
  1.5 5.0 %collective-permute-start.2 = (bf16[32,512]{1,0:T(8,128)(2,1)S(1)}, bf16[32,512]{1,0:T(8,128)(2,1)S(1)}, u32[]{:S(2)}, u32[]{:S(2)}) collective-permute-start(bf16[32,512]{1,0:T(8,128)(2,1)S(1)} %get-tuple-element.85), channel_id=1, source_target_pairs={{0,6},{1,7},{2,4},{3,5},{4,2},{5,3},{6,0},{7,1},{8,14},{9,15},{10,... | collective-permute-start | bytes 98312 | tf_op jit(solution)/shard_map/ppermute | solution.py:212
  6.6 0.6 collective-permute-start
  7.2 1.2 %copy-done = f32[512,512]{1,0:T(8,128)S(1)} copy-done((f32[512,512]{1,0:T(8,128)S(1)}, f32[512,512]{1,0:T(8,128)}, u32[]{:S(2)}) %copy-start) | copy-done | bytes 1048600
  8.4 1.2 %copy-done.2 = f32[512,512]{1,0:T(8,128)S(1)} copy-done((f32[512,512]{1,0:T(8,128)S(1)}, f32[512,512]{1,0:T(8,128)}, u32[]{:S(2)}) %copy-start.2) | copy-done | bytes 1048600
  9.7 0.7 shard_map.139
  10.4 0.1 collective-permute-done.1
  10.5 1.0 %collective-permute-done = bf16[32,512]{1,0:T(8,128)(2,1)S(1)} collective-permute-done((bf16[32,512]{1,0:T(8,128)(2,1)S(1)}, bf16[32,512]{1,0:T(8,128)(2,1)S(1)}, u32[]{:S(2)}, u32[]{:S(2)}) %collective-permute-start) | collective-permute-done | bytes 32800 | tf_op jit(solution)/shard_map/ppermute | solution.py:212
  11.5 2.5 %collective-permute-start.5 = (bf16[128,512]{1,0:T(8,128)(2,1)S(1)}, bf16[128,512]{1,0:T(8,128)(2,1)S(1)}, u32[]{:S(2)}, u32[]{:S(2)}) collective-permute-start(bf16[128,512]{1,0:T(8,128)(2,1)S(1)} %pad_maximum_fusion), channel_id=1, source_target_pairs={{0,17},{1,16},{2,19},{3,18},{4,21},{5,20},{6,23},{7,22},{8,25},{9,... | collective-permute-start | bytes 393224 | tf_op jit(solution)/shard_map/ppermute | solution.py:212
  14.0 0.5 collective-permute-start.4
  14.5 0.5 collective-permute-start.3
  15.1 3.6 %collective-permute-done.5 = bf16[128,512]{1,0:T(8,128)(2,1)S(1)} collective-permute-done((bf16[128,512]{1,0:T(8,128)(2,1)S(1)}, bf16[128,512]{1,0:T(8,128)(2,1)S(1)}, u32[]{:S(2)}, u32[]{:S(2)}) %collective-permute-start.5) | collective-permute-done | bytes 131104 | tf_op jit(solution)/shard_map/ppermute | solution.py:212
  18.7 0.9 collective-permute-done.4
  19.8 0.6 copy-done.12
  20.4 0.1 copy.16.live_ref
  20.5 0.7 copy-done.13
  21.2 0.5 collective-permute-done.6.hi_ref
  21.7 0.2 copy-done.9
  21.9 3.0 %shard_map.140 = (bf16[512,512]{1,0:T(8,128)(2,1)S(1)}, bf16[512,512]{1,0:T(8,128)(2,1)S(1)}, bf16[512,512]{1,0:T(8,128)(2,1)S(1)}, bf16[512,512]{1,0:T(8,128)(2,1)S(1)}, bf16[512,512]{1,0:T(8,128)(2,1)S(1)}) custom-call(s32[32]{0:T(128)S(1)} %broadcast_xor_fusion.nat_ref, s32[2,1]{1,0:T(2,128)S(1)} %copy.16.live_ref, s32[2,4]{1,0:T(2,128)S(1)} %copy-done.9, ...), custom_call_target="tpu_custom_call" | custom-call | flops 1610612736 | bytes 5259432 | tf_op jit(solution)/shard_map/pallas_call | solution.py:179
  24.9 0.6 collective-permute-start.7
  25.4 1.5 %collective-permute-done.7 = bf16[512,512]{1,0:T(8,128)(2,1)S(1)} collective-permute-done((bf16[512,512]{1,0:T(8,128)(2,1)S(1)}, bf16[512,512]{1,0:T(8,128)(2,1)S(1)}, u32[]{:S(2)}, u32[]{:S(2)}) %collective-permute-start.7) | collective-permute-done | bytes 524320 | tf_op jit(solution)/shard_map/ppermute | solution.py:212
  27.0 0.1 add_convert_fusion.4
  27.1 1.4 %collective-permute-start.10 = (bf16[128,512]{1,0:T(8,128)(2,1)S(1)}, bf16[128,512]{1,0:T(8,128)(2,1)S(1)}, u32[]{:S(2)}, u32[]{:S(2)}) collective-permute-start(bf16[128,512]{1,0:T(8,128)(2,1)S(1)} %get-tuple-element.90), channel_id=1, source_target_pairs={{0,17},{1,16},{2,19},{3,18},{4,21},{5,20},{6,23},{7,22},{8,25},{9,... | collective-permute-start | bytes 393224 | tf_op jit(solution)/shard_map/ppermute | solution.py:212
  28.6 1.1 %collective-permute-start.9 = (bf16[128,512]{1,0:T(8,128)(2,1)S(1)}, bf16[128,512]{1,0:T(8,128)(2,1)S(1)}, u32[]{:S(2)}, u32[]{:S(2)}) collective-permute-start(bf16[128,512]{1,0:T(8,128)(2,1)S(1)} %get-tuple-element.91), channel_id=1, source_target_pairs={{0,16},{1,17},{2,18},{3,19},{4,20},{5,21},{6,22},{7,23},{8,24},{9,... | collective-permute-start | bytes 393224 | tf_op jit(solution)/shard_map/ppermute | solution.py:212
  29.7 1.0 %collective-permute-start.8 = (bf16[128,512]{1,0:T(8,128)(2,1)S(1)}, bf16[128,512]{1,0:T(8,128)(2,1)S(1)}, u32[]{:S(2)}, u32[]{:S(2)}) collective-permute-start(bf16[128,512]{1,0:T(8,128)(2,1)S(1)} %get-tuple-element.92), channel_id=1, source_target_pairs={{0,1},{1,0},{2,3},{3,2},{4,5},{5,4},{6,7},{7,6},{8,9},{9,8},{10,11... | collective-permute-start | bytes 393224 | tf_op jit(solution)/shard_map/ppermute | solution.py:212
  30.7 0.7 copy-done.7
  31.4 0.7 shard_map.141
  32.1 0.5 copy-done.3
  32.6 0.2 copy-done.8
  32.8 2.3 %shard_map.142 = (f32[512,512]{1,0:T(8,128)S(1)}, f32[1,512]{1,0:T(1,128)S(1)}, bf16[512,512]{1,0:T(8,128)(2,1)S(1)}) custom-call(s32[32]{0:T(128)S(1)} %broadcast_xor_fusion.nat_ref, s32[2,4]{1,0:T(2,128)S(1)} %copy-done.9, bf16[512,512]{1,0:T(8,128)(2,1)S(1)} %constant_dynamic-update-slice_fusion.lo_ref, ...), custom_call_target="tpu_custom_call" | custom-call | flops 1073741824 | bytes 4202656 | tf_op jit(solution)/shard_map/pallas_call | solution.py:179
  35.1 1.6 %collective-permute-done.9 = bf16[128,512]{1,0:T(8,128)(2,1)S(1)} collective-permute-done((bf16[128,512]{1,0:T(8,128)(2,1)S(1)}, bf16[128,512]{1,0:T(8,128)(2,1)S(1)}, u32[]{:S(2)}, u32[]{:S(2)}) %collective-permute-start.9) | collective-permute-done | bytes 131104 | tf_op jit(solution)/shard_map/ppermute | solution.py:212
  36.7 1.7 %collective-permute-start.11 = (bf16[32,512]{1,0:T(8,128)(2,1)S(1)}, bf16[32,512]{1,0:T(8,128)(2,1)S(1)}, u32[]{:S(2)}, u32[]{:S(2)}) collective-permute-start(bf16[32,512]{1,0:T(8,128)(2,1)S(1)} %get-tuple-element.97), channel_id=1, source_target_pairs={{0,4},{1,5},{2,6},{3,7},{4,0},{5,1},{6,2},{7,3},{8,12},{9,13},{10,... | collective-permute-start | bytes 98312 | tf_op jit(solution)/shard_map/ppermute | solution.py:212
  38.5 2.6 %collective-permute-start.13 = (bf16[32,512]{1,0:T(8,128)(2,1)S(1)}, bf16[32,512]{1,0:T(8,128)(2,1)S(1)}, u32[]{:S(2)}, u32[]{:S(2)}) collective-permute-start(bf16[32,512]{1,0:T(8,128)(2,1)S(1)} %get-tuple-element.98), channel_id=1, source_target_pairs={{0,6},{1,7},{2,4},{3,5},{4,2},{5,3},{6,0},{7,1},{8,14},{9,15},{10,... | collective-permute-start | bytes 98312 | tf_op jit(solution)/shard_map/ppermute | solution.py:212
  41.1 0.6 collective-permute-done.11
  41.6 2.5 %collective-permute-done.13 = bf16[32,512]{1,0:T(8,128)(2,1)S(1)} collective-permute-done((bf16[32,512]{1,0:T(8,128)(2,1)S(1)}, bf16[32,512]{1,0:T(8,128)(2,1)S(1)}, u32[]{:S(2)}, u32[]{:S(2)}) %collective-permute-start.13) | collective-permute-done | bytes 32800 | tf_op jit(solution)/shard_map/ppermute | solution.py:212
  44.2 0.8 collective-permute-done.12
  45.0 1.9 %collective-permute-start.16 = (bf16[32,512]{1,0:T(8,128)(2,1)S(1)}, bf16[32,512]{1,0:T(8,128)(2,1)S(1)}, u32[]{:S(2)}, u32[]{:S(2)}) collective-permute-start(bf16[32,512]{1,0:T(8,128)(2,1)S(1)} %get-tuple-element.82), channel_id=1, source_target_pairs={{0,6},{1,7},{2,4},{3,5},{4,2},{5,3},{6,0},{7,1},{8,14},{9,15},{10,... | collective-permute-start | bytes 98312 | tf_op jit(solution)/shard_map/ppermute | solution.py:212
  46.9 2.6 %collective-permute-start.14 = (bf16[32,512]{1,0:T(8,128)(2,1)S(1)}, bf16[32,512]{1,0:T(8,128)(2,1)S(1)}, u32[]{:S(2)}, u32[]{:S(2)}) collective-permute-start(bf16[32,512]{1,0:T(8,128)(2,1)S(1)} %get-tuple-element.82), channel_id=1, source_target_pairs={{0,4},{1,5},{2,6},{3,7},{4,0},{5,1},{6,2},{7,3},{8,12},{9,13},{10,... | collective-permute-start | bytes 98312 | tf_op jit(solution)/shard_map/ppermute | solution.py:212
  49.5 1.1 %collective-permute-start.21 = (bf16[528,512]{1,0:T(8,128)(2,1)S(1)}, bf16[528,512]{1,0:T(8,128)(2,1)S(1)}, u32[]{:S(2)}, u32[]{:S(2)}) collective-permute-start(bf16[528,512]{1,0:T(8,128)(2,1)S(1)} %shard_map.141), channel_id=1, source_target_pairs={{0,1},{1,2},{2,3},{3,4},{4,5},{5,6},{6,7},{7,0},{8,9},{9,10},{10,1... | collective-permute-start | bytes 1622024 | tf_op jit(solution)/shard_map/ppermute | solution.py:320
  50.6 0.3 collective-permute-done.16
  50.9 0.3 collective-permute-done.15
  51.2 0.6 collective-permute-done.14
  51.8 1.5 %collective-permute-start.19 = (bf16[128,512]{1,0:T(8,128)(2,1)S(1)}, bf16[128,512]{1,0:T(8,128)(2,1)S(1)}, u32[]{:S(2)}, u32[]{:S(2)}) collective-permute-start(bf16[128,512]{1,0:T(8,128)(2,1)S(1)} %pad_maximum_fusion.1), channel_id=1, source_target_pairs={{0,17},{1,16},{2,19},{3,18},{4,21},{5,20},{6,23},{7,22},{8,25},{9,... | collective-permute-start | bytes 393224 | tf_op jit(solution)/shard_map/ppermute | solution.py:212
  53.2 1.3 %collective-permute-start.18 = (bf16[128,512]{1,0:T(8,128)(2,1)S(1)}, bf16[128,512]{1,0:T(8,128)(2,1)S(1)}, u32[]{:S(2)}, u32[]{:S(2)}) collective-permute-start(bf16[128,512]{1,0:T(8,128)(2,1)S(1)} %pad_maximum_fusion.1), channel_id=1, source_target_pairs={{0,16},{1,17},{2,18},{3,19},{4,20},{5,21},{6,22},{7,23},{8,24},{9,... | collective-permute-start | bytes 393224 | tf_op jit(solution)/shard_map/ppermute | solution.py:212
  54.5 0.8 collective-permute-start.17
  55.3 12.7 %collective-permute-done.19 = bf16[128,512]{1,0:T(8,128)(2,1)S(1)} collective-permute-done((bf16[128,512]{1,0:T(8,128)(2,1)S(1)}, bf16[128,512]{1,0:T(8,128)(2,1)S(1)}, u32[]{:S(2)}, u32[]{:S(2)}) %collective-permute-start.19) | collective-permute-done | bytes 131104 | tf_op jit(solution)/shard_map/ppermute | solution.py:212
  68.1 1.5 %collective-permute-done.17 = bf16[128,512]{1,0:T(8,128)(2,1)S(1)} collective-permute-done((bf16[128,512]{1,0:T(8,128)(2,1)S(1)}, bf16[128,512]{1,0:T(8,128)(2,1)S(1)}, u32[]{:S(2)}, u32[]{:S(2)}) %collective-permute-start.17) | collective-permute-done | bytes 131104 | tf_op jit(solution)/shard_map/ppermute | solution.py:212
  69.7 1.9 %collective-permute-done.20.hi_ref = bf16[512,512]{1,0:T(8,128)(2,1)S(1)} collective-permute-done((bf16[512,512]{1,0:T(8,128)(2,1)S(1)}, bf16[512,512]{1,0:T(8,128)(2,1)S(1)}, u32[]{:S(2)}, u32[]{:S(2)}) %collective-permute-start.20) | collective-permute-done | bytes 524320 | tf_op jit(solution)/shard_map/ppermute | solution.py:212
  71.6 3.0 %shard_map.143 = (bf16[512,512]{1,0:T(8,128)(2,1)S(1)}, bf16[512,512]{1,0:T(8,128)(2,1)S(1)}, bf16[512,512]{1,0:T(8,128)(2,1)S(1)}, bf16[512,512]{1,0:T(8,128)(2,1)S(1)}, bf16[512,512]{1,0:T(8,128)(2,1)S(1)}) custom-call(s32[32]{0:T(128)S(1)} %broadcast_xor_fusion.nat_ref, s32[2,1]{1,0:T(2,128)S(1)} %copy.16.live_ref, s32[2,4]{1,0:T(2,128)S(1)} %copy-done.9, ...), custom_call_target="tpu_custom_call" | custom-call | flops 1610612736 | bytes 5275816 | tf_op jit(solution)/shard_map/pallas_call | solution.py:179
  74.6 0.2 collective-permute-start.22
  74.8 1.8 %collective-permute-done.22 = bf16[512,512]{1,0:T(8,128)(2,1)S(1)} collective-permute-done((bf16[512,512]{1,0:T(8,128)(2,1)S(1)}, bf16[512,512]{1,0:T(8,128)(2,1)S(1)}, u32[]{:S(2)}, u32[]{:S(2)}) %collective-permute-start.22) | collective-permute-done | bytes 524320 | tf_op jit(solution)/shard_map/ppermute | solution.py:212
  76.6 0.1 add_convert_fusion
  76.8 1.0 %collective-permute-start.24 = (bf16[128,512]{1,0:T(8,128)(2,1)S(1)}, bf16[128,512]{1,0:T(8,128)(2,1)S(1)}, u32[]{:S(2)}, u32[]{:S(2)}) collective-permute-start(bf16[128,512]{1,0:T(8,128)(2,1)S(1)} %get-tuple-element.88), channel_id=1, source_target_pairs={{0,16},{1,17},{2,18},{3,19},{4,20},{5,21},{6,22},{7,23},{8,24},{9,... | collective-permute-start | bytes 393224 | tf_op jit(solution)/shard_map/ppermute | solution.py:212
  77.8 2.5 %collective-permute-start.23 = (bf16[128,512]{1,0:T(8,128)(2,1)S(1)}, bf16[128,512]{1,0:T(8,128)(2,1)S(1)}, u32[]{:S(2)}, u32[]{:S(2)}) collective-permute-start(bf16[128,512]{1,0:T(8,128)(2,1)S(1)} %get-tuple-element.89), channel_id=1, source_target_pairs={{0,1},{1,0},{2,3},{3,2},{4,5},{5,4},{6,7},{7,6},{8,9},{9,8},{10,11... | collective-permute-start | bytes 393224 | tf_op jit(solution)/shard_map/ppermute | solution.py:212
  80.3 1.7 %shard_map.144 = f32[512,512]{1,0:T(8,128)} custom-call(bf16[512,512]{1,0:T(8,128)(2,1)S(1)} %get-tuple-element.71.w_ref, bf16[512,512]{1,0:T(8,128)(2,1)S(1)} %get-tuple-element.72.u_ref, bf16[528,512]{1,0:T(8,128)(2,1)S(1)} %collective-permute-done.21.t_ref.packed_ref), custom_call_target="tpu_custom_call" | custom-call | flops 268435456 | bytes 2637824 | tf_op jit(solution)/shard_map/pallas_call | solution.py:179
  82.0 2.9 %shard_map.145 = f32[512,512]{1,0:T(8,128)} custom-call(s32[32]{0:T(128)S(1)} %broadcast_xor_fusion.nat_ref, s32[2,4]{1,0:T(2,128)S(1)} %copy-done.9, bf16[512,512]{1,0:T(8,128)(2,1)S(1)} %constant_dynamic-update-slice_fusion.7.lo_ref, bf16[512,512]{1,0:T(8,128)(2,1)S(1)} %collective-permute-done.20.hi_ref, bf16[512,512]{1,0:T(8,128)(2,1)S(1)} %get-tuple-element.73.gu_ref, ...), custom_call_target="tpu_custom_call" | custom-call | flops 1073741824 | bytes 3676320 | tf_op jit(solution)/shard_map/pallas_call | solution.py:179
  84.9 0.3 collective-permute-done.24
  85.2 0.3 collective-permute-done.23
  85.5 0.5 collective-permute-start.26
  86.1 1.6 %collective-permute-start.28 = (bf16[32,512]{1,0:T(8,128)(2,1)S(1)}, bf16[32,512]{1,0:T(8,128)(2,1)S(1)}, u32[]{:S(2)}, u32[]{:S(2)}) collective-permute-start(bf16[32,512]{1,0:T(8,128)(2,1)S(1)} %get-tuple-element.95), channel_id=1, source_target_pairs={{0,6},{1,7},{2,4},{3,5},{4,2},{5,3},{6,0},{7,1},{8,14},{9,15},{10,... | collective-permute-start | bytes 98312 | tf_op jit(solution)/shard_map/ppermute | solution.py:212
  87.6 1.4 %collective-permute-start.27 = (bf16[32,512]{1,0:T(8,128)(2,1)S(1)}, bf16[32,512]{1,0:T(8,128)(2,1)S(1)}, u32[]{:S(2)}, u32[]{:S(2)}) collective-permute-start(bf16[32,512]{1,0:T(8,128)(2,1)S(1)} %get-tuple-element.96), channel_id=1, source_target_pairs={{0,2},{1,3},{2,0},{3,1},{4,6},{5,7},{6,4},{7,5},{8,10},{9,11},{10,... | collective-permute-start | bytes 98312 | tf_op jit(solution)/shard_map/ppermute | solution.py:212
  89.1 1.3 %collective-permute-done.26 = bf16[32,512]{1,0:T(8,128)(2,1)S(1)} collective-permute-done((bf16[32,512]{1,0:T(8,128)(2,1)S(1)}, bf16[32,512]{1,0:T(8,128)(2,1)S(1)}, u32[]{:S(2)}, u32[]{:S(2)}) %collective-permute-start.26) | collective-permute-done | bytes 32800 | tf_op jit(solution)/shard_map/ppermute | solution.py:212
  90.4 1.5 %collective-permute-done.28 = bf16[32,512]{1,0:T(8,128)(2,1)S(1)} collective-permute-done((bf16[32,512]{1,0:T(8,128)(2,1)S(1)}, bf16[32,512]{1,0:T(8,128)(2,1)S(1)}, u32[]{:S(2)}, u32[]{:S(2)}) %collective-permute-start.28) | collective-permute-done | bytes 32800 | tf_op jit(solution)/shard_map/ppermute | solution.py:212
  91.9 0.7 divide_subtract_fusion
  (52 shorter events, 0.6 us)
Async XLA Ops:
  0.6 6.6 %copy-start.4 = (s32[2,512]{1,0:T(2,128)S(1)}, s32[2,512]{1,0:T(2,128)}, u32[]{:S(2)}) copy-start(s32[2,512]{1,0:T(2,128)} %trows_ref.1) | copy-start | bytes 12292
  0.6 6.6 %copy-start.5 = (s32[2,4,128]{2,1,0:T(4,128)S(1)}, s32[2,4,128]{2,1,0:T(4,128)}, u32[]{:S(2)}) copy-start(s32[2,4,128]{2,1,0:T(4,128)} %neg_ref.1) | copy-start | bytes 12292
  0.7 6.6 %copy-start.6 = (s32[2,512]{1,0:T(2,128)S(1)}, s32[2,512]{1,0:T(2,128)}, u32[]{:S(2)}) copy-start(s32[2,512]{1,0:T(2,128)} %hrows_ref.5) | copy-start | bytes 12292
  1.5 8.9 %collective-permute-start.2 = (bf16[32,512]{1,0:T(8,128)(2,1)S(1)}, bf16[32,512]{1,0:T(8,128)(2,1)S(1)}, u32[]{:S(2)}, u32[]{:S(2)}) collective-permute-start(bf16[32,512]{1,0:T(8,128)(2,1)S(1)} %get-tuple-element.85), channel_id=1, source_target_pairs={{0,6},{1,7},{2,4},{3,5},{4,2},{5,3},{6,0},{7,1},{8,14},{9,15},{10,... | collective-permute-start | bytes 98312 | tf_op jit(solution)/shard_map/ppermute | solution.py:212
  6.6 3.9 %collective-permute-start.1 = (bf16[32,512]{1,0:T(8,128)(2,1)S(1)}, bf16[32,512]{1,0:T(8,128)(2,1)S(1)}, u32[]{:S(2)}, u32[]{:S(2)}) collective-permute-start(bf16[32,512]{1,0:T(8,128)(2,1)S(1)} %get-tuple-element.85), channel_id=1, source_target_pairs={{0,2},{1,3},{2,0},{3,1},{4,6},{5,7},{6,4},{7,5},{8,10},{9,11},{10,... | collective-permute-start | bytes 98312 | tf_op jit(solution)/shard_map/ppermute | solution.py:212
  6.6 4.9 %collective-permute-start = (bf16[32,512]{1,0:T(8,128)(2,1)S(1)}, bf16[32,512]{1,0:T(8,128)(2,1)S(1)}, u32[]{:S(2)}, u32[]{:S(2)}) collective-permute-start(bf16[32,512]{1,0:T(8,128)(2,1)S(1)} %get-tuple-element.85), channel_id=1, source_target_pairs={{0,4},{1,5},{2,6},{3,7},{4,0},{5,1},{6,2},{7,3},{8,12},{9,13},{10,... | collective-permute-start | bytes 98312 | tf_op jit(solution)/shard_map/ppermute | solution.py:212
  7.2 1.2 %copy-start = (f32[512,512]{1,0:T(8,128)S(1)}, f32[512,512]{1,0:T(8,128)}, u32[]{:S(2)}) copy-start(f32[512,512]{1,0:T(8,128)} %table_ref.2) | copy-start | bytes 3145732
  8.4 1.2 %copy-start.2 = (f32[512,512]{1,0:T(8,128)S(1)}, f32[512,512]{1,0:T(8,128)}, u32[]{:S(2)}) copy-start(f32[512,512]{1,0:T(8,128)} %table_ref.3) | copy-start | bytes 3145732
  11.5 7.2 %collective-permute-start.5 = (bf16[128,512]{1,0:T(8,128)(2,1)S(1)}, bf16[128,512]{1,0:T(8,128)(2,1)S(1)}, u32[]{:S(2)}, u32[]{:S(2)}) collective-permute-start(bf16[128,512]{1,0:T(8,128)(2,1)S(1)} %pad_maximum_fusion), channel_id=1, source_target_pairs={{0,17},{1,16},{2,19},{3,18},{4,21},{5,20},{6,23},{7,22},{8,25},{9,... | collective-permute-start | bytes 393224 | tf_op jit(solution)/shard_map/ppermute | solution.py:212
  14.0 5.6 %collective-permute-start.4 = (bf16[128,512]{1,0:T(8,128)(2,1)S(1)}, bf16[128,512]{1,0:T(8,128)(2,1)S(1)}, u32[]{:S(2)}, u32[]{:S(2)}) collective-permute-start(bf16[128,512]{1,0:T(8,128)(2,1)S(1)} %pad_maximum_fusion), channel_id=1, source_target_pairs={{0,16},{1,17},{2,18},{3,19},{4,20},{5,21},{6,22},{7,23},{8,24},{9,... | collective-permute-start | bytes 393224 | tf_op jit(solution)/shard_map/ppermute | solution.py:212
  14.5 5.1 %collective-permute-start.3 = (bf16[128,512]{1,0:T(8,128)(2,1)S(1)}, bf16[128,512]{1,0:T(8,128)(2,1)S(1)}, u32[]{:S(2)}, u32[]{:S(2)}) collective-permute-start(bf16[128,512]{1,0:T(8,128)(2,1)S(1)} %pad_maximum_fusion), channel_id=1, source_target_pairs={{0,1},{1,0},{2,3},{3,2},{4,5},{5,4},{6,7},{7,6},{8,9},{9,8},{10,11... | collective-permute-start | bytes 393224 | tf_op jit(solution)/shard_map/ppermute | solution.py:212
  19.7 2.0 %collective-permute-start.6 = (bf16[512,512]{1,0:T(8,128)(2,1)S(1)}, bf16[512,512]{1,0:T(8,128)(2,1)S(1)}, u32[]{:S(2)}, u32[]{:S(2)}) collective-permute-start(bf16[512,512]{1,0:T(8,128)(2,1)S(1)} %constant_dynamic-update-slice_fusion.lo_ref), channel_id=1, source_target_pairs={{0,8},{1,9},{2,10},{3,11},{4,12},{5,13},{6,14},{7,15},{8,0},{9,1},... | collective-permute-start | bytes 1572872 | tf_op jit(solution)/shard_map/ppermute | solution.py:212
  19.8 0.7 copy-start.12
  20.5 0.7 copy-start.13
  21.2 0.7 copy-start.9
  24.9 5.8 %copy-start.1 = (f32[512,512]{1,0:T(8,128)S(1)}, f32[512,512]{1,0:T(8,128)}, u32[]{:S(2)}) copy-start(f32[512,512]{1,0:T(8,128)} %table_ref.2) | copy-start | bytes 3145732
  24.9 2.1 %collective-permute-start.7 = (bf16[512,512]{1,0:T(8,128)(2,1)S(1)}, bf16[512,512]{1,0:T(8,128)(2,1)S(1)}, u32[]{:S(2)}, u32[]{:S(2)}) collective-permute-start(bf16[512,512]{1,0:T(8,128)(2,1)S(1)} %get-tuple-element.54), channel_id=1, source_target_pairs={{0,8},{1,9},{2,10},{3,11},{4,12},{5,13},{6,14},{7,15},{8,0},{9,1},... | collective-permute-start | bytes 1572872 | tf_op jit(solution)/shard_map/ppermute | solution.py:212
  27.1 8.0 %collective-permute-start.10 = (bf16[128,512]{1,0:T(8,128)(2,1)S(1)}, bf16[128,512]{1,0:T(8,128)(2,1)S(1)}, u32[]{:S(2)}, u32[]{:S(2)}) collective-permute-start(bf16[128,512]{1,0:T(8,128)(2,1)S(1)} %get-tuple-element.90), channel_id=1, source_target_pairs={{0,17},{1,16},{2,19},{3,18},{4,21},{5,20},{6,23},{7,22},{8,25},{9,... | collective-permute-start | bytes 393224 | tf_op jit(solution)/shard_map/ppermute | solution.py:212
  28.6 8.1 %collective-permute-start.9 = (bf16[128,512]{1,0:T(8,128)(2,1)S(1)}, bf16[128,512]{1,0:T(8,128)(2,1)S(1)}, u32[]{:S(2)}, u32[]{:S(2)}) collective-permute-start(bf16[128,512]{1,0:T(8,128)(2,1)S(1)} %get-tuple-element.91), channel_id=1, source_target_pairs={{0,16},{1,17},{2,18},{3,19},{4,20},{5,21},{6,22},{7,23},{8,24},{9,... | collective-permute-start | bytes 393224 | tf_op jit(solution)/shard_map/ppermute | solution.py:212
  29.7 7.0 %collective-permute-start.8 = (bf16[128,512]{1,0:T(8,128)(2,1)S(1)}, bf16[128,512]{1,0:T(8,128)(2,1)S(1)}, u32[]{:S(2)}, u32[]{:S(2)}) collective-permute-start(bf16[128,512]{1,0:T(8,128)(2,1)S(1)} %get-tuple-element.92), channel_id=1, source_target_pairs={{0,1},{1,0},{2,3},{3,2},{4,5},{5,4},{6,7},{7,6},{8,9},{9,8},{10,11... | collective-permute-start | bytes 393224 | tf_op jit(solution)/shard_map/ppermute | solution.py:212
  30.7 0.7 copy-start.7
  31.4 1.2 %copy-start.3 = (f32[512,512]{1,0:T(8,128)S(1)}, f32[512,512]{1,0:T(8,128)}, u32[]{:S(2)}) copy-start(f32[512,512]{1,0:T(8,128)} %table_ref.3) | copy-start | bytes 3145732
  32.1 0.8 copy-start.8
  36.7 8.3 %copy-start.10 = (f32[32,512]{1,0:T(8,128)S(1)}, f32[32,512]{1,0:T(8,128)}, u32[]{:S(2)}) copy-start(f32[32,512]{1,0:T(8,128)} %param.16) | copy-start | bytes 196612
  36.7 8.3 %copy-start.11 = (f32[32,512]{1,0:T(8,128)S(1)}, f32[32,512]{1,0:T(8,128)}, u32[]{:S(2)}) copy-start(f32[32,512]{1,0:T(8,128)} %param.17) | copy-start | bytes 196612
  36.7 4.9 %collective-permute-start.11 = (bf16[32,512]{1,0:T(8,128)(2,1)S(1)}, bf16[32,512]{1,0:T(8,128)(2,1)S(1)}, u32[]{:S(2)}, u32[]{:S(2)}) collective-permute-start(bf16[32,512]{1,0:T(8,128)(2,1)S(1)} %get-tuple-element.97), channel_id=1, source_target_pairs={{0,4},{1,5},{2,6},{3,7},{4,0},{5,1},{6,2},{7,3},{8,12},{9,13},{10,... | collective-permute-start | bytes 98312 | tf_op jit(solution)/shard_map/ppermute | solution.py:212
  38.5 5.7 %collective-permute-start.13 = (bf16[32,512]{1,0:T(8,128)(2,1)S(1)}, bf16[32,512]{1,0:T(8,128)(2,1)S(1)}, u32[]{:S(2)}, u32[]{:S(2)}) collective-permute-start(bf16[32,512]{1,0:T(8,128)(2,1)S(1)} %get-tuple-element.98), channel_id=1, source_target_pairs={{0,6},{1,7},{2,4},{3,5},{4,2},{5,3},{6,0},{7,1},{8,14},{9,15},{10,... | collective-permute-start | bytes 98312 | tf_op jit(solution)/shard_map/ppermute | solution.py:212
  41.0 3.9 %collective-permute-start.12 = (bf16[32,512]{1,0:T(8,128)(2,1)S(1)}, bf16[32,512]{1,0:T(8,128)(2,1)S(1)}, u32[]{:S(2)}, u32[]{:S(2)}) collective-permute-start(bf16[32,512]{1,0:T(8,128)(2,1)S(1)} %get-tuple-element.99), channel_id=1, source_target_pairs={{0,2},{1,3},{2,0},{3,1},{4,6},{5,7},{6,4},{7,5},{8,10},{9,11},{10,... | collective-permute-start | bytes 98312 | tf_op jit(solution)/shard_map/ppermute | solution.py:212
  45.0 5.8 %collective-permute-start.16 = (bf16[32,512]{1,0:T(8,128)(2,1)S(1)}, bf16[32,512]{1,0:T(8,128)(2,1)S(1)}, u32[]{:S(2)}, u32[]{:S(2)}) collective-permute-start(bf16[32,512]{1,0:T(8,128)(2,1)S(1)} %get-tuple-element.82), channel_id=1, source_target_pairs={{0,6},{1,7},{2,4},{3,5},{4,2},{5,3},{6,0},{7,1},{8,14},{9,15},{10,... | collective-permute-start | bytes 98312 | tf_op jit(solution)/shard_map/ppermute | solution.py:212
  46.9 4.3 %collective-permute-start.15 = (bf16[32,512]{1,0:T(8,128)(2,1)S(1)}, bf16[32,512]{1,0:T(8,128)(2,1)S(1)}, u32[]{:S(2)}, u32[]{:S(2)}) collective-permute-start(bf16[32,512]{1,0:T(8,128)(2,1)S(1)} %get-tuple-element.82), channel_id=1, source_target_pairs={{0,2},{1,3},{2,0},{3,1},{4,6},{5,7},{6,4},{7,5},{8,10},{9,11},{10,... | collective-permute-start | bytes 98312 | tf_op jit(solution)/shard_map/ppermute | solution.py:212
  46.9 4.8 %collective-permute-start.14 = (bf16[32,512]{1,0:T(8,128)(2,1)S(1)}, bf16[32,512]{1,0:T(8,128)(2,1)S(1)}, u32[]{:S(2)}, u32[]{:S(2)}) collective-permute-start(bf16[32,512]{1,0:T(8,128)(2,1)S(1)} %get-tuple-element.82), channel_id=1, source_target_pairs={{0,4},{1,5},{2,6},{3,7},{4,0},{5,1},{6,2},{7,3},{8,12},{9,13},{10,... | collective-permute-start | bytes 98312 | tf_op jit(solution)/shard_map/ppermute | solution.py:212
  49.5 20.2 %collective-permute-start.21 = (bf16[528,512]{1,0:T(8,128)(2,1)S(1)}, bf16[528,512]{1,0:T(8,128)(2,1)S(1)}, u32[]{:S(2)}, u32[]{:S(2)}) collective-permute-start(bf16[528,512]{1,0:T(8,128)(2,1)S(1)} %shard_map.141), channel_id=1, source_target_pairs={{0,1},{1,2},{2,3},{3,4},{4,5},{5,6},{6,7},{7,0},{8,9},{9,10},{10,1... | collective-permute-start | bytes 1622024 | tf_op jit(solution)/shard_map/ppermute | solution.py:320
  51.8 16.3 %collective-permute-start.19 = (bf16[128,512]{1,0:T(8,128)(2,1)S(1)}, bf16[128,512]{1,0:T(8,128)(2,1)S(1)}, u32[]{:S(2)}, u32[]{:S(2)}) collective-permute-start(bf16[128,512]{1,0:T(8,128)(2,1)S(1)} %pad_maximum_fusion.1), channel_id=1, source_target_pairs={{0,17},{1,16},{2,19},{3,18},{4,21},{5,20},{6,23},{7,22},{8,25},{9,... | collective-permute-start | bytes 393224 | tf_op jit(solution)/shard_map/ppermute | solution.py:212
  53.2 14.8 %collective-permute-start.18 = (bf16[128,512]{1,0:T(8,128)(2,1)S(1)}, bf16[128,512]{1,0:T(8,128)(2,1)S(1)}, u32[]{:S(2)}, u32[]{:S(2)}) collective-permute-start(bf16[128,512]{1,0:T(8,128)(2,1)S(1)} %pad_maximum_fusion.1), channel_id=1, source_target_pairs={{0,16},{1,17},{2,18},{3,19},{4,20},{5,21},{6,22},{7,23},{8,24},{9,... | collective-permute-start | bytes 393224 | tf_op jit(solution)/shard_map/ppermute | solution.py:212
  54.5 15.1 %collective-permute-start.17 = (bf16[128,512]{1,0:T(8,128)(2,1)S(1)}, bf16[128,512]{1,0:T(8,128)(2,1)S(1)}, u32[]{:S(2)}, u32[]{:S(2)}) collective-permute-start(bf16[128,512]{1,0:T(8,128)(2,1)S(1)} %pad_maximum_fusion.1), channel_id=1, source_target_pairs={{0,1},{1,0},{2,3},{3,2},{4,5},{5,4},{6,7},{7,6},{8,9},{9,8},{10,11... | collective-permute-start | bytes 393224 | tf_op jit(solution)/shard_map/ppermute | solution.py:212
  69.6 2.0 %collective-permute-start.20 = (bf16[512,512]{1,0:T(8,128)(2,1)S(1)}, bf16[512,512]{1,0:T(8,128)(2,1)S(1)}, u32[]{:S(2)}, u32[]{:S(2)}) collective-permute-start(bf16[512,512]{1,0:T(8,128)(2,1)S(1)} %constant_dynamic-update-slice_fusion.7.lo_ref), channel_id=1, source_target_pairs={{0,8},{1,9},{2,10},{3,11},{4,12},{5,13},{6,14},{7,15},{8,0},{9,1},... | collective-permute-start | bytes 1572872 | tf_op jit(solution)/shard_map/ppermute | solution.py:212
  74.6 2.0 %collective-permute-start.22 = (bf16[512,512]{1,0:T(8,128)(2,1)S(1)}, bf16[512,512]{1,0:T(8,128)(2,1)S(1)}, u32[]{:S(2)}, u32[]{:S(2)}) collective-permute-start(bf16[512,512]{1,0:T(8,128)(2,1)S(1)} %get-tuple-element.70), channel_id=1, source_target_pairs={{0,8},{1,9},{2,10},{3,11},{4,12},{5,13},{6,14},{7,15},{8,0},{9,1},... | collective-permute-start | bytes 1572872 | tf_op jit(solution)/shard_map/ppermute | solution.py:212
  76.7 8.2 %collective-permute-start.25 = (bf16[128,512]{1,0:T(8,128)(2,1)S(1)}, bf16[128,512]{1,0:T(8,128)(2,1)S(1)}, u32[]{:S(2)}, u32[]{:S(2)}) collective-permute-start(bf16[128,512]{1,0:T(8,128)(2,1)S(1)} %get-tuple-element.87), channel_id=1, source_target_pairs={{0,17},{1,16},{2,19},{3,18},{4,21},{5,20},{6,23},{7,22},{8,25},{9,... | collective-permute-start | bytes 393224 | tf_op jit(solution)/shard_map/ppermute | solution.py:212
  76.8 8.4 %collective-permute-start.24 = (bf16[128,512]{1,0:T(8,128)(2,1)S(1)}, bf16[128,512]{1,0:T(8,128)(2,1)S(1)}, u32[]{:S(2)}, u32[]{:S(2)}) collective-permute-start(bf16[128,512]{1,0:T(8,128)(2,1)S(1)} %get-tuple-element.88), channel_id=1, source_target_pairs={{0,16},{1,17},{2,18},{3,19},{4,20},{5,21},{6,22},{7,23},{8,24},{9,... | collective-permute-start | bytes 393224 | tf_op jit(solution)/shard_map/ppermute | solution.py:212
  77.8 7.7 %collective-permute-start.23 = (bf16[128,512]{1,0:T(8,128)(2,1)S(1)}, bf16[128,512]{1,0:T(8,128)(2,1)S(1)}, u32[]{:S(2)}, u32[]{:S(2)}) collective-permute-start(bf16[128,512]{1,0:T(8,128)(2,1)S(1)} %get-tuple-element.89), channel_id=1, source_target_pairs={{0,1},{1,0},{2,3},{3,2},{4,5},{5,4},{6,7},{7,6},{8,9},{9,8},{10,11... | collective-permute-start | bytes 393224 | tf_op jit(solution)/shard_map/ppermute | solution.py:212
  85.5 4.9 %collective-permute-start.26 = (bf16[32,512]{1,0:T(8,128)(2,1)S(1)}, bf16[32,512]{1,0:T(8,128)(2,1)S(1)}, u32[]{:S(2)}, u32[]{:S(2)}) collective-permute-start(bf16[32,512]{1,0:T(8,128)(2,1)S(1)} %get-tuple-element.94), channel_id=1, source_target_pairs={{0,4},{1,5},{2,6},{3,7},{4,0},{5,1},{6,2},{7,3},{8,12},{9,13},{10,... | collective-permute-start | bytes 98312 | tf_op jit(solution)/shard_map/ppermute | solution.py:212
  86.1 5.8 %collective-permute-start.28 = (bf16[32,512]{1,0:T(8,128)(2,1)S(1)}, bf16[32,512]{1,0:T(8,128)(2,1)S(1)}, u32[]{:S(2)}, u32[]{:S(2)}) collective-permute-start(bf16[32,512]{1,0:T(8,128)(2,1)S(1)} %get-tuple-element.95), channel_id=1, source_target_pairs={{0,6},{1,7},{2,4},{3,5},{4,2},{5,3},{6,0},{7,1},{8,14},{9,15},{10,... | collective-permute-start | bytes 98312 | tf_op jit(solution)/shard_map/ppermute | solution.py:212
  87.6 4.3 %collective-permute-start.27 = (bf16[32,512]{1,0:T(8,128)(2,1)S(1)}, bf16[32,512]{1,0:T(8,128)(2,1)S(1)}, u32[]{:S(2)}, u32[]{:S(2)}) collective-permute-start(bf16[32,512]{1,0:T(8,128)(2,1)S(1)} %get-tuple-element.96), channel_id=1, source_target_pairs={{0,2},{1,3},{2,0},{3,1},{4,6},{5,7},{6,4},{7,5},{8,10},{9,11},{10,... | collective-permute-start | bytes 98312 | tf_op jit(solution)/shard_map/ppermute | solution.py:212

commit v3 on v2

--- a/solution.py
+++ b/solution.py
@@ -86,9 +86,9 @@
 
 
 def score_kernel(
-    k, nneg, nat_ref, live_ref, rel_ref, lo_ref, hi_ref, h_ref, t_ref, tcol_ref, cnt_ref,
-    keep_ref, send_ref, w_ref, u_ref, gu_ref, rel_s, grad_s,
+    k, nneg, nat_ref, live_ref, rel_ref, lo_ref, hi_ref, h_ref, tcol_ref, cnt_ref, *rest
 ):
+    tail_refs, (keep_ref, send_ref, w_ref, u_ref, gu_ref, rel_s, grad_s) = rest[:-7], rest[-7:]
     edges, width = h_ref.shape
     blocks, rows = cnt_ref.shape[1:]
     size = edges // blocks
@@ -100,7 +100,7 @@
         u = u + dot(masked[r], rel_s[r * width : (r + 1) * width], COLS, ROWS)
     u = u.astype(BF16)
     u_ref[...] = u
-    tails = t_ref[0:rows]
+    tails = jnp.concatenate([ref[...] for ref in tail_refs])[0:rows]
     score = dot(u, tails, COLS, COLS)
     row_id = lax.broadcasted_iota(jnp.int32, (size, rows), 1).astype(F32)
     for b in range(blocks):
@@ -129,24 +129,28 @@
             ref[j * own : (j + 1) * own] = grad_s[rows_of].astype(BF16)
 
 
-def tail_kernel(w_ref, u_ref, table_ref, state_ref, out_ref):
+def tail_kernel(w_ref, u_ref, table_ref, state_ref, *out_refs):
     rows, width = table_ref.shape
     gradient = dot(w_ref[...], u_ref[...], ROWS, ROWS)
     table, state = adagrad_rows(table_ref[...], state_ref[...], gradient)
-    out_ref[0:rows] = table.astype(BF16)
     state_row = state.T[0:1, :]
     high = state_row.astype(BF16).astype(F32)
     row_id = lax.broadcasted_iota(jnp.int32, (PACK_ROWS, width), 0)
     packed = jnp.where(row_id == 0, high, jnp.where(row_id == 1, state_row - high, 0.0))
-    out_ref[rows : rows + PACK_ROWS] = packed.astype(BF16)
-
-
-def last_tail_kernel(w_ref, u_ref, packed_ref, out_ref):
+    packed = jnp.concatenate([table, packed]).astype(BF16)
+    start = 0
+    for ref in out_refs:
+        ref[...] = packed[start : start + ref.shape[0]]
+        start += ref.shape[0]
+
+
+def last_tail_kernel(w_ref, u_ref, *refs):
+    tail_refs, out_ref = refs[:-1], refs[-1]
     rows = out_ref.shape[0]
     gradient = dot(w_ref[...], u_ref[...], ROWS, ROWS)
-    packed = packed_ref[rows : rows + PACK_ROWS].astype(F32)
-    state_row = packed[0:1, :] + packed[1:2, :]
-    out_ref[...] = adagrad_rows(packed_ref[0:rows].astype(F32), state_row, gradient)[0]
+    packed = jnp.concatenate([ref[...] for ref in tail_refs]).astype(F32)
+    state_row = packed[rows : rows + 1] + packed[rows + 1 : rows + 2]
+    out_ref[...] = adagrad_rows(packed[0:rows], state_row, gradient)[0]
 
 
 def head_kernel(
@@ -193,8 +197,9 @@
         head_bits = [tails << i for i in range(heads.bit_length() - 1)]
         tail_bits = [1 << i for i in range(tails.bit_length() - 1)]
         rest = head_bits[1:2] + tail_bits + head_bits[2:]
-        self.stages = [head_bits[:1]] + [rest[i : i + 2] for i in range(0, len(rest), 2)]
-        bits = [bit for stage in self.stages for bit in stage]
+        pairs = [rest[i : i + 2] for i in range(0, len(rest), 2)]
+        self.stages = [head_bits[:1]] + pairs
+        bits = head_bits[:1] + rest
         places = [self.others(bits, j) for j in range(self.devices)]
         slots = np.zeros(self.devices, np.int32)
         slots[places] = np.arange(self.devices)
@@ -211,7 +216,7 @@
     def swap(self, x, mask):
         return lax.ppermute(x, AXES, [(i, i ^ mask) for i in range(self.devices)])
 
-    def reduce_scatter(self, keep, send, beside):
+    def reduce_scatter(self, keep, send, hooks):
         if (2 * keep.shape[0] // self.devices) % PACK_ROWS:
             both = jnp.concatenate([keep, send])
             both = both.reshape(self.devices, -1, both.shape[1])[self.block_of_slot]
@@ -219,11 +224,9 @@
         parts = [keep, send]
         for i, stage in enumerate(self.stages):
             got = [self.swap(part, mask) for part, mask in zip(parts[1:], self.masks(stage))]
-            if i == 1:
-                got, beside = lax.optimization_barrier((got, beside))
-            pieces = parts[:1] + got
+            pieces = parts[:1] + hooks.get(i, list)(got)
             if i + 1 == len(self.stages):
-                return sum(piece.astype(F32) for piece in pieces), beside
+                return sum(piece.astype(F32) for piece in pieces)
             count = 1 << len(self.stages[i + 1])
             size = pieces[0].shape[0] // count
             parts = [
@@ -231,18 +234,16 @@
                 for j in range(count)
             ]
 
-    def all_gather(self, own, beside=()):
+    def all_gather(self, own, hooks):
         rows = own.shape[0]
         for i, stage in reversed(list(enumerate(self.stages))[1:]):
             got = [self.swap(own, mask) for mask in self.masks(stage)]
-            if i == 1:
-                got, beside = lax.optimization_barrier((got, beside))
-            own = jnp.concatenate([own] + got)
+            own = jnp.concatenate([own] + hooks.get(i, list)(got))
         lo, hi = own, self.swap(own, self.masks(self.stages[0])[0])
         if rows % PACK_ROWS:
             both = jnp.concatenate([lo, hi]).reshape(self.devices, rows, -1)[self.slot_of_block]
             lo, hi = jnp.split(both.reshape(self.devices * rows, -1), 2)
-        return lo, hi, beside
+        return lo, hi
 
 
 def shards(
@@ -268,7 +269,7 @@
     half = all_rows // 2
     square = 2 * rows * edges * width
 
-    beside = call(
+    prepared = call(
         prepare_kernel,
         [
             ((edges, width), BF16),
@@ -281,10 +282,41 @@
     )
     head_state = head_state.reshape(1, -1)
     tail_state = tail_state.reshape(1, -1)
+    held = {"prepared": prepared}
+    rotated = []
+
+    def with_(name):
+        def hook(got):
+            got, held[name] = lax.optimization_barrier((got, held[name]))
+            return got
+
+        return hook
+
+    def rotate(x, step):
+        if step == 0:
+            return lax.ppermute(x, "tail", [(i, (i + i % 2 * 2) % tails) for i in range(tails)])
+        return lax.ppermute(x, "tail", [(i, i ^ 1) for i in range(tails)])
+
+    def rotation(start, wait):
+        def hook(got):
+            if start is not None:
+                got[0], part = lax.optimization_barrier((got[0], step0[start]))
+                moved = rotate(part, 1)
+            if wait is not None:
+                got, rotated[wait] = lax.optimization_barrier((got, rotated[wait]))
+            if start is not None:
+                rotated.append(moved)
+            return got
+
+        return hook
+
+    gather_hooks = {1: with_("prepared")}
     for k in range(2):
-        lo, hi, beside = exchange.all_gather(relations.astype(BF16), beside)
+        lo, hi = exchange.all_gather(relations.astype(BF16), gather_hooks)
         if k == 0:
-            head_vecs, tail_vecs, tail_col, counts = beside
+            head_vecs, *tail_vecs, tail_col, counts = held["prepared"]
+        else:
+            tail_vecs = rotated
         keep, send, weights, projected, edge_grad = call(
             functools.partial(score_kernel, k, float(nneg)),
             [
@@ -295,33 +327,45 @@
                 ((edges, width), BF16),
             ],
             3, [pltpu.VMEM((all_rows, width), BF16), pltpu.VMEM((all_rows, width), F32)], 6 * square,
-            nat, block_counts, relation_ids, lo, hi, head_vecs, tail_vecs, tail_col, counts,
+            nat, block_counts, relation_ids, lo, hi, head_vecs, tail_col, counts, *tail_vecs,
         )
         head_outs = [(head_table.shape, F32)]
         if k == 0:
             tail_new = call(
-                tail_kernel, [((rows + PACK_ROWS, width), BF16)], 0, [], square,
+                tail_kernel, [((n, width), BF16) for n in [rows + PACK_ROWS]], 0, [], square,
                 weights, projected, tail_table, tail_state,
             )
             head_outs += [(head_state.shape, F32), ((edges, width), BF16)]
         else:
             tail_new = call(
                 last_tail_kernel, [((rows, width), F32)], 0, [], square,
-                weights, projected, tail_vecs,
+                weights, projected, *tail_vecs,
             )
         head_new = call(
             functools.partial(head_kernel, k, blocks), head_outs,
             2, [pltpu.VMEM((all_rows, width), BF16)], 4 * square,
             nat, relation_ids, lo, hi, edge_grad, head_rows, head_table, head_state,
         )
-        grad, ((tail_new,), head_new) = exchange.reduce_scatter(keep, send, (tail_new, head_new))
+        held.update(tail=tail_new, head=list(head_new))
         if k == 0:
-            head_table, head_state, head_vecs = head_new
-            tail_vecs = lax.ppermute(tail_new, "tail", [(i, (i + 1) % tails) for i in range(tails)])
+            step0 = []
+
+            def begin(got):
+                got = with_("tail")(got)
+                step0.extend(rotate(x, 0) for x in held["tail"])
+                return got
+
+            hooks = {0: begin, 1: with_("head"), 2: rotation(0, None)}
+        else:
+            first, second = with_("tail"), with_("head")
+            hooks = {1: lambda got: first(second(got))}
+        grad = exchange.reduce_scatter(keep, send, hooks)
+        if k == 0:
+            head_table, head_state, head_vecs = held["head"]
+            gather_hooks = {1: rotation(None, 0)}
         relation_state = relation_state + grad * grad
         relations = relations - RATE_RELATIONS * grad / (jnp.sqrt(relation_state) + EPSILON)
-        beside = ()
-    return (head_new[0], tail_new, relations)
+    return (held["head"][0], held["tail"][0], relations)
 
 
 def solution(mesh):

time: 93 us -> 89.6 us (0.963)
  waiting for transfers between devices: 35.6 us -> 27.4 us
  starting transfers between devices: 34.2 us -> 39 us
    ppermute x28, waiting for transfers between devices: 35.6 us -> 27.4 us  [swap(): return lax.ppermute(x, AXES, [(i, i ^ mask) for i in range(self.devices)])]
    ppermute x1 -> x2, starting transfers between devices: 1.05 us -> 4.76 us  [the longest x1 3.94 us: rotate(): return lax.ppermute(x, 'tail', [(i, i ^ 1) for i in range(tails)])]
    ppermute x28, starting transfers between devices: 33.1 us -> 34.3 us  [swap(): return lax.ppermute(x, AXES, [(i, i ^ mask) for i in range(self.devices)])]
  transfers between devices with their start and end apart: 29 -> 30, of which waited for: 21 -> 17; matrix products, arithmetic and copies ran while one was open for 0% -> 0% of each run, Pallas kernels for 9% -> 9%
where the time goes in v3:
time: 89.6 us; the launch traced here: 89.2 us
  starting transfers between devices  39 us (44%)
  waiting for transfers between devices  27.4 us (31%)
  Pallas kernels  14.3 us (16%)
  local copies, waits for them, and re-layouts  5.5 us (6%)
  other arithmetic  2.09 us (2%)
    ppermute x28, starting transfers between devices, swap(): return lax.ppermute(x, AXES, [(i, i ^ mask) for i in range(self.devices)])  34.3 us
    ppermute x28, waiting for transfers between devices, swap(): return lax.ppermute(x, AXES, [(i, i ^ mask) for i in range(self.devices)])  27.4 us
    pallas_call x7, Pallas kernels, call(): pl.pallas_call(kernel, out_shape=outs, in_specs=[SMEM] * smem + [VMEM] *...  14.3 us
    unnamed x39, local copies, waits for them, and re-layouts  5.48 us
    ppermute x1, starting transfers between devices, rotate(): return lax.ppermute(x, 'tail', [(i, i ^ 1) for i in range(tails)])  3.94 us
  transfers between devices with their start and end apart: 30, of which 17 were waited for; matrix products, arithmetic and copies ran while one was open for 0% of the time, Pallas kernels for 9%

profile of v3, /device:TPU:0, one launch (start us, length us, event | category | flops | bytes accessed | tf_op | source)
XLA Modules:
  0.0 89.2 jit_solution(16145908973509766119)
XLA Ops:
  0.7 0.9 constant_dynamic-update-slice_fusion.6
  1.5 5.0 %collective-permute-start.2 = (bf16[32,512]{1,0:T(8,128)(2,1)S(1)}, bf16[32,512]{1,0:T(8,128)(2,1)S(1)}, u32[]{:S(2)}, u32[]{:S(2)}) collective-permute-start(bf16[32,512]{1,0:T(8,128)(2,1)S(1)} %get-tuple-element.99), channel_id=1, source_target_pairs={{0,6},{1,7},{2,4},{3,5},{4,2},{5,3},{6,0},{7,1},{8,14},{9,15},{10,... | collective-permute-start | bytes 98312 | tf_op jit(solution)/shard_map/ppermute | solution.py:217
  6.6 0.6 collective-permute-start
  7.2 1.2 %copy-done = f32[512,512]{1,0:T(8,128)S(1)} copy-done((f32[512,512]{1,0:T(8,128)S(1)}, f32[512,512]{1,0:T(8,128)}, u32[]{:S(2)}) %copy-start) | copy-done | bytes 1048600
  8.4 1.2 %copy-done.2 = f32[512,512]{1,0:T(8,128)S(1)} copy-done((f32[512,512]{1,0:T(8,128)S(1)}, f32[512,512]{1,0:T(8,128)}, u32[]{:S(2)}) %copy-start.2) | copy-done | bytes 1048600
  9.7 0.7 shard_map.139
  10.4 0.1 collective-permute-done.1
  10.5 1.0 %collective-permute-done = bf16[32,512]{1,0:T(8,128)(2,1)S(1)} collective-permute-done((bf16[32,512]{1,0:T(8,128)(2,1)S(1)}, bf16[32,512]{1,0:T(8,128)(2,1)S(1)}, u32[]{:S(2)}, u32[]{:S(2)}) %collective-permute-start) | collective-permute-done | bytes 32800 | tf_op jit(solution)/shard_map/ppermute | solution.py:217
  11.5 2.5 %collective-permute-start.5 = (bf16[128,512]{1,0:T(8,128)(2,1)S(1)}, bf16[128,512]{1,0:T(8,128)(2,1)S(1)}, u32[]{:S(2)}, u32[]{:S(2)}) collective-permute-start(bf16[128,512]{1,0:T(8,128)(2,1)S(1)} %pad_maximum_fusion), channel_id=1, source_target_pairs={{0,17},{1,16},{2,19},{3,18},{4,21},{5,20},{6,23},{7,22},{8,25},{9,... | collective-permute-start | bytes 393224 | tf_op jit(solution)/shard_map/ppermute | solution.py:217
  14.0 0.5 collective-permute-start.4
  14.5 0.5 collective-permute-start.3
  15.1 3.6 %collective-permute-done.5 = bf16[128,512]{1,0:T(8,128)(2,1)S(1)} collective-permute-done((bf16[128,512]{1,0:T(8,128)(2,1)S(1)}, bf16[128,512]{1,0:T(8,128)(2,1)S(1)}, u32[]{:S(2)}, u32[]{:S(2)}) %collective-permute-start.5) | collective-permute-done | bytes 131104 | tf_op jit(solution)/shard_map/ppermute | solution.py:217
  18.7 0.9 %collective-permute-done.4 = bf16[128,512]{1,0:T(8,128)(2,1)S(1)} collective-permute-done((bf16[128,512]{1,0:T(8,128)(2,1)S(1)}, bf16[128,512]{1,0:T(8,128)(2,1)S(1)}, u32[]{:S(2)}, u32[]{:S(2)}) %collective-permute-start.4) | collective-permute-done | bytes 131104 | tf_op jit(solution)/shard_map/ppermute | solution.py:217
  19.7 0.1 collective-permute-start.6
  19.8 0.6 copy-done.12
  20.4 0.1 copy.16.live_ref
  20.5 0.7 copy-done.13
  21.2 0.5 collective-permute-done.6.hi_ref
  21.7 0.2 copy-done.9
  21.9 3.0 %shard_map.140 = (bf16[512,512]{1,0:T(8,128)(2,1)S(1)}, bf16[512,512]{1,0:T(8,128)(2,1)S(1)}, bf16[512,512]{1,0:T(8,128)(2,1)S(1)}, bf16[512,512]{1,0:T(8,128)(2,1)S(1)}, bf16[512,512]{1,0:T(8,128)(2,1)S(1)}) custom-call(s32[32]{0:T(128)S(1)} %broadcast_xor_fusion.nat_ref, s32[2,1]{1,0:T(2,128)S(1)} %copy.16.live_ref, s32[2,4]{1,0:T(2,128)S(1)} %copy-done.9, ...), custom_call_target="tpu_custom_call" | custom-call | flops 1610612736 | bytes 5259432 | tf_op jit(solution)/shard_map/pallas_call | solution.py:183
  24.9 0.6 collective-permute-start.7
  25.4 0.7 copy-done.7
  26.1 0.7 shard_map.141
  26.8 0.2 collective-permute-done.7
  27.0 0.8 collective-permute-start.12
  27.8 0.1 add_convert_fusion.4
  27.9 4.6 %collective-permute-start.10 = (bf16[128,512]{1,0:T(8,128)(2,1)S(1)}, bf16[128,512]{1,0:T(8,128)(2,1)S(1)}, u32[]{:S(2)}, u32[]{:S(2)}) collective-permute-start(bf16[128,512]{1,0:T(8,128)(2,1)S(1)} %get-tuple-element.104), channel_id=1, source_target_pairs={{0,17},{1,16},{2,19},{3,18},{4,21},{5,20},{6,23},{7,22},{8,25},{9,... | collective-permute-start | bytes 393224 | tf_op jit(solution)/shard_map/ppermute | solution.py:217
  32.5 0.9 %collective-permute-start.9 = (bf16[128,512]{1,0:T(8,128)(2,1)S(1)}, bf16[128,512]{1,0:T(8,128)(2,1)S(1)}, u32[]{:S(2)}, u32[]{:S(2)}) collective-permute-start(bf16[128,512]{1,0:T(8,128)(2,1)S(1)} %get-tuple-element.105), channel_id=1, source_target_pairs={{0,16},{1,17},{2,18},{3,19},{4,20},{5,21},{6,22},{7,23},{8,24},{9,... | collective-permute-start | bytes 393224 | tf_op jit(solution)/shard_map/ppermute | solution.py:217
  33.4 0.7 copy-done.8
  34.1 2.2 %shard_map.142 = (f32[512,512]{1,0:T(8,128)S(1)}, f32[1,512]{1,0:T(1,128)S(1)}, bf16[512,512]{1,0:T(8,128)(2,1)S(1)}) custom-call(s32[32]{0:T(128)S(1)} %broadcast_xor_fusion.nat_ref, s32[2,4]{1,0:T(2,128)S(1)} %copy-done.9, bf16[512,512]{1,0:T(8,128)(2,1)S(1)} %constant_dynamic-update-slice_fusion.lo_ref, ...), custom_call_target="tpu_custom_call" | custom-call | flops 1073741824 | bytes 4202656 | tf_op jit(solution)/shard_map/pallas_call | solution.py:183
  36.4 2.5 %collective-permute-done.9 = bf16[128,512]{1,0:T(8,128)(2,1)S(1)} collective-permute-done((bf16[128,512]{1,0:T(8,128)(2,1)S(1)}, bf16[128,512]{1,0:T(8,128)(2,1)S(1)}, u32[]{:S(2)}, u32[]{:S(2)}) %collective-permute-start.9) | collective-permute-done | bytes 131104 | tf_op jit(solution)/shard_map/ppermute | solution.py:217
  39.0 1.8 %collective-permute-start.11 = (bf16[32,512]{1,0:T(8,128)(2,1)S(1)}, bf16[32,512]{1,0:T(8,128)(2,1)S(1)}, u32[]{:S(2)}, u32[]{:S(2)}) collective-permute-start(bf16[32,512]{1,0:T(8,128)(2,1)S(1)} %get-tuple-element.111), channel_id=1, source_target_pairs={{0,4},{1,5},{2,6},{3,7},{4,0},{5,1},{6,2},{7,3},{8,12},{9,13},{10,... | collective-permute-start | bytes 98312 | tf_op jit(solution)/shard_map/ppermute | solution.py:217
  40.8 1.2 %collective-permute-start.14 = (bf16[32,512]{1,0:T(8,128)(2,1)S(1)}, bf16[32,512]{1,0:T(8,128)(2,1)S(1)}, u32[]{:S(2)}, u32[]{:S(2)}) collective-permute-start(bf16[32,512]{1,0:T(8,128)(2,1)S(1)} %get-tuple-element.112), channel_id=1, source_target_pairs={{0,6},{1,7},{2,4},{3,5},{4,2},{5,3},{6,0},{7,1},{8,14},{9,15},{10,... | collective-permute-start | bytes 98312 | tf_op jit(solution)/shard_map/ppermute | solution.py:217
  42.0 0.6 collective-permute-start.13
  42.6 1.9 %collective-permute-done.11 = bf16[32,512]{1,0:T(8,128)(2,1)S(1)} collective-permute-done((bf16[32,512]{1,0:T(8,128)(2,1)S(1)}, bf16[32,512]{1,0:T(8,128)(2,1)S(1)}, u32[]{:S(2)}, u32[]{:S(2)}) %collective-permute-start.11) | collective-permute-done | bytes 32800 | tf_op jit(solution)/shard_map/ppermute | solution.py:217
  44.5 3.9 %collective-permute-start.21 = (bf16[528,512]{1,0:T(8,128)(2,1)S(1)}, bf16[528,512]{1,0:T(8,128)(2,1)S(1)}, u32[]{:S(2)}, u32[]{:S(2)}) collective-permute-start(bf16[528,512]{1,0:T(8,128)(2,1)S(1)} %collective-permute-done.12), channel_id=1, source_target_pairs={{0,1},{1,0},{2,3},{3,2},{4,5},{5,4},{6,7},{7,6},{8,9},{9,8},{10,11... | collective-permute-start | bytes 1622024 | tf_op jit(solution)/shard_map/ppermute | solution.py:298
  48.4 0.1 constant_dynamic-update-slice_fusion.13
  48.5 1.6 %collective-permute-start.17 = (bf16[32,512]{1,0:T(8,128)(2,1)S(1)}, bf16[32,512]{1,0:T(8,128)(2,1)S(1)}, u32[]{:S(2)}, u32[]{:S(2)}) collective-permute-start(bf16[32,512]{1,0:T(8,128)(2,1)S(1)} %get-tuple-element.96), channel_id=1, source_target_pairs={{0,6},{1,7},{2,4},{3,5},{4,2},{5,3},{6,0},{7,1},{8,14},{9,15},{10,... | collective-permute-start | bytes 98312 | tf_op jit(solution)/shard_map/ppermute | solution.py:217
  50.1 2.9 %collective-permute-start.15 = (bf16[32,512]{1,0:T(8,128)(2,1)S(1)}, bf16[32,512]{1,0:T(8,128)(2,1)S(1)}, u32[]{:S(2)}, u32[]{:S(2)}) collective-permute-start(bf16[32,512]{1,0:T(8,128)(2,1)S(1)} %get-tuple-element.96), channel_id=1, source_target_pairs={{0,4},{1,5},{2,6},{3,7},{4,0},{5,1},{6,2},{7,3},{8,12},{9,13},{10,... | collective-permute-start | bytes 98312 | tf_op jit(solution)/shard_map/ppermute | solution.py:217
  53.0 1.4 %collective-permute-done.17 = bf16[32,512]{1,0:T(8,128)(2,1)S(1)} collective-permute-done((bf16[32,512]{1,0:T(8,128)(2,1)S(1)}, bf16[32,512]{1,0:T(8,128)(2,1)S(1)}, u32[]{:S(2)}, u32[]{:S(2)}) %collective-permute-start.17) | collective-permute-done | bytes 32800 | tf_op jit(solution)/shard_map/ppermute | solution.py:217
  54.3 0.5 collective-permute-done.15
  54.9 1.2 %collective-permute-start.20 = (bf16[128,512]{1,0:T(8,128)(2,1)S(1)}, bf16[128,512]{1,0:T(8,128)(2,1)S(1)}, u32[]{:S(2)}, u32[]{:S(2)}) collective-permute-start(bf16[128,512]{1,0:T(8,128)(2,1)S(1)} %pad_maximum_fusion.1), channel_id=1, source_target_pairs={{0,17},{1,16},{2,19},{3,18},{4,21},{5,20},{6,23},{7,22},{8,25},{9,... | collective-permute-start | bytes 393224 | tf_op jit(solution)/shard_map/ppermute | solution.py:217
  56.1 0.7 collective-permute-start.19
  56.9 1.6 %collective-permute-start.18 = (bf16[128,512]{1,0:T(8,128)(2,1)S(1)}, bf16[128,512]{1,0:T(8,128)(2,1)S(1)}, u32[]{:S(2)}, u32[]{:S(2)}) collective-permute-start(bf16[128,512]{1,0:T(8,128)(2,1)S(1)} %pad_maximum_fusion.1), channel_id=1, source_target_pairs={{0,1},{1,0},{2,3},{3,2},{4,5},{5,4},{6,7},{7,6},{8,9},{9,8},{10,11... | collective-permute-start | bytes 393224 | tf_op jit(solution)/shard_map/ppermute | solution.py:217
  58.5 5.9 %collective-permute-done.20 = bf16[128,512]{1,0:T(8,128)(2,1)S(1)} collective-permute-done((bf16[128,512]{1,0:T(8,128)(2,1)S(1)}, bf16[128,512]{1,0:T(8,128)(2,1)S(1)}, u32[]{:S(2)}, u32[]{:S(2)}) %collective-permute-start.20) | collective-permute-done | bytes 131104 | tf_op jit(solution)/shard_map/ppermute | solution.py:217
  64.4 1.7 %collective-permute-done.18 = bf16[128,512]{1,0:T(8,128)(2,1)S(1)} collective-permute-done((bf16[128,512]{1,0:T(8,128)(2,1)S(1)}, bf16[128,512]{1,0:T(8,128)(2,1)S(1)}, u32[]{:S(2)}, u32[]{:S(2)}) %collective-permute-start.18) | collective-permute-done | bytes 131104 | tf_op jit(solution)/shard_map/ppermute | solution.py:217
  66.1 0.1 collective-permute-start.22
  66.2 1.9 %collective-permute-done.22.hi_ref = bf16[512,512]{1,0:T(8,128)(2,1)S(1)} collective-permute-done((bf16[512,512]{1,0:T(8,128)(2,1)S(1)}, bf16[512,512]{1,0:T(8,128)(2,1)S(1)}, u32[]{:S(2)}, u32[]{:S(2)}) %collective-permute-start.22) | collective-permute-done | bytes 524320 | tf_op jit(solution)/shard_map/ppermute | solution.py:217
  68.1 3.0 %shard_map.143 = (bf16[512,512]{1,0:T(8,128)(2,1)S(1)}, bf16[512,512]{1,0:T(8,128)(2,1)S(1)}, bf16[512,512]{1,0:T(8,128)(2,1)S(1)}, bf16[512,512]{1,0:T(8,128)(2,1)S(1)}, bf16[512,512]{1,0:T(8,128)(2,1)S(1)}) custom-call(s32[32]{0:T(128)S(1)} %broadcast_xor_fusion.nat_ref, s32[2,1]{1,0:T(2,128)S(1)} %copy.16.live_ref, s32[2,4]{1,0:T(2,128)S(1)} %copy-done.9, ...), custom_call_target="tpu_custom_call" | custom-call | flops 1610612736 | bytes 5275816 | tf_op jit(solution)/shard_map/pallas_call | solution.py:183
  71.1 0.2 collective-permute-start.23
  71.3 1.8 %collective-permute-done.23 = bf16[512,512]{1,0:T(8,128)(2,1)S(1)} collective-permute-done((bf16[512,512]{1,0:T(8,128)(2,1)S(1)}, bf16[512,512]{1,0:T(8,128)(2,1)S(1)}, u32[]{:S(2)}, u32[]{:S(2)}) %collective-permute-start.23) | collective-permute-done | bytes 524320 | tf_op jit(solution)/shard_map/ppermute | solution.py:217
  73.0 0.1 add_convert_fusion
  73.2 2.2 %collective-permute-start.26 = (bf16[128,512]{1,0:T(8,128)(2,1)S(1)}, bf16[128,512]{1,0:T(8,128)(2,1)S(1)}, u32[]{:S(2)}, u32[]{:S(2)}) collective-permute-start(bf16[128,512]{1,0:T(8,128)(2,1)S(1)} %get-tuple-element.101), channel_id=1, source_target_pairs={{0,17},{1,16},{2,19},{3,18},{4,21},{5,20},{6,23},{7,22},{8,25},{9,... | collective-permute-start | bytes 393224 | tf_op jit(solution)/shard_map/ppermute | solution.py:217
  75.4 1.1 %collective-permute-start.25 = (bf16[128,512]{1,0:T(8,128)(2,1)S(1)}, bf16[128,512]{1,0:T(8,128)(2,1)S(1)}, u32[]{:S(2)}, u32[]{:S(2)}) collective-permute-start(bf16[128,512]{1,0:T(8,128)(2,1)S(1)} %get-tuple-element.102), channel_id=1, source_target_pairs={{0,16},{1,17},{2,18},{3,19},{4,20},{5,21},{6,22},{7,23},{8,24},{9,... | collective-permute-start | bytes 393224 | tf_op jit(solution)/shard_map/ppermute | solution.py:217
  76.5 0.3 collective-permute-start.24
  76.7 1.7 %shard_map.145 = f32[512,512]{1,0:T(8,128)} custom-call(bf16[512,512]{1,0:T(8,128)(2,1)S(1)} %get-tuple-element.89.w_ref, bf16[512,512]{1,0:T(8,128)(2,1)S(1)} %get-tuple-element.90.u_ref, bf16[528,512]{1,0:T(8,128)(2,1)S(1)} %collective-permute-done.21.rest_0_.refs_0_), custom_call_target="tpu_custom_call" | custom-call | flops 268435456 | bytes 2637824 | tf_op jit(solution)/shard_map/pallas_call | solution.py:183
  78.4 2.9 %shard_map.144 = f32[512,512]{1,0:T(8,128)} custom-call(s32[32]{0:T(128)S(1)} %broadcast_xor_fusion.nat_ref, s32[2,4]{1,0:T(2,128)S(1)} %copy-done.9, bf16[512,512]{1,0:T(8,128)(2,1)S(1)} %constant_dynamic-update-slice_fusion.7.lo_ref, bf16[512,512]{1,0:T(8,128)(2,1)S(1)} %collective-permute-done.22.hi_ref, bf16[512,512]{1,0:T(8,128)(2,1)S(1)} %get-tuple-element.82.gu_ref, ...), custom_call_target="tpu_custom_call" | custom-call | flops 1073741824 | bytes 3676320 | tf_op jit(solution)/shard_map/pallas_call | solution.py:183
  81.4 1.1 %collective-permute-done.25 = bf16[128,512]{1,0:T(8,128)(2,1)S(1)} collective-permute-done((bf16[128,512]{1,0:T(8,128)(2,1)S(1)}, bf16[128,512]{1,0:T(8,128)(2,1)S(1)}, u32[]{:S(2)}, u32[]{:S(2)}) %collective-permute-start.25) | collective-permute-done | bytes 131104 | tf_op jit(solution)/shard_map/ppermute | solution.py:217
  82.6 0.1 collective-permute-start.27
  82.6 1.1 %collective-permute-start.29 = (bf16[32,512]{1,0:T(8,128)(2,1)S(1)}, bf16[32,512]{1,0:T(8,128)(2,1)S(1)}, u32[]{:S(2)}, u32[]{:S(2)}) collective-permute-start(bf16[32,512]{1,0:T(8,128)(2,1)S(1)} %get-tuple-element.109), channel_id=1, source_target_pairs={{0,6},{1,7},{2,4},{3,5},{4,2},{5,3},{6,0},{7,1},{8,14},{9,15},{10,... | collective-permute-start | bytes 98312 | tf_op jit(solution)/shard_map/ppermute | solution.py:217
  83.7 2.4 %collective-permute-start.28 = (bf16[32,512]{1,0:T(8,128)(2,1)S(1)}, bf16[32,512]{1,0:T(8,128)(2,1)S(1)}, u32[]{:S(2)}, u32[]{:S(2)}) collective-permute-start(bf16[32,512]{1,0:T(8,128)(2,1)S(1)} %get-tuple-element.110), channel_id=1, source_target_pairs={{0,2},{1,3},{2,0},{3,1},{4,6},{5,7},{6,4},{7,5},{8,10},{9,11},{10,... | collective-permute-start | bytes 98312 | tf_op jit(solution)/shard_map/ppermute | solution.py:217
  86.1 1.7 %collective-permute-done.27 = bf16[32,512]{1,0:T(8,128)(2,1)S(1)} collective-permute-done((bf16[32,512]{1,0:T(8,128)(2,1)S(1)}, bf16[32,512]{1,0:T(8,128)(2,1)S(1)}, u32[]{:S(2)}, u32[]{:S(2)}) %collective-permute-start.27) | collective-permute-done | bytes 32800 | tf_op jit(solution)/shard_map/ppermute | solution.py:217
  87.8 0.7 collective-permute-done.29
  88.5 0.7 divide_subtract_fusion
  (54 shorter events, 0.3 us)
Async XLA Ops:
  0.6 6.6 %copy-start.4 = (s32[2,512]{1,0:T(2,128)S(1)}, s32[2,512]{1,0:T(2,128)}, u32[]{:S(2)}) copy-start(s32[2,512]{1,0:T(2,128)} %trows_ref.1) | copy-start | bytes 12292
  0.6 6.6 %copy-start.5 = (s32[2,4,128]{2,1,0:T(4,128)S(1)}, s32[2,4,128]{2,1,0:T(4,128)}, u32[]{:S(2)}) copy-start(s32[2,4,128]{2,1,0:T(4,128)} %neg_ref.1) | copy-start | bytes 12292
  0.7 6.6 %copy-start.6 = (s32[2,512]{1,0:T(2,128)S(1)}, s32[2,512]{1,0:T(2,128)}, u32[]{:S(2)}) copy-start(s32[2,512]{1,0:T(2,128)} %hrows_ref.5) | copy-start | bytes 12292
  1.5 8.9 %collective-permute-start.2 = (bf16[32,512]{1,0:T(8,128)(2,1)S(1)}, bf16[32,512]{1,0:T(8,128)(2,1)S(1)}, u32[]{:S(2)}, u32[]{:S(2)}) collective-permute-start(bf16[32,512]{1,0:T(8,128)(2,1)S(1)} %get-tuple-element.99), channel_id=1, source_target_pairs={{0,6},{1,7},{2,4},{3,5},{4,2},{5,3},{6,0},{7,1},{8,14},{9,15},{10,... | collective-permute-start | bytes 98312 | tf_op jit(solution)/shard_map/ppermute | solution.py:217
  6.6 3.9 %collective-permute-start.1 = (bf16[32,512]{1,0:T(8,128)(2,1)S(1)}, bf16[32,512]{1,0:T(8,128)(2,1)S(1)}, u32[]{:S(2)}, u32[]{:S(2)}) collective-permute-start(bf16[32,512]{1,0:T(8,128)(2,1)S(1)} %get-tuple-element.99), channel_id=1, source_target_pairs={{0,2},{1,3},{2,0},{3,1},{4,6},{5,7},{6,4},{7,5},{8,10},{9,11},{10,... | collective-permute-start | bytes 98312 | tf_op jit(solution)/shard_map/ppermute | solution.py:217
  6.6 4.9 %collective-permute-start = (bf16[32,512]{1,0:T(8,128)(2,1)S(1)}, bf16[32,512]{1,0:T(8,128)(2,1)S(1)}, u32[]{:S(2)}, u32[]{:S(2)}) collective-permute-start(bf16[32,512]{1,0:T(8,128)(2,1)S(1)} %get-tuple-element.99), channel_id=1, source_target_pairs={{0,4},{1,5},{2,6},{3,7},{4,0},{5,1},{6,2},{7,3},{8,12},{9,13},{10,... | collective-permute-start | bytes 98312 | tf_op jit(solution)/shard_map/ppermute | solution.py:217
  7.2 1.2 %copy-start = (f32[512,512]{1,0:T(8,128)S(1)}, f32[512,512]{1,0:T(8,128)}, u32[]{:S(2)}) copy-start(f32[512,512]{1,0:T(8,128)} %table_ref.2) | copy-start | bytes 3145732
  8.4 1.2 %copy-start.2 = (f32[512,512]{1,0:T(8,128)S(1)}, f32[512,512]{1,0:T(8,128)}, u32[]{:S(2)}) copy-start(f32[512,512]{1,0:T(8,128)} %table_ref.3) | copy-start | bytes 3145732
  11.5 7.2 %collective-permute-start.5 = (bf16[128,512]{1,0:T(8,128)(2,1)S(1)}, bf16[128,512]{1,0:T(8,128)(2,1)S(1)}, u32[]{:S(2)}, u32[]{:S(2)}) collective-permute-start(bf16[128,512]{1,0:T(8,128)(2,1)S(1)} %pad_maximum_fusion), channel_id=1, source_target_pairs={{0,17},{1,16},{2,19},{3,18},{4,21},{5,20},{6,23},{7,22},{8,25},{9,... | collective-permute-start | bytes 393224 | tf_op jit(solution)/shard_map/ppermute | solution.py:217
  14.0 5.6 %collective-permute-start.4 = (bf16[128,512]{1,0:T(8,128)(2,1)S(1)}, bf16[128,512]{1,0:T(8,128)(2,1)S(1)}, u32[]{:S(2)}, u32[]{:S(2)}) collective-permute-start(bf16[128,512]{1,0:T(8,128)(2,1)S(1)} %pad_maximum_fusion), channel_id=1, source_target_pairs={{0,16},{1,17},{2,18},{3,19},{4,20},{5,21},{6,22},{7,23},{8,24},{9,... | collective-permute-start | bytes 393224 | tf_op jit(solution)/shard_map/ppermute | solution.py:217
  14.5 5.1 %collective-permute-start.3 = (bf16[128,512]{1,0:T(8,128)(2,1)S(1)}, bf16[128,512]{1,0:T(8,128)(2,1)S(1)}, u32[]{:S(2)}, u32[]{:S(2)}) collective-permute-start(bf16[128,512]{1,0:T(8,128)(2,1)S(1)} %pad_maximum_fusion), channel_id=1, source_target_pairs={{0,1},{1,0},{2,3},{3,2},{4,5},{5,4},{6,7},{7,6},{8,9},{9,8},{10,11... | collective-permute-start | bytes 393224 | tf_op jit(solution)/shard_map/ppermute | solution.py:217
  19.7 2.0 %collective-permute-start.6 = (bf16[512,512]{1,0:T(8,128)(2,1)S(1)}, bf16[512,512]{1,0:T(8,128)(2,1)S(1)}, u32[]{:S(2)}, u32[]{:S(2)}) collective-permute-start(bf16[512,512]{1,0:T(8,128)(2,1)S(1)} %constant_dynamic-update-slice_fusion.lo_ref), channel_id=1, source_target_pairs={{0,8},{1,9},{2,10},{3,11},{4,12},{5,13},{6,14},{7,15},{8,0},{9,1},... | collective-permute-start | bytes 1572872 | tf_op jit(solution)/shard_map/ppermute | solution.py:217
  19.8 0.7 copy-start.12
  20.5 0.7 copy-start.13
  21.2 0.7 copy-start.9
  21.2 4.2 %copy-start.1 = (f32[512,512]{1,0:T(8,128)S(1)}, f32[512,512]{1,0:T(8,128)}, u32[]{:S(2)}) copy-start(f32[512,512]{1,0:T(8,128)} %table_ref.2) | copy-start | bytes 3145732
  24.9 2.1 %collective-permute-start.7 = (bf16[512,512]{1,0:T(8,128)(2,1)S(1)}, bf16[512,512]{1,0:T(8,128)(2,1)S(1)}, u32[]{:S(2)}, u32[]{:S(2)}) collective-permute-start(bf16[512,512]{1,0:T(8,128)(2,1)S(1)} %get-tuple-element.61), channel_id=1, source_target_pairs={{0,8},{1,9},{2,10},{3,11},{4,12},{5,13},{6,14},{7,15},{8,0},{9,1},... | collective-permute-start | bytes 1572872 | tf_op jit(solution)/shard_map/ppermute | solution.py:217
  25.4 0.7 copy-start.7
  26.8 6.6 %copy-start.3 = (f32[512,512]{1,0:T(8,128)S(1)}, f32[512,512]{1,0:T(8,128)}, u32[]{:S(2)}) copy-start(f32[512,512]{1,0:T(8,128)} %table_ref.3) | copy-start | bytes 3145732
  27.0 17.5 %collective-permute-start.12 = (bf16[528,512]{1,0:T(8,128)(2,1)S(1)}, bf16[528,512]{1,0:T(8,128)(2,1)S(1)}, u32[]{:S(2)}, u32[]{:S(2)}) collective-permute-start(bf16[528,512]{1,0:T(8,128)(2,1)S(1)} %shard_map.141), channel_id=1, source_target_pairs={{0,0},{1,3},{2,2},{3,5},{4,4},{5,7},{6,6},{7,1},{8,8},{9,11},{10,1... | collective-permute-start | bytes 1622024 | tf_op jit(solution)/shard_map/ppermute | solution.py:297
  27.9 8.4 %collective-permute-start.10 = (bf16[128,512]{1,0:T(8,128)(2,1)S(1)}, bf16[128,512]{1,0:T(8,128)(2,1)S(1)}, u32[]{:S(2)}, u32[]{:S(2)}) collective-permute-start(bf16[128,512]{1,0:T(8,128)(2,1)S(1)} %get-tuple-element.104), channel_id=1, source_target_pairs={{0,17},{1,16},{2,19},{3,18},{4,21},{5,20},{6,23},{7,22},{8,25},{9,... | collective-permute-start | bytes 393224 | tf_op jit(solution)/shard_map/ppermute | solution.py:217
  32.5 6.4 %collective-permute-start.9 = (bf16[128,512]{1,0:T(8,128)(2,1)S(1)}, bf16[128,512]{1,0:T(8,128)(2,1)S(1)}, u32[]{:S(2)}, u32[]{:S(2)}) collective-permute-start(bf16[128,512]{1,0:T(8,128)(2,1)S(1)} %get-tuple-element.105), channel_id=1, source_target_pairs={{0,16},{1,17},{2,18},{3,19},{4,20},{5,21},{6,22},{7,23},{8,24},{9,... | collective-permute-start | bytes 393224 | tf_op jit(solution)/shard_map/ppermute | solution.py:217
  33.4 0.7 copy-start.8
  33.4 5.5 %collective-permute-start.8 = (bf16[128,512]{1,0:T(8,128)(2,1)S(1)}, bf16[128,512]{1,0:T(8,128)(2,1)S(1)}, u32[]{:S(2)}, u32[]{:S(2)}) collective-permute-start(bf16[128,512]{1,0:T(8,128)(2,1)S(1)} %get-tuple-element.106), channel_id=1, source_target_pairs={{0,1},{1,0},{2,3},{3,2},{4,5},{5,4},{6,7},{7,6},{8,9},{9,8},{10,11... | collective-permute-start | bytes 393224 | tf_op jit(solution)/shard_map/ppermute | solution.py:217
  38.9 9.5 %copy-start.10 = (f32[32,512]{1,0:T(8,128)S(1)}, f32[32,512]{1,0:T(8,128)}, u32[]{:S(2)}) copy-start(f32[32,512]{1,0:T(8,128)} %param.16) | copy-start | bytes 196612
  38.9 9.5 %copy-start.11 = (f32[32,512]{1,0:T(8,128)S(1)}, f32[32,512]{1,0:T(8,128)}, u32[]{:S(2)}) copy-start(f32[32,512]{1,0:T(8,128)} %param.17) | copy-start | bytes 196612
  39.0 5.5 %collective-permute-start.11 = (bf16[32,512]{1,0:T(8,128)(2,1)S(1)}, bf16[32,512]{1,0:T(8,128)(2,1)S(1)}, u32[]{:S(2)}, u32[]{:S(2)}) collective-permute-start(bf16[32,512]{1,0:T(8,128)(2,1)S(1)} %get-tuple-element.111), channel_id=1, source_target_pairs={{0,4},{1,5},{2,6},{3,7},{4,0},{5,1},{6,2},{7,3},{8,12},{9,13},{10,... | collective-permute-start | bytes 98312 | tf_op jit(solution)/shard_map/ppermute | solution.py:217
  40.8 7.6 %collective-permute-start.14 = (bf16[32,512]{1,0:T(8,128)(2,1)S(1)}, bf16[32,512]{1,0:T(8,128)(2,1)S(1)}, u32[]{:S(2)}, u32[]{:S(2)}) collective-permute-start(bf16[32,512]{1,0:T(8,128)(2,1)S(1)} %get-tuple-element.112), channel_id=1, source_target_pairs={{0,6},{1,7},{2,4},{3,5},{4,2},{5,3},{6,0},{7,1},{8,14},{9,15},{10,... | collective-permute-start | bytes 98312 | tf_op jit(solution)/shard_map/ppermute | solution.py:217
  42.0 6.4 %collective-permute-start.13 = (bf16[32,512]{1,0:T(8,128)(2,1)S(1)}, bf16[32,512]{1,0:T(8,128)(2,1)S(1)}, u32[]{:S(2)}, u32[]{:S(2)}) collective-permute-start(bf16[32,512]{1,0:T(8,128)(2,1)S(1)} %get-tuple-element.113), channel_id=1, source_target_pairs={{0,2},{1,3},{2,0},{3,1},{4,6},{5,7},{6,4},{7,5},{8,10},{9,11},{10,... | collective-permute-start | bytes 98312 | tf_op jit(solution)/shard_map/ppermute | solution.py:217
  44.5 21.6 %collective-permute-start.21 = (bf16[528,512]{1,0:T(8,128)(2,1)S(1)}, bf16[528,512]{1,0:T(8,128)(2,1)S(1)}, u32[]{:S(2)}, u32[]{:S(2)}) collective-permute-start(bf16[528,512]{1,0:T(8,128)(2,1)S(1)} %collective-permute-done.12), channel_id=1, source_target_pairs={{0,1},{1,0},{2,3},{3,2},{4,5},{5,4},{6,7},{7,6},{8,9},{9,8},{10,11... | collective-permute-start | bytes 1622024 | tf_op jit(solution)/shard_map/ppermute | solution.py:298
  48.5 5.8 %collective-permute-start.17 = (bf16[32,512]{1,0:T(8,128)(2,1)S(1)}, bf16[32,512]{1,0:T(8,128)(2,1)S(1)}, u32[]{:S(2)}, u32[]{:S(2)}) collective-permute-start(bf16[32,512]{1,0:T(8,128)(2,1)S(1)} %get-tuple-element.96), channel_id=1, source_target_pairs={{0,6},{1,7},{2,4},{3,5},{4,2},{5,3},{6,0},{7,1},{8,14},{9,15},{10,... | collective-permute-start | bytes 98312 | tf_op jit(solution)/shard_map/ppermute | solution.py:217
  50.1 4.3 %collective-permute-start.16 = (bf16[32,512]{1,0:T(8,128)(2,1)S(1)}, bf16[32,512]{1,0:T(8,128)(2,1)S(1)}, u32[]{:S(2)}, u32[]{:S(2)}) collective-permute-start(bf16[32,512]{1,0:T(8,128)(2,1)S(1)} %get-tuple-element.96), channel_id=1, source_target_pairs={{0,2},{1,3},{2,0},{3,1},{4,6},{5,7},{6,4},{7,5},{8,10},{9,11},{10,... | collective-permute-start | bytes 98312 | tf_op jit(solution)/shard_map/ppermute | solution.py:217
  50.1 4.8 %collective-permute-start.15 = (bf16[32,512]{1,0:T(8,128)(2,1)S(1)}, bf16[32,512]{1,0:T(8,128)(2,1)S(1)}, u32[]{:S(2)}, u32[]{:S(2)}) collective-permute-start(bf16[32,512]{1,0:T(8,128)(2,1)S(1)} %get-tuple-element.96), channel_id=1, source_target_pairs={{0,4},{1,5},{2,6},{3,7},{4,0},{5,1},{6,2},{7,3},{8,12},{9,13},{10,... | collective-permute-start | bytes 98312 | tf_op jit(solution)/shard_map/ppermute | solution.py:217
  54.9 9.5 %collective-permute-start.20 = (bf16[128,512]{1,0:T(8,128)(2,1)S(1)}, bf16[128,512]{1,0:T(8,128)(2,1)S(1)}, u32[]{:S(2)}, u32[]{:S(2)}) collective-permute-start(bf16[128,512]{1,0:T(8,128)(2,1)S(1)} %pad_maximum_fusion.1), channel_id=1, source_target_pairs={{0,17},{1,16},{2,19},{3,18},{4,21},{5,20},{6,23},{7,22},{8,25},{9,... | collective-permute-start | bytes 393224 | tf_op jit(solution)/shard_map/ppermute | solution.py:217
  56.1 8.2 %collective-permute-start.19 = (bf16[128,512]{1,0:T(8,128)(2,1)S(1)}, bf16[128,512]{1,0:T(8,128)(2,1)S(1)}, u32[]{:S(2)}, u32[]{:S(2)}) collective-permute-start(bf16[128,512]{1,0:T(8,128)(2,1)S(1)} %pad_maximum_fusion.1), channel_id=1, source_target_pairs={{0,16},{1,17},{2,18},{3,19},{4,20},{5,21},{6,22},{7,23},{8,24},{9,... | collective-permute-start | bytes 393224 | tf_op jit(solution)/shard_map/ppermute | solution.py:217
  56.9 9.2 %collective-permute-start.18 = (bf16[128,512]{1,0:T(8,128)(2,1)S(1)}, bf16[128,512]{1,0:T(8,128)(2,1)S(1)}, u32[]{:S(2)}, u32[]{:S(2)}) collective-permute-start(bf16[128,512]{1,0:T(8,128)(2,1)S(1)} %pad_maximum_fusion.1), channel_id=1, source_target_pairs={{0,1},{1,0},{2,3},{3,2},{4,5},{5,4},{6,7},{7,6},{8,9},{9,8},{10,11... | collective-permute-start | bytes 393224 | tf_op jit(solution)/shard_map/ppermute | solution.py:217
  66.1 2.0 %collective-permute-start.22 = (bf16[512,512]{1,0:T(8,128)(2,1)S(1)}, bf16[512,512]{1,0:T(8,128)(2,1)S(1)}, u32[]{:S(2)}, u32[]{:S(2)}) collective-permute-start(bf16[512,512]{1,0:T(8,128)(2,1)S(1)} %constant_dynamic-update-slice_fusion.7.lo_ref), channel_id=1, source_target_pairs={{0,8},{1,9},{2,10},{3,11},{4,12},{5,13},{6,14},{7,15},{8,0},{9,1},... | collective-permute-start | bytes 1572872 | tf_op jit(solution)/shard_map/ppermute | solution.py:217
  71.1 2.0 %collective-permute-start.23 = (bf16[512,512]{1,0:T(8,128)(2,1)S(1)}, bf16[512,512]{1,0:T(8,128)(2,1)S(1)}, u32[]{:S(2)}, u32[]{:S(2)}) collective-permute-start(bf16[512,512]{1,0:T(8,128)(2,1)S(1)} %get-tuple-element.81), channel_id=1, source_target_pairs={{0,8},{1,9},{2,10},{3,11},{4,12},{5,13},{6,14},{7,15},{8,0},{9,1},... | collective-permute-start | bytes 1572872 | tf_op jit(solution)/shard_map/ppermute | solution.py:217
  73.2 8.2 %collective-permute-start.26 = (bf16[128,512]{1,0:T(8,128)(2,1)S(1)}, bf16[128,512]{1,0:T(8,128)(2,1)S(1)}, u32[]{:S(2)}, u32[]{:S(2)}) collective-permute-start(bf16[128,512]{1,0:T(8,128)(2,1)S(1)} %get-tuple-element.101), channel_id=1, source_target_pairs={{0,17},{1,16},{2,19},{3,18},{4,21},{5,20},{6,23},{7,22},{8,25},{9,... | collective-permute-start | bytes 393224 | tf_op jit(solution)/shard_map/ppermute | solution.py:217
  75.4 7.1 %collective-permute-start.25 = (bf16[128,512]{1,0:T(8,128)(2,1)S(1)}, bf16[128,512]{1,0:T(8,128)(2,1)S(1)}, u32[]{:S(2)}, u32[]{:S(2)}) collective-permute-start(bf16[128,512]{1,0:T(8,128)(2,1)S(1)} %get-tuple-element.102), channel_id=1, source_target_pairs={{0,16},{1,17},{2,18},{3,19},{4,20},{5,21},{6,22},{7,23},{8,24},{9,... | collective-permute-start | bytes 393224 | tf_op jit(solution)/shard_map/ppermute | solution.py:217
  76.5 6.0 %collective-permute-start.24 = (bf16[128,512]{1,0:T(8,128)(2,1)S(1)}, bf16[128,512]{1,0:T(8,128)(2,1)S(1)}, u32[]{:S(2)}, u32[]{:S(2)}) collective-permute-start(bf16[128,512]{1,0:T(8,128)(2,1)S(1)} %get-tuple-element.103), channel_id=1, source_target_pairs={{0,1},{1,0},{2,3},{3,2},{4,5},{5,4},{6,7},{7,6},{8,9},{9,8},{10,11... | collective-permute-start | bytes 393224 | tf_op jit(solution)/shard_map/ppermute | solution.py:217
  82.6 5.2 %collective-permute-start.27 = (bf16[32,512]{1,0:T(8,128)(2,1)S(1)}, bf16[32,512]{1,0:T(8,128)(2,1)S(1)}, u32[]{:S(2)}, u32[]{:S(2)}) collective-permute-start(bf16[32,512]{1,0:T(8,128)(2,1)S(1)} %get-tuple-element.108), channel_id=1, source_target_pairs={{0,4},{1,5},{2,6},{3,7},{4,0},{5,1},{6,2},{7,3},{8,12},{9,13},{10,... | collective-permute-start | bytes 98312 | tf_op jit(solution)/shard_map/ppermute | solution.py:217
  82.6 5.9 %collective-permute-start.29 = (bf16[32,512]{1,0:T(8,128)(2,1)S(1)}, bf16[32,512]{1,0:T(8,128)(2,1)S(1)}, u32[]{:S(2)}, u32[]{:S(2)}) collective-permute-start(bf16[32,512]{1,0:T(8,128)(2,1)S(1)} %get-tuple-element.109), channel_id=1, source_target_pairs={{0,6},{1,7},{2,4},{3,5},{4,2},{5,3},{6,0},{7,1},{8,14},{9,15},{10,... | collective-permute-start | bytes 98312 | tf_op jit(solution)/shard_map/ppermute | solution.py:217
  83.7 4.8 %collective-permute-start.28 = (bf16[32,512]{1,0:T(8,128)(2,1)S(1)}, bf16[32,512]{1,0:T(8,128)(2,1)S(1)}, u32[]{:S(2)}, u32[]{:S(2)}) collective-permute-start(bf16[32,512]{1,0:T(8,128)(2,1)S(1)} %get-tuple-element.110), channel_id=1, source_target_pairs={{0,2},{1,3},{2,0},{3,1},{4,6},{5,7},{6,4},{7,5},{8,10},{9,11},{10,... | collective-permute-start | bytes 98312 | tf_op jit(solution)/shard_map/ppermute | solution.py:217

commit v4 on v3

--- a/solution.py
+++ b/solution.py
@@ -47,18 +47,8 @@
     return (lax.broadcasted_iota(jnp.int32, (rows, n), 0) == index_row).astype(F32).astype(BF16)
 
 
-def by_relation(x, rel_ref, k, blocks, relation):
-    size = x.shape[0] // blocks
-    parts = []
-    for b in range(blocks):
-        part = x[b * size : (b + 1) * size]
-        parts.append(jnp.where(rel_ref[k, b] == relation, part, jnp.zeros_like(part)))
-    return jnp.concatenate(parts, axis=0)
-
-
-def restore_relations(nat_ref, lo_ref, hi_ref, rel_s):
+def restore_relations(nat_ref, lo_ref, hi_ref, rel_s, own):
     half = lo_ref.shape[0]
-    own = 2 * half // nat_ref.shape[0]
     if own % PACK_ROWS:
         rel_s[:half] = lo_ref[...]
         rel_s[half:] = hi_ref[...]
@@ -86,38 +76,38 @@
 
 
 def score_kernel(
-    k, nneg, nat_ref, live_ref, rel_ref, lo_ref, hi_ref, h_ref, tcol_ref, cnt_ref, *rest
+    k, own, nneg, nat_ref, live_ref, rel_ref, lo_ref, hi_ref, h_ref, tcol_ref, cnt_ref, *rest
 ):
     tail_refs, (keep_ref, send_ref, w_ref, u_ref, gu_ref, rel_s, grad_s) = rest[:-7], rest[-7:]
     edges, width = h_ref.shape
     blocks, rows = cnt_ref.shape[1:]
     size = edges // blocks
     relations = rel_s.shape[0] // width
-    restore_relations(nat_ref, lo_ref, hi_ref, rel_s)
-    masked = [by_relation(h_ref[...], rel_ref, k, blocks, r) for r in range(relations)]
-    u = dot(masked[0], rel_s[0:width], COLS, ROWS)
-    for r in range(1, relations):
-        u = u + dot(masked[r], rel_s[r * width : (r + 1) * width], COLS, ROWS)
-    u = u.astype(BF16)
-    u_ref[...] = u
+    restore_relations(nat_ref, lo_ref, hi_ref, rel_s, own)
+    half = keep_ref.shape[0]
+    for b in range(blocks):
+        part = slice(b * size, (b + 1) * size)
+        chosen = rel_s[pl.ds(pl.multiple_of(rel_ref[k, b] * width, width), width)]
+        u_ref[part] = dot(h_ref[part], chosen, COLS, ROWS).astype(BF16)
     tails = jnp.concatenate([ref[...] for ref in tail_refs])[0:rows]
-    score = dot(u, tails, COLS, COLS)
+    score = dot(u_ref[...], tails, COLS, COLS)
     row_id = lax.broadcasted_iota(jnp.int32, (size, rows), 1).astype(F32)
     for b in range(blocks):
         part = slice(b * size, (b + 1) * size)
-        live = jnp.where(live_ref[k, 0] > b, 1.0, 0.0)
-        half_tanh = 0.5 * jnp.tanh(0.5 * score[part])
-        negative = ((0.5 + half_tanh) * (live / nneg)).astype(BF16).astype(F32)
-        positive = (0.5 - half_tanh) * live
+        half_live = jnp.where(live_ref[k, 0] > b, 0.5, 0.0)
+        share = cnt_ref[k, b : b + 1, :] * (half_live / nneg)
+        t = jnp.tanh(0.5 * score[part])
         is_tail = spread(tcol_ref[k, part], rows) == row_id
-        weight = cnt_ref[k, b : b + 1, :] * negative - jnp.where(is_tail, positive, 0.0)
+        weight = (share + share * t) - jnp.where(is_tail, half_live - half_live * t, 0.0)
         w_ref[part] = weight.astype(BF16)
     gu = dot(w_ref[...], tails, COLS, ROWS).astype(BF16)
     gu_ref[...] = gu
     for r in range(relations):
-        grad_s[r * width : (r + 1) * width] = dot(masked[r], gu, ROWS, ROWS)
-    half = keep_ref.shape[0]
-    own = 2 * half // nat_ref.shape[0]
+        parts = []
+        for b in range(blocks):
+            part = h_ref[b * size : (b + 1) * size]
+            parts.append(jnp.where(rel_ref[k, b] == r, part, jnp.zeros_like(part)))
+        grad_s[r * width : (r + 1) * width] = dot(jnp.concatenate(parts), gu, ROWS, ROWS)
     if own % PACK_ROWS:
         keep_ref[...] = grad_s[:half].astype(BF16)
         send_ref[...] = grad_s[half:].astype(BF16)
@@ -154,20 +144,18 @@
 
 
 def head_kernel(
-    k, blocks, nat_ref, rel_ref, lo_ref, hi_ref, gu_ref, hrows_ref, table_ref, state_ref, *rest
+    k, own, blocks, nat_ref, rel_ref, lo_ref, hi_ref, gu_ref, hrows_ref, table_ref, state_ref, *rest
 ):
     out_ref, rel_s = rest[0], rest[-1]
     rows, width = table_ref.shape
-    relations = rel_s.shape[0] // width
-    restore_relations(nat_ref, lo_ref, hi_ref, rel_s)
-    gu = gu_ref[...]
-    terms = None
-    for r in range(relations):
-        part = by_relation(gu, rel_ref, k, blocks, r)
-        term = dot(part, rel_s[r * width : (r + 1) * width], COLS, COLS)
-        terms = term if terms is None else terms + term
+    restore_relations(nat_ref, lo_ref, hi_ref, rel_s, own)
+    size = gu_ref.shape[0] // blocks
+    terms = []
+    for b in range(blocks):
+        chosen = rel_s[pl.ds(pl.multiple_of(rel_ref[k, b] * width, width), width)]
+        terms.append(dot(gu_ref[b * size : (b + 1) * size], chosen, COLS, COLS).astype(BF16))
     hot = one_hot_rows(hrows_ref[k : k + 1, :], rows)
-    gradient = dot(hot, terms.astype(BF16), COLS, ROWS)
+    gradient = dot(hot, jnp.concatenate(terms), COLS, ROWS)
     table, state = adagrad_rows(table_ref[...], state_ref[...], gradient)
     out_ref[...] = table
     if len(rest) > 2:
@@ -262,6 +250,7 @@
     heads, tails = lax.axis_size("head"), lax.axis_size("tail")
     exchange = Exchange(heads, tails)
     nat = exchange.block_of_slot
+    own = relations.shape[0]
     rows, width = tail_table.shape
     edges = head_rows.shape[1]
     blocks, nneg = negatives.shape[1:]
@@ -318,7 +307,7 @@
         else:
             tail_vecs = rotated
         keep, send, weights, projected, edge_grad = call(
-            functools.partial(score_kernel, k, float(nneg)),
+            functools.partial(score_kernel, k, own, float(nneg)),
             [
                 ((half, width), BF16),
                 ((half, width), BF16),
@@ -326,7 +315,7 @@
                 ((edges, width), BF16),
                 ((edges, width), BF16),
             ],
-            3, [pltpu.VMEM((all_rows, width), BF16), pltpu.VMEM((all_rows, width), F32)], 6 * square,
+            3, [pltpu.VMEM((all_rows, width), BF16), pltpu.VMEM((all_rows, width), F32)], 5 * square,
             nat, block_counts, relation_ids, lo, hi, head_vecs, tail_col, counts, *tail_vecs,
         )
         head_outs = [(head_table.shape, F32)]
@@ -342,7 +331,7 @@
                 weights, projected, *tail_vecs,
             )
         head_new = call(
-            functools.partial(head_kernel, k, blocks), head_outs,
+            functools.partial(head_kernel, k, own, blocks), head_outs,
             2, [pltpu.VMEM((all_rows, width), BF16)], 4 * square,
             nat, relation_ids, lo, hi, edge_grad, head_rows, head_table, head_state,
         )

time: 89.6 us -> 88.8 us (level)
  no operation moved by 1% of the time
where the time goes in v4:
time: 88.8 us; the launch traced here: 88.5 us
  starting transfers between devices  39 us (44%)
  waiting for transfers between devices  27.4 us (31%)
  Pallas kernels  13.6 us (15%)
  local copies, waits for them, and re-layouts  5.5 us (6%)
  other arithmetic  2.09 us (2%)
    ppermute x28, starting transfers between devices, swap(): return lax.ppermute(x, AXES, [(i, i ^ mask) for i in range(self.devices)])  34.3 us
    ppermute x28, waiting for transfers between devices, swap(): return lax.ppermute(x, AXES, [(i, i ^ mask) for i in range(self.devices)])  27.4 us
    pallas_call x7, Pallas kernels, call(): pl.pallas_call(kernel, out_shape=outs, in_specs=[SMEM] * smem + [VMEM] *...  13.6 us
    unnamed x39, local copies, waits for them, and re-layouts  5.48 us
    ppermute x1, starting transfers between devices, rotate(): return lax.ppermute(x, 'tail', [(i, i ^ 1) for i in range(tails)])  3.94 us
  transfers between devices with their start and end apart: 30, of which 17 were waited for; matrix products, arithmetic and copies ran while one was open for 0% of the time, Pallas kernels for 9%

profile of v4, /device:TPU:0, one launch (start us, length us, event | category | flops | bytes accessed | tf_op | source)
XLA Modules:
  0.0 88.5 jit_solution(317608942974445352)
XLA Ops:
  0.7 0.9 constant_dynamic-update-slice_fusion.6
  1.5 5.0 %collective-permute-start.2 = (bf16[32,512]{1,0:T(8,128)(2,1)S(1)}, bf16[32,512]{1,0:T(8,128)(2,1)S(1)}, u32[]{:S(2)}, u32[]{:S(2)}) collective-permute-start(bf16[32,512]{1,0:T(8,128)(2,1)S(1)} %get-tuple-element.99), channel_id=1, source_target_pairs={{0,6},{1,7},{2,4},{3,5},{4,2},{5,3},{6,0},{7,1},{8,14},{9,15},{10,... | collective-permute-start | bytes 98312 | tf_op jit(solution)/shard_map/ppermute | solution.py:205
  6.6 0.6 collective-permute-start
  7.2 1.2 %copy-done = f32[512,512]{1,0:T(8,128)S(1)} copy-done((f32[512,512]{1,0:T(8,128)S(1)}, f32[512,512]{1,0:T(8,128)}, u32[]{:S(2)}) %copy-start) | copy-done | bytes 1048600
  8.4 1.2 %copy-done.2 = f32[512,512]{1,0:T(8,128)S(1)} copy-done((f32[512,512]{1,0:T(8,128)S(1)}, f32[512,512]{1,0:T(8,128)}, u32[]{:S(2)}) %copy-start.2) | copy-done | bytes 1048600
  9.7 0.7 shard_map.139
  10.4 0.1 collective-permute-done.1
  10.5 1.0 %collective-permute-done = bf16[32,512]{1,0:T(8,128)(2,1)S(1)} collective-permute-done((bf16[32,512]{1,0:T(8,128)(2,1)S(1)}, bf16[32,512]{1,0:T(8,128)(2,1)S(1)}, u32[]{:S(2)}, u32[]{:S(2)}) %collective-permute-start) | collective-permute-done | bytes 32800 | tf_op jit(solution)/shard_map/ppermute | solution.py:205
  11.5 2.5 %collective-permute-start.5 = (bf16[128,512]{1,0:T(8,128)(2,1)S(1)}, bf16[128,512]{1,0:T(8,128)(2,1)S(1)}, u32[]{:S(2)}, u32[]{:S(2)}) collective-permute-start(bf16[128,512]{1,0:T(8,128)(2,1)S(1)} %pad_maximum_fusion), channel_id=1, source_target_pairs={{0,17},{1,16},{2,19},{3,18},{4,21},{5,20},{6,23},{7,22},{8,25},{9,... | collective-permute-start | bytes 393224 | tf_op jit(solution)/shard_map/ppermute | solution.py:205
  14.0 0.5 collective-permute-start.4
  14.5 0.5 collective-permute-start.3
  15.1 3.6 %collective-permute-done.5 = bf16[128,512]{1,0:T(8,128)(2,1)S(1)} collective-permute-done((bf16[128,512]{1,0:T(8,128)(2,1)S(1)}, bf16[128,512]{1,0:T(8,128)(2,1)S(1)}, u32[]{:S(2)}, u32[]{:S(2)}) %collective-permute-start.5) | collective-permute-done | bytes 131104 | tf_op jit(solution)/shard_map/ppermute | solution.py:205
  18.7 0.9 %collective-permute-done.4 = bf16[128,512]{1,0:T(8,128)(2,1)S(1)} collective-permute-done((bf16[128,512]{1,0:T(8,128)(2,1)S(1)}, bf16[128,512]{1,0:T(8,128)(2,1)S(1)}, u32[]{:S(2)}, u32[]{:S(2)}) %collective-permute-start.4) | collective-permute-done | bytes 131104 | tf_op jit(solution)/shard_map/ppermute | solution.py:205
  19.7 0.1 collective-permute-start.6
  19.8 0.6 copy-done.12
  20.4 0.1 copy.16.live_ref
  20.5 0.7 copy-done.13
  21.2 0.5 collective-permute-done.6.hi_ref
  21.7 0.2 copy-done.9
  21.9 2.6 %shard_map.140 = (bf16[512,512]{1,0:T(8,128)(2,1)S(1)}, bf16[512,512]{1,0:T(8,128)(2,1)S(1)}, bf16[512,512]{1,0:T(8,128)(2,1)S(1)}, bf16[512,512]{1,0:T(8,128)(2,1)S(1)}, bf16[512,512]{1,0:T(8,128)(2,1)S(1)}) custom-call(s32[32]{0:T(128)S(1)} %broadcast_xor_fusion.nat_ref, s32[2,1]{1,0:T(2,128)S(1)} %copy.16.live_ref, s32[2,4]{1,0:T(2,128)S(1)} %copy-done.9, ...), custom_call_target="tpu_custom_call" | custom-call | flops 1342177280 | bytes 5259432 | tf_op jit(solution)/shard_map/pallas_call | solution.py:171
  24.5 0.6 collective-permute-start.7
  25.1 0.7 copy-done.7
  25.7 0.7 shard_map.141
  26.4 0.2 collective-permute-done.7
  26.6 0.8 collective-permute-start.12
  27.4 0.1 add_convert_fusion.4
  27.6 4.5 %collective-permute-start.10 = (bf16[128,512]{1,0:T(8,128)(2,1)S(1)}, bf16[128,512]{1,0:T(8,128)(2,1)S(1)}, u32[]{:S(2)}, u32[]{:S(2)}) collective-permute-start(bf16[128,512]{1,0:T(8,128)(2,1)S(1)} %get-tuple-element.104), channel_id=1, source_target_pairs={{0,17},{1,16},{2,19},{3,18},{4,21},{5,20},{6,23},{7,22},{8,25},{9,... | collective-permute-start | bytes 393224 | tf_op jit(solution)/shard_map/ppermute | solution.py:205
  32.1 0.9 %collective-permute-start.9 = (bf16[128,512]{1,0:T(8,128)(2,1)S(1)}, bf16[128,512]{1,0:T(8,128)(2,1)S(1)}, u32[]{:S(2)}, u32[]{:S(2)}) collective-permute-start(bf16[128,512]{1,0:T(8,128)(2,1)S(1)} %get-tuple-element.105), channel_id=1, source_target_pairs={{0,16},{1,17},{2,18},{3,19},{4,20},{5,21},{6,22},{7,23},{8,24},{9,... | collective-permute-start | bytes 393224 | tf_op jit(solution)/shard_map/ppermute | solution.py:205
  33.1 0.7 copy-done.8
  33.8 2.2 %shard_map.142 = (f32[512,512]{1,0:T(8,128)S(1)}, f32[1,512]{1,0:T(1,128)S(1)}, bf16[512,512]{1,0:T(8,128)(2,1)S(1)}) custom-call(s32[32]{0:T(128)S(1)} %broadcast_xor_fusion.nat_ref, s32[2,4]{1,0:T(2,128)S(1)} %copy-done.9, bf16[512,512]{1,0:T(8,128)(2,1)S(1)} %constant_dynamic-update-slice_fusion.lo_ref, ...), custom_call_target="tpu_custom_call" | custom-call | flops 1073741824 | bytes 4202656 | tf_op jit(solution)/shard_map/pallas_call | solution.py:171
  36.0 2.5 %collective-permute-done.9 = bf16[128,512]{1,0:T(8,128)(2,1)S(1)} collective-permute-done((bf16[128,512]{1,0:T(8,128)(2,1)S(1)}, bf16[128,512]{1,0:T(8,128)(2,1)S(1)}, u32[]{:S(2)}, u32[]{:S(2)}) %collective-permute-start.9) | collective-permute-done | bytes 131104 | tf_op jit(solution)/shard_map/ppermute | solution.py:205
  38.6 1.8 %collective-permute-start.11 = (bf16[32,512]{1,0:T(8,128)(2,1)S(1)}, bf16[32,512]{1,0:T(8,128)(2,1)S(1)}, u32[]{:S(2)}, u32[]{:S(2)}) collective-permute-start(bf16[32,512]{1,0:T(8,128)(2,1)S(1)} %get-tuple-element.111), channel_id=1, source_target_pairs={{0,4},{1,5},{2,6},{3,7},{4,0},{5,1},{6,2},{7,3},{8,12},{9,13},{10,... | collective-permute-start | bytes 98312 | tf_op jit(solution)/shard_map/ppermute | solution.py:205
  40.5 1.2 %collective-permute-start.14 = (bf16[32,512]{1,0:T(8,128)(2,1)S(1)}, bf16[32,512]{1,0:T(8,128)(2,1)S(1)}, u32[]{:S(2)}, u32[]{:S(2)}) collective-permute-start(bf16[32,512]{1,0:T(8,128)(2,1)S(1)} %get-tuple-element.112), channel_id=1, source_target_pairs={{0,6},{1,7},{2,4},{3,5},{4,2},{5,3},{6,0},{7,1},{8,14},{9,15},{10,... | collective-permute-start | bytes 98312 | tf_op jit(solution)/shard_map/ppermute | solution.py:205
  41.6 0.5 collective-permute-start.13
  42.2 1.9 %collective-permute-done.11 = bf16[32,512]{1,0:T(8,128)(2,1)S(1)} collective-permute-done((bf16[32,512]{1,0:T(8,128)(2,1)S(1)}, bf16[32,512]{1,0:T(8,128)(2,1)S(1)}, u32[]{:S(2)}, u32[]{:S(2)}) %collective-permute-start.11) | collective-permute-done | bytes 32800 | tf_op jit(solution)/shard_map/ppermute | solution.py:205
  44.1 3.9 %collective-permute-start.21 = (bf16[528,512]{1,0:T(8,128)(2,1)S(1)}, bf16[528,512]{1,0:T(8,128)(2,1)S(1)}, u32[]{:S(2)}, u32[]{:S(2)}) collective-permute-start(bf16[528,512]{1,0:T(8,128)(2,1)S(1)} %collective-permute-done.12), channel_id=1, source_target_pairs={{0,1},{1,0},{2,3},{3,2},{4,5},{5,4},{6,7},{7,6},{8,9},{9,8},{10,11... | collective-permute-start | bytes 1622024 | tf_op jit(solution)/shard_map/ppermute | solution.py:287
  48.1 0.1 constant_dynamic-update-slice_fusion.13
  48.1 1.6 %collective-permute-start.17 = (bf16[32,512]{1,0:T(8,128)(2,1)S(1)}, bf16[32,512]{1,0:T(8,128)(2,1)S(1)}, u32[]{:S(2)}, u32[]{:S(2)}) collective-permute-start(bf16[32,512]{1,0:T(8,128)(2,1)S(1)} %get-tuple-element.96), channel_id=1, source_target_pairs={{0,6},{1,7},{2,4},{3,5},{4,2},{5,3},{6,0},{7,1},{8,14},{9,15},{10,... | collective-permute-start | bytes 98312 | tf_op jit(solution)/shard_map/ppermute | solution.py:205
  49.7 2.9 %collective-permute-start.15 = (bf16[32,512]{1,0:T(8,128)(2,1)S(1)}, bf16[32,512]{1,0:T(8,128)(2,1)S(1)}, u32[]{:S(2)}, u32[]{:S(2)}) collective-permute-start(bf16[32,512]{1,0:T(8,128)(2,1)S(1)} %get-tuple-element.96), channel_id=1, source_target_pairs={{0,4},{1,5},{2,6},{3,7},{4,0},{5,1},{6,2},{7,3},{8,12},{9,13},{10,... | collective-permute-start | bytes 98312 | tf_op jit(solution)/shard_map/ppermute | solution.py:205
  52.6 1.4 %collective-permute-done.17 = bf16[32,512]{1,0:T(8,128)(2,1)S(1)} collective-permute-done((bf16[32,512]{1,0:T(8,128)(2,1)S(1)}, bf16[32,512]{1,0:T(8,128)(2,1)S(1)}, u32[]{:S(2)}, u32[]{:S(2)}) %collective-permute-start.17) | collective-permute-done | bytes 32800 | tf_op jit(solution)/shard_map/ppermute | solution.py:205
  54.0 0.5 collective-permute-done.15
  54.5 1.2 %collective-permute-start.20 = (bf16[128,512]{1,0:T(8,128)(2,1)S(1)}, bf16[128,512]{1,0:T(8,128)(2,1)S(1)}, u32[]{:S(2)}, u32[]{:S(2)}) collective-permute-start(bf16[128,512]{1,0:T(8,128)(2,1)S(1)} %pad_maximum_fusion.1), channel_id=1, source_target_pairs={{0,17},{1,16},{2,19},{3,18},{4,21},{5,20},{6,23},{7,22},{8,25},{9,... | collective-permute-start | bytes 393224 | tf_op jit(solution)/shard_map/ppermute | solution.py:205
  55.8 0.7 collective-permute-start.19
  56.5 1.6 %collective-permute-start.18 = (bf16[128,512]{1,0:T(8,128)(2,1)S(1)}, bf16[128,512]{1,0:T(8,128)(2,1)S(1)}, u32[]{:S(2)}, u32[]{:S(2)}) collective-permute-start(bf16[128,512]{1,0:T(8,128)(2,1)S(1)} %pad_maximum_fusion.1), channel_id=1, source_target_pairs={{0,1},{1,0},{2,3},{3,2},{4,5},{5,4},{6,7},{7,6},{8,9},{9,8},{10,11... | collective-permute-start | bytes 393224 | tf_op jit(solution)/shard_map/ppermute | solution.py:205
  58.1 5.9 %collective-permute-done.20 = bf16[128,512]{1,0:T(8,128)(2,1)S(1)} collective-permute-done((bf16[128,512]{1,0:T(8,128)(2,1)S(1)}, bf16[128,512]{1,0:T(8,128)(2,1)S(1)}, u32[]{:S(2)}, u32[]{:S(2)}) %collective-permute-start.20) | collective-permute-done | bytes 131104 | tf_op jit(solution)/shard_map/ppermute | solution.py:205
  64.0 1.7 %collective-permute-done.18 = bf16[128,512]{1,0:T(8,128)(2,1)S(1)} collective-permute-done((bf16[128,512]{1,0:T(8,128)(2,1)S(1)}, bf16[128,512]{1,0:T(8,128)(2,1)S(1)}, u32[]{:S(2)}, u32[]{:S(2)}) %collective-permute-start.18) | collective-permute-done | bytes 131104 | tf_op jit(solution)/shard_map/ppermute | solution.py:205
  65.7 0.1 collective-permute-start.22
  65.8 1.9 %collective-permute-done.22.hi_ref = bf16[512,512]{1,0:T(8,128)(2,1)S(1)} collective-permute-done((bf16[512,512]{1,0:T(8,128)(2,1)S(1)}, bf16[512,512]{1,0:T(8,128)(2,1)S(1)}, u32[]{:S(2)}, u32[]{:S(2)}) %collective-permute-start.22) | collective-permute-done | bytes 524320 | tf_op jit(solution)/shard_map/ppermute | solution.py:205
  67.7 2.6 %shard_map.143 = (bf16[512,512]{1,0:T(8,128)(2,1)S(1)}, bf16[512,512]{1,0:T(8,128)(2,1)S(1)}, bf16[512,512]{1,0:T(8,128)(2,1)S(1)}, bf16[512,512]{1,0:T(8,128)(2,1)S(1)}, bf16[512,512]{1,0:T(8,128)(2,1)S(1)}) custom-call(s32[32]{0:T(128)S(1)} %broadcast_xor_fusion.nat_ref, s32[2,1]{1,0:T(2,128)S(1)} %copy.16.live_ref, s32[2,4]{1,0:T(2,128)S(1)} %copy-done.9, ...), custom_call_target="tpu_custom_call" | custom-call | flops 1342177280 | bytes 5275816 | tf_op jit(solution)/shard_map/pallas_call | solution.py:171
  70.3 0.2 collective-permute-start.23
  70.5 1.8 %collective-permute-done.23 = bf16[512,512]{1,0:T(8,128)(2,1)S(1)} collective-permute-done((bf16[512,512]{1,0:T(8,128)(2,1)S(1)}, bf16[512,512]{1,0:T(8,128)(2,1)S(1)}, u32[]{:S(2)}, u32[]{:S(2)}) %collective-permute-start.23) | collective-permute-done | bytes 524320 | tf_op jit(solution)/shard_map/ppermute | solution.py:205
  72.3 0.1 add_convert_fusion
  72.5 2.2 %collective-permute-start.26 = (bf16[128,512]{1,0:T(8,128)(2,1)S(1)}, bf16[128,512]{1,0:T(8,128)(2,1)S(1)}, u32[]{:S(2)}, u32[]{:S(2)}) collective-permute-start(bf16[128,512]{1,0:T(8,128)(2,1)S(1)} %get-tuple-element.101), channel_id=1, source_target_pairs={{0,17},{1,16},{2,19},{3,18},{4,21},{5,20},{6,23},{7,22},{8,25},{9,... | collective-permute-start | bytes 393224 | tf_op jit(solution)/shard_map/ppermute | solution.py:205
  74.6 1.1 %collective-permute-start.25 = (bf16[128,512]{1,0:T(8,128)(2,1)S(1)}, bf16[128,512]{1,0:T(8,128)(2,1)S(1)}, u32[]{:S(2)}, u32[]{:S(2)}) collective-permute-start(bf16[128,512]{1,0:T(8,128)(2,1)S(1)} %get-tuple-element.102), channel_id=1, source_target_pairs={{0,16},{1,17},{2,18},{3,19},{4,20},{5,21},{6,22},{7,23},{8,24},{9,... | collective-permute-start | bytes 393224 | tf_op jit(solution)/shard_map/ppermute | solution.py:205
  75.7 0.3 collective-permute-start.24
  76.0 1.7 %shard_map.145 = f32[512,512]{1,0:T(8,128)} custom-call(bf16[512,512]{1,0:T(8,128)(2,1)S(1)} %get-tuple-element.89.w_ref, bf16[512,512]{1,0:T(8,128)(2,1)S(1)} %get-tuple-element.90.u_ref, bf16[528,512]{1,0:T(8,128)(2,1)S(1)} %collective-permute-done.21.rest_0_.refs_0_), custom_call_target="tpu_custom_call" | custom-call | flops 268435456 | bytes 2637824 | tf_op jit(solution)/shard_map/pallas_call | solution.py:171
  77.7 2.9 %shard_map.144 = f32[512,512]{1,0:T(8,128)} custom-call(s32[32]{0:T(128)S(1)} %broadcast_xor_fusion.nat_ref, s32[2,4]{1,0:T(2,128)S(1)} %copy-done.9, bf16[512,512]{1,0:T(8,128)(2,1)S(1)} %constant_dynamic-update-slice_fusion.7.lo_ref, bf16[512,512]{1,0:T(8,128)(2,1)S(1)} %collective-permute-done.22.hi_ref, bf16[512,512]{1,0:T(8,128)(2,1)S(1)} %get-tuple-element.82.gu_ref, ...), custom_call_target="tpu_custom_call" | custom-call | flops 1073741824 | bytes 3676320 | tf_op jit(solution)/shard_map/pallas_call | solution.py:171
  80.6 1.1 %collective-permute-done.25 = bf16[128,512]{1,0:T(8,128)(2,1)S(1)} collective-permute-done((bf16[128,512]{1,0:T(8,128)(2,1)S(1)}, bf16[128,512]{1,0:T(8,128)(2,1)S(1)}, u32[]{:S(2)}, u32[]{:S(2)}) %collective-permute-start.25) | collective-permute-done | bytes 131104 | tf_op jit(solution)/shard_map/ppermute | solution.py:205
  81.8 0.1 collective-permute-start.27
  81.9 1.1 %collective-permute-start.29 = (bf16[32,512]{1,0:T(8,128)(2,1)S(1)}, bf16[32,512]{1,0:T(8,128)(2,1)S(1)}, u32[]{:S(2)}, u32[]{:S(2)}) collective-permute-start(bf16[32,512]{1,0:T(8,128)(2,1)S(1)} %get-tuple-element.109), channel_id=1, source_target_pairs={{0,6},{1,7},{2,4},{3,5},{4,2},{5,3},{6,0},{7,1},{8,14},{9,15},{10,... | collective-permute-start | bytes 98312 | tf_op jit(solution)/shard_map/ppermute | solution.py:205
  83.0 2.4 %collective-permute-start.28 = (bf16[32,512]{1,0:T(8,128)(2,1)S(1)}, bf16[32,512]{1,0:T(8,128)(2,1)S(1)}, u32[]{:S(2)}, u32[]{:S(2)}) collective-permute-start(bf16[32,512]{1,0:T(8,128)(2,1)S(1)} %get-tuple-element.110), channel_id=1, source_target_pairs={{0,2},{1,3},{2,0},{3,1},{4,6},{5,7},{6,4},{7,5},{8,10},{9,11},{10,... | collective-permute-start | bytes 98312 | tf_op jit(solution)/shard_map/ppermute | solution.py:205
  85.4 1.7 %collective-permute-done.27 = bf16[32,512]{1,0:T(8,128)(2,1)S(1)} collective-permute-done((bf16[32,512]{1,0:T(8,128)(2,1)S(1)}, bf16[32,512]{1,0:T(8,128)(2,1)S(1)}, u32[]{:S(2)}, u32[]{:S(2)}) %collective-permute-start.27) | collective-permute-done | bytes 32800 | tf_op jit(solution)/shard_map/ppermute | solution.py:205
  87.1 0.7 collective-permute-done.29
  87.8 0.7 divide_subtract_fusion
  (54 shorter events, 0.3 us)
Async XLA Ops:
  0.6 6.6 %copy-start.4 = (s32[2,512]{1,0:T(2,128)S(1)}, s32[2,512]{1,0:T(2,128)}, u32[]{:S(2)}) copy-start(s32[2,512]{1,0:T(2,128)} %trows_ref.1) | copy-start | bytes 12292
  0.6 6.6 %copy-start.5 = (s32[2,4,128]{2,1,0:T(4,128)S(1)}, s32[2,4,128]{2,1,0:T(4,128)}, u32[]{:S(2)}) copy-start(s32[2,4,128]{2,1,0:T(4,128)} %neg_ref.1) | copy-start | bytes 12292
  0.7 6.6 %copy-start.6 = (s32[2,512]{1,0:T(2,128)S(1)}, s32[2,512]{1,0:T(2,128)}, u32[]{:S(2)}) copy-start(s32[2,512]{1,0:T(2,128)} %hrows_ref.5) | copy-start | bytes 12292
  1.5 8.9 %collective-permute-start.2 = (bf16[32,512]{1,0:T(8,128)(2,1)S(1)}, bf16[32,512]{1,0:T(8,128)(2,1)S(1)}, u32[]{:S(2)}, u32[]{:S(2)}) collective-permute-start(bf16[32,512]{1,0:T(8,128)(2,1)S(1)} %get-tuple-element.99), channel_id=1, source_target_pairs={{0,6},{1,7},{2,4},{3,5},{4,2},{5,3},{6,0},{7,1},{8,14},{9,15},{10,... | collective-permute-start | bytes 98312 | tf_op jit(solution)/shard_map/ppermute | solution.py:205
  6.6 3.9 %collective-permute-start.1 = (bf16[32,512]{1,0:T(8,128)(2,1)S(1)}, bf16[32,512]{1,0:T(8,128)(2,1)S(1)}, u32[]{:S(2)}, u32[]{:S(2)}) collective-permute-start(bf16[32,512]{1,0:T(8,128)(2,1)S(1)} %get-tuple-element.99), channel_id=1, source_target_pairs={{0,2},{1,3},{2,0},{3,1},{4,6},{5,7},{6,4},{7,5},{8,10},{9,11},{10,... | collective-permute-start | bytes 98312 | tf_op jit(solution)/shard_map/ppermute | solution.py:205
  6.6 4.9 %collective-permute-start = (bf16[32,512]{1,0:T(8,128)(2,1)S(1)}, bf16[32,512]{1,0:T(8,128)(2,1)S(1)}, u32[]{:S(2)}, u32[]{:S(2)}) collective-permute-start(bf16[32,512]{1,0:T(8,128)(2,1)S(1)} %get-tuple-element.99), channel_id=1, source_target_pairs={{0,4},{1,5},{2,6},{3,7},{4,0},{5,1},{6,2},{7,3},{8,12},{9,13},{10,... | collective-permute-start | bytes 98312 | tf_op jit(solution)/shard_map/ppermute | solution.py:205
  7.2 1.2 %copy-start = (f32[512,512]{1,0:T(8,128)S(1)}, f32[512,512]{1,0:T(8,128)}, u32[]{:S(2)}) copy-start(f32[512,512]{1,0:T(8,128)} %table_ref.2) | copy-start | bytes 3145732
  8.4 1.2 %copy-start.2 = (f32[512,512]{1,0:T(8,128)S(1)}, f32[512,512]{1,0:T(8,128)}, u32[]{:S(2)}) copy-start(f32[512,512]{1,0:T(8,128)} %table_ref.3) | copy-start | bytes 3145732
  11.5 7.2 %collective-permute-start.5 = (bf16[128,512]{1,0:T(8,128)(2,1)S(1)}, bf16[128,512]{1,0:T(8,128)(2,1)S(1)}, u32[]{:S(2)}, u32[]{:S(2)}) collective-permute-start(bf16[128,512]{1,0:T(8,128)(2,1)S(1)} %pad_maximum_fusion), channel_id=1, source_target_pairs={{0,17},{1,16},{2,19},{3,18},{4,21},{5,20},{6,23},{7,22},{8,25},{9,... | collective-permute-start | bytes 393224 | tf_op jit(solution)/shard_map/ppermute | solution.py:205
  14.0 5.6 %collective-permute-start.4 = (bf16[128,512]{1,0:T(8,128)(2,1)S(1)}, bf16[128,512]{1,0:T(8,128)(2,1)S(1)}, u32[]{:S(2)}, u32[]{:S(2)}) collective-permute-start(bf16[128,512]{1,0:T(8,128)(2,1)S(1)} %pad_maximum_fusion), channel_id=1, source_target_pairs={{0,16},{1,17},{2,18},{3,19},{4,20},{5,21},{6,22},{7,23},{8,24},{9,... | collective-permute-start | bytes 393224 | tf_op jit(solution)/shard_map/ppermute | solution.py:205
  14.5 5.1 %collective-permute-start.3 = (bf16[128,512]{1,0:T(8,128)(2,1)S(1)}, bf16[128,512]{1,0:T(8,128)(2,1)S(1)}, u32[]{:S(2)}, u32[]{:S(2)}) collective-permute-start(bf16[128,512]{1,0:T(8,128)(2,1)S(1)} %pad_maximum_fusion), channel_id=1, source_target_pairs={{0,1},{1,0},{2,3},{3,2},{4,5},{5,4},{6,7},{7,6},{8,9},{9,8},{10,11... | collective-permute-start | bytes 393224 | tf_op jit(solution)/shard_map/ppermute | solution.py:205
  19.7 2.0 %collective-permute-start.6 = (bf16[512,512]{1,0:T(8,128)(2,1)S(1)}, bf16[512,512]{1,0:T(8,128)(2,1)S(1)}, u32[]{:S(2)}, u32[]{:S(2)}) collective-permute-start(bf16[512,512]{1,0:T(8,128)(2,1)S(1)} %constant_dynamic-update-slice_fusion.lo_ref), channel_id=1, source_target_pairs={{0,8},{1,9},{2,10},{3,11},{4,12},{5,13},{6,14},{7,15},{8,0},{9,1},... | collective-permute-start | bytes 1572872 | tf_op jit(solution)/shard_map/ppermute | solution.py:205
  19.8 0.7 copy-start.12
  20.5 0.7 copy-start.13
  21.2 0.7 copy-start.9
  21.2 3.9 %copy-start.1 = (f32[512,512]{1,0:T(8,128)S(1)}, f32[512,512]{1,0:T(8,128)}, u32[]{:S(2)}) copy-start(f32[512,512]{1,0:T(8,128)} %table_ref.2) | copy-start | bytes 3145732
  24.5 2.1 %collective-permute-start.7 = (bf16[512,512]{1,0:T(8,128)(2,1)S(1)}, bf16[512,512]{1,0:T(8,128)(2,1)S(1)}, u32[]{:S(2)}, u32[]{:S(2)}) collective-permute-start(bf16[512,512]{1,0:T(8,128)(2,1)S(1)} %get-tuple-element.61), channel_id=1, source_target_pairs={{0,8},{1,9},{2,10},{3,11},{4,12},{5,13},{6,14},{7,15},{8,0},{9,1},... | collective-permute-start | bytes 1572872 | tf_op jit(solution)/shard_map/ppermute | solution.py:205
  25.1 0.7 copy-start.7
  26.4 6.6 %copy-start.3 = (f32[512,512]{1,0:T(8,128)S(1)}, f32[512,512]{1,0:T(8,128)}, u32[]{:S(2)}) copy-start(f32[512,512]{1,0:T(8,128)} %table_ref.3) | copy-start | bytes 3145732
  26.6 17.5 %collective-permute-start.12 = (bf16[528,512]{1,0:T(8,128)(2,1)S(1)}, bf16[528,512]{1,0:T(8,128)(2,1)S(1)}, u32[]{:S(2)}, u32[]{:S(2)}) collective-permute-start(bf16[528,512]{1,0:T(8,128)(2,1)S(1)} %shard_map.141), channel_id=1, source_target_pairs={{0,0},{1,3},{2,2},{3,5},{4,4},{5,7},{6,6},{7,1},{8,8},{9,11},{10,1... | collective-permute-start | bytes 1622024 | tf_op jit(solution)/shard_map/ppermute | solution.py:286
  27.6 8.4 %collective-permute-start.10 = (bf16[128,512]{1,0:T(8,128)(2,1)S(1)}, bf16[128,512]{1,0:T(8,128)(2,1)S(1)}, u32[]{:S(2)}, u32[]{:S(2)}) collective-permute-start(bf16[128,512]{1,0:T(8,128)(2,1)S(1)} %get-tuple-element.104), channel_id=1, source_target_pairs={{0,17},{1,16},{2,19},{3,18},{4,21},{5,20},{6,23},{7,22},{8,25},{9,... | collective-permute-start | bytes 393224 | tf_op jit(solution)/shard_map/ppermute | solution.py:205
  32.1 6.4 %collective-permute-start.9 = (bf16[128,512]{1,0:T(8,128)(2,1)S(1)}, bf16[128,512]{1,0:T(8,128)(2,1)S(1)}, u32[]{:S(2)}, u32[]{:S(2)}) collective-permute-start(bf16[128,512]{1,0:T(8,128)(2,1)S(1)} %get-tuple-element.105), channel_id=1, source_target_pairs={{0,16},{1,17},{2,18},{3,19},{4,20},{5,21},{6,22},{7,23},{8,24},{9,... | collective-permute-start | bytes 393224 | tf_op jit(solution)/shard_map/ppermute | solution.py:205
  33.1 0.7 copy-start.8
  33.1 5.5 %collective-permute-start.8 = (bf16[128,512]{1,0:T(8,128)(2,1)S(1)}, bf16[128,512]{1,0:T(8,128)(2,1)S(1)}, u32[]{:S(2)}, u32[]{:S(2)}) collective-permute-start(bf16[128,512]{1,0:T(8,128)(2,1)S(1)} %get-tuple-element.106), channel_id=1, source_target_pairs={{0,1},{1,0},{2,3},{3,2},{4,5},{5,4},{6,7},{7,6},{8,9},{9,8},{10,11... | collective-permute-start | bytes 393224 | tf_op jit(solution)/shard_map/ppermute | solution.py:205
  38.6 9.5 %copy-start.10 = (f32[32,512]{1,0:T(8,128)S(1)}, f32[32,512]{1,0:T(8,128)}, u32[]{:S(2)}) copy-start(f32[32,512]{1,0:T(8,128)} %param.16) | copy-start | bytes 196612
  38.6 9.5 %copy-start.11 = (f32[32,512]{1,0:T(8,128)S(1)}, f32[32,512]{1,0:T(8,128)}, u32[]{:S(2)}) copy-start(f32[32,512]{1,0:T(8,128)} %param.17) | copy-start | bytes 196612
  38.6 5.5 %collective-permute-start.11 = (bf16[32,512]{1,0:T(8,128)(2,1)S(1)}, bf16[32,512]{1,0:T(8,128)(2,1)S(1)}, u32[]{:S(2)}, u32[]{:S(2)}) collective-permute-start(bf16[32,512]{1,0:T(8,128)(2,1)S(1)} %get-tuple-element.111), channel_id=1, source_target_pairs={{0,4},{1,5},{2,6},{3,7},{4,0},{5,1},{6,2},{7,3},{8,12},{9,13},{10,... | collective-permute-start | bytes 98312 | tf_op jit(solution)/shard_map/ppermute | solution.py:205
  40.5 7.6 %collective-permute-start.14 = (bf16[32,512]{1,0:T(8,128)(2,1)S(1)}, bf16[32,512]{1,0:T(8,128)(2,1)S(1)}, u32[]{:S(2)}, u32[]{:S(2)}) collective-permute-start(bf16[32,512]{1,0:T(8,128)(2,1)S(1)} %get-tuple-element.112), channel_id=1, source_target_pairs={{0,6},{1,7},{2,4},{3,5},{4,2},{5,3},{6,0},{7,1},{8,14},{9,15},{10,... | collective-permute-start | bytes 98312 | tf_op jit(solution)/shard_map/ppermute | solution.py:205
  41.6 6.4 %collective-permute-start.13 = (bf16[32,512]{1,0:T(8,128)(2,1)S(1)}, bf16[32,512]{1,0:T(8,128)(2,1)S(1)}, u32[]{:S(2)}, u32[]{:S(2)}) collective-permute-start(bf16[32,512]{1,0:T(8,128)(2,1)S(1)} %get-tuple-element.113), channel_id=1, source_target_pairs={{0,2},{1,3},{2,0},{3,1},{4,6},{5,7},{6,4},{7,5},{8,10},{9,11},{10,... | collective-permute-start | bytes 98312 | tf_op jit(solution)/shard_map/ppermute | solution.py:205
  44.1 21.6 %collective-permute-start.21 = (bf16[528,512]{1,0:T(8,128)(2,1)S(1)}, bf16[528,512]{1,0:T(8,128)(2,1)S(1)}, u32[]{:S(2)}, u32[]{:S(2)}) collective-permute-start(bf16[528,512]{1,0:T(8,128)(2,1)S(1)} %collective-permute-done.12), channel_id=1, source_target_pairs={{0,1},{1,0},{2,3},{3,2},{4,5},{5,4},{6,7},{7,6},{8,9},{9,8},{10,11... | collective-permute-start | bytes 1622024 | tf_op jit(solution)/shard_map/ppermute | solution.py:287
  48.1 5.8 %collective-permute-start.17 = (bf16[32,512]{1,0:T(8,128)(2,1)S(1)}, bf16[32,512]{1,0:T(8,128)(2,1)S(1)}, u32[]{:S(2)}, u32[]{:S(2)}) collective-permute-start(bf16[32,512]{1,0:T(8,128)(2,1)S(1)} %get-tuple-element.96), channel_id=1, source_target_pairs={{0,6},{1,7},{2,4},{3,5},{4,2},{5,3},{6,0},{7,1},{8,14},{9,15},{10,... | collective-permute-start | bytes 98312 | tf_op jit(solution)/shard_map/ppermute | solution.py:205
  49.7 4.3 %collective-permute-start.16 = (bf16[32,512]{1,0:T(8,128)(2,1)S(1)}, bf16[32,512]{1,0:T(8,128)(2,1)S(1)}, u32[]{:S(2)}, u32[]{:S(2)}) collective-permute-start(bf16[32,512]{1,0:T(8,128)(2,1)S(1)} %get-tuple-element.96), channel_id=1, source_target_pairs={{0,2},{1,3},{2,0},{3,1},{4,6},{5,7},{6,4},{7,5},{8,10},{9,11},{10,... | collective-permute-start | bytes 98312 | tf_op jit(solution)/shard_map/ppermute | solution.py:205
  49.7 4.8 %collective-permute-start.15 = (bf16[32,512]{1,0:T(8,128)(2,1)S(1)}, bf16[32,512]{1,0:T(8,128)(2,1)S(1)}, u32[]{:S(2)}, u32[]{:S(2)}) collective-permute-start(bf16[32,512]{1,0:T(8,128)(2,1)S(1)} %get-tuple-element.96), channel_id=1, source_target_pairs={{0,4},{1,5},{2,6},{3,7},{4,0},{5,1},{6,2},{7,3},{8,12},{9,13},{10,... | collective-permute-start | bytes 98312 | tf_op jit(solution)/shard_map/ppermute | solution.py:205
  54.5 9.5 %collective-permute-start.20 = (bf16[128,512]{1,0:T(8,128)(2,1)S(1)}, bf16[128,512]{1,0:T(8,128)(2,1)S(1)}, u32[]{:S(2)}, u32[]{:S(2)}) collective-permute-start(bf16[128,512]{1,0:T(8,128)(2,1)S(1)} %pad_maximum_fusion.1), channel_id=1, source_target_pairs={{0,17},{1,16},{2,19},{3,18},{4,21},{5,20},{6,23},{7,22},{8,25},{9,... | collective-permute-start | bytes 393224 | tf_op jit(solution)/shard_map/ppermute | solution.py:205
  55.8 8.2 %collective-permute-start.19 = (bf16[128,512]{1,0:T(8,128)(2,1)S(1)}, bf16[128,512]{1,0:T(8,128)(2,1)S(1)}, u32[]{:S(2)}, u32[]{:S(2)}) collective-permute-start(bf16[128,512]{1,0:T(8,128)(2,1)S(1)} %pad_maximum_fusion.1), channel_id=1, source_target_pairs={{0,16},{1,17},{2,18},{3,19},{4,20},{5,21},{6,22},{7,23},{8,24},{9,... | collective-permute-start | bytes 393224 | tf_op jit(solution)/shard_map/ppermute | solution.py:205
  56.5 9.2 %collective-permute-start.18 = (bf16[128,512]{1,0:T(8,128)(2,1)S(1)}, bf16[128,512]{1,0:T(8,128)(2,1)S(1)}, u32[]{:S(2)}, u32[]{:S(2)}) collective-permute-start(bf16[128,512]{1,0:T(8,128)(2,1)S(1)} %pad_maximum_fusion.1), channel_id=1, source_target_pairs={{0,1},{1,0},{2,3},{3,2},{4,5},{5,4},{6,7},{7,6},{8,9},{9,8},{10,11... | collective-permute-start | bytes 393224 | tf_op jit(solution)/shard_map/ppermute | solution.py:205
  65.7 2.0 %collective-permute-start.22 = (bf16[512,512]{1,0:T(8,128)(2,1)S(1)}, bf16[512,512]{1,0:T(8,128)(2,1)S(1)}, u32[]{:S(2)}, u32[]{:S(2)}) collective-permute-start(bf16[512,512]{1,0:T(8,128)(2,1)S(1)} %constant_dynamic-update-slice_fusion.7.lo_ref), channel_id=1, source_target_pairs={{0,8},{1,9},{2,10},{3,11},{4,12},{5,13},{6,14},{7,15},{8,0},{9,1},... | collective-permute-start | bytes 1572872 | tf_op jit(solution)/shard_map/ppermute | solution.py:205
  70.3 2.0 %collective-permute-start.23 = (bf16[512,512]{1,0:T(8,128)(2,1)S(1)}, bf16[512,512]{1,0:T(8,128)(2,1)S(1)}, u32[]{:S(2)}, u32[]{:S(2)}) collective-permute-start(bf16[512,512]{1,0:T(8,128)(2,1)S(1)} %get-tuple-element.81), channel_id=1, source_target_pairs={{0,8},{1,9},{2,10},{3,11},{4,12},{5,13},{6,14},{7,15},{8,0},{9,1},... | collective-permute-start | bytes 1572872 | tf_op jit(solution)/shard_map/ppermute | solution.py:205
  72.5 8.2 %collective-permute-start.26 = (bf16[128,512]{1,0:T(8,128)(2,1)S(1)}, bf16[128,512]{1,0:T(8,128)(2,1)S(1)}, u32[]{:S(2)}, u32[]{:S(2)}) collective-permute-start(bf16[128,512]{1,0:T(8,128)(2,1)S(1)} %get-tuple-element.101), channel_id=1, source_target_pairs={{0,17},{1,16},{2,19},{3,18},{4,21},{5,20},{6,23},{7,22},{8,25},{9,... | collective-permute-start | bytes 393224 | tf_op jit(solution)/shard_map/ppermute | solution.py:205
  74.6 7.1 %collective-permute-start.25 = (bf16[128,512]{1,0:T(8,128)(2,1)S(1)}, bf16[128,512]{1,0:T(8,128)(2,1)S(1)}, u32[]{:S(2)}, u32[]{:S(2)}) collective-permute-start(bf16[128,512]{1,0:T(8,128)(2,1)S(1)} %get-tuple-element.102), channel_id=1, source_target_pairs={{0,16},{1,17},{2,18},{3,19},{4,20},{5,21},{6,22},{7,23},{8,24},{9,... | collective-permute-start | bytes 393224 | tf_op jit(solution)/shard_map/ppermute | solution.py:205
  75.7 6.1 %collective-permute-start.24 = (bf16[128,512]{1,0:T(8,128)(2,1)S(1)}, bf16[128,512]{1,0:T(8,128)(2,1)S(1)}, u32[]{:S(2)}, u32[]{:S(2)}) collective-permute-start(bf16[128,512]{1,0:T(8,128)(2,1)S(1)} %get-tuple-element.103), channel_id=1, source_target_pairs={{0,1},{1,0},{2,3},{3,2},{4,5},{5,4},{6,7},{7,6},{8,9},{9,8},{10,11... | collective-permute-start | bytes 393224 | tf_op jit(solution)/shard_map/ppermute | solution.py:205
  81.8 5.2 %collective-permute-start.27 = (bf16[32,512]{1,0:T(8,128)(2,1)S(1)}, bf16[32,512]{1,0:T(8,128)(2,1)S(1)}, u32[]{:S(2)}, u32[]{:S(2)}) collective-permute-start(bf16[32,512]{1,0:T(8,128)(2,1)S(1)} %get-tuple-element.108), channel_id=1, source_target_pairs={{0,4},{1,5},{2,6},{3,7},{4,0},{5,1},{6,2},{7,3},{8,12},{9,13},{10,... | collective-permute-start | bytes 98312 | tf_op jit(solution)/shard_map/ppermute | solution.py:205
  81.9 5.9 %collective-permute-start.29 = (bf16[32,512]{1,0:T(8,128)(2,1)S(1)}, bf16[32,512]{1,0:T(8,128)(2,1)S(1)}, u32[]{:S(2)}, u32[]{:S(2)}) collective-permute-start(bf16[32,512]{1,0:T(8,128)(2,1)S(1)} %get-tuple-element.109), channel_id=1, source_target_pairs={{0,6},{1,7},{2,4},{3,5},{4,2},{5,3},{6,0},{7,1},{8,14},{9,15},{10,... | collective-permute-start | bytes 98312 | tf_op jit(solution)/shard_map/ppermute | solution.py:205
  83.0 4.8 %collective-permute-start.28 = (bf16[32,512]{1,0:T(8,128)(2,1)S(1)}, bf16[32,512]{1,0:T(8,128)(2,1)S(1)}, u32[]{:S(2)}, u32[]{:S(2)}) collective-permute-start(bf16[32,512]{1,0:T(8,128)(2,1)S(1)} %get-tuple-element.110), channel_id=1, source_target_pairs={{0,2},{1,3},{2,0},{3,1},{4,6},{5,7},{6,4},{7,5},{8,10},{9,11},{10,... | collective-permute-start | bytes 98312 | tf_op jit(solution)/shard_map/ppermute | solution.py:205

commit v5 on v4

--- a/solution.py
+++ b/solution.py
@@ -60,8 +60,11 @@
 
 
 def prepare_kernel(
-    head_ref, tail_ref, hrows_ref, trows_ref, neg_ref, h_ref, t_ref, tcol_ref, cnt_ref
+    head_ref, tail_ref, hrows_ref, trows_ref, neg_ref, hstate_ref, tstate_ref,
+    h_ref, t_ref, tcol_ref, cnt_ref, hstate_out_ref, tstate_out_ref,
 ):
+    hstate_out_ref[...] = hstate_ref[...]
+    tstate_out_ref[...] = tstate_ref[...]
     buckets = hrows_ref.shape[0]
     blocks, nneg = neg_ref.shape[1:]
     pick = one_hot_rows(hrows_ref[0:1, :], head_ref.shape[0])
@@ -258,6 +261,8 @@
     half = all_rows // 2
     square = 2 * rows * edges * width
 
+    head_state = head_state.reshape(1, -1)
+    tail_state = tail_state.reshape(1, -1)
     prepared = call(
         prepare_kernel,
         [
@@ -265,12 +270,12 @@
             ((rows, width), BF16),
             ((2, edges, 128), F32),
             ((2, blocks, rows), F32),
+            (head_state.shape, F32),
+            (tail_state.shape, F32),
         ],
         0, [], square,
-        head_table, tail_table, head_rows, tail_rows, negatives,
+        head_table, tail_table, head_rows, tail_rows, negatives, head_state, tail_state,
     )
-    head_state = head_state.reshape(1, -1)
-    tail_state = tail_state.reshape(1, -1)
     held = {"prepared": prepared}
     rotated = []
 
@@ -303,7 +308,7 @@
     for k in range(2):
         lo, hi = exchange.all_gather(relations.astype(BF16), gather_hooks)
         if k == 0:
-            head_vecs, *tail_vecs, tail_col, counts = held["prepared"]
+            head_vecs, *tail_vecs, tail_col, counts, head_state, tail_state = held["prepared"]
         else:
             tail_vecs = rotated
         keep, send, weights, projected, edge_grad = call(
@@ -337,14 +342,8 @@
         )
         held.update(tail=tail_new, head=list(head_new))
         if k == 0:
-            step0 = []
-
-            def begin(got):
-                got = with_("tail")(got)
-                step0.extend(rotate(x, 0) for x in held["tail"])
-                return got
-
-            hooks = {0: begin, 1: with_("head"), 2: rotation(0, None)}
+            step0 = [rotate(x, 0) for x in tail_new]
+            hooks = {1: with_("head"), 2: rotation(0, None)}
         else:
             first, second = with_("tail"), with_("head")
             hooks = {1: lambda got: first(second(got))}

time: 88.8 us -> 87.8 us (0.989)
  local copies, waits for them, and re-layouts: 5.5 us -> 4.15 us
    unnamed x39, local copies, waits for them, and re-layouts: 5.48 us -> 4.13 us
where the time goes in v5:
time: 87.8 us; the launch traced here: 87.5 us
  starting transfers between devices  39.2 us (45%)
  waiting for transfers between devices  27.6 us (31%)
  Pallas kernels  13.6 us (15%)
  local copies, waits for them, and re-layouts  4.15 us (5%)
  other arithmetic  2.09 us (2%)
  between operations  0.88 us (1%)
    ppermute x28, starting transfers between devices, swap(): return lax.ppermute(x, AXES, [(i, i ^ mask) for i in range(self.devices)])  34.3 us
    ppermute x28, waiting for transfers between devices, swap(): return lax.ppermute(x, AXES, [(i, i ^ mask) for i in range(self.devices)])  27.6 us
    pallas_call x7, Pallas kernels, call(): pl.pallas_call(kernel, out_shape=outs, in_specs=[SMEM] * smem + [VMEM] *...  13.6 us
    unnamed x39, local copies, waits for them, and re-layouts  4.13 us
    ppermute x1, starting transfers between devices, rotate(): return lax.ppermute(x, 'tail', [(i, i ^ 1) for i in range(tails)])  4.08 us
  transfers between devices with their start and end apart: 30, of which 17 were waited for; matrix products, arithmetic and copies ran while one was open for 0% of the time, Pallas kernels for 9%

profile of v5, /device:TPU:0, one launch (start us, length us, event | category | flops | bytes accessed | tf_op | source)
XLA Modules:
  0.0 87.5 jit_solution(3111056521669565169)
XLA Ops:
  0.7 0.9 constant_dynamic-update-slice_fusion.6
  1.5 5.1 %collective-permute-start.2 = (bf16[32,512]{1,0:T(8,128)(2,1)S(1)}, bf16[32,512]{1,0:T(8,128)(2,1)S(1)}, u32[]{:S(2)}, u32[]{:S(2)}) collective-permute-start(bf16[32,512]{1,0:T(8,128)(2,1)S(1)} %get-tuple-element.103), channel_id=1, source_target_pairs={{0,6},{1,7},{2,4},{3,5},{4,2},{5,3},{6,0},{7,1},{8,14},{9,15},{10,... | collective-permute-start | bytes 98312 | tf_op jit(solution)/shard_map/ppermute | solution.py:208
  6.7 0.6 collective-permute-start
  7.3 1.2 %copy-done = f32[512,512]{1,0:T(8,128)S(1)} copy-done((f32[512,512]{1,0:T(8,128)S(1)}, f32[512,512]{1,0:T(8,128)}, u32[]{:S(2)}) %copy-start) | copy-done | bytes 1048600
  8.6 1.2 %copy-done.2 = f32[512,512]{1,0:T(8,128)S(1)} copy-done((f32[512,512]{1,0:T(8,128)S(1)}, f32[512,512]{1,0:T(8,128)}, u32[]{:S(2)}) %copy-start.2) | copy-done | bytes 1048600
  9.8 0.7 shard_map.139
  10.5 0.1 collective-permute-done.1
  10.6 1.0 %collective-permute-done = bf16[32,512]{1,0:T(8,128)(2,1)S(1)} collective-permute-done((bf16[32,512]{1,0:T(8,128)(2,1)S(1)}, bf16[32,512]{1,0:T(8,128)(2,1)S(1)}, u32[]{:S(2)}, u32[]{:S(2)}) %collective-permute-start) | collective-permute-done | bytes 32800 | tf_op jit(solution)/shard_map/ppermute | solution.py:208
  11.6 2.5 %collective-permute-start.5 = (bf16[128,512]{1,0:T(8,128)(2,1)S(1)}, bf16[128,512]{1,0:T(8,128)(2,1)S(1)}, u32[]{:S(2)}, u32[]{:S(2)}) collective-permute-start(bf16[128,512]{1,0:T(8,128)(2,1)S(1)} %pad_maximum_fusion), channel_id=1, source_target_pairs={{0,17},{1,16},{2,19},{3,18},{4,21},{5,20},{6,23},{7,22},{8,25},{9,... | collective-permute-start | bytes 393224 | tf_op jit(solution)/shard_map/ppermute | solution.py:208
  14.1 0.5 collective-permute-start.4
  14.6 0.5 collective-permute-start.3
  15.2 3.6 %collective-permute-done.5 = bf16[128,512]{1,0:T(8,128)(2,1)S(1)} collective-permute-done((bf16[128,512]{1,0:T(8,128)(2,1)S(1)}, bf16[128,512]{1,0:T(8,128)(2,1)S(1)}, u32[]{:S(2)}, u32[]{:S(2)}) %collective-permute-start.5) | collective-permute-done | bytes 131104 | tf_op jit(solution)/shard_map/ppermute | solution.py:208
  18.8 0.9 %collective-permute-done.4 = bf16[128,512]{1,0:T(8,128)(2,1)S(1)} collective-permute-done((bf16[128,512]{1,0:T(8,128)(2,1)S(1)}, bf16[128,512]{1,0:T(8,128)(2,1)S(1)}, u32[]{:S(2)}, u32[]{:S(2)}) %collective-permute-start.4) | collective-permute-done | bytes 131104 | tf_op jit(solution)/shard_map/ppermute | solution.py:208
  19.8 0.1 collective-permute-start.6
  19.9 0.6 copy-done.12
  20.5 0.1 copy.16.live_ref
  20.6 0.7 copy-done.13
  21.3 0.5 collective-permute-done.6.hi_ref
  21.7 0.2 copy-done.9
  21.9 2.6 %shard_map.140 = (bf16[512,512]{1,0:T(8,128)(2,1)S(1)}, bf16[512,512]{1,0:T(8,128)(2,1)S(1)}, bf16[512,512]{1,0:T(8,128)(2,1)S(1)}, bf16[512,512]{1,0:T(8,128)(2,1)S(1)}, bf16[512,512]{1,0:T(8,128)(2,1)S(1)}) custom-call(s32[32]{0:T(128)S(1)} %broadcast_xor_fusion.nat_ref, s32[2,1]{1,0:T(2,128)S(1)} %copy.16.live_ref, s32[2,4]{1,0:T(2,128)S(1)} %copy-done.9, ...), custom_call_target="tpu_custom_call" | custom-call | flops 1342177280 | bytes 5259432 | tf_op jit(solution)/shard_map/pallas_call | solution.py:174
  24.6 0.5 collective-permute-start.7
  25.1 0.7 shard_map.142
  25.8 0.8 collective-permute-start.12
  26.7 0.1 add_convert_fusion.4
  26.8 4.5 %collective-permute-start.10 = (bf16[128,512]{1,0:T(8,128)(2,1)S(1)}, bf16[128,512]{1,0:T(8,128)(2,1)S(1)}, u32[]{:S(2)}, u32[]{:S(2)}) collective-permute-start(bf16[128,512]{1,0:T(8,128)(2,1)S(1)} %get-tuple-element.108), channel_id=1, source_target_pairs={{0,17},{1,16},{2,19},{3,18},{4,21},{5,20},{6,23},{7,22},{8,25},{9,... | collective-permute-start | bytes 393224 | tf_op jit(solution)/shard_map/ppermute | solution.py:208
  31.4 0.9 %collective-permute-start.9 = (bf16[128,512]{1,0:T(8,128)(2,1)S(1)}, bf16[128,512]{1,0:T(8,128)(2,1)S(1)}, u32[]{:S(2)}, u32[]{:S(2)}) collective-permute-start(bf16[128,512]{1,0:T(8,128)(2,1)S(1)} %get-tuple-element.109), channel_id=1, source_target_pairs={{0,16},{1,17},{2,18},{3,19},{4,20},{5,21},{6,22},{7,23},{8,24},{9,... | collective-permute-start | bytes 393224 | tf_op jit(solution)/shard_map/ppermute | solution.py:208
  32.3 2.2 %shard_map.141 = (f32[512,512]{1,0:T(8,128)S(1)}, f32[1,512]{1,0:T(1,128)S(1)}, bf16[512,512]{1,0:T(8,128)(2,1)S(1)}) custom-call(s32[32]{0:T(128)S(1)} %broadcast_xor_fusion.nat_ref, s32[2,4]{1,0:T(2,128)S(1)} %copy-done.9, bf16[512,512]{1,0:T(8,128)(2,1)S(1)} %constant_dynamic-update-slice_fusion.lo_ref, ...), custom_call_target="tpu_custom_call" | custom-call | flops 1073741824 | bytes 4202656 | tf_op jit(solution)/shard_map/pallas_call | solution.py:174
  34.6 0.7 collective-permute-done.10
  35.3 2.3 %collective-permute-done.9 = bf16[128,512]{1,0:T(8,128)(2,1)S(1)} collective-permute-done((bf16[128,512]{1,0:T(8,128)(2,1)S(1)}, bf16[128,512]{1,0:T(8,128)(2,1)S(1)}, u32[]{:S(2)}, u32[]{:S(2)}) %collective-permute-start.9) | collective-permute-done | bytes 131104 | tf_op jit(solution)/shard_map/ppermute | solution.py:208
  37.6 0.1 add_convert_fusion.14
  37.6 1.9 %collective-permute-start.11 = (bf16[32,512]{1,0:T(8,128)(2,1)S(1)}, bf16[32,512]{1,0:T(8,128)(2,1)S(1)}, u32[]{:S(2)}, u32[]{:S(2)}) collective-permute-start(bf16[32,512]{1,0:T(8,128)(2,1)S(1)} %get-tuple-element.115), channel_id=1, source_target_pairs={{0,4},{1,5},{2,6},{3,7},{4,0},{5,1},{6,2},{7,3},{8,12},{9,13},{10,... | collective-permute-start | bytes 98312 | tf_op jit(solution)/shard_map/ppermute | solution.py:208
  39.6 1.2 %collective-permute-start.14 = (bf16[32,512]{1,0:T(8,128)(2,1)S(1)}, bf16[32,512]{1,0:T(8,128)(2,1)S(1)}, u32[]{:S(2)}, u32[]{:S(2)}) collective-permute-start(bf16[32,512]{1,0:T(8,128)(2,1)S(1)} %get-tuple-element.116), channel_id=1, source_target_pairs={{0,6},{1,7},{2,4},{3,5},{4,2},{5,3},{6,0},{7,1},{8,14},{9,15},{10,... | collective-permute-start | bytes 98312 | tf_op jit(solution)/shard_map/ppermute | solution.py:208
  40.7 0.5 collective-permute-start.13
  41.2 1.8 %collective-permute-done.11 = bf16[32,512]{1,0:T(8,128)(2,1)S(1)} collective-permute-done((bf16[32,512]{1,0:T(8,128)(2,1)S(1)}, bf16[32,512]{1,0:T(8,128)(2,1)S(1)}, u32[]{:S(2)}, u32[]{:S(2)}) %collective-permute-start.11) | collective-permute-done | bytes 32800 | tf_op jit(solution)/shard_map/ppermute | solution.py:208
  43.0 4.1 %collective-permute-start.21 = (bf16[528,512]{1,0:T(8,128)(2,1)S(1)}, bf16[528,512]{1,0:T(8,128)(2,1)S(1)}, u32[]{:S(2)}, u32[]{:S(2)}) collective-permute-start(bf16[528,512]{1,0:T(8,128)(2,1)S(1)} %collective-permute-done.12), channel_id=1, source_target_pairs={{0,1},{1,0},{2,3},{3,2},{4,5},{5,4},{6,7},{7,6},{8,9},{9,8},{10,11... | collective-permute-start | bytes 1622024 | tf_op jit(solution)/shard_map/ppermute | solution.py:292
  47.1 0.1 constant_dynamic-update-slice_fusion.13
  47.2 1.6 %collective-permute-start.17 = (bf16[32,512]{1,0:T(8,128)(2,1)S(1)}, bf16[32,512]{1,0:T(8,128)(2,1)S(1)}, u32[]{:S(2)}, u32[]{:S(2)}) collective-permute-start(bf16[32,512]{1,0:T(8,128)(2,1)S(1)} %get-tuple-element.100), channel_id=1, source_target_pairs={{0,6},{1,7},{2,4},{3,5},{4,2},{5,3},{6,0},{7,1},{8,14},{9,15},{10,... | collective-permute-start | bytes 98312 | tf_op jit(solution)/shard_map/ppermute | solution.py:208
  48.7 2.9 %collective-permute-start.15 = (bf16[32,512]{1,0:T(8,128)(2,1)S(1)}, bf16[32,512]{1,0:T(8,128)(2,1)S(1)}, u32[]{:S(2)}, u32[]{:S(2)}) collective-permute-start(bf16[32,512]{1,0:T(8,128)(2,1)S(1)} %get-tuple-element.100), channel_id=1, source_target_pairs={{0,4},{1,5},{2,6},{3,7},{4,0},{5,1},{6,2},{7,3},{8,12},{9,13},{10,... | collective-permute-start | bytes 98312 | tf_op jit(solution)/shard_map/ppermute | solution.py:208
  51.6 1.4 %collective-permute-done.17 = bf16[32,512]{1,0:T(8,128)(2,1)S(1)} collective-permute-done((bf16[32,512]{1,0:T(8,128)(2,1)S(1)}, bf16[32,512]{1,0:T(8,128)(2,1)S(1)}, u32[]{:S(2)}, u32[]{:S(2)}) %collective-permute-start.17) | collective-permute-done | bytes 32800 | tf_op jit(solution)/shard_map/ppermute | solution.py:208
  53.0 0.5 collective-permute-done.15
  53.6 1.2 %collective-permute-start.20 = (bf16[128,512]{1,0:T(8,128)(2,1)S(1)}, bf16[128,512]{1,0:T(8,128)(2,1)S(1)}, u32[]{:S(2)}, u32[]{:S(2)}) collective-permute-start(bf16[128,512]{1,0:T(8,128)(2,1)S(1)} %pad_maximum_fusion.1), channel_id=1, source_target_pairs={{0,17},{1,16},{2,19},{3,18},{4,21},{5,20},{6,23},{7,22},{8,25},{9,... | collective-permute-start | bytes 393224 | tf_op jit(solution)/shard_map/ppermute | solution.py:208
  54.8 0.7 collective-permute-start.19
  55.5 1.6 %collective-permute-start.18 = (bf16[128,512]{1,0:T(8,128)(2,1)S(1)}, bf16[128,512]{1,0:T(8,128)(2,1)S(1)}, u32[]{:S(2)}, u32[]{:S(2)}) collective-permute-start(bf16[128,512]{1,0:T(8,128)(2,1)S(1)} %pad_maximum_fusion.1), channel_id=1, source_target_pairs={{0,1},{1,0},{2,3},{3,2},{4,5},{5,4},{6,7},{7,6},{8,9},{9,8},{10,11... | collective-permute-start | bytes 393224 | tf_op jit(solution)/shard_map/ppermute | solution.py:208
  57.1 5.9 %collective-permute-done.20 = bf16[128,512]{1,0:T(8,128)(2,1)S(1)} collective-permute-done((bf16[128,512]{1,0:T(8,128)(2,1)S(1)}, bf16[128,512]{1,0:T(8,128)(2,1)S(1)}, u32[]{:S(2)}, u32[]{:S(2)}) %collective-permute-start.20) | collective-permute-done | bytes 131104 | tf_op jit(solution)/shard_map/ppermute | solution.py:208
  63.0 1.7 %collective-permute-done.18 = bf16[128,512]{1,0:T(8,128)(2,1)S(1)} collective-permute-done((bf16[128,512]{1,0:T(8,128)(2,1)S(1)}, bf16[128,512]{1,0:T(8,128)(2,1)S(1)}, u32[]{:S(2)}, u32[]{:S(2)}) %collective-permute-start.18) | collective-permute-done | bytes 131104 | tf_op jit(solution)/shard_map/ppermute | solution.py:208
  64.7 0.1 collective-permute-start.22
  64.8 1.9 %collective-permute-done.22.hi_ref = bf16[512,512]{1,0:T(8,128)(2,1)S(1)} collective-permute-done((bf16[512,512]{1,0:T(8,128)(2,1)S(1)}, bf16[512,512]{1,0:T(8,128)(2,1)S(1)}, u32[]{:S(2)}, u32[]{:S(2)}) %collective-permute-start.22) | collective-permute-done | bytes 524320 | tf_op jit(solution)/shard_map/ppermute | solution.py:208
  66.7 2.6 %shard_map.143 = (bf16[512,512]{1,0:T(8,128)(2,1)S(1)}, bf16[512,512]{1,0:T(8,128)(2,1)S(1)}, bf16[512,512]{1,0:T(8,128)(2,1)S(1)}, bf16[512,512]{1,0:T(8,128)(2,1)S(1)}, bf16[512,512]{1,0:T(8,128)(2,1)S(1)}) custom-call(s32[32]{0:T(128)S(1)} %broadcast_xor_fusion.nat_ref, s32[2,1]{1,0:T(2,128)S(1)} %copy.16.live_ref, s32[2,4]{1,0:T(2,128)S(1)} %copy-done.9, ...), custom_call_target="tpu_custom_call" | custom-call | flops 1342177280 | bytes 5275816 | tf_op jit(solution)/shard_map/pallas_call | solution.py:174
  69.4 0.2 collective-permute-start.23
  69.6 1.8 %collective-permute-done.23 = bf16[512,512]{1,0:T(8,128)(2,1)S(1)} collective-permute-done((bf16[512,512]{1,0:T(8,128)(2,1)S(1)}, bf16[512,512]{1,0:T(8,128)(2,1)S(1)}, u32[]{:S(2)}, u32[]{:S(2)}) %collective-permute-start.23) | collective-permute-done | bytes 524320 | tf_op jit(solution)/shard_map/ppermute | solution.py:208
  71.3 0.1 add_convert_fusion
  71.5 2.2 %collective-permute-start.26 = (bf16[128,512]{1,0:T(8,128)(2,1)S(1)}, bf16[128,512]{1,0:T(8,128)(2,1)S(1)}, u32[]{:S(2)}, u32[]{:S(2)}) collective-permute-start(bf16[128,512]{1,0:T(8,128)(2,1)S(1)} %get-tuple-element.105), channel_id=1, source_target_pairs={{0,17},{1,16},{2,19},{3,18},{4,21},{5,20},{6,23},{7,22},{8,25},{9,... | collective-permute-start | bytes 393224 | tf_op jit(solution)/shard_map/ppermute | solution.py:208
  73.7 1.1 %collective-permute-start.25 = (bf16[128,512]{1,0:T(8,128)(2,1)S(1)}, bf16[128,512]{1,0:T(8,128)(2,1)S(1)}, u32[]{:S(2)}, u32[]{:S(2)}) collective-permute-start(bf16[128,512]{1,0:T(8,128)(2,1)S(1)} %get-tuple-element.106), channel_id=1, source_target_pairs={{0,16},{1,17},{2,18},{3,19},{4,20},{5,21},{6,22},{7,23},{8,24},{9,... | collective-permute-start | bytes 393224 | tf_op jit(solution)/shard_map/ppermute | solution.py:208
  74.7 0.3 collective-permute-start.24
  75.0 1.7 %shard_map.145 = f32[512,512]{1,0:T(8,128)} custom-call(bf16[512,512]{1,0:T(8,128)(2,1)S(1)} %get-tuple-element.93.w_ref, bf16[512,512]{1,0:T(8,128)(2,1)S(1)} %get-tuple-element.94.u_ref, bf16[528,512]{1,0:T(8,128)(2,1)S(1)} %collective-permute-done.21.rest_0_.refs_0_), custom_call_target="tpu_custom_call" | custom-call | flops 268435456 | bytes 2637824 | tf_op jit(solution)/shard_map/pallas_call | solution.py:174
  76.7 2.9 %shard_map.144 = f32[512,512]{1,0:T(8,128)} custom-call(s32[32]{0:T(128)S(1)} %broadcast_xor_fusion.nat_ref, s32[2,4]{1,0:T(2,128)S(1)} %copy-done.9, bf16[512,512]{1,0:T(8,128)(2,1)S(1)} %constant_dynamic-update-slice_fusion.7.lo_ref, bf16[512,512]{1,0:T(8,128)(2,1)S(1)} %collective-permute-done.22.hi_ref, bf16[512,512]{1,0:T(8,128)(2,1)S(1)} %get-tuple-element.86.gu_ref, ...), custom_call_target="tpu_custom_call" | custom-call | flops 1073741824 | bytes 3676320 | tf_op jit(solution)/shard_map/pallas_call | solution.py:174
  79.7 1.1 %collective-permute-done.25 = bf16[128,512]{1,0:T(8,128)(2,1)S(1)} collective-permute-done((bf16[128,512]{1,0:T(8,128)(2,1)S(1)}, bf16[128,512]{1,0:T(8,128)(2,1)S(1)}, u32[]{:S(2)}, u32[]{:S(2)}) %collective-permute-start.25) | collective-permute-done | bytes 131104 | tf_op jit(solution)/shard_map/ppermute | solution.py:208
  80.8 0.1 add_convert_fusion.10
  80.8 0.1 collective-permute-start.27
  80.9 0.8 collective-permute-start.29
  81.8 2.7 %collective-permute-start.28 = (bf16[32,512]{1,0:T(8,128)(2,1)S(1)}, bf16[32,512]{1,0:T(8,128)(2,1)S(1)}, u32[]{:S(2)}, u32[]{:S(2)}) collective-permute-start(bf16[32,512]{1,0:T(8,128)(2,1)S(1)} %get-tuple-element.114), channel_id=1, source_target_pairs={{0,2},{1,3},{2,0},{3,1},{4,6},{5,7},{6,4},{7,5},{8,10},{9,11},{10,... | collective-permute-start | bytes 98312 | tf_op jit(solution)/shard_map/ppermute | solution.py:208
  84.4 1.7 %collective-permute-done.27 = bf16[32,512]{1,0:T(8,128)(2,1)S(1)} collective-permute-done((bf16[32,512]{1,0:T(8,128)(2,1)S(1)}, bf16[32,512]{1,0:T(8,128)(2,1)S(1)}, u32[]{:S(2)}, u32[]{:S(2)}) %collective-permute-start.27) | collective-permute-done | bytes 32800 | tf_op jit(solution)/shard_map/ppermute | solution.py:208
  86.1 0.7 collective-permute-done.29
  86.8 0.7 divide_subtract_fusion
  (54 shorter events, 0.2 us)
Async XLA Ops:
  0.6 6.7 %copy-start.5 = (s32[2,4,128]{2,1,0:T(4,128)S(1)}, s32[2,4,128]{2,1,0:T(4,128)}, u32[]{:S(2)}) copy-start(s32[2,4,128]{2,1,0:T(4,128)} %neg_ref.1) | copy-start | bytes 12292
  0.6 6.7 %copy-start.6 = (s32[2,512]{1,0:T(2,128)S(1)}, s32[2,512]{1,0:T(2,128)}, u32[]{:S(2)}) copy-start(s32[2,512]{1,0:T(2,128)} %hrows_ref.5) | copy-start | bytes 12292
  0.7 6.7 %copy-start.7 = (f32[512]{0:T(512)S(1)}, f32[512]{0:T(512)}, u32[]{:S(2)}) copy-start(f32[512]{0:T(512)} %param.13) | copy-start | bytes 6148
  0.7 6.6 %copy-start.8 = (f32[512]{0:T(512)S(1)}, f32[512]{0:T(512)}, u32[]{:S(2)}) copy-start(f32[512]{0:T(512)} %param.15) | copy-start | bytes 6148
  1.5 5.8 %copy-start.4 = (s32[2,512]{1,0:T(2,128)S(1)}, s32[2,512]{1,0:T(2,128)}, u32[]{:S(2)}) copy-start(s32[2,512]{1,0:T(2,128)} %trows_ref.1) | copy-start | bytes 12292
  1.5 9.0 %collective-permute-start.2 = (bf16[32,512]{1,0:T(8,128)(2,1)S(1)}, bf16[32,512]{1,0:T(8,128)(2,1)S(1)}, u32[]{:S(2)}, u32[]{:S(2)}) collective-permute-start(bf16[32,512]{1,0:T(8,128)(2,1)S(1)} %get-tuple-element.103), channel_id=1, source_target_pairs={{0,6},{1,7},{2,4},{3,5},{4,2},{5,3},{6,0},{7,1},{8,14},{9,15},{10,... | collective-permute-start | bytes 98312 | tf_op jit(solution)/shard_map/ppermute | solution.py:208
  6.7 3.9 %collective-permute-start.1 = (bf16[32,512]{1,0:T(8,128)(2,1)S(1)}, bf16[32,512]{1,0:T(8,128)(2,1)S(1)}, u32[]{:S(2)}, u32[]{:S(2)}) collective-permute-start(bf16[32,512]{1,0:T(8,128)(2,1)S(1)} %get-tuple-element.103), channel_id=1, source_target_pairs={{0,2},{1,3},{2,0},{3,1},{4,6},{5,7},{6,4},{7,5},{8,10},{9,11},{10,... | collective-permute-start | bytes 98312 | tf_op jit(solution)/shard_map/ppermute | solution.py:208
  6.7 4.9 %collective-permute-start = (bf16[32,512]{1,0:T(8,128)(2,1)S(1)}, bf16[32,512]{1,0:T(8,128)(2,1)S(1)}, u32[]{:S(2)}, u32[]{:S(2)}) collective-permute-start(bf16[32,512]{1,0:T(8,128)(2,1)S(1)} %get-tuple-element.103), channel_id=1, source_target_pairs={{0,4},{1,5},{2,6},{3,7},{4,0},{5,1},{6,2},{7,3},{8,12},{9,13},{10,... | collective-permute-start | bytes 98312 | tf_op jit(solution)/shard_map/ppermute | solution.py:208
  7.3 1.2 %copy-start = (f32[512,512]{1,0:T(8,128)S(1)}, f32[512,512]{1,0:T(8,128)}, u32[]{:S(2)}) copy-start(f32[512,512]{1,0:T(8,128)} %table_ref.3) | copy-start | bytes 3145732
  8.5 1.2 %copy-start.2 = (f32[512,512]{1,0:T(8,128)S(1)}, f32[512,512]{1,0:T(8,128)}, u32[]{:S(2)}) copy-start(f32[512,512]{1,0:T(8,128)} %table_ref.2) | copy-start | bytes 3145732
  11.6 7.2 %collective-permute-start.5 = (bf16[128,512]{1,0:T(8,128)(2,1)S(1)}, bf16[128,512]{1,0:T(8,128)(2,1)S(1)}, u32[]{:S(2)}, u32[]{:S(2)}) collective-permute-start(bf16[128,512]{1,0:T(8,128)(2,1)S(1)} %pad_maximum_fusion), channel_id=1, source_target_pairs={{0,17},{1,16},{2,19},{3,18},{4,21},{5,20},{6,23},{7,22},{8,25},{9,... | collective-permute-start | bytes 393224 | tf_op jit(solution)/shard_map/ppermute | solution.py:208
  14.1 5.6 %collective-permute-start.4 = (bf16[128,512]{1,0:T(8,128)(2,1)S(1)}, bf16[128,512]{1,0:T(8,128)(2,1)S(1)}, u32[]{:S(2)}, u32[]{:S(2)}) collective-permute-start(bf16[128,512]{1,0:T(8,128)(2,1)S(1)} %pad_maximum_fusion), channel_id=1, source_target_pairs={{0,16},{1,17},{2,18},{3,19},{4,20},{5,21},{6,22},{7,23},{8,24},{9,... | collective-permute-start | bytes 393224 | tf_op jit(solution)/shard_map/ppermute | solution.py:208
  14.6 5.1 %collective-permute-start.3 = (bf16[128,512]{1,0:T(8,128)(2,1)S(1)}, bf16[128,512]{1,0:T(8,128)(2,1)S(1)}, u32[]{:S(2)}, u32[]{:S(2)}) collective-permute-start(bf16[128,512]{1,0:T(8,128)(2,1)S(1)} %pad_maximum_fusion), channel_id=1, source_target_pairs={{0,1},{1,0},{2,3},{3,2},{4,5},{5,4},{6,7},{7,6},{8,9},{9,8},{10,11... | collective-permute-start | bytes 393224 | tf_op jit(solution)/shard_map/ppermute | solution.py:208
  19.8 2.0 %collective-permute-start.6 = (bf16[512,512]{1,0:T(8,128)(2,1)S(1)}, bf16[512,512]{1,0:T(8,128)(2,1)S(1)}, u32[]{:S(2)}, u32[]{:S(2)}) collective-permute-start(bf16[512,512]{1,0:T(8,128)(2,1)S(1)} %constant_dynamic-update-slice_fusion.lo_ref), channel_id=1, source_target_pairs={{0,8},{1,9},{2,10},{3,11},{4,12},{5,13},{6,14},{7,15},{8,0},{9,1},... | collective-permute-start | bytes 1572872 | tf_op jit(solution)/shard_map/ppermute | solution.py:208
  19.9 0.7 copy-start.12
  20.6 0.7 copy-start.13
  21.3 0.7 copy-start.9
  21.3 3.9 %copy-start.1 = (f32[512,512]{1,0:T(8,128)S(1)}, f32[512,512]{1,0:T(8,128)}, u32[]{:S(2)}) copy-start(f32[512,512]{1,0:T(8,128)} %table_ref.3) | copy-start | bytes 3145732
  24.6 2.1 %collective-permute-start.7 = (bf16[512,512]{1,0:T(8,128)(2,1)S(1)}, bf16[512,512]{1,0:T(8,128)(2,1)S(1)}, u32[]{:S(2)}, u32[]{:S(2)}) collective-permute-start(bf16[512,512]{1,0:T(8,128)(2,1)S(1)} %get-tuple-element.65), channel_id=1, source_target_pairs={{0,8},{1,9},{2,10},{3,11},{4,12},{5,13},{6,14},{7,15},{8,0},{9,1},... | collective-permute-start | bytes 1572872 | tf_op jit(solution)/shard_map/ppermute | solution.py:208
  25.8 6.5 %copy-start.3 = (f32[512,512]{1,0:T(8,128)S(1)}, f32[512,512]{1,0:T(8,128)}, u32[]{:S(2)}) copy-start(f32[512,512]{1,0:T(8,128)} %table_ref.2) | copy-start | bytes 3145732
  25.8 15.4 %collective-permute-start.12 = (bf16[528,512]{1,0:T(8,128)(2,1)S(1)}, bf16[528,512]{1,0:T(8,128)(2,1)S(1)}, u32[]{:S(2)}, u32[]{:S(2)}) collective-permute-start(bf16[528,512]{1,0:T(8,128)(2,1)S(1)} %shard_map.142), channel_id=1, source_target_pairs={{0,0},{1,3},{2,2},{3,5},{4,4},{5,7},{6,6},{7,1},{8,8},{9,11},{10,1... | collective-permute-start | bytes 1622024 | tf_op jit(solution)/shard_map/ppermute | solution.py:291
  26.8 8.5 %collective-permute-start.10 = (bf16[128,512]{1,0:T(8,128)(2,1)S(1)}, bf16[128,512]{1,0:T(8,128)(2,1)S(1)}, u32[]{:S(2)}, u32[]{:S(2)}) collective-permute-start(bf16[128,512]{1,0:T(8,128)(2,1)S(1)} %get-tuple-element.108), channel_id=1, source_target_pairs={{0,17},{1,16},{2,19},{3,18},{4,21},{5,20},{6,23},{7,22},{8,25},{9,... | collective-permute-start | bytes 393224 | tf_op jit(solution)/shard_map/ppermute | solution.py:208
  31.4 6.2 %collective-permute-start.9 = (bf16[128,512]{1,0:T(8,128)(2,1)S(1)}, bf16[128,512]{1,0:T(8,128)(2,1)S(1)}, u32[]{:S(2)}, u32[]{:S(2)}) collective-permute-start(bf16[128,512]{1,0:T(8,128)(2,1)S(1)} %get-tuple-element.109), channel_id=1, source_target_pairs={{0,16},{1,17},{2,18},{3,19},{4,20},{5,21},{6,22},{7,23},{8,24},{9,... | collective-permute-start | bytes 393224 | tf_op jit(solution)/shard_map/ppermute | solution.py:208
  32.3 5.3 %collective-permute-start.8 = (bf16[128,512]{1,0:T(8,128)(2,1)S(1)}, bf16[128,512]{1,0:T(8,128)(2,1)S(1)}, u32[]{:S(2)}, u32[]{:S(2)}) collective-permute-start(bf16[128,512]{1,0:T(8,128)(2,1)S(1)} %get-tuple-element.110), channel_id=1, source_target_pairs={{0,1},{1,0},{2,3},{3,2},{4,5},{5,4},{6,7},{7,6},{8,9},{9,8},{10,11... | collective-permute-start | bytes 393224 | tf_op jit(solution)/shard_map/ppermute | solution.py:208
  37.6 9.5 %copy-start.10 = (f32[32,512]{1,0:T(8,128)S(1)}, f32[32,512]{1,0:T(8,128)}, u32[]{:S(2)}) copy-start(f32[32,512]{1,0:T(8,128)} %param.16) | copy-start | bytes 196612
  37.6 9.5 %copy-start.11 = (f32[32,512]{1,0:T(8,128)S(1)}, f32[32,512]{1,0:T(8,128)}, u32[]{:S(2)}) copy-start(f32[32,512]{1,0:T(8,128)} %param.17) | copy-start | bytes 196612
  37.6 5.3 %collective-permute-start.11 = (bf16[32,512]{1,0:T(8,128)(2,1)S(1)}, bf16[32,512]{1,0:T(8,128)(2,1)S(1)}, u32[]{:S(2)}, u32[]{:S(2)}) collective-permute-start(bf16[32,512]{1,0:T(8,128)(2,1)S(1)} %get-tuple-element.115), channel_id=1, source_target_pairs={{0,4},{1,5},{2,6},{3,7},{4,0},{5,1},{6,2},{7,3},{8,12},{9,13},{10,... | collective-permute-start | bytes 98312 | tf_op jit(solution)/shard_map/ppermute | solution.py:208
  39.6 7.5 %collective-permute-start.14 = (bf16[32,512]{1,0:T(8,128)(2,1)S(1)}, bf16[32,512]{1,0:T(8,128)(2,1)S(1)}, u32[]{:S(2)}, u32[]{:S(2)}) collective-permute-start(bf16[32,512]{1,0:T(8,128)(2,1)S(1)} %get-tuple-element.116), channel_id=1, source_target_pairs={{0,6},{1,7},{2,4},{3,5},{4,2},{5,3},{6,0},{7,1},{8,14},{9,15},{10,... | collective-permute-start | bytes 98312 | tf_op jit(solution)/shard_map/ppermute | solution.py:208
  40.7 6.3 %collective-permute-start.13 = (bf16[32,512]{1,0:T(8,128)(2,1)S(1)}, bf16[32,512]{1,0:T(8,128)(2,1)S(1)}, u32[]{:S(2)}, u32[]{:S(2)}) collective-permute-start(bf16[32,512]{1,0:T(8,128)(2,1)S(1)} %get-tuple-element.117), channel_id=1, source_target_pairs={{0,2},{1,3},{2,0},{3,1},{4,6},{5,7},{6,4},{7,5},{8,10},{9,11},{10,... | collective-permute-start | bytes 98312 | tf_op jit(solution)/shard_map/ppermute | solution.py:208
  43.0 21.7 %collective-permute-start.21 = (bf16[528,512]{1,0:T(8,128)(2,1)S(1)}, bf16[528,512]{1,0:T(8,128)(2,1)S(1)}, u32[]{:S(2)}, u32[]{:S(2)}) collective-permute-start(bf16[528,512]{1,0:T(8,128)(2,1)S(1)} %collective-permute-done.12), channel_id=1, source_target_pairs={{0,1},{1,0},{2,3},{3,2},{4,5},{5,4},{6,7},{7,6},{8,9},{9,8},{10,11... | collective-permute-start | bytes 1622024 | tf_op jit(solution)/shard_map/ppermute | solution.py:292
  47.2 5.8 %collective-permute-start.17 = (bf16[32,512]{1,0:T(8,128)(2,1)S(1)}, bf16[32,512]{1,0:T(8,128)(2,1)S(1)}, u32[]{:S(2)}, u32[]{:S(2)}) collective-permute-start(bf16[32,512]{1,0:T(8,128)(2,1)S(1)} %get-tuple-element.100), channel_id=1, source_target_pairs={{0,6},{1,7},{2,4},{3,5},{4,2},{5,3},{6,0},{7,1},{8,14},{9,15},{10,... | collective-permute-start | bytes 98312 | tf_op jit(solution)/shard_map/ppermute | solution.py:208
  48.7 4.3 %collective-permute-start.16 = (bf16[32,512]{1,0:T(8,128)(2,1)S(1)}, bf16[32,512]{1,0:T(8,128)(2,1)S(1)}, u32[]{:S(2)}, u32[]{:S(2)}) collective-permute-start(bf16[32,512]{1,0:T(8,128)(2,1)S(1)} %get-tuple-element.100), channel_id=1, source_target_pairs={{0,2},{1,3},{2,0},{3,1},{4,6},{5,7},{6,4},{7,5},{8,10},{9,11},{10,... | collective-permute-start | bytes 98312 | tf_op jit(solution)/shard_map/ppermute | solution.py:208
  48.7 4.8 %collective-permute-start.15 = (bf16[32,512]{1,0:T(8,128)(2,1)S(1)}, bf16[32,512]{1,0:T(8,128)(2,1)S(1)}, u32[]{:S(2)}, u32[]{:S(2)}) collective-permute-start(bf16[32,512]{1,0:T(8,128)(2,1)S(1)} %get-tuple-element.100), channel_id=1, source_target_pairs={{0,4},{1,5},{2,6},{3,7},{4,0},{5,1},{6,2},{7,3},{8,12},{9,13},{10,... | collective-permute-start | bytes 98312 | tf_op jit(solution)/shard_map/ppermute | solution.py:208
  53.6 9.4 %collective-permute-start.20 = (bf16[128,512]{1,0:T(8,128)(2,1)S(1)}, bf16[128,512]{1,0:T(8,128)(2,1)S(1)}, u32[]{:S(2)}, u32[]{:S(2)}) collective-permute-start(bf16[128,512]{1,0:T(8,128)(2,1)S(1)} %pad_maximum_fusion.1), channel_id=1, source_target_pairs={{0,17},{1,16},{2,19},{3,18},{4,21},{5,20},{6,23},{7,22},{8,25},{9,... | collective-permute-start | bytes 393224 | tf_op jit(solution)/shard_map/ppermute | solution.py:208
  54.8 8.2 %collective-permute-start.19 = (bf16[128,512]{1,0:T(8,128)(2,1)S(1)}, bf16[128,512]{1,0:T(8,128)(2,1)S(1)}, u32[]{:S(2)}, u32[]{:S(2)}) collective-permute-start(bf16[128,512]{1,0:T(8,128)(2,1)S(1)} %pad_maximum_fusion.1), channel_id=1, source_target_pairs={{0,16},{1,17},{2,18},{3,19},{4,20},{5,21},{6,22},{7,23},{8,24},{9,... | collective-permute-start | bytes 393224 | tf_op jit(solution)/shard_map/ppermute | solution.py:208
  55.5 9.2 %collective-permute-start.18 = (bf16[128,512]{1,0:T(8,128)(2,1)S(1)}, bf16[128,512]{1,0:T(8,128)(2,1)S(1)}, u32[]{:S(2)}, u32[]{:S(2)}) collective-permute-start(bf16[128,512]{1,0:T(8,128)(2,1)S(1)} %pad_maximum_fusion.1), channel_id=1, source_target_pairs={{0,1},{1,0},{2,3},{3,2},{4,5},{5,4},{6,7},{7,6},{8,9},{9,8},{10,11... | collective-permute-start | bytes 393224 | tf_op jit(solution)/shard_map/ppermute | solution.py:208
  64.7 2.0 %collective-permute-start.22 = (bf16[512,512]{1,0:T(8,128)(2,1)S(1)}, bf16[512,512]{1,0:T(8,128)(2,1)S(1)}, u32[]{:S(2)}, u32[]{:S(2)}) collective-permute-start(bf16[512,512]{1,0:T(8,128)(2,1)S(1)} %constant_dynamic-update-slice_fusion.7.lo_ref), channel_id=1, source_target_pairs={{0,8},{1,9},{2,10},{3,11},{4,12},{5,13},{6,14},{7,15},{8,0},{9,1},... | collective-permute-start | bytes 1572872 | tf_op jit(solution)/shard_map/ppermute | solution.py:208
  69.4 2.0 %collective-permute-start.23 = (bf16[512,512]{1,0:T(8,128)(2,1)S(1)}, bf16[512,512]{1,0:T(8,128)(2,1)S(1)}, u32[]{:S(2)}, u32[]{:S(2)}) collective-permute-start(bf16[512,512]{1,0:T(8,128)(2,1)S(1)} %get-tuple-element.85), channel_id=1, source_target_pairs={{0,8},{1,9},{2,10},{3,11},{4,12},{5,13},{6,14},{7,15},{8,0},{9,1},... | collective-permute-start | bytes 1572872 | tf_op jit(solution)/shard_map/ppermute | solution.py:208
  71.5 8.2 %collective-permute-start.26 = (bf16[128,512]{1,0:T(8,128)(2,1)S(1)}, bf16[128,512]{1,0:T(8,128)(2,1)S(1)}, u32[]{:S(2)}, u32[]{:S(2)}) collective-permute-start(bf16[128,512]{1,0:T(8,128)(2,1)S(1)} %get-tuple-element.105), channel_id=1, source_target_pairs={{0,17},{1,16},{2,19},{3,18},{4,21},{5,20},{6,23},{7,22},{8,25},{9,... | collective-permute-start | bytes 393224 | tf_op jit(solution)/shard_map/ppermute | solution.py:208
  73.7 7.1 %collective-permute-start.25 = (bf16[128,512]{1,0:T(8,128)(2,1)S(1)}, bf16[128,512]{1,0:T(8,128)(2,1)S(1)}, u32[]{:S(2)}, u32[]{:S(2)}) collective-permute-start(bf16[128,512]{1,0:T(8,128)(2,1)S(1)} %get-tuple-element.106), channel_id=1, source_target_pairs={{0,16},{1,17},{2,18},{3,19},{4,20},{5,21},{6,22},{7,23},{8,24},{9,... | collective-permute-start | bytes 393224 | tf_op jit(solution)/shard_map/ppermute | solution.py:208
  74.7 6.1 %collective-permute-start.24 = (bf16[128,512]{1,0:T(8,128)(2,1)S(1)}, bf16[128,512]{1,0:T(8,128)(2,1)S(1)}, u32[]{:S(2)}, u32[]{:S(2)}) collective-permute-start(bf16[128,512]{1,0:T(8,128)(2,1)S(1)} %get-tuple-element.107), channel_id=1, source_target_pairs={{0,1},{1,0},{2,3},{3,2},{4,5},{5,4},{6,7},{7,6},{8,9},{9,8},{10,11... | collective-permute-start | bytes 393224 | tf_op jit(solution)/shard_map/ppermute | solution.py:208
  80.8 5.2 %collective-permute-start.27 = (bf16[32,512]{1,0:T(8,128)(2,1)S(1)}, bf16[32,512]{1,0:T(8,128)(2,1)S(1)}, u32[]{:S(2)}, u32[]{:S(2)}) collective-permute-start(bf16[32,512]{1,0:T(8,128)(2,1)S(1)} %get-tuple-element.112), channel_id=1, source_target_pairs={{0,4},{1,5},{2,6},{3,7},{4,0},{5,1},{6,2},{7,3},{8,12},{9,13},{10,... | collective-permute-start | bytes 98312 | tf_op jit(solution)/shard_map/ppermute | solution.py:208
  80.9 5.9 %collective-permute-start.29 = (bf16[32,512]{1,0:T(8,128)(2,1)S(1)}, bf16[32,512]{1,0:T(8,128)(2,1)S(1)}, u32[]{:S(2)}, u32[]{:S(2)}) collective-permute-start(bf16[32,512]{1,0:T(8,128)(2,1)S(1)} %get-tuple-element.113), channel_id=1, source_target_pairs={{0,6},{1,7},{2,4},{3,5},{4,2},{5,3},{6,0},{7,1},{8,14},{9,15},{10,... | collective-permute-start | bytes 98312 | tf_op jit(solution)/shard_map/ppermute | solution.py:208
  81.8 5.0 %collective-permute-start.28 = (bf16[32,512]{1,0:T(8,128)(2,1)S(1)}, bf16[32,512]{1,0:T(8,128)(2,1)S(1)}, u32[]{:S(2)}, u32[]{:S(2)}) collective-permute-start(bf16[32,512]{1,0:T(8,128)(2,1)S(1)} %get-tuple-element.114), channel_id=1, source_target_pairs={{0,2},{1,3},{2,0},{3,1},{4,6},{5,7},{6,4},{7,5},{8,10},{9,11},{10,... | collective-permute-start | bytes 98312 | tf_op jit(solution)/shard_map/ppermute | solution.py:208

commit v6 on v5

--- a/solution.py
+++ b/solution.py
@@ -79,9 +79,9 @@
 
 
 def score_kernel(
-    k, own, nneg, nat_ref, live_ref, rel_ref, lo_ref, hi_ref, h_ref, tcol_ref, cnt_ref, *rest
+    k, own, nneg, nat_ref, live_ref, rel_ref, lo_ref, hi_ref, h_ref, t_ref, tcol_ref, cnt_ref,
+    keep_ref, send_ref, w_ref, u_ref, gu_ref, rel_s, grad_s,
 ):
-    tail_refs, (keep_ref, send_ref, w_ref, u_ref, gu_ref, rel_s, grad_s) = rest[:-7], rest[-7:]
     edges, width = h_ref.shape
     blocks, rows = cnt_ref.shape[1:]
     size = edges // blocks
@@ -92,7 +92,7 @@
         part = slice(b * size, (b + 1) * size)
         chosen = rel_s[pl.ds(pl.multiple_of(rel_ref[k, b] * width, width), width)]
         u_ref[part] = dot(h_ref[part], chosen, COLS, ROWS).astype(BF16)
-    tails = jnp.concatenate([ref[...] for ref in tail_refs])[0:rows]
+    tails = t_ref[0:rows]
     score = dot(u_ref[...], tails, COLS, COLS)
     row_id = lax.broadcasted_iota(jnp.int32, (size, rows), 1).astype(F32)
     for b in range(blocks):
@@ -122,28 +122,24 @@
             ref[j * own : (j + 1) * own] = grad_s[rows_of].astype(BF16)
 
 
-def tail_kernel(w_ref, u_ref, table_ref, state_ref, *out_refs):
+def tail_kernel(w_ref, u_ref, table_ref, state_ref, out_ref):
     rows, width = table_ref.shape
     gradient = dot(w_ref[...], u_ref[...], ROWS, ROWS)
     table, state = adagrad_rows(table_ref[...], state_ref[...], gradient)
+    out_ref[0:rows] = table.astype(BF16)
     state_row = state.T[0:1, :]
     high = state_row.astype(BF16).astype(F32)
     row_id = lax.broadcasted_iota(jnp.int32, (PACK_ROWS, width), 0)
     packed = jnp.where(row_id == 0, high, jnp.where(row_id == 1, state_row - high, 0.0))
-    packed = jnp.concatenate([table, packed]).astype(BF16)
-    start = 0
-    for ref in out_refs:
-        ref[...] = packed[start : start + ref.shape[0]]
-        start += ref.shape[0]
-
-
-def last_tail_kernel(w_ref, u_ref, *refs):
-    tail_refs, out_ref = refs[:-1], refs[-1]
+    out_ref[rows : rows + PACK_ROWS] = packed.astype(BF16)
+
+
+def last_tail_kernel(w_ref, u_ref, packed_ref, out_ref):
     rows = out_ref.shape[0]
     gradient = dot(w_ref[...], u_ref[...], ROWS, ROWS)
-    packed = jnp.concatenate([ref[...] for ref in tail_refs]).astype(F32)
-    state_row = packed[rows : rows + 1] + packed[rows + 1 : rows + 2]
-    out_ref[...] = adagrad_rows(packed[0:rows], state_row, gradient)[0]
+    packed = packed_ref[rows : rows + PACK_ROWS].astype(F32)
+    state_row = packed[0:1, :] + packed[1:2, :]
+    out_ref[...] = adagrad_rows(packed_ref[0:rows].astype(F32), state_row, gradient)[0]
 
 
 def head_kernel(
@@ -263,21 +259,7 @@
 
     head_state = head_state.reshape(1, -1)
     tail_state = tail_state.reshape(1, -1)
-    prepared = call(
-        prepare_kernel,
-        [
-            ((edges, width), BF16),
-            ((rows, width), BF16),
-            ((2, edges, 128), F32),
-            ((2, blocks, rows), F32),
-            (head_state.shape, F32),
-            (tail_state.shape, F32),
-        ],
-        0, [], square,
-        head_table, tail_table, head_rows, tail_rows, negatives, head_state, tail_state,
-    )
-    held = {"prepared": prepared}
-    rotated = []
+    held = {"indices": [head_rows, tail_rows, negatives]}
 
     def with_(name):
         def hook(got):
@@ -286,31 +268,33 @@
 
         return hook
 
-    def rotate(x, step):
-        if step == 0:
-            return lax.ppermute(x, "tail", [(i, (i + i % 2 * 2) % tails) for i in range(tails)])
+    def rotate(x):
+        x = lax.ppermute(x, "tail", [(i, (i + i % 2 * 2) % tails) for i in range(tails)])
         return lax.ppermute(x, "tail", [(i, i ^ 1) for i in range(tails)])
 
-    def rotation(start, wait):
-        def hook(got):
-            if start is not None:
-                got[0], part = lax.optimization_barrier((got[0], step0[start]))
-                moved = rotate(part, 1)
-            if wait is not None:
-                got, rotated[wait] = lax.optimization_barrier((got, rotated[wait]))
-            if start is not None:
-                rotated.append(moved)
-            return got
-
-        return hook
-
-    gather_hooks = {1: with_("prepared")}
+    def prepare(got):
+        held["prepared"] = call(
+            prepare_kernel,
+            [
+                ((edges, width), BF16),
+                ((rows, width), BF16),
+                ((2, edges, 128), F32),
+                ((2, blocks, rows), F32),
+                (head_state.shape, F32),
+                (tail_state.shape, F32),
+            ],
+            0, [], square,
+            head_table, tail_table, *held["indices"], head_state, tail_state,
+        )
+        return with_("prepared")(got)
+
+    gather_hooks = {2: with_("indices"), 1: prepare}
     for k in range(2):
         lo, hi = exchange.all_gather(relations.astype(BF16), gather_hooks)
         if k == 0:
-            head_vecs, *tail_vecs, tail_col, counts, head_state, tail_state = held["prepared"]
+            head_vecs, tail_vecs, tail_col, counts, head_state, tail_state = held["prepared"]
         else:
-            tail_vecs = rotated
+            tail_vecs = held["tail"]
         keep, send, weights, projected, edge_grad = call(
             functools.partial(score_kernel, k, own, float(nneg)),
             [
@@ -321,39 +305,38 @@
                 ((edges, width), BF16),
             ],
             3, [pltpu.VMEM((all_rows, width), BF16), pltpu.VMEM((all_rows, width), F32)], 5 * square,
-            nat, block_counts, relation_ids, lo, hi, head_vecs, tail_col, counts, *tail_vecs,
+            nat, block_counts, relation_ids, lo, hi, head_vecs, tail_vecs, tail_col, counts,
         )
         head_outs = [(head_table.shape, F32)]
         if k == 0:
-            tail_new = call(
-                tail_kernel, [((n, width), BF16) for n in [rows + PACK_ROWS]], 0, [], square,
+            (tail_new,) = call(
+                tail_kernel, [((rows + PACK_ROWS, width), BF16)], 0, [], square,
                 weights, projected, tail_table, tail_state,
             )
             head_outs += [(head_state.shape, F32), ((edges, width), BF16)]
         else:
-            tail_new = call(
+            (tail_new,) = call(
                 last_tail_kernel, [((rows, width), F32)], 0, [], square,
-                weights, projected, *tail_vecs,
+                weights, projected, tail_vecs,
             )
         head_new = call(
             functools.partial(head_kernel, k, own, blocks), head_outs,
             2, [pltpu.VMEM((all_rows, width), BF16)], 4 * square,
             nat, relation_ids, lo, hi, edge_grad, head_rows, head_table, head_state,
         )
-        held.update(tail=tail_new, head=list(head_new))
+        held["head"] = head_new
         if k == 0:
-            step0 = [rotate(x, 0) for x in tail_new]
-            hooks = {1: with_("head"), 2: rotation(0, None)}
+            held["tail"] = rotate(tail_new)
+            grad = exchange.reduce_scatter(keep, send, {1: with_("head")})
+            head_table, head_state, head_vecs = held["head"]
+            gather_hooks = {1: with_("tail")}
         else:
+            held["tail"] = tail_new
             first, second = with_("tail"), with_("head")
-            hooks = {1: lambda got: first(second(got))}
-        grad = exchange.reduce_scatter(keep, send, hooks)
-        if k == 0:
-            head_table, head_state, head_vecs = held["head"]
-            gather_hooks = {1: rotation(None, 0)}
+            grad = exchange.reduce_scatter(keep, send, {1: lambda got: second(first(got))})
         relation_state = relation_state + grad * grad
         relations = relations - RATE_RELATIONS * grad / (jnp.sqrt(relation_state) + EPSILON)
-    return (held["head"][0], held["tail"][0], relations)
+    return (held["head"][0], held["tail"], relations)
 
 
 def solution(mesh):

time: 87.8 us -> 86.4 us (0.984)
  waiting for transfers between devices: 27.6 us -> 25.2 us
    ppermute x28, waiting for transfers between devices: 27.6 us -> 25.2 us  [swap(): return lax.ppermute(x, AXES, [(i, i ^ mask) for i in range(self.devices)])]
  transfers between devices with their start and end apart: 30 -> 30, of which waited for: 17 -> 17; matrix products, arithmetic and copies ran while one was open for 0% -> 0% of each run, Pallas kernels for 9% -> 10%
where the time goes in v6:
time: 86.4 us; the launch traced here: 86.1 us
  starting transfers between devices  39.5 us (46%)
  waiting for transfers between devices  25.2 us (29%)
  Pallas kernels  13.6 us (16%)
  local copies, waits for them, and re-layouts  4.85 us (6%)
  other arithmetic  2.07 us (2%)
    ppermute x28, starting transfers between devices, swap(): return lax.ppermute(x, AXES, [(i, i ^ mask) for i in range(self.devices)])  34.5 us
    ppermute x28, waiting for transfers between devices, swap(): return lax.ppermute(x, AXES, [(i, i ^ mask) for i in range(self.devices)])  25.2 us
    pallas_call x7, Pallas kernels, call(): pl.pallas_call(kernel, out_shape=outs, in_specs=[SMEM] * smem + [VMEM] *...  13.6 us
    unnamed x39, local copies, waits for them, and re-layouts  4.83 us
    ppermute x1, starting transfers between devices, rotate(): return lax.ppermute(x, 'tail', [(i, i ^ 1) for i in range(tails)])  4.18 us
  transfers between devices with their start and end apart: 30, of which 17 were waited for; matrix products, arithmetic and copies ran while one was open for 0% of the time, Pallas kernels for 10%

profile of v6, /device:TPU:0, one launch (start us, length us, event | category | flops | bytes accessed | tf_op | source)
XLA Modules:
  0.0 86.1 jit_solution(5543918015079643987)
XLA Ops:
  0.6 0.8 constant_dynamic-update-slice_fusion.6
  1.5 5.0 %collective-permute-start.2 = (bf16[32,512]{1,0:T(8,128)(2,1)S(1)}, bf16[32,512]{1,0:T(8,128)(2,1)S(1)}, u32[]{:S(2)}, u32[]{:S(2)}) collective-permute-start(bf16[32,512]{1,0:T(8,128)(2,1)S(1)} %get-tuple-element.111), channel_id=1, source_target_pairs={{0,6},{1,7},{2,4},{3,5},{4,2},{5,3},{6,0},{7,1},{8,14},{9,15},{10,... | collective-permute-start | bytes 98312 | tf_op jit(solution)/shard_map/ppermute | solution.py:204
  6.5 0.6 collective-permute-start
  7.2 1.3 %collective-permute-done.2 = bf16[32,512]{1,0:T(8,128)(2,1)S(1)} collective-permute-done((bf16[32,512]{1,0:T(8,128)(2,1)S(1)}, bf16[32,512]{1,0:T(8,128)(2,1)S(1)}, u32[]{:S(2)}, u32[]{:S(2)}) %collective-permute-start.2) | collective-permute-done | bytes 32800 | tf_op jit(solution)/shard_map/ppermute | solution.py:204
  8.4 2.0 %collective-permute-done.1 = bf16[32,512]{1,0:T(8,128)(2,1)S(1)} collective-permute-done((bf16[32,512]{1,0:T(8,128)(2,1)S(1)}, bf16[32,512]{1,0:T(8,128)(2,1)S(1)}, u32[]{:S(2)}, u32[]{:S(2)}) %collective-permute-start.1) | collective-permute-done | bytes 32800 | tf_op jit(solution)/shard_map/ppermute | solution.py:204
  10.4 1.0 %collective-permute-done = bf16[32,512]{1,0:T(8,128)(2,1)S(1)} collective-permute-done((bf16[32,512]{1,0:T(8,128)(2,1)S(1)}, bf16[32,512]{1,0:T(8,128)(2,1)S(1)}, u32[]{:S(2)}, u32[]{:S(2)}) %collective-permute-start) | collective-permute-done | bytes 32800 | tf_op jit(solution)/shard_map/ppermute | solution.py:204
  11.5 2.5 %collective-permute-start.5 = (bf16[128,512]{1,0:T(8,128)(2,1)S(1)}, bf16[128,512]{1,0:T(8,128)(2,1)S(1)}, u32[]{:S(2)}, u32[]{:S(2)}) collective-permute-start(bf16[128,512]{1,0:T(8,128)(2,1)S(1)} %pad_maximum_fusion), channel_id=1, source_target_pairs={{0,17},{1,16},{2,19},{3,18},{4,21},{5,20},{6,23},{7,22},{8,25},{9,... | collective-permute-start | bytes 393224 | tf_op jit(solution)/shard_map/ppermute | solution.py:204
  14.0 0.5 collective-permute-start.4
  14.5 0.5 collective-permute-start.3
  15.1 0.6 copy-done.4
  15.8 1.2 %copy-done = f32[512,512]{1,0:T(8,128)S(1)} copy-done((f32[512,512]{1,0:T(8,128)S(1)}, f32[512,512]{1,0:T(8,128)}, u32[]{:S(2)}) %copy-start) | copy-done | bytes 1048600
  17.0 1.2 %copy-done.2 = f32[512,512]{1,0:T(8,128)S(1)} copy-done((f32[512,512]{1,0:T(8,128)S(1)}, f32[512,512]{1,0:T(8,128)}, u32[]{:S(2)}) %copy-start.2) | copy-done | bytes 1048600
  18.2 0.7 shard_map.139
  19.0 0.6 collective-permute-done.4
  19.6 0.1 collective-permute-start.6
  19.7 0.6 copy-done.12
  20.4 0.1 copy.16.live_ref
  20.5 0.7 copy-done.13
  21.1 0.5 collective-permute-done.6.hi_ref
  21.6 0.2 copy-done.9
  21.8 2.6 %shard_map.140 = (bf16[512,512]{1,0:T(8,128)(2,1)S(1)}, bf16[512,512]{1,0:T(8,128)(2,1)S(1)}, bf16[512,512]{1,0:T(8,128)(2,1)S(1)}, bf16[512,512]{1,0:T(8,128)(2,1)S(1)}, bf16[512,512]{1,0:T(8,128)(2,1)S(1)}) custom-call(s32[32]{0:T(128)S(1)} %broadcast_xor_fusion.nat_ref, s32[2,1]{1,0:T(2,128)S(1)} %copy.16.live_ref, s32[2,4]{1,0:T(2,128)S(1)} %copy-done.9, ...), custom_call_target="tpu_custom_call" | custom-call | flops 1342177280 | bytes 5259432 | tf_op jit(solution)/shard_map/pallas_call | solution.py:170
  24.5 0.5 collective-permute-start.7
  25.0 0.7 shard_map.142
  25.7 0.8 collective-permute-start.20
  26.5 0.1 add_convert_fusion.4
  26.7 5.0 %collective-permute-start.10 = (bf16[128,512]{1,0:T(8,128)(2,1)S(1)}, bf16[128,512]{1,0:T(8,128)(2,1)S(1)}, u32[]{:S(2)}, u32[]{:S(2)}) collective-permute-start(bf16[128,512]{1,0:T(8,128)(2,1)S(1)} %get-tuple-element.116), channel_id=1, source_target_pairs={{0,17},{1,16},{2,19},{3,18},{4,21},{5,20},{6,23},{7,22},{8,25},{9,... | collective-permute-start | bytes 393224 | tf_op jit(solution)/shard_map/ppermute | solution.py:204
  31.7 0.5 collective-permute-start.9
  32.2 0.1 collective-permute-start.8
  32.4 2.3 %shard_map.141 = (f32[512,512]{1,0:T(8,128)S(1)}, f32[1,512]{1,0:T(1,128)S(1)}, bf16[512,512]{1,0:T(8,128)(2,1)S(1)}) custom-call(s32[32]{0:T(128)S(1)} %broadcast_xor_fusion.nat_ref, s32[2,4]{1,0:T(2,128)S(1)} %copy-done.9, bf16[512,512]{1,0:T(8,128)(2,1)S(1)} %constant_dynamic-update-slice_fusion.lo_ref, ...), custom_call_target="tpu_custom_call" | custom-call | flops 1073741824 | bytes 4202656 | tf_op jit(solution)/shard_map/pallas_call | solution.py:170
  34.6 1.0 %collective-permute-done.10 = bf16[128,512]{1,0:T(8,128)(2,1)S(1)} collective-permute-done((bf16[128,512]{1,0:T(8,128)(2,1)S(1)}, bf16[128,512]{1,0:T(8,128)(2,1)S(1)}, u32[]{:S(2)}, u32[]{:S(2)}) %collective-permute-start.10) | collective-permute-done | bytes 131104 | tf_op jit(solution)/shard_map/ppermute | solution.py:204
  35.6 2.3 %collective-permute-done.9 = bf16[128,512]{1,0:T(8,128)(2,1)S(1)} collective-permute-done((bf16[128,512]{1,0:T(8,128)(2,1)S(1)}, bf16[128,512]{1,0:T(8,128)(2,1)S(1)}, u32[]{:S(2)}, u32[]{:S(2)}) %collective-permute-start.9) | collective-permute-done | bytes 131104 | tf_op jit(solution)/shard_map/ppermute | solution.py:204
  38.0 0.4 collective-permute-start.11
  38.4 2.3 %collective-permute-start.13 = (bf16[32,512]{1,0:T(8,128)(2,1)S(1)}, bf16[32,512]{1,0:T(8,128)(2,1)S(1)}, u32[]{:S(2)}, u32[]{:S(2)}) collective-permute-start(bf16[32,512]{1,0:T(8,128)(2,1)S(1)} %get-tuple-element.124), channel_id=1, source_target_pairs={{0,6},{1,7},{2,4},{3,5},{4,2},{5,3},{6,0},{7,1},{8,14},{9,15},{10,... | collective-permute-start | bytes 98312 | tf_op jit(solution)/shard_map/ppermute | solution.py:204
  40.7 0.8 collective-permute-start.12
  41.6 4.2 %collective-permute-start.21 = (bf16[528,512]{1,0:T(8,128)(2,1)S(1)}, bf16[528,512]{1,0:T(8,128)(2,1)S(1)}, u32[]{:S(2)}, u32[]{:S(2)}) collective-permute-start(bf16[528,512]{1,0:T(8,128)(2,1)S(1)} %collective-permute-done.20), channel_id=1, source_target_pairs={{0,1},{1,0},{2,3},{3,2},{4,5},{5,4},{6,7},{7,6},{8,9},{9,8},{10,11... | collective-permute-start | bytes 1622024 | tf_op jit(solution)/shard_map/ppermute | solution.py:273
  45.8 0.1 constant_dynamic-update-slice_fusion.13
  45.9 0.8 collective-permute-start.16
  46.7 3.6 %collective-permute-start.14 = (bf16[32,512]{1,0:T(8,128)(2,1)S(1)}, bf16[32,512]{1,0:T(8,128)(2,1)S(1)}, u32[]{:S(2)}, u32[]{:S(2)}) collective-permute-start(bf16[32,512]{1,0:T(8,128)(2,1)S(1)} %get-tuple-element.108), channel_id=1, source_target_pairs={{0,4},{1,5},{2,6},{3,7},{4,0},{5,1},{6,2},{7,3},{8,12},{9,13},{10,... | collective-permute-start | bytes 98312 | tf_op jit(solution)/shard_map/ppermute | solution.py:204
  50.3 1.3 %collective-permute-done.16 = bf16[32,512]{1,0:T(8,128)(2,1)S(1)} collective-permute-done((bf16[32,512]{1,0:T(8,128)(2,1)S(1)}, bf16[32,512]{1,0:T(8,128)(2,1)S(1)}, u32[]{:S(2)}, u32[]{:S(2)}) %collective-permute-start.16) | collective-permute-done | bytes 32800 | tf_op jit(solution)/shard_map/ppermute | solution.py:204
  51.6 0.6 collective-permute-done.14
  52.2 2.1 %collective-permute-start.19 = (bf16[128,512]{1,0:T(8,128)(2,1)S(1)}, bf16[128,512]{1,0:T(8,128)(2,1)S(1)}, u32[]{:S(2)}, u32[]{:S(2)}) collective-permute-start(bf16[128,512]{1,0:T(8,128)(2,1)S(1)} %pad_maximum_fusion.1), channel_id=1, source_target_pairs={{0,17},{1,16},{2,19},{3,18},{4,21},{5,20},{6,23},{7,22},{8,25},{9,... | collective-permute-start | bytes 393224 | tf_op jit(solution)/shard_map/ppermute | solution.py:204
  54.3 0.8 collective-permute-start.18
  55.1 0.7 collective-permute-start.17
  55.8 5.7 %collective-permute-done.19 = bf16[128,512]{1,0:T(8,128)(2,1)S(1)} collective-permute-done((bf16[128,512]{1,0:T(8,128)(2,1)S(1)}, bf16[128,512]{1,0:T(8,128)(2,1)S(1)}, u32[]{:S(2)}, u32[]{:S(2)}) %collective-permute-start.19) | collective-permute-done | bytes 131104 | tf_op jit(solution)/shard_map/ppermute | solution.py:204
  61.5 0.5 collective-permute-done.17
  62.0 0.1 collective-permute-start.22
  62.1 1.9 %collective-permute-done.22.hi_ref = bf16[512,512]{1,0:T(8,128)(2,1)S(1)} collective-permute-done((bf16[512,512]{1,0:T(8,128)(2,1)S(1)}, bf16[512,512]{1,0:T(8,128)(2,1)S(1)}, u32[]{:S(2)}, u32[]{:S(2)}) %collective-permute-start.22) | collective-permute-done | bytes 524320 | tf_op jit(solution)/shard_map/ppermute | solution.py:204
  64.0 2.6 %shard_map.143 = (bf16[512,512]{1,0:T(8,128)(2,1)S(1)}, bf16[512,512]{1,0:T(8,128)(2,1)S(1)}, bf16[512,512]{1,0:T(8,128)(2,1)S(1)}, bf16[512,512]{1,0:T(8,128)(2,1)S(1)}, bf16[512,512]{1,0:T(8,128)(2,1)S(1)}) custom-call(s32[32]{0:T(128)S(1)} %broadcast_xor_fusion.nat_ref, s32[2,1]{1,0:T(2,128)S(1)} %copy.16.live_ref, s32[2,4]{1,0:T(2,128)S(1)} %copy-done.9, ...), custom_call_target="tpu_custom_call" | custom-call | flops 1342177280 | bytes 5275816 | tf_op jit(solution)/shard_map/pallas_call | solution.py:170
  66.6 0.2 collective-permute-start.23
  66.8 1.8 %collective-permute-done.23 = bf16[512,512]{1,0:T(8,128)(2,1)S(1)} collective-permute-done((bf16[512,512]{1,0:T(8,128)(2,1)S(1)}, bf16[512,512]{1,0:T(8,128)(2,1)S(1)}, u32[]{:S(2)}, u32[]{:S(2)}) %collective-permute-start.23) | collective-permute-done | bytes 524320 | tf_op jit(solution)/shard_map/ppermute | solution.py:204
  68.6 0.1 add_convert_fusion
  68.8 2.7 %collective-permute-start.26 = (bf16[128,512]{1,0:T(8,128)(2,1)S(1)}, bf16[128,512]{1,0:T(8,128)(2,1)S(1)}, u32[]{:S(2)}, u32[]{:S(2)}) collective-permute-start(bf16[128,512]{1,0:T(8,128)(2,1)S(1)} %get-tuple-element.113), channel_id=1, source_target_pairs={{0,17},{1,16},{2,19},{3,18},{4,21},{5,20},{6,23},{7,22},{8,25},{9,... | collective-permute-start | bytes 393224 | tf_op jit(solution)/shard_map/ppermute | solution.py:204
  71.5 0.5 collective-permute-start.25
  72.0 0.3 collective-permute-start.24
  72.3 1.7 %shard_map.144 = f32[512,512]{1,0:T(8,128)} custom-call(bf16[512,512]{1,0:T(8,128)(2,1)S(1)} %get-tuple-element.94.w_ref, bf16[512,512]{1,0:T(8,128)(2,1)S(1)} %get-tuple-element.95.u_ref, bf16[528,512]{1,0:T(8,128)(2,1)S(1)} %collective-permute-done.21.t_ref.packed_ref), custom_call_target="tpu_custom_call" | custom-call | flops 268435456 | bytes 2637824 | tf_op jit(solution)/shard_map/pallas_call | solution.py:170
  74.0 2.9 %shard_map.145 = f32[512,512]{1,0:T(8,128)} custom-call(s32[32]{0:T(128)S(1)} %broadcast_xor_fusion.nat_ref, s32[2,4]{1,0:T(2,128)S(1)} %copy-done.9, bf16[512,512]{1,0:T(8,128)(2,1)S(1)} %constant_dynamic-update-slice_fusion.7.lo_ref, bf16[512,512]{1,0:T(8,128)(2,1)S(1)} %collective-permute-done.22.hi_ref, bf16[512,512]{1,0:T(8,128)(2,1)S(1)} %get-tuple-element.99.gu_ref, ...), custom_call_target="tpu_custom_call" | custom-call | flops 1073741824 | bytes 3676320 | tf_op jit(solution)/shard_map/pallas_call | solution.py:170
  76.9 1.1 %collective-permute-done.25 = bf16[128,512]{1,0:T(8,128)(2,1)S(1)} collective-permute-done((bf16[128,512]{1,0:T(8,128)(2,1)S(1)}, bf16[128,512]{1,0:T(8,128)(2,1)S(1)}, u32[]{:S(2)}, u32[]{:S(2)}) %collective-permute-start.25) | collective-permute-done | bytes 131104 | tf_op jit(solution)/shard_map/ppermute | solution.py:204
  78.1 1.1 %collective-permute-start.27 = (bf16[32,512]{1,0:T(8,128)(2,1)S(1)}, bf16[32,512]{1,0:T(8,128)(2,1)S(1)}, u32[]{:S(2)}, u32[]{:S(2)}) collective-permute-start(bf16[32,512]{1,0:T(8,128)(2,1)S(1)} %get-tuple-element.120), channel_id=1, source_target_pairs={{0,4},{1,5},{2,6},{3,7},{4,0},{5,1},{6,2},{7,3},{8,12},{9,13},{10,... | collective-permute-start | bytes 98312 | tf_op jit(solution)/shard_map/ppermute | solution.py:204
  79.3 2.0 %collective-permute-start.29 = (bf16[32,512]{1,0:T(8,128)(2,1)S(1)}, bf16[32,512]{1,0:T(8,128)(2,1)S(1)}, u32[]{:S(2)}, u32[]{:S(2)}) collective-permute-start(bf16[32,512]{1,0:T(8,128)(2,1)S(1)} %get-tuple-element.121), channel_id=1, source_target_pairs={{0,6},{1,7},{2,4},{3,5},{4,2},{5,3},{6,0},{7,1},{8,14},{9,15},{10,... | collective-permute-start | bytes 98312 | tf_op jit(solution)/shard_map/ppermute | solution.py:204
  81.2 0.4 collective-permute-start.28
  81.7 2.2 %collective-permute-done.27 = bf16[32,512]{1,0:T(8,128)(2,1)S(1)} collective-permute-done((bf16[32,512]{1,0:T(8,128)(2,1)S(1)}, bf16[32,512]{1,0:T(8,128)(2,1)S(1)}, u32[]{:S(2)}, u32[]{:S(2)}) %collective-permute-start.27) | collective-permute-done | bytes 32800 | tf_op jit(solution)/shard_map/ppermute | solution.py:204
  83.9 1.1 %collective-permute-done.29 = bf16[32,512]{1,0:T(8,128)(2,1)S(1)} collective-permute-done((bf16[32,512]{1,0:T(8,128)(2,1)S(1)}, bf16[32,512]{1,0:T(8,128)(2,1)S(1)}, u32[]{:S(2)}, u32[]{:S(2)}) %collective-permute-start.29) | collective-permute-done | bytes 32800 | tf_op jit(solution)/shard_map/ppermute | solution.py:204
  85.0 0.3 collective-permute-done.28
  85.3 0.7 divide_subtract_fusion
  (54 shorter events, 0.3 us)
Async XLA Ops:
  1.5 6.9 %collective-permute-start.2 = (bf16[32,512]{1,0:T(8,128)(2,1)S(1)}, bf16[32,512]{1,0:T(8,128)(2,1)S(1)}, u32[]{:S(2)}, u32[]{:S(2)}) collective-permute-start(bf16[32,512]{1,0:T(8,128)(2,1)S(1)} %get-tuple-element.111), channel_id=1, source_target_pairs={{0,6},{1,7},{2,4},{3,5},{4,2},{5,3},{6,0},{7,1},{8,14},{9,15},{10,... | collective-permute-start | bytes 98312 | tf_op jit(solution)/shard_map/ppermute | solution.py:204
  6.5 3.9 %collective-permute-start.1 = (bf16[32,512]{1,0:T(8,128)(2,1)S(1)}, bf16[32,512]{1,0:T(8,128)(2,1)S(1)}, u32[]{:S(2)}, u32[]{:S(2)}) collective-permute-start(bf16[32,512]{1,0:T(8,128)(2,1)S(1)} %get-tuple-element.111), channel_id=1, source_target_pairs={{0,2},{1,3},{2,0},{3,1},{4,6},{5,7},{6,4},{7,5},{8,10},{9,11},{10,... | collective-permute-start | bytes 98312 | tf_op jit(solution)/shard_map/ppermute | solution.py:204
  6.5 4.9 %collective-permute-start = (bf16[32,512]{1,0:T(8,128)(2,1)S(1)}, bf16[32,512]{1,0:T(8,128)(2,1)S(1)}, u32[]{:S(2)}, u32[]{:S(2)}) collective-permute-start(bf16[32,512]{1,0:T(8,128)(2,1)S(1)} %get-tuple-element.111), channel_id=1, source_target_pairs={{0,4},{1,5},{2,6},{3,7},{4,0},{5,1},{6,2},{7,3},{8,12},{9,13},{10,... | collective-permute-start | bytes 98312 | tf_op jit(solution)/shard_map/ppermute | solution.py:204
  11.5 7.5 %collective-permute-start.5 = (bf16[128,512]{1,0:T(8,128)(2,1)S(1)}, bf16[128,512]{1,0:T(8,128)(2,1)S(1)}, u32[]{:S(2)}, u32[]{:S(2)}) collective-permute-start(bf16[128,512]{1,0:T(8,128)(2,1)S(1)} %pad_maximum_fusion), channel_id=1, source_target_pairs={{0,17},{1,16},{2,19},{3,18},{4,21},{5,20},{6,23},{7,22},{8,25},{9,... | collective-permute-start | bytes 393224 | tf_op jit(solution)/shard_map/ppermute | solution.py:204
  14.0 5.6 %collective-permute-start.4 = (bf16[128,512]{1,0:T(8,128)(2,1)S(1)}, bf16[128,512]{1,0:T(8,128)(2,1)S(1)}, u32[]{:S(2)}, u32[]{:S(2)}) collective-permute-start(bf16[128,512]{1,0:T(8,128)(2,1)S(1)} %pad_maximum_fusion), channel_id=1, source_target_pairs={{0,16},{1,17},{2,18},{3,19},{4,20},{5,21},{6,22},{7,23},{8,24},{9,... | collective-permute-start | bytes 393224 | tf_op jit(solution)/shard_map/ppermute | solution.py:204
  14.5 5.1 %collective-permute-start.3 = (bf16[128,512]{1,0:T(8,128)(2,1)S(1)}, bf16[128,512]{1,0:T(8,128)(2,1)S(1)}, u32[]{:S(2)}, u32[]{:S(2)}) collective-permute-start(bf16[128,512]{1,0:T(8,128)(2,1)S(1)} %pad_maximum_fusion), channel_id=1, source_target_pairs={{0,1},{1,0},{2,3},{3,2},{4,5},{5,4},{6,7},{7,6},{8,9},{9,8},{10,11... | collective-permute-start | bytes 393224 | tf_op jit(solution)/shard_map/ppermute | solution.py:204
  15.0 0.7 copy-start.4
  15.0 0.7 copy-start.5
  15.0 0.7 copy-start.6
  15.0 0.7 copy-start.8
  15.1 0.7 copy-start.7
  15.8 1.2 %copy-start = (f32[512,512]{1,0:T(8,128)S(1)}, f32[512,512]{1,0:T(8,128)}, u32[]{:S(2)}) copy-start(f32[512,512]{1,0:T(8,128)} %table_ref.3) | copy-start | bytes 3145732
  17.0 1.2 %copy-start.2 = (f32[512,512]{1,0:T(8,128)S(1)}, f32[512,512]{1,0:T(8,128)}, u32[]{:S(2)}) copy-start(f32[512,512]{1,0:T(8,128)} %table_ref.2) | copy-start | bytes 3145732
  19.6 2.0 %collective-permute-start.6 = (bf16[512,512]{1,0:T(8,128)(2,1)S(1)}, bf16[512,512]{1,0:T(8,128)(2,1)S(1)}, u32[]{:S(2)}, u32[]{:S(2)}) collective-permute-start(bf16[512,512]{1,0:T(8,128)(2,1)S(1)} %constant_dynamic-update-slice_fusion.lo_ref), channel_id=1, source_target_pairs={{0,8},{1,9},{2,10},{3,11},{4,12},{5,13},{6,14},{7,15},{8,0},{9,1},... | collective-permute-start | bytes 1572872 | tf_op jit(solution)/shard_map/ppermute | solution.py:204
  19.7 0.7 copy-start.12
  20.5 0.7 copy-start.13
  21.1 0.7 copy-start.9
  21.1 3.9 %copy-start.1 = (f32[512,512]{1,0:T(8,128)S(1)}, f32[512,512]{1,0:T(8,128)}, u32[]{:S(2)}) copy-start(f32[512,512]{1,0:T(8,128)} %table_ref.3) | copy-start | bytes 3145732
  24.5 2.1 %collective-permute-start.7 = (bf16[512,512]{1,0:T(8,128)(2,1)S(1)}, bf16[512,512]{1,0:T(8,128)(2,1)S(1)}, u32[]{:S(2)}, u32[]{:S(2)}) collective-permute-start(bf16[512,512]{1,0:T(8,128)(2,1)S(1)} %get-tuple-element.75), channel_id=1, source_target_pairs={{0,8},{1,9},{2,10},{3,11},{4,12},{5,13},{6,14},{7,15},{8,0},{9,1},... | collective-permute-start | bytes 1572872 | tf_op jit(solution)/shard_map/ppermute | solution.py:204
  25.7 6.7 %copy-start.3 = (f32[512,512]{1,0:T(8,128)S(1)}, f32[512,512]{1,0:T(8,128)}, u32[]{:S(2)}) copy-start(f32[512,512]{1,0:T(8,128)} %table_ref.2) | copy-start | bytes 3145732
  25.7 15.9 %collective-permute-start.20 = (bf16[528,512]{1,0:T(8,128)(2,1)S(1)}, bf16[528,512]{1,0:T(8,128)(2,1)S(1)}, u32[]{:S(2)}, u32[]{:S(2)}) collective-permute-start(bf16[528,512]{1,0:T(8,128)(2,1)S(1)} %shard_map.142), channel_id=1, source_target_pairs={{0,0},{1,3},{2,2},{3,5},{4,4},{5,7},{6,6},{7,1},{8,8},{9,11},{10,1... | collective-permute-start | bytes 1622024 | tf_op jit(solution)/shard_map/ppermute | solution.py:272
  26.7 9.0 %collective-permute-start.10 = (bf16[128,512]{1,0:T(8,128)(2,1)S(1)}, bf16[128,512]{1,0:T(8,128)(2,1)S(1)}, u32[]{:S(2)}, u32[]{:S(2)}) collective-permute-start(bf16[128,512]{1,0:T(8,128)(2,1)S(1)} %get-tuple-element.116), channel_id=1, source_target_pairs={{0,17},{1,16},{2,19},{3,18},{4,21},{5,20},{6,23},{7,22},{8,25},{9,... | collective-permute-start | bytes 393224 | tf_op jit(solution)/shard_map/ppermute | solution.py:204
  31.7 6.2 %collective-permute-start.9 = (bf16[128,512]{1,0:T(8,128)(2,1)S(1)}, bf16[128,512]{1,0:T(8,128)(2,1)S(1)}, u32[]{:S(2)}, u32[]{:S(2)}) collective-permute-start(bf16[128,512]{1,0:T(8,128)(2,1)S(1)} %get-tuple-element.117), channel_id=1, source_target_pairs={{0,16},{1,17},{2,18},{3,19},{4,20},{5,21},{6,22},{7,23},{8,24},{9,... | collective-permute-start | bytes 393224 | tf_op jit(solution)/shard_map/ppermute | solution.py:204
  32.2 5.7 %collective-permute-start.8 = (bf16[128,512]{1,0:T(8,128)(2,1)S(1)}, bf16[128,512]{1,0:T(8,128)(2,1)S(1)}, u32[]{:S(2)}, u32[]{:S(2)}) collective-permute-start(bf16[128,512]{1,0:T(8,128)(2,1)S(1)} %get-tuple-element.118), channel_id=1, source_target_pairs={{0,1},{1,0},{2,3},{3,2},{4,5},{5,4},{6,7},{7,6},{8,9},{9,8},{10,11... | collective-permute-start | bytes 393224 | tf_op jit(solution)/shard_map/ppermute | solution.py:204
  38.0 7.8 %copy-start.10 = (f32[32,512]{1,0:T(8,128)S(1)}, f32[32,512]{1,0:T(8,128)}, u32[]{:S(2)}) copy-start(f32[32,512]{1,0:T(8,128)} %param.16) | copy-start | bytes 196612
  38.0 7.8 %copy-start.11 = (f32[32,512]{1,0:T(8,128)S(1)}, f32[32,512]{1,0:T(8,128)}, u32[]{:S(2)}) copy-start(f32[32,512]{1,0:T(8,128)} %param.17) | copy-start | bytes 196612
  38.0 7.7 %collective-permute-start.11 = (bf16[32,512]{1,0:T(8,128)(2,1)S(1)}, bf16[32,512]{1,0:T(8,128)(2,1)S(1)}, u32[]{:S(2)}, u32[]{:S(2)}) collective-permute-start(bf16[32,512]{1,0:T(8,128)(2,1)S(1)} %get-tuple-element.123), channel_id=1, source_target_pairs={{0,4},{1,5},{2,6},{3,7},{4,0},{5,1},{6,2},{7,3},{8,12},{9,13},{10,... | collective-permute-start | bytes 98312 | tf_op jit(solution)/shard_map/ppermute | solution.py:204
  38.4 7.3 %collective-permute-start.13 = (bf16[32,512]{1,0:T(8,128)(2,1)S(1)}, bf16[32,512]{1,0:T(8,128)(2,1)S(1)}, u32[]{:S(2)}, u32[]{:S(2)}) collective-permute-start(bf16[32,512]{1,0:T(8,128)(2,1)S(1)} %get-tuple-element.124), channel_id=1, source_target_pairs={{0,6},{1,7},{2,4},{3,5},{4,2},{5,3},{6,0},{7,1},{8,14},{9,15},{10,... | collective-permute-start | bytes 98312 | tf_op jit(solution)/shard_map/ppermute | solution.py:204
  40.7 5.0 %collective-permute-start.12 = (bf16[32,512]{1,0:T(8,128)(2,1)S(1)}, bf16[32,512]{1,0:T(8,128)(2,1)S(1)}, u32[]{:S(2)}, u32[]{:S(2)}) collective-permute-start(bf16[32,512]{1,0:T(8,128)(2,1)S(1)} %get-tuple-element.125), channel_id=1, source_target_pairs={{0,2},{1,3},{2,0},{3,1},{4,6},{5,7},{6,4},{7,5},{8,10},{9,11},{10,... | collective-permute-start | bytes 98312 | tf_op jit(solution)/shard_map/ppermute | solution.py:204
  41.6 20.4 %collective-permute-start.21 = (bf16[528,512]{1,0:T(8,128)(2,1)S(1)}, bf16[528,512]{1,0:T(8,128)(2,1)S(1)}, u32[]{:S(2)}, u32[]{:S(2)}) collective-permute-start(bf16[528,512]{1,0:T(8,128)(2,1)S(1)} %collective-permute-done.20), channel_id=1, source_target_pairs={{0,1},{1,0},{2,3},{3,2},{4,5},{5,4},{6,7},{7,6},{8,9},{9,8},{10,11... | collective-permute-start | bytes 1622024 | tf_op jit(solution)/shard_map/ppermute | solution.py:273
  45.9 5.8 %collective-permute-start.16 = (bf16[32,512]{1,0:T(8,128)(2,1)S(1)}, bf16[32,512]{1,0:T(8,128)(2,1)S(1)}, u32[]{:S(2)}, u32[]{:S(2)}) collective-permute-start(bf16[32,512]{1,0:T(8,128)(2,1)S(1)} %get-tuple-element.108), channel_id=1, source_target_pairs={{0,6},{1,7},{2,4},{3,5},{4,2},{5,3},{6,0},{7,1},{8,14},{9,15},{10,... | collective-permute-start | bytes 98312 | tf_op jit(solution)/shard_map/ppermute | solution.py:204
  46.7 5.0 %collective-permute-start.15 = (bf16[32,512]{1,0:T(8,128)(2,1)S(1)}, bf16[32,512]{1,0:T(8,128)(2,1)S(1)}, u32[]{:S(2)}, u32[]{:S(2)}) collective-permute-start(bf16[32,512]{1,0:T(8,128)(2,1)S(1)} %get-tuple-element.108), channel_id=1, source_target_pairs={{0,2},{1,3},{2,0},{3,1},{4,6},{5,7},{6,4},{7,5},{8,10},{9,11},{10,... | collective-permute-start | bytes 98312 | tf_op jit(solution)/shard_map/ppermute | solution.py:204
  46.7 5.5 %collective-permute-start.14 = (bf16[32,512]{1,0:T(8,128)(2,1)S(1)}, bf16[32,512]{1,0:T(8,128)(2,1)S(1)}, u32[]{:S(2)}, u32[]{:S(2)}) collective-permute-start(bf16[32,512]{1,0:T(8,128)(2,1)S(1)} %get-tuple-element.108), channel_id=1, source_target_pairs={{0,4},{1,5},{2,6},{3,7},{4,0},{5,1},{6,2},{7,3},{8,12},{9,13},{10,... | collective-permute-start | bytes 98312 | tf_op jit(solution)/shard_map/ppermute | solution.py:204
  52.2 9.2 %collective-permute-start.19 = (bf16[128,512]{1,0:T(8,128)(2,1)S(1)}, bf16[128,512]{1,0:T(8,128)(2,1)S(1)}, u32[]{:S(2)}, u32[]{:S(2)}) collective-permute-start(bf16[128,512]{1,0:T(8,128)(2,1)S(1)} %pad_maximum_fusion.1), channel_id=1, source_target_pairs={{0,17},{1,16},{2,19},{3,18},{4,21},{5,20},{6,23},{7,22},{8,25},{9,... | collective-permute-start | bytes 393224 | tf_op jit(solution)/shard_map/ppermute | solution.py:204
  54.3 7.1 %collective-permute-start.18 = (bf16[128,512]{1,0:T(8,128)(2,1)S(1)}, bf16[128,512]{1,0:T(8,128)(2,1)S(1)}, u32[]{:S(2)}, u32[]{:S(2)}) collective-permute-start(bf16[128,512]{1,0:T(8,128)(2,1)S(1)} %pad_maximum_fusion.1), channel_id=1, source_target_pairs={{0,16},{1,17},{2,18},{3,19},{4,20},{5,21},{6,22},{7,23},{8,24},{9,... | collective-permute-start | bytes 393224 | tf_op jit(solution)/shard_map/ppermute | solution.py:204
  55.1 6.9 %collective-permute-start.17 = (bf16[128,512]{1,0:T(8,128)(2,1)S(1)}, bf16[128,512]{1,0:T(8,128)(2,1)S(1)}, u32[]{:S(2)}, u32[]{:S(2)}) collective-permute-start(bf16[128,512]{1,0:T(8,128)(2,1)S(1)} %pad_maximum_fusion.1), channel_id=1, source_target_pairs={{0,1},{1,0},{2,3},{3,2},{4,5},{5,4},{6,7},{7,6},{8,9},{9,8},{10,11... | collective-permute-start | bytes 393224 | tf_op jit(solution)/shard_map/ppermute | solution.py:204
  62.0 2.0 %collective-permute-start.22 = (bf16[512,512]{1,0:T(8,128)(2,1)S(1)}, bf16[512,512]{1,0:T(8,128)(2,1)S(1)}, u32[]{:S(2)}, u32[]{:S(2)}) collective-permute-start(bf16[512,512]{1,0:T(8,128)(2,1)S(1)} %constant_dynamic-update-slice_fusion.7.lo_ref), channel_id=1, source_target_pairs={{0,8},{1,9},{2,10},{3,11},{4,12},{5,13},{6,14},{7,15},{8,0},{9,1},... | collective-permute-start | bytes 1572872 | tf_op jit(solution)/shard_map/ppermute | solution.py:204
  66.6 2.0 %collective-permute-start.23 = (bf16[512,512]{1,0:T(8,128)(2,1)S(1)}, bf16[512,512]{1,0:T(8,128)(2,1)S(1)}, u32[]{:S(2)}, u32[]{:S(2)}) collective-permute-start(bf16[512,512]{1,0:T(8,128)(2,1)S(1)} %get-tuple-element.93), channel_id=1, source_target_pairs={{0,8},{1,9},{2,10},{3,11},{4,12},{5,13},{6,14},{7,15},{8,0},{9,1},... | collective-permute-start | bytes 1572872 | tf_op jit(solution)/shard_map/ppermute | solution.py:204
  68.8 8.2 %collective-permute-start.26 = (bf16[128,512]{1,0:T(8,128)(2,1)S(1)}, bf16[128,512]{1,0:T(8,128)(2,1)S(1)}, u32[]{:S(2)}, u32[]{:S(2)}) collective-permute-start(bf16[128,512]{1,0:T(8,128)(2,1)S(1)} %get-tuple-element.113), channel_id=1, source_target_pairs={{0,17},{1,16},{2,19},{3,18},{4,21},{5,20},{6,23},{7,22},{8,25},{9,... | collective-permute-start | bytes 393224 | tf_op jit(solution)/shard_map/ppermute | solution.py:204
  71.5 6.6 %collective-permute-start.25 = (bf16[128,512]{1,0:T(8,128)(2,1)S(1)}, bf16[128,512]{1,0:T(8,128)(2,1)S(1)}, u32[]{:S(2)}, u32[]{:S(2)}) collective-permute-start(bf16[128,512]{1,0:T(8,128)(2,1)S(1)} %get-tuple-element.114), channel_id=1, source_target_pairs={{0,16},{1,17},{2,18},{3,19},{4,20},{5,21},{6,22},{7,23},{8,24},{9,... | collective-permute-start | bytes 393224 | tf_op jit(solution)/shard_map/ppermute | solution.py:204
  72.0 6.1 %collective-permute-start.24 = (bf16[128,512]{1,0:T(8,128)(2,1)S(1)}, bf16[128,512]{1,0:T(8,128)(2,1)S(1)}, u32[]{:S(2)}, u32[]{:S(2)}) collective-permute-start(bf16[128,512]{1,0:T(8,128)(2,1)S(1)} %get-tuple-element.115), channel_id=1, source_target_pairs={{0,1},{1,0},{2,3},{3,2},{4,5},{5,4},{6,7},{7,6},{8,9},{9,8},{10,11... | collective-permute-start | bytes 393224 | tf_op jit(solution)/shard_map/ppermute | solution.py:204
  78.1 5.7 %collective-permute-start.27 = (bf16[32,512]{1,0:T(8,128)(2,1)S(1)}, bf16[32,512]{1,0:T(8,128)(2,1)S(1)}, u32[]{:S(2)}, u32[]{:S(2)}) collective-permute-start(bf16[32,512]{1,0:T(8,128)(2,1)S(1)} %get-tuple-element.120), channel_id=1, source_target_pairs={{0,4},{1,5},{2,6},{3,7},{4,0},{5,1},{6,2},{7,3},{8,12},{9,13},{10,... | collective-permute-start | bytes 98312 | tf_op jit(solution)/shard_map/ppermute | solution.py:204
  79.3 5.7 %collective-permute-start.29 = (bf16[32,512]{1,0:T(8,128)(2,1)S(1)}, bf16[32,512]{1,0:T(8,128)(2,1)S(1)}, u32[]{:S(2)}, u32[]{:S(2)}) collective-permute-start(bf16[32,512]{1,0:T(8,128)(2,1)S(1)} %get-tuple-element.121), channel_id=1, source_target_pairs={{0,6},{1,7},{2,4},{3,5},{4,2},{5,3},{6,0},{7,1},{8,14},{9,15},{10,... | collective-permute-start | bytes 98312 | tf_op jit(solution)/shard_map/ppermute | solution.py:204
  81.2 4.1 %collective-permute-start.28 = (bf16[32,512]{1,0:T(8,128)(2,1)S(1)}, bf16[32,512]{1,0:T(8,128)(2,1)S(1)}, u32[]{:S(2)}, u32[]{:S(2)}) collective-permute-start(bf16[32,512]{1,0:T(8,128)(2,1)S(1)} %get-tuple-element.122), channel_id=1, source_target_pairs={{0,2},{1,3},{2,0},{3,1},{4,6},{5,7},{6,4},{7,5},{8,10},{9,11},{10,... | collective-permute-start | bytes 98312 | tf_op jit(solution)/shard_map/ppermute | solution.py:204

commit v7 on v6

--- a/solution.py
+++ b/solution.py
@@ -110,16 +110,16 @@
         for b in range(blocks):
             part = h_ref[b * size : (b + 1) * size]
             parts.append(jnp.where(rel_ref[k, b] == r, part, jnp.zeros_like(part)))
-        grad_s[r * width : (r + 1) * width] = dot(jnp.concatenate(parts), gu, ROWS, ROWS)
+        grad_s[r * width : (r + 1) * width] = dot(jnp.concatenate(parts), gu, ROWS, ROWS).astype(BF16)
     if own % PACK_ROWS:
-        keep_ref[...] = grad_s[:half].astype(BF16)
-        send_ref[...] = grad_s[half:].astype(BF16)
+        keep_ref[...] = grad_s[:half]
+        send_ref[...] = grad_s[half:]
         return
     for part, ref in enumerate((keep_ref, send_ref)):
         for j in range(half // own):
             block = nat_ref[part * (half // own) + j]
             rows_of = pl.ds(pl.multiple_of(block * own, own), own)
-            ref[j * own : (j + 1) * own] = grad_s[rows_of].astype(BF16)
+            ref[j * own : (j + 1) * own] = grad_s[rows_of]
 
 
 def tail_kernel(w_ref, u_ref, table_ref, state_ref, out_ref):
@@ -304,7 +304,7 @@
                 ((edges, width), BF16),
                 ((edges, width), BF16),
             ],
-            3, [pltpu.VMEM((all_rows, width), BF16), pltpu.VMEM((all_rows, width), F32)], 5 * square,
+            3, [pltpu.VMEM((all_rows, width), BF16), pltpu.VMEM((all_rows, width), BF16)], 5 * square,
             nat, block_counts, relation_ids, lo, hi, head_vecs, tail_vecs, tail_col, counts,
         )
         head_outs = [(head_table.shape, F32)]
@@ -332,8 +332,7 @@
             gather_hooks = {1: with_("tail")}
         else:
             held["tail"] = tail_new
-            first, second = with_("tail"), with_("head")
-            grad = exchange.reduce_scatter(keep, send, {1: lambda got: second(first(got))})
+            grad = exchange.reduce_scatter(keep, send, {1: with_("head"), 2: with_("tail")})
         relation_state = relation_state + grad * grad
         relations = relations - RATE_RELATIONS * grad / (jnp.sqrt(relation_state) + EPSILON)
     return (held["head"][0], held["tail"], relations)

time: 86.4 us -> 85.6 us (level)
  waiting for transfers between devices: 25.2 us -> 23.6 us
  starting transfers between devices: 39.5 us -> 40.4 us
    ppermute x28, waiting for transfers between devices: 25.2 us -> 23.6 us  [swap(): return lax.ppermute(x, AXES, [(i, i ^ mask) for i in range(self.devices)])]
    ppermute x28, starting transfers between devices: 34.5 us -> 35.4 us  [swap(): return lax.ppermute(x, AXES, [(i, i ^ mask) for i in range(self.devices)])]
  transfers between devices with their start and end apart: 30 -> 30, of which waited for: 17 -> 16; matrix products, arithmetic and copies ran while one was open for 0% -> 0% of each run, Pallas kernels for 10% -> 10%
where the time goes in v7:
time: 85.6 us; the launch traced here: 85.3 us
  starting transfers between devices  40.4 us (47%)
  waiting for transfers between devices  23.6 us (28%)
  Pallas kernels  13.5 us (16%)
  local copies, waits for them, and re-layouts  4.85 us (6%)
  other arithmetic  2.07 us (2%)
  between operations  0.86 us (1%)
    ppermute x28, starting transfers between devices, swap(): return lax.ppermute(x, AXES, [(i, i ^ mask) for i in range(self.devices)])  35.4 us
    ppermute x28, waiting for transfers between devices, swap(): return lax.ppermute(x, AXES, [(i, i ^ mask) for i in range(self.devices)])  23.6 us
    pallas_call x7, Pallas kernels, call(): pl.pallas_call(kernel, out_shape=outs, in_specs=[SMEM] * smem + [VMEM] *...  13.5 us
    unnamed x39, local copies, waits for them, and re-layouts  4.83 us
    ppermute x1, starting transfers between devices, rotate(): return lax.ppermute(x, 'tail', [(i, i ^ 1) for i in range(tails)])  4.17 us
  transfers between devices with their start and end apart: 30, of which 16 were waited for; matrix products, arithmetic and copies ran while one was open for 0% of the time, Pallas kernels for 10%

profile of v7, /device:TPU:0, one launch (start us, length us, event | category | flops | bytes accessed | tf_op | source)
XLA Modules:
  0.0 85.3 jit_solution(4341037833282446578)
XLA Ops:
  0.6 0.8 constant_dynamic-update-slice_fusion.6
  1.5 5.0 %collective-permute-start.2 = (bf16[32,512]{1,0:T(8,128)(2,1)S(1)}, bf16[32,512]{1,0:T(8,128)(2,1)S(1)}, u32[]{:S(2)}, u32[]{:S(2)}) collective-permute-start(bf16[32,512]{1,0:T(8,128)(2,1)S(1)} %get-tuple-element.111), channel_id=1, source_target_pairs={{0,6},{1,7},{2,4},{3,5},{4,2},{5,3},{6,0},{7,1},{8,14},{9,15},{10,... | collective-permute-start | bytes 98312 | tf_op jit(solution)/shard_map/ppermute | solution.py:204
  6.5 0.6 collective-permute-start
  7.2 1.3 %collective-permute-done.2 = bf16[32,512]{1,0:T(8,128)(2,1)S(1)} collective-permute-done((bf16[32,512]{1,0:T(8,128)(2,1)S(1)}, bf16[32,512]{1,0:T(8,128)(2,1)S(1)}, u32[]{:S(2)}, u32[]{:S(2)}) %collective-permute-start.2) | collective-permute-done | bytes 32800 | tf_op jit(solution)/shard_map/ppermute | solution.py:204
  8.4 2.0 %collective-permute-done.1 = bf16[32,512]{1,0:T(8,128)(2,1)S(1)} collective-permute-done((bf16[32,512]{1,0:T(8,128)(2,1)S(1)}, bf16[32,512]{1,0:T(8,128)(2,1)S(1)}, u32[]{:S(2)}, u32[]{:S(2)}) %collective-permute-start.1) | collective-permute-done | bytes 32800 | tf_op jit(solution)/shard_map/ppermute | solution.py:204
  10.4 1.0 %collective-permute-done = bf16[32,512]{1,0:T(8,128)(2,1)S(1)} collective-permute-done((bf16[32,512]{1,0:T(8,128)(2,1)S(1)}, bf16[32,512]{1,0:T(8,128)(2,1)S(1)}, u32[]{:S(2)}, u32[]{:S(2)}) %collective-permute-start) | collective-permute-done | bytes 32800 | tf_op jit(solution)/shard_map/ppermute | solution.py:204
  11.5 2.5 %collective-permute-start.5 = (bf16[128,512]{1,0:T(8,128)(2,1)S(1)}, bf16[128,512]{1,0:T(8,128)(2,1)S(1)}, u32[]{:S(2)}, u32[]{:S(2)}) collective-permute-start(bf16[128,512]{1,0:T(8,128)(2,1)S(1)} %pad_maximum_fusion), channel_id=1, source_target_pairs={{0,17},{1,16},{2,19},{3,18},{4,21},{5,20},{6,23},{7,22},{8,25},{9,... | collective-permute-start | bytes 393224 | tf_op jit(solution)/shard_map/ppermute | solution.py:204
  14.0 0.5 collective-permute-start.4
  14.5 0.5 collective-permute-start.3
  15.1 0.6 copy-done.4
  15.8 1.2 %copy-done = f32[512,512]{1,0:T(8,128)S(1)} copy-done((f32[512,512]{1,0:T(8,128)S(1)}, f32[512,512]{1,0:T(8,128)}, u32[]{:S(2)}) %copy-start) | copy-done | bytes 1048600
  17.0 1.2 %copy-done.2 = f32[512,512]{1,0:T(8,128)S(1)} copy-done((f32[512,512]{1,0:T(8,128)S(1)}, f32[512,512]{1,0:T(8,128)}, u32[]{:S(2)}) %copy-start.2) | copy-done | bytes 1048600
  18.2 0.7 shard_map.139
  19.0 0.6 collective-permute-done.4
  19.6 0.1 collective-permute-start.6
  19.7 0.6 copy-done.12
  20.4 0.1 copy.16.live_ref
  20.5 0.7 copy-done.13
  21.1 0.5 collective-permute-done.6.hi_ref
  21.6 0.2 copy-done.9
  21.8 2.6 %shard_map.140 = (bf16[512,512]{1,0:T(8,128)(2,1)S(1)}, bf16[512,512]{1,0:T(8,128)(2,1)S(1)}, bf16[512,512]{1,0:T(8,128)(2,1)S(1)}, bf16[512,512]{1,0:T(8,128)(2,1)S(1)}, bf16[512,512]{1,0:T(8,128)(2,1)S(1)}) custom-call(s32[32]{0:T(128)S(1)} %broadcast_xor_fusion.nat_ref, s32[2,1]{1,0:T(2,128)S(1)} %copy.16.live_ref, s32[2,4]{1,0:T(2,128)S(1)} %copy-done.9, ...), custom_call_target="tpu_custom_call" | custom-call | flops 1342177280 | bytes 5259432 | tf_op jit(solution)/shard_map/pallas_call | solution.py:170
  24.4 0.6 collective-permute-start.7
  25.0 0.7 shard_map.142
  25.7 0.8 collective-permute-start.20
  26.5 0.1 add_convert_fusion.4
  26.7 5.0 %collective-permute-start.10 = (bf16[128,512]{1,0:T(8,128)(2,1)S(1)}, bf16[128,512]{1,0:T(8,128)(2,1)S(1)}, u32[]{:S(2)}, u32[]{:S(2)}) collective-permute-start(bf16[128,512]{1,0:T(8,128)(2,1)S(1)} %get-tuple-element.116), channel_id=1, source_target_pairs={{0,17},{1,16},{2,19},{3,18},{4,21},{5,20},{6,23},{7,22},{8,25},{9,... | collective-permute-start | bytes 393224 | tf_op jit(solution)/shard_map/ppermute | solution.py:204
  31.7 0.5 collective-permute-start.9
  32.2 0.1 collective-permute-start.8
  32.3 2.2 %shard_map.141 = (f32[512,512]{1,0:T(8,128)S(1)}, f32[1,512]{1,0:T(1,128)S(1)}, bf16[512,512]{1,0:T(8,128)(2,1)S(1)}) custom-call(s32[32]{0:T(128)S(1)} %broadcast_xor_fusion.nat_ref, s32[2,4]{1,0:T(2,128)S(1)} %copy-done.9, bf16[512,512]{1,0:T(8,128)(2,1)S(1)} %constant_dynamic-update-slice_fusion.lo_ref, ...), custom_call_target="tpu_custom_call" | custom-call | flops 1073741824 | bytes 4202656 | tf_op jit(solution)/shard_map/pallas_call | solution.py:170
  34.6 1.0 %collective-permute-done.10 = bf16[128,512]{1,0:T(8,128)(2,1)S(1)} collective-permute-done((bf16[128,512]{1,0:T(8,128)(2,1)S(1)}, bf16[128,512]{1,0:T(8,128)(2,1)S(1)}, u32[]{:S(2)}, u32[]{:S(2)}) %collective-permute-start.10) | collective-permute-done | bytes 131104 | tf_op jit(solution)/shard_map/ppermute | solution.py:204
  35.6 2.3 %collective-permute-done.9 = bf16[128,512]{1,0:T(8,128)(2,1)S(1)} collective-permute-done((bf16[128,512]{1,0:T(8,128)(2,1)S(1)}, bf16[128,512]{1,0:T(8,128)(2,1)S(1)}, u32[]{:S(2)}, u32[]{:S(2)}) %collective-permute-start.9) | collective-permute-done | bytes 131104 | tf_op jit(solution)/shard_map/ppermute | solution.py:204
  37.9 0.1 add_convert_fusion.14
  38.0 0.4 collective-permute-start.11
  38.4 2.3 %collective-permute-start.13 = (bf16[32,512]{1,0:T(8,128)(2,1)S(1)}, bf16[32,512]{1,0:T(8,128)(2,1)S(1)}, u32[]{:S(2)}, u32[]{:S(2)}) collective-permute-start(bf16[32,512]{1,0:T(8,128)(2,1)S(1)} %get-tuple-element.124), channel_id=1, source_target_pairs={{0,6},{1,7},{2,4},{3,5},{4,2},{5,3},{6,0},{7,1},{8,14},{9,15},{10,... | collective-permute-start | bytes 98312 | tf_op jit(solution)/shard_map/ppermute | solution.py:204
  40.7 0.8 collective-permute-start.12
  41.5 4.2 %collective-permute-start.21 = (bf16[528,512]{1,0:T(8,128)(2,1)S(1)}, bf16[528,512]{1,0:T(8,128)(2,1)S(1)}, u32[]{:S(2)}, u32[]{:S(2)}) collective-permute-start(bf16[528,512]{1,0:T(8,128)(2,1)S(1)} %collective-permute-done.20), channel_id=1, source_target_pairs={{0,1},{1,0},{2,3},{3,2},{4,5},{5,4},{6,7},{7,6},{8,9},{9,8},{10,11... | collective-permute-start | bytes 1622024 | tf_op jit(solution)/shard_map/ppermute | solution.py:273
  45.7 0.1 constant_dynamic-update-slice_fusion.13
  45.8 0.8 collective-permute-start.16
  46.7 3.6 %collective-permute-start.14 = (bf16[32,512]{1,0:T(8,128)(2,1)S(1)}, bf16[32,512]{1,0:T(8,128)(2,1)S(1)}, u32[]{:S(2)}, u32[]{:S(2)}) collective-permute-start(bf16[32,512]{1,0:T(8,128)(2,1)S(1)} %get-tuple-element.108), channel_id=1, source_target_pairs={{0,4},{1,5},{2,6},{3,7},{4,0},{5,1},{6,2},{7,3},{8,12},{9,13},{10,... | collective-permute-start | bytes 98312 | tf_op jit(solution)/shard_map/ppermute | solution.py:204
  50.3 1.3 %collective-permute-done.16 = bf16[32,512]{1,0:T(8,128)(2,1)S(1)} collective-permute-done((bf16[32,512]{1,0:T(8,128)(2,1)S(1)}, bf16[32,512]{1,0:T(8,128)(2,1)S(1)}, u32[]{:S(2)}, u32[]{:S(2)}) %collective-permute-start.16) | collective-permute-done | bytes 32800 | tf_op jit(solution)/shard_map/ppermute | solution.py:204
  51.6 0.6 collective-permute-done.14
  52.2 2.1 %collective-permute-start.19 = (bf16[128,512]{1,0:T(8,128)(2,1)S(1)}, bf16[128,512]{1,0:T(8,128)(2,1)S(1)}, u32[]{:S(2)}, u32[]{:S(2)}) collective-permute-start(bf16[128,512]{1,0:T(8,128)(2,1)S(1)} %pad_maximum_fusion.1), channel_id=1, source_target_pairs={{0,17},{1,16},{2,19},{3,18},{4,21},{5,20},{6,23},{7,22},{8,25},{9,... | collective-permute-start | bytes 393224 | tf_op jit(solution)/shard_map/ppermute | solution.py:204
  54.3 0.8 collective-permute-start.18
  55.1 0.7 collective-permute-start.17
  55.7 5.7 %collective-permute-done.19 = bf16[128,512]{1,0:T(8,128)(2,1)S(1)} collective-permute-done((bf16[128,512]{1,0:T(8,128)(2,1)S(1)}, bf16[128,512]{1,0:T(8,128)(2,1)S(1)}, u32[]{:S(2)}, u32[]{:S(2)}) %collective-permute-start.19) | collective-permute-done | bytes 131104 | tf_op jit(solution)/shard_map/ppermute | solution.py:204
  61.4 0.5 collective-permute-done.17
  62.0 0.1 collective-permute-start.22
  62.1 1.9 %collective-permute-done.22.hi_ref = bf16[512,512]{1,0:T(8,128)(2,1)S(1)} collective-permute-done((bf16[512,512]{1,0:T(8,128)(2,1)S(1)}, bf16[512,512]{1,0:T(8,128)(2,1)S(1)}, u32[]{:S(2)}, u32[]{:S(2)}) %collective-permute-start.22) | collective-permute-done | bytes 524320 | tf_op jit(solution)/shard_map/ppermute | solution.py:204
  64.0 2.6 %shard_map.143 = (bf16[512,512]{1,0:T(8,128)(2,1)S(1)}, bf16[512,512]{1,0:T(8,128)(2,1)S(1)}, bf16[512,512]{1,0:T(8,128)(2,1)S(1)}, bf16[512,512]{1,0:T(8,128)(2,1)S(1)}, bf16[512,512]{1,0:T(8,128)(2,1)S(1)}) custom-call(s32[32]{0:T(128)S(1)} %broadcast_xor_fusion.nat_ref, s32[2,1]{1,0:T(2,128)S(1)} %copy.16.live_ref, s32[2,4]{1,0:T(2,128)S(1)} %copy-done.9, ...), custom_call_target="tpu_custom_call" | custom-call | flops 1342177280 | bytes 5275816 | tf_op jit(solution)/shard_map/pallas_call | solution.py:170
  66.6 0.2 collective-permute-start.23
  66.8 1.8 %collective-permute-done.23 = bf16[512,512]{1,0:T(8,128)(2,1)S(1)} collective-permute-done((bf16[512,512]{1,0:T(8,128)(2,1)S(1)}, bf16[512,512]{1,0:T(8,128)(2,1)S(1)}, u32[]{:S(2)}, u32[]{:S(2)}) %collective-permute-start.23) | collective-permute-done | bytes 524320 | tf_op jit(solution)/shard_map/ppermute | solution.py:204
  68.6 0.1 add_convert_fusion
  68.7 2.7 %collective-permute-start.26 = (bf16[128,512]{1,0:T(8,128)(2,1)S(1)}, bf16[128,512]{1,0:T(8,128)(2,1)S(1)}, u32[]{:S(2)}, u32[]{:S(2)}) collective-permute-start(bf16[128,512]{1,0:T(8,128)(2,1)S(1)} %get-tuple-element.113), channel_id=1, source_target_pairs={{0,17},{1,16},{2,19},{3,18},{4,21},{5,20},{6,23},{7,22},{8,25},{9,... | collective-permute-start | bytes 393224 | tf_op jit(solution)/shard_map/ppermute | solution.py:204
  71.4 0.6 collective-permute-start.25
  72.0 0.3 collective-permute-start.24
  72.3 2.9 %shard_map.144 = f32[512,512]{1,0:T(8,128)} custom-call(s32[32]{0:T(128)S(1)} %broadcast_xor_fusion.nat_ref, s32[2,4]{1,0:T(2,128)S(1)} %copy-done.9, bf16[512,512]{1,0:T(8,128)(2,1)S(1)} %constant_dynamic-update-slice_fusion.7.lo_ref, bf16[512,512]{1,0:T(8,128)(2,1)S(1)} %collective-permute-done.22.hi_ref, bf16[512,512]{1,0:T(8,128)(2,1)S(1)} %get-tuple-element.94.gu_ref, ...), custom_call_target="tpu_custom_call" | custom-call | flops 1073741824 | bytes 3676320 | tf_op jit(solution)/shard_map/pallas_call | solution.py:170
  75.2 0.1 collective-permute-done.26
  75.3 2.7 %collective-permute-done.25 = bf16[128,512]{1,0:T(8,128)(2,1)S(1)} collective-permute-done((bf16[128,512]{1,0:T(8,128)(2,1)S(1)}, bf16[128,512]{1,0:T(8,128)(2,1)S(1)}, u32[]{:S(2)}, u32[]{:S(2)}) %collective-permute-start.25) | collective-permute-done | bytes 131104 | tf_op jit(solution)/shard_map/ppermute | solution.py:204
  78.1 0.7 collective-permute-start.29
  78.8 1.0 %collective-permute-start.28 = (bf16[32,512]{1,0:T(8,128)(2,1)S(1)}, bf16[32,512]{1,0:T(8,128)(2,1)S(1)}, u32[]{:S(2)}, u32[]{:S(2)}) collective-permute-start(bf16[32,512]{1,0:T(8,128)(2,1)S(1)} %get-tuple-element.121), channel_id=1, source_target_pairs={{0,2},{1,3},{2,0},{3,1},{4,6},{5,7},{6,4},{7,5},{8,10},{9,11},{10,... | collective-permute-start | bytes 98312 | tf_op jit(solution)/shard_map/ppermute | solution.py:204
  79.8 2.8 %collective-permute-start.27 = (bf16[32,512]{1,0:T(8,128)(2,1)S(1)}, bf16[32,512]{1,0:T(8,128)(2,1)S(1)}, u32[]{:S(2)}, u32[]{:S(2)}) collective-permute-start(bf16[32,512]{1,0:T(8,128)(2,1)S(1)} %get-tuple-element.122), channel_id=1, source_target_pairs={{0,4},{1,5},{2,6},{3,7},{4,0},{5,1},{6,2},{7,3},{8,12},{9,13},{10,... | collective-permute-start | bytes 98312 | tf_op jit(solution)/shard_map/ppermute | solution.py:204
  82.5 1.7 %shard_map.145 = f32[512,512]{1,0:T(8,128)} custom-call(bf16[512,512]{1,0:T(8,128)(2,1)S(1)} %get-tuple-element.101.w_ref, bf16[512,512]{1,0:T(8,128)(2,1)S(1)} %get-tuple-element.102.u_ref, bf16[528,512]{1,0:T(8,128)(2,1)S(1)} %collective-permute-done.21.t_ref.packed_ref), custom_call_target="tpu_custom_call" | custom-call | flops 268435456 | bytes 2637824 | tf_op jit(solution)/shard_map/pallas_call | solution.py:170
  84.2 0.3 collective-permute-done.27
  84.6 0.7 divide_subtract_fusion
  (54 shorter events, 0.3 us)
Async XLA Ops:
  1.5 6.9 %collective-permute-start.2 = (bf16[32,512]{1,0:T(8,128)(2,1)S(1)}, bf16[32,512]{1,0:T(8,128)(2,1)S(1)}, u32[]{:S(2)}, u32[]{:S(2)}) collective-permute-start(bf16[32,512]{1,0:T(8,128)(2,1)S(1)} %get-tuple-element.111), channel_id=1, source_target_pairs={{0,6},{1,7},{2,4},{3,5},{4,2},{5,3},{6,0},{7,1},{8,14},{9,15},{10,... | collective-permute-start | bytes 98312 | tf_op jit(solution)/shard_map/ppermute | solution.py:204
  6.5 3.9 %collective-permute-start.1 = (bf16[32,512]{1,0:T(8,128)(2,1)S(1)}, bf16[32,512]{1,0:T(8,128)(2,1)S(1)}, u32[]{:S(2)}, u32[]{:S(2)}) collective-permute-start(bf16[32,512]{1,0:T(8,128)(2,1)S(1)} %get-tuple-element.111), channel_id=1, source_target_pairs={{0,2},{1,3},{2,0},{3,1},{4,6},{5,7},{6,4},{7,5},{8,10},{9,11},{10,... | collective-permute-start | bytes 98312 | tf_op jit(solution)/shard_map/ppermute | solution.py:204
  6.5 4.9 %collective-permute-start = (bf16[32,512]{1,0:T(8,128)(2,1)S(1)}, bf16[32,512]{1,0:T(8,128)(2,1)S(1)}, u32[]{:S(2)}, u32[]{:S(2)}) collective-permute-start(bf16[32,512]{1,0:T(8,128)(2,1)S(1)} %get-tuple-element.111), channel_id=1, source_target_pairs={{0,4},{1,5},{2,6},{3,7},{4,0},{5,1},{6,2},{7,3},{8,12},{9,13},{10,... | collective-permute-start | bytes 98312 | tf_op jit(solution)/shard_map/ppermute | solution.py:204
  11.5 7.5 %collective-permute-start.5 = (bf16[128,512]{1,0:T(8,128)(2,1)S(1)}, bf16[128,512]{1,0:T(8,128)(2,1)S(1)}, u32[]{:S(2)}, u32[]{:S(2)}) collective-permute-start(bf16[128,512]{1,0:T(8,128)(2,1)S(1)} %pad_maximum_fusion), channel_id=1, source_target_pairs={{0,17},{1,16},{2,19},{3,18},{4,21},{5,20},{6,23},{7,22},{8,25},{9,... | collective-permute-start | bytes 393224 | tf_op jit(solution)/shard_map/ppermute | solution.py:204
  14.0 5.6 %collective-permute-start.4 = (bf16[128,512]{1,0:T(8,128)(2,1)S(1)}, bf16[128,512]{1,0:T(8,128)(2,1)S(1)}, u32[]{:S(2)}, u32[]{:S(2)}) collective-permute-start(bf16[128,512]{1,0:T(8,128)(2,1)S(1)} %pad_maximum_fusion), channel_id=1, source_target_pairs={{0,16},{1,17},{2,18},{3,19},{4,20},{5,21},{6,22},{7,23},{8,24},{9,... | collective-permute-start | bytes 393224 | tf_op jit(solution)/shard_map/ppermute | solution.py:204
  14.5 5.1 %collective-permute-start.3 = (bf16[128,512]{1,0:T(8,128)(2,1)S(1)}, bf16[128,512]{1,0:T(8,128)(2,1)S(1)}, u32[]{:S(2)}, u32[]{:S(2)}) collective-permute-start(bf16[128,512]{1,0:T(8,128)(2,1)S(1)} %pad_maximum_fusion), channel_id=1, source_target_pairs={{0,1},{1,0},{2,3},{3,2},{4,5},{5,4},{6,7},{7,6},{8,9},{9,8},{10,11... | collective-permute-start | bytes 393224 | tf_op jit(solution)/shard_map/ppermute | solution.py:204
  15.0 0.7 copy-start.4
  15.0 0.7 copy-start.5
  15.0 0.7 copy-start.6
  15.0 0.7 copy-start.8
  15.1 0.7 copy-start.7
  15.8 1.2 %copy-start = (f32[512,512]{1,0:T(8,128)S(1)}, f32[512,512]{1,0:T(8,128)}, u32[]{:S(2)}) copy-start(f32[512,512]{1,0:T(8,128)} %table_ref.3) | copy-start | bytes 3145732
  17.0 1.2 %copy-start.2 = (f32[512,512]{1,0:T(8,128)S(1)}, f32[512,512]{1,0:T(8,128)}, u32[]{:S(2)}) copy-start(f32[512,512]{1,0:T(8,128)} %table_ref.2) | copy-start | bytes 3145732
  19.6 2.0 %collective-permute-start.6 = (bf16[512,512]{1,0:T(8,128)(2,1)S(1)}, bf16[512,512]{1,0:T(8,128)(2,1)S(1)}, u32[]{:S(2)}, u32[]{:S(2)}) collective-permute-start(bf16[512,512]{1,0:T(8,128)(2,1)S(1)} %constant_dynamic-update-slice_fusion.lo_ref), channel_id=1, source_target_pairs={{0,8},{1,9},{2,10},{3,11},{4,12},{5,13},{6,14},{7,15},{8,0},{9,1},... | collective-permute-start | bytes 1572872 | tf_op jit(solution)/shard_map/ppermute | solution.py:204
  19.7 0.7 copy-start.12
  20.5 0.7 copy-start.13
  21.1 0.7 copy-start.9
  21.1 3.8 %copy-start.1 = (f32[512,512]{1,0:T(8,128)S(1)}, f32[512,512]{1,0:T(8,128)}, u32[]{:S(2)}) copy-start(f32[512,512]{1,0:T(8,128)} %table_ref.3) | copy-start | bytes 3145732
  24.4 2.1 %collective-permute-start.7 = (bf16[512,512]{1,0:T(8,128)(2,1)S(1)}, bf16[512,512]{1,0:T(8,128)(2,1)S(1)}, u32[]{:S(2)}, u32[]{:S(2)}) collective-permute-start(bf16[512,512]{1,0:T(8,128)(2,1)S(1)} %get-tuple-element.75), channel_id=1, source_target_pairs={{0,8},{1,9},{2,10},{3,11},{4,12},{5,13},{6,14},{7,15},{8,0},{9,1},... | collective-permute-start | bytes 1572872 | tf_op jit(solution)/shard_map/ppermute | solution.py:204
  25.7 6.7 %copy-start.3 = (f32[512,512]{1,0:T(8,128)S(1)}, f32[512,512]{1,0:T(8,128)}, u32[]{:S(2)}) copy-start(f32[512,512]{1,0:T(8,128)} %table_ref.2) | copy-start | bytes 3145732
  25.7 15.9 %collective-permute-start.20 = (bf16[528,512]{1,0:T(8,128)(2,1)S(1)}, bf16[528,512]{1,0:T(8,128)(2,1)S(1)}, u32[]{:S(2)}, u32[]{:S(2)}) collective-permute-start(bf16[528,512]{1,0:T(8,128)(2,1)S(1)} %shard_map.142), channel_id=1, source_target_pairs={{0,0},{1,3},{2,2},{3,5},{4,4},{5,7},{6,6},{7,1},{8,8},{9,11},{10,1... | collective-permute-start | bytes 1622024 | tf_op jit(solution)/shard_map/ppermute | solution.py:272
  26.7 9.0 %collective-permute-start.10 = (bf16[128,512]{1,0:T(8,128)(2,1)S(1)}, bf16[128,512]{1,0:T(8,128)(2,1)S(1)}, u32[]{:S(2)}, u32[]{:S(2)}) collective-permute-start(bf16[128,512]{1,0:T(8,128)(2,1)S(1)} %get-tuple-element.116), channel_id=1, source_target_pairs={{0,17},{1,16},{2,19},{3,18},{4,21},{5,20},{6,23},{7,22},{8,25},{9,... | collective-permute-start | bytes 393224 | tf_op jit(solution)/shard_map/ppermute | solution.py:204
  31.7 6.2 %collective-permute-start.9 = (bf16[128,512]{1,0:T(8,128)(2,1)S(1)}, bf16[128,512]{1,0:T(8,128)(2,1)S(1)}, u32[]{:S(2)}, u32[]{:S(2)}) collective-permute-start(bf16[128,512]{1,0:T(8,128)(2,1)S(1)} %get-tuple-element.117), channel_id=1, source_target_pairs={{0,16},{1,17},{2,18},{3,19},{4,20},{5,21},{6,22},{7,23},{8,24},{9,... | collective-permute-start | bytes 393224 | tf_op jit(solution)/shard_map/ppermute | solution.py:204
  32.2 5.7 %collective-permute-start.8 = (bf16[128,512]{1,0:T(8,128)(2,1)S(1)}, bf16[128,512]{1,0:T(8,128)(2,1)S(1)}, u32[]{:S(2)}, u32[]{:S(2)}) collective-permute-start(bf16[128,512]{1,0:T(8,128)(2,1)S(1)} %get-tuple-element.118), channel_id=1, source_target_pairs={{0,1},{1,0},{2,3},{3,2},{4,5},{5,4},{6,7},{7,6},{8,9},{9,8},{10,11... | collective-permute-start | bytes 393224 | tf_op jit(solution)/shard_map/ppermute | solution.py:204
  37.9 7.8 %copy-start.10 = (f32[32,512]{1,0:T(8,128)S(1)}, f32[32,512]{1,0:T(8,128)}, u32[]{:S(2)}) copy-start(f32[32,512]{1,0:T(8,128)} %param.16) | copy-start | bytes 196612
  37.9 7.8 %copy-start.11 = (f32[32,512]{1,0:T(8,128)S(1)}, f32[32,512]{1,0:T(8,128)}, u32[]{:S(2)}) copy-start(f32[32,512]{1,0:T(8,128)} %param.17) | copy-start | bytes 196612
  38.0 7.7 %collective-permute-start.11 = (bf16[32,512]{1,0:T(8,128)(2,1)S(1)}, bf16[32,512]{1,0:T(8,128)(2,1)S(1)}, u32[]{:S(2)}, u32[]{:S(2)}) collective-permute-start(bf16[32,512]{1,0:T(8,128)(2,1)S(1)} %get-tuple-element.123), channel_id=1, source_target_pairs={{0,4},{1,5},{2,6},{3,7},{4,0},{5,1},{6,2},{7,3},{8,12},{9,13},{10,... | collective-permute-start | bytes 98312 | tf_op jit(solution)/shard_map/ppermute | solution.py:204
  38.4 7.3 %collective-permute-start.13 = (bf16[32,512]{1,0:T(8,128)(2,1)S(1)}, bf16[32,512]{1,0:T(8,128)(2,1)S(1)}, u32[]{:S(2)}, u32[]{:S(2)}) collective-permute-start(bf16[32,512]{1,0:T(8,128)(2,1)S(1)} %get-tuple-element.124), channel_id=1, source_target_pairs={{0,6},{1,7},{2,4},{3,5},{4,2},{5,3},{6,0},{7,1},{8,14},{9,15},{10,... | collective-permute-start | bytes 98312 | tf_op jit(solution)/shard_map/ppermute | solution.py:204
  40.7 5.0 %collective-permute-start.12 = (bf16[32,512]{1,0:T(8,128)(2,1)S(1)}, bf16[32,512]{1,0:T(8,128)(2,1)S(1)}, u32[]{:S(2)}, u32[]{:S(2)}) collective-permute-start(bf16[32,512]{1,0:T(8,128)(2,1)S(1)} %get-tuple-element.125), channel_id=1, source_target_pairs={{0,2},{1,3},{2,0},{3,1},{4,6},{5,7},{6,4},{7,5},{8,10},{9,11},{10,... | collective-permute-start | bytes 98312 | tf_op jit(solution)/shard_map/ppermute | solution.py:204
  41.5 20.4 %collective-permute-start.21 = (bf16[528,512]{1,0:T(8,128)(2,1)S(1)}, bf16[528,512]{1,0:T(8,128)(2,1)S(1)}, u32[]{:S(2)}, u32[]{:S(2)}) collective-permute-start(bf16[528,512]{1,0:T(8,128)(2,1)S(1)} %collective-permute-done.20), channel_id=1, source_target_pairs={{0,1},{1,0},{2,3},{3,2},{4,5},{5,4},{6,7},{7,6},{8,9},{9,8},{10,11... | collective-permute-start | bytes 1622024 | tf_op jit(solution)/shard_map/ppermute | solution.py:273
  45.8 5.8 %collective-permute-start.16 = (bf16[32,512]{1,0:T(8,128)(2,1)S(1)}, bf16[32,512]{1,0:T(8,128)(2,1)S(1)}, u32[]{:S(2)}, u32[]{:S(2)}) collective-permute-start(bf16[32,512]{1,0:T(8,128)(2,1)S(1)} %get-tuple-element.108), channel_id=1, source_target_pairs={{0,6},{1,7},{2,4},{3,5},{4,2},{5,3},{6,0},{7,1},{8,14},{9,15},{10,... | collective-permute-start | bytes 98312 | tf_op jit(solution)/shard_map/ppermute | solution.py:204
  46.6 5.0 %collective-permute-start.15 = (bf16[32,512]{1,0:T(8,128)(2,1)S(1)}, bf16[32,512]{1,0:T(8,128)(2,1)S(1)}, u32[]{:S(2)}, u32[]{:S(2)}) collective-permute-start(bf16[32,512]{1,0:T(8,128)(2,1)S(1)} %get-tuple-element.108), channel_id=1, source_target_pairs={{0,2},{1,3},{2,0},{3,1},{4,6},{5,7},{6,4},{7,5},{8,10},{9,11},{10,... | collective-permute-start | bytes 98312 | tf_op jit(solution)/shard_map/ppermute | solution.py:204
  46.7 5.5 %collective-permute-start.14 = (bf16[32,512]{1,0:T(8,128)(2,1)S(1)}, bf16[32,512]{1,0:T(8,128)(2,1)S(1)}, u32[]{:S(2)}, u32[]{:S(2)}) collective-permute-start(bf16[32,512]{1,0:T(8,128)(2,1)S(1)} %get-tuple-element.108), channel_id=1, source_target_pairs={{0,4},{1,5},{2,6},{3,7},{4,0},{5,1},{6,2},{7,3},{8,12},{9,13},{10,... | collective-permute-start | bytes 98312 | tf_op jit(solution)/shard_map/ppermute | solution.py:204
  52.2 9.2 %collective-permute-start.19 = (bf16[128,512]{1,0:T(8,128)(2,1)S(1)}, bf16[128,512]{1,0:T(8,128)(2,1)S(1)}, u32[]{:S(2)}, u32[]{:S(2)}) collective-permute-start(bf16[128,512]{1,0:T(8,128)(2,1)S(1)} %pad_maximum_fusion.1), channel_id=1, source_target_pairs={{0,17},{1,16},{2,19},{3,18},{4,21},{5,20},{6,23},{7,22},{8,25},{9,... | collective-permute-start | bytes 393224 | tf_op jit(solution)/shard_map/ppermute | solution.py:204
  54.3 7.2 %collective-permute-start.18 = (bf16[128,512]{1,0:T(8,128)(2,1)S(1)}, bf16[128,512]{1,0:T(8,128)(2,1)S(1)}, u32[]{:S(2)}, u32[]{:S(2)}) collective-permute-start(bf16[128,512]{1,0:T(8,128)(2,1)S(1)} %pad_maximum_fusion.1), channel_id=1, source_target_pairs={{0,16},{1,17},{2,18},{3,19},{4,20},{5,21},{6,22},{7,23},{8,24},{9,... | collective-permute-start | bytes 393224 | tf_op jit(solution)/shard_map/ppermute | solution.py:204
  55.1 6.9 %collective-permute-start.17 = (bf16[128,512]{1,0:T(8,128)(2,1)S(1)}, bf16[128,512]{1,0:T(8,128)(2,1)S(1)}, u32[]{:S(2)}, u32[]{:S(2)}) collective-permute-start(bf16[128,512]{1,0:T(8,128)(2,1)S(1)} %pad_maximum_fusion.1), channel_id=1, source_target_pairs={{0,1},{1,0},{2,3},{3,2},{4,5},{5,4},{6,7},{7,6},{8,9},{9,8},{10,11... | collective-permute-start | bytes 393224 | tf_op jit(solution)/shard_map/ppermute | solution.py:204
  62.0 2.0 %collective-permute-start.22 = (bf16[512,512]{1,0:T(8,128)(2,1)S(1)}, bf16[512,512]{1,0:T(8,128)(2,1)S(1)}, u32[]{:S(2)}, u32[]{:S(2)}) collective-permute-start(bf16[512,512]{1,0:T(8,128)(2,1)S(1)} %constant_dynamic-update-slice_fusion.7.lo_ref), channel_id=1, source_target_pairs={{0,8},{1,9},{2,10},{3,11},{4,12},{5,13},{6,14},{7,15},{8,0},{9,1},... | collective-permute-start | bytes 1572872 | tf_op jit(solution)/shard_map/ppermute | solution.py:204
  66.6 2.0 %collective-permute-start.23 = (bf16[512,512]{1,0:T(8,128)(2,1)S(1)}, bf16[512,512]{1,0:T(8,128)(2,1)S(1)}, u32[]{:S(2)}, u32[]{:S(2)}) collective-permute-start(bf16[512,512]{1,0:T(8,128)(2,1)S(1)} %get-tuple-element.93), channel_id=1, source_target_pairs={{0,8},{1,9},{2,10},{3,11},{4,12},{5,13},{6,14},{7,15},{8,0},{9,1},... | collective-permute-start | bytes 1572872 | tf_op jit(solution)/shard_map/ppermute | solution.py:204
  68.7 6.6 %collective-permute-start.26 = (bf16[128,512]{1,0:T(8,128)(2,1)S(1)}, bf16[128,512]{1,0:T(8,128)(2,1)S(1)}, u32[]{:S(2)}, u32[]{:S(2)}) collective-permute-start(bf16[128,512]{1,0:T(8,128)(2,1)S(1)} %get-tuple-element.113), channel_id=1, source_target_pairs={{0,17},{1,16},{2,19},{3,18},{4,21},{5,20},{6,23},{7,22},{8,25},{9,... | collective-permute-start | bytes 393224 | tf_op jit(solution)/shard_map/ppermute | solution.py:204
  71.4 6.6 %collective-permute-start.25 = (bf16[128,512]{1,0:T(8,128)(2,1)S(1)}, bf16[128,512]{1,0:T(8,128)(2,1)S(1)}, u32[]{:S(2)}, u32[]{:S(2)}) collective-permute-start(bf16[128,512]{1,0:T(8,128)(2,1)S(1)} %get-tuple-element.114), channel_id=1, source_target_pairs={{0,16},{1,17},{2,18},{3,19},{4,20},{5,21},{6,22},{7,23},{8,24},{9,... | collective-permute-start | bytes 393224 | tf_op jit(solution)/shard_map/ppermute | solution.py:204
  72.0 6.1 %collective-permute-start.24 = (bf16[128,512]{1,0:T(8,128)(2,1)S(1)}, bf16[128,512]{1,0:T(8,128)(2,1)S(1)}, u32[]{:S(2)}, u32[]{:S(2)}) collective-permute-start(bf16[128,512]{1,0:T(8,128)(2,1)S(1)} %get-tuple-element.115), channel_id=1, source_target_pairs={{0,1},{1,0},{2,3},{3,2},{4,5},{5,4},{6,7},{7,6},{8,9},{9,8},{10,11... | collective-permute-start | bytes 393224 | tf_op jit(solution)/shard_map/ppermute | solution.py:204
  78.1 6.2 %collective-permute-start.29 = (bf16[32,512]{1,0:T(8,128)(2,1)S(1)}, bf16[32,512]{1,0:T(8,128)(2,1)S(1)}, u32[]{:S(2)}, u32[]{:S(2)}) collective-permute-start(bf16[32,512]{1,0:T(8,128)(2,1)S(1)} %get-tuple-element.120), channel_id=1, source_target_pairs={{0,6},{1,7},{2,4},{3,5},{4,2},{5,3},{6,0},{7,1},{8,14},{9,15},{10,... | collective-permute-start | bytes 98312 | tf_op jit(solution)/shard_map/ppermute | solution.py:204
  78.8 5.4 %collective-permute-start.28 = (bf16[32,512]{1,0:T(8,128)(2,1)S(1)}, bf16[32,512]{1,0:T(8,128)(2,1)S(1)}, u32[]{:S(2)}, u32[]{:S(2)}) collective-permute-start(bf16[32,512]{1,0:T(8,128)(2,1)S(1)} %get-tuple-element.121), channel_id=1, source_target_pairs={{0,2},{1,3},{2,0},{3,1},{4,6},{5,7},{6,4},{7,5},{8,10},{9,11},{10,... | collective-permute-start | bytes 98312 | tf_op jit(solution)/shard_map/ppermute | solution.py:204
  79.8 4.8 %collective-permute-start.27 = (bf16[32,512]{1,0:T(8,128)(2,1)S(1)}, bf16[32,512]{1,0:T(8,128)(2,1)S(1)}, u32[]{:S(2)}, u32[]{:S(2)}) collective-permute-start(bf16[32,512]{1,0:T(8,128)(2,1)S(1)} %get-tuple-element.122), channel_id=1, source_target_pairs={{0,4},{1,5},{2,6},{3,7},{4,0},{5,1},{6,2},{7,3},{8,12},{9,13},{10,... | collective-permute-start | bytes 98312 | tf_op jit(solution)/shard_map/ppermute | solution.py:204

commit v8 on v7

--- a/solution.py
+++ b/solution.py
@@ -79,15 +79,15 @@
 
 
 def score_kernel(
-    k, own, nneg, nat_ref, live_ref, rel_ref, lo_ref, hi_ref, h_ref, t_ref, tcol_ref, cnt_ref,
-    keep_ref, send_ref, w_ref, u_ref, gu_ref, rel_s, grad_s,
+    k, own, nneg, cuts, nat_ref, live_ref, rel_ref, lo_ref, hi_ref, h_ref, t_ref, tcol_ref, cnt_ref,
+    w_ref, u_ref, gu_ref, *rest,
 ):
+    grad_refs, (rel_s, grad_s) = rest[:cuts], rest[cuts:]
     edges, width = h_ref.shape
     blocks, rows = cnt_ref.shape[1:]
     size = edges // blocks
     relations = rel_s.shape[0] // width
     restore_relations(nat_ref, lo_ref, hi_ref, rel_s, own)
-    half = keep_ref.shape[0]
     for b in range(blocks):
         part = slice(b * size, (b + 1) * size)
         chosen = rel_s[pl.ds(pl.multiple_of(rel_ref[k, b] * width, width), width)]
@@ -111,15 +111,14 @@
             part = h_ref[b * size : (b + 1) * size]
             parts.append(jnp.where(rel_ref[k, b] == r, part, jnp.zeros_like(part)))
         grad_s[r * width : (r + 1) * width] = dot(jnp.concatenate(parts), gu, ROWS, ROWS).astype(BF16)
-    if own % PACK_ROWS:
-        keep_ref[...] = grad_s[:half]
-        send_ref[...] = grad_s[half:]
-        return
-    for part, ref in enumerate((keep_ref, send_ref)):
-        for j in range(half // own):
-            block = nat_ref[part * (half // own) + j]
-            rows_of = pl.ds(pl.multiple_of(block * own, own), own)
-            ref[j * own : (j + 1) * own] = grad_s[rows_of]
+    for i, ref in enumerate(grad_refs):
+        count = ref.shape[0]
+        if own % PACK_ROWS:
+            ref[...] = grad_s[i * count : (i + 1) * count]
+            continue
+        for j in range(count // own):
+            block = nat_ref[i * (count // own) + j]
+            ref[j * own : (j + 1) * own] = grad_s[pl.ds(pl.multiple_of(block * own, own), own)]
 
 
 def tail_kernel(w_ref, u_ref, table_ref, state_ref, out_ref):
@@ -203,13 +202,20 @@
     def swap(self, x, mask):
         return lax.ppermute(x, AXES, [(i, i ^ mask) for i in range(self.devices)])
 
-    def reduce_scatter(self, keep, send, hooks):
-        if (2 * keep.shape[0] // self.devices) % PACK_ROWS:
-            both = jnp.concatenate([keep, send])
+    def reduce_scatter(self, parts, hooks):
+        if sum(part.shape[0] for part in parts) // self.devices % PACK_ROWS:
+            both = jnp.concatenate(parts)
             both = both.reshape(self.devices, -1, both.shape[1])[self.block_of_slot]
-            keep, send = jnp.split(both.reshape(-1, both.shape[2]), 2)
-        parts = [keep, send]
+            parts = jnp.split(both.reshape(-1, both.shape[2]), len(parts))
+        if len(parts) > 2:
+            half = len(parts) // 2
+            mask = self.masks(self.stages[0])[0]
+            got = [self.swap(part, mask) for part in parts[half:]]
+            parts = [(a.astype(F32) + b.astype(F32)).astype(BF16) for a, b in zip(parts[:half], got)]
+            parts[0] = hooks["own"](parts[0])
         for i, stage in enumerate(self.stages):
+            if len(parts) != 1 << len(stage):
+                continue
             got = [self.swap(part, mask) for part, mask in zip(parts[1:], self.masks(stage))]
             pieces = parts[:1] + hooks.get(i, list)(got)
             if i + 1 == len(self.stages):
@@ -295,47 +301,47 @@
             head_vecs, tail_vecs, tail_col, counts, head_state, tail_state = held["prepared"]
         else:
             tail_vecs = held["tail"]
-        keep, send, weights, projected, edge_grad = call(
-            functools.partial(score_kernel, k, own, float(nneg)),
-            [
-                ((half, width), BF16),
-                ((half, width), BF16),
-                ((edges, rows), BF16),
-                ((edges, width), BF16),
-                ((edges, width), BF16),
-            ],
+        cuts = 2 if k == 0 else 2 << len(exchange.stages[1])
+        weights, projected, edge_grad, *terms = call(
+            functools.partial(score_kernel, k, own, float(nneg), cuts),
+            [((edges, rows), BF16), ((edges, width), BF16), ((edges, width), BF16)]
+            + [((all_rows // cuts, width), BF16)] * cuts,
             3, [pltpu.VMEM((all_rows, width), BF16), pltpu.VMEM((all_rows, width), BF16)], 5 * square,
             nat, block_counts, relation_ids, lo, hi, head_vecs, tail_vecs, tail_col, counts,
         )
-        head_outs = [(head_table.shape, F32)]
+
+        def update_heads(edge_grad, outs):
+            return call(
+                functools.partial(head_kernel, k, own, blocks), [(head_table.shape, F32), *outs],
+                2, [pltpu.VMEM((all_rows, width), BF16)], 4 * square,
+                nat, relation_ids, lo, hi, edge_grad, head_rows, head_table, head_state,
+            )
+
         if k == 0:
             (tail_new,) = call(
                 tail_kernel, [((rows + PACK_ROWS, width), BF16)], 0, [], square,
                 weights, projected, tail_table, tail_state,
             )
-            head_outs += [(head_state.shape, F32), ((edges, width), BF16)]
-        else:
-            (tail_new,) = call(
-                last_tail_kernel, [((rows, width), F32)], 0, [], square,
-                weights, projected, tail_vecs,
-            )
-        head_new = call(
-            functools.partial(head_kernel, k, own, blocks), head_outs,
-            2, [pltpu.VMEM((all_rows, width), BF16)], 4 * square,
-            nat, relation_ids, lo, hi, edge_grad, head_rows, head_table, head_state,
-        )
-        held["head"] = head_new
-        if k == 0:
             held["tail"] = rotate(tail_new)
-            grad = exchange.reduce_scatter(keep, send, {1: with_("head")})
+            held["head"] = update_heads(edge_grad, [(head_state.shape, F32), ((edges, width), BF16)])
+            grad = exchange.reduce_scatter(terms, {1: with_("head")})
             head_table, head_state, head_vecs = held["head"]
             gather_hooks = {1: with_("tail")}
         else:
-            held["tail"] = tail_new
-            grad = exchange.reduce_scatter(keep, send, {1: with_("head"), 2: with_("tail")})
+
+            def last_updates(part):
+                part, ready = lax.optimization_barrier((part, [weights, projected, edge_grad]))
+                held["tail"] = call(
+                    last_tail_kernel, [((rows, width), F32)], 0, [], square, *ready[:2], tail_vecs
+                )
+                held["head"] = update_heads(ready[2], [])
+                return part
+
+            hooks = {"own": last_updates, 1: lambda got: with_("head")(got[::-1])[::-1], 2: with_("tail")}
+            grad = exchange.reduce_scatter(terms, hooks)
         relation_state = relation_state + grad * grad
         relations = relations - RATE_RELATIONS * grad / (jnp.sqrt(relation_state) + EPSILON)
-    return (held["head"][0], held["tail"], relations)
+    return (held["head"][0], held["tail"][0], relations)
 
 
 def solution(mesh):

time: 85.6 us -> 85 us (level)
  waiting for transfers between devices: 23.6 us -> 22 us
  starting transfers between devices: 40.4 us -> 41.4 us
    ppermute x28 -> x31, waiting for transfers between devices: 23.6 us -> 22 us  [swap(): return lax.ppermute(x, AXES, [(i, i ^ mask) for i in range(self.devices)])]
    ppermute x28 -> x31, starting transfers between devices: 35.4 us -> 36.4 us  [swap(): return lax.ppermute(x, AXES, [(i, i ^ mask) for i in range(self.devices)])]
  transfers between devices with their start and end apart: 30 -> 33, of which waited for: 16 -> 15; matrix products, arithmetic and copies ran while one was open for 0% -> 1% of each run, Pallas kernels for 10% -> 10%
where the time goes in v8:
time: 85 us; the launch traced here: 84.6 us
  starting transfers between devices  41.4 us (49%)
  waiting for transfers between devices  22 us (26%)
  Pallas kernels  13.5 us (16%)
  local copies, waits for them, and re-layouts  4.85 us (6%)
  other arithmetic  2.07 us (2%)
  between operations  0.88 us (1%)
    ppermute x31, starting transfers between devices, swap(): return lax.ppermute(x, AXES, [(i, i ^ mask) for i in range(self.devices)])  36.4 us
    ppermute x31, waiting for transfers between devices, swap(): return lax.ppermute(x, AXES, [(i, i ^ mask) for i in range(self.devices)])  22 us
    pallas_call x7, Pallas kernels, call(): pl.pallas_call(kernel, out_shape=outs, in_specs=[SMEM] * smem + [VMEM] *...  13.5 us
    unnamed x39, local copies, waits for them, and re-layouts  4.83 us
    ppermute x1, starting transfers between devices, rotate(): return lax.ppermute(x, 'tail', [(i, i ^ 1) for i in range(tails)])  4.17 us
  transfers between devices with their start and end apart: 33, of which 15 were waited for; matrix products, arithmetic and copies ran while one was open for 1% of the time, Pallas kernels for 10%

profile of v8, /device:TPU:0, one launch (start us, length us, event | category | flops | bytes accessed | tf_op | source)
XLA Modules:
  0.0 84.6 jit_solution(902801678580562172)
XLA Ops:
  0.6 0.8 %constant_dynamic-update-slice_fusion.6 = (bf16[512,512]{1,0:T(8,128)(2,1)S(1)}, bf16[32,512]{1,0:T(8,128)(2,1)S(1)}) fusion(f32[32,512]{1,0:T(8,128)} %param.16), kind=kLoop, calls=%fused_computation.28 | loop fusion | flops 16383 | bytes 131072
  1.5 5.0 %collective-permute-start.2 = (bf16[32,512]{1,0:T(8,128)(2,1)S(1)}, bf16[32,512]{1,0:T(8,128)(2,1)S(1)}, u32[]{:S(2)}, u32[]{:S(2)}) collective-permute-start(bf16[32,512]{1,0:T(8,128)(2,1)S(1)} %get-tuple-element.131), channel_id=1, source_target_pairs={{0,6},{1,7},{2,4},{3,5},{4,2},{5,3},{6,0},{7,1},{8,14},{9,15},{10,... | collective-permute-start | bytes 98312 | tf_op jit(solution)/shard_map/ppermute | solution.py:203
  6.5 0.6 collective-permute-start
  7.2 1.3 %collective-permute-done.2 = bf16[32,512]{1,0:T(8,128)(2,1)S(1)} collective-permute-done((bf16[32,512]{1,0:T(8,128)(2,1)S(1)}, bf16[32,512]{1,0:T(8,128)(2,1)S(1)}, u32[]{:S(2)}, u32[]{:S(2)}) %collective-permute-start.2) | collective-permute-done | bytes 32800 | tf_op jit(solution)/shard_map/ppermute | solution.py:203
  8.4 2.0 %collective-permute-done.1 = bf16[32,512]{1,0:T(8,128)(2,1)S(1)} collective-permute-done((bf16[32,512]{1,0:T(8,128)(2,1)S(1)}, bf16[32,512]{1,0:T(8,128)(2,1)S(1)}, u32[]{:S(2)}, u32[]{:S(2)}) %collective-permute-start.1) | collective-permute-done | bytes 32800 | tf_op jit(solution)/shard_map/ppermute | solution.py:203
  10.4 1.0 %collective-permute-done = bf16[32,512]{1,0:T(8,128)(2,1)S(1)} collective-permute-done((bf16[32,512]{1,0:T(8,128)(2,1)S(1)}, bf16[32,512]{1,0:T(8,128)(2,1)S(1)}, u32[]{:S(2)}, u32[]{:S(2)}) %collective-permute-start) | collective-permute-done | bytes 32800 | tf_op jit(solution)/shard_map/ppermute | solution.py:203
  11.5 2.5 %collective-permute-start.5 = (bf16[128,512]{1,0:T(8,128)(2,1)S(1)}, bf16[128,512]{1,0:T(8,128)(2,1)S(1)}, u32[]{:S(2)}, u32[]{:S(2)}) collective-permute-start(bf16[128,512]{1,0:T(8,128)(2,1)S(1)} %pad_maximum_fusion), channel_id=1, source_target_pairs={{0,17},{1,16},{2,19},{3,18},{4,21},{5,20},{6,23},{7,22},{8,25},{9,... | collective-permute-start | bytes 393224 | tf_op jit(solution)/shard_map/ppermute | solution.py:203
  14.0 0.5 collective-permute-start.4
  14.5 0.5 collective-permute-start.3
  15.1 0.6 copy-done.4
  15.8 1.2 %copy-done = f32[512,512]{1,0:T(8,128)S(1)} copy-done((f32[512,512]{1,0:T(8,128)S(1)}, f32[512,512]{1,0:T(8,128)}, u32[]{:S(2)}) %copy-start) | copy-done | bytes 1048600
  17.0 1.2 %copy-done.2 = f32[512,512]{1,0:T(8,128)S(1)} copy-done((f32[512,512]{1,0:T(8,128)S(1)}, f32[512,512]{1,0:T(8,128)}, u32[]{:S(2)}) %copy-start.2) | copy-done | bytes 1048600
  18.2 0.7 shard_map.139
  19.0 0.6 collective-permute-done.4
  19.6 0.1 collective-permute-start.6
  19.7 0.6 copy-done.12
  20.4 0.1 copy.16.live_ref
  20.5 0.7 copy-done.13
  21.1 0.5 collective-permute-done.6.hi_ref
  21.6 0.2 copy-done.9
  21.8 2.6 %shard_map.140 = (bf16[512,512]{1,0:T(8,128)(2,1)S(1)}, bf16[512,512]{1,0:T(8,128)(2,1)S(1)}, bf16[512,512]{1,0:T(8,128)(2,1)S(1)}, bf16[512,512]{1,0:T(8,128)(2,1)S(1)}, bf16[512,512]{1,0:T(8,128)(2,1)S(1)}) custom-call(s32[32]{0:T(128)S(1)} %broadcast_xor_fusion.nat_ref, s32[2,1]{1,0:T(2,128)S(1)} %copy.16.live_ref, s32[2,4]{1,0:T(2,128)S(1)} %copy-done.9, ...), custom_call_target="tpu_custom_call" | custom-call | flops 1342177280 | bytes 5259432 | tf_op jit(solution)/shard_map/pallas_call | solution.py:169
  24.4 0.5 collective-permute-start.7
  25.0 0.7 shard_map.142
  25.7 0.8 collective-permute-start.20
  26.5 0.1 add_convert_fusion.4
  26.7 5.0 %collective-permute-start.10 = (bf16[128,512]{1,0:T(8,128)(2,1)S(1)}, bf16[128,512]{1,0:T(8,128)(2,1)S(1)}, u32[]{:S(2)}, u32[]{:S(2)}) collective-permute-start(bf16[128,512]{1,0:T(8,128)(2,1)S(1)} %get-tuple-element.132), channel_id=1, source_target_pairs={{0,17},{1,16},{2,19},{3,18},{4,21},{5,20},{6,23},{7,22},{8,25},{9,... | collective-permute-start | bytes 393224 | tf_op jit(solution)/shard_map/ppermute | solution.py:203
  31.7 0.5 collective-permute-start.9
  32.2 0.1 collective-permute-start.8
  32.3 2.2 %shard_map.141 = (f32[512,512]{1,0:T(8,128)S(1)}, f32[1,512]{1,0:T(1,128)S(1)}, bf16[512,512]{1,0:T(8,128)(2,1)S(1)}) custom-call(s32[32]{0:T(128)S(1)} %broadcast_xor_fusion.nat_ref, s32[2,4]{1,0:T(2,128)S(1)} %copy-done.9, bf16[512,512]{1,0:T(8,128)(2,1)S(1)} %constant_dynamic-update-slice_fusion.lo_ref, ...), custom_call_target="tpu_custom_call" | custom-call | flops 1073741824 | bytes 4202656 | tf_op jit(solution)/shard_map/pallas_call | solution.py:169
  34.6 1.0 %collective-permute-done.10 = bf16[128,512]{1,0:T(8,128)(2,1)S(1)} collective-permute-done((bf16[128,512]{1,0:T(8,128)(2,1)S(1)}, bf16[128,512]{1,0:T(8,128)(2,1)S(1)}, u32[]{:S(2)}, u32[]{:S(2)}) %collective-permute-start.10) | collective-permute-done | bytes 131104 | tf_op jit(solution)/shard_map/ppermute | solution.py:203
  35.6 2.3 %collective-permute-done.9 = bf16[128,512]{1,0:T(8,128)(2,1)S(1)} collective-permute-done((bf16[128,512]{1,0:T(8,128)(2,1)S(1)}, bf16[128,512]{1,0:T(8,128)(2,1)S(1)}, u32[]{:S(2)}, u32[]{:S(2)}) %collective-permute-start.9) | collective-permute-done | bytes 131104 | tf_op jit(solution)/shard_map/ppermute | solution.py:203
  38.0 0.4 collective-permute-start.11
  38.4 2.3 %collective-permute-start.13 = (bf16[32,512]{1,0:T(8,128)(2,1)S(1)}, bf16[32,512]{1,0:T(8,128)(2,1)S(1)}, u32[]{:S(2)}, u32[]{:S(2)}) collective-permute-start(bf16[32,512]{1,0:T(8,128)(2,1)S(1)} %get-tuple-element.140), channel_id=1, source_target_pairs={{0,6},{1,7},{2,4},{3,5},{4,2},{5,3},{6,0},{7,1},{8,14},{9,15},{10,... | collective-permute-start | bytes 98312 | tf_op jit(solution)/shard_map/ppermute | solution.py:203
  40.7 0.8 collective-permute-start.12
  41.5 4.2 %collective-permute-start.21 = (bf16[528,512]{1,0:T(8,128)(2,1)S(1)}, bf16[528,512]{1,0:T(8,128)(2,1)S(1)}, u32[]{:S(2)}, u32[]{:S(2)}) collective-permute-start(bf16[528,512]{1,0:T(8,128)(2,1)S(1)} %collective-permute-done.20), channel_id=1, source_target_pairs={{0,1},{1,0},{2,3},{3,2},{4,5},{5,4},{6,7},{7,6},{8,9},{9,8},{10,11... | collective-permute-start | bytes 1622024 | tf_op jit(solution)/shard_map/ppermute | solution.py:279
  45.7 0.1 constant_dynamic-update-slice_fusion.13
  45.8 0.8 collective-permute-start.16
  46.7 3.6 %collective-permute-start.14 = (bf16[32,512]{1,0:T(8,128)(2,1)S(1)}, bf16[32,512]{1,0:T(8,128)(2,1)S(1)}, u32[]{:S(2)}, u32[]{:S(2)}) collective-permute-start(bf16[32,512]{1,0:T(8,128)(2,1)S(1)} %get-tuple-element.128), channel_id=1, source_target_pairs={{0,4},{1,5},{2,6},{3,7},{4,0},{5,1},{6,2},{7,3},{8,12},{9,13},{10,... | collective-permute-start | bytes 98312 | tf_op jit(solution)/shard_map/ppermute | solution.py:203
  50.3 1.3 %collective-permute-done.16 = bf16[32,512]{1,0:T(8,128)(2,1)S(1)} collective-permute-done((bf16[32,512]{1,0:T(8,128)(2,1)S(1)}, bf16[32,512]{1,0:T(8,128)(2,1)S(1)}, u32[]{:S(2)}, u32[]{:S(2)}) %collective-permute-start.16) | collective-permute-done | bytes 32800 | tf_op jit(solution)/shard_map/ppermute | solution.py:203
  51.6 0.6 collective-permute-done.14
  52.2 2.1 %collective-permute-start.19 = (bf16[128,512]{1,0:T(8,128)(2,1)S(1)}, bf16[128,512]{1,0:T(8,128)(2,1)S(1)}, u32[]{:S(2)}, u32[]{:S(2)}) collective-permute-start(bf16[128,512]{1,0:T(8,128)(2,1)S(1)} %pad_maximum_fusion.1), channel_id=1, source_target_pairs={{0,17},{1,16},{2,19},{3,18},{4,21},{5,20},{6,23},{7,22},{8,25},{9,... | collective-permute-start | bytes 393224 | tf_op jit(solution)/shard_map/ppermute | solution.py:203
  54.3 0.8 collective-permute-start.18
  55.1 0.7 collective-permute-start.17
  55.7 5.7 %collective-permute-done.19 = bf16[128,512]{1,0:T(8,128)(2,1)S(1)} collective-permute-done((bf16[128,512]{1,0:T(8,128)(2,1)S(1)}, bf16[128,512]{1,0:T(8,128)(2,1)S(1)}, u32[]{:S(2)}, u32[]{:S(2)}) %collective-permute-start.19) | collective-permute-done | bytes 131104 | tf_op jit(solution)/shard_map/ppermute | solution.py:203
  61.4 0.5 collective-permute-done.17
  62.0 0.1 collective-permute-start.22
  62.1 1.9 %collective-permute-done.22.hi_ref = bf16[512,512]{1,0:T(8,128)(2,1)S(1)} collective-permute-done((bf16[512,512]{1,0:T(8,128)(2,1)S(1)}, bf16[512,512]{1,0:T(8,128)(2,1)S(1)}, u32[]{:S(2)}, u32[]{:S(2)}) %collective-permute-start.22) | collective-permute-done | bytes 524320 | tf_op jit(solution)/shard_map/ppermute | solution.py:203
  64.0 2.6 %shard_map.143 = (bf16[512,512]{1,0:T(8,128)(2,1)S(1)}, bf16[512,512]{1,0:T(8,128)(2,1)S(1)}, bf16[512,512]{1,0:T(8,128)(2,1)S(1)}, bf16[128,512]{1,0:T(8,128)(2...) custom-call(s32[32]{0:T(128)S(1)} %broadcast_xor_fusion.nat_ref, ...), custom_call_target="tpu_custom_call" | custom-call | flops 1342177280 | bytes 5275816 | tf_op jit(solution)/shard_map/pallas_call | solution.py:169
  66.6 0.2 collective-permute-start.23
  66.8 0.4 collective-permute-start.25
  67.1 0.1 collective-permute-start.27
  67.3 0.4 collective-permute-start.29
  67.7 0.3 collective-permute-done.23
  68.0 2.7 %collective-permute-start.24 = (bf16[128,512]{1,0:T(8,128)(2,1)S(1)}, bf16[128,512]{1,0:T(8,128)(2,1)S(1)}, u32[]{:S(2)}, u32[]{:S(2)}) collective-permute-start(bf16[128,512]{1,0:T(8,128)(2,1)S(1)} %add_convert_fusion.3), channel_id=1, source_target_pairs={{0,17},{1,16},{2,19},{3,18},{4,21},{5,20},{6,23},{7,22},{8,25},{9,... | collective-permute-start | bytes 393224 | tf_op jit(solution)/shard_map/ppermute | solution.py:203
  70.8 0.6 collective-permute-start.26
  71.4 0.3 collective-permute-start.28
  71.8 2.9 %shard_map.144 = f32[512,512]{1,0:T(8,128)} custom-call(s32[32]{0:T(128)S(1)} %broadcast_xor_fusion.nat_ref, s32[2,4]{1,0:T(2,128)S(1)} %copy-done.9, bf16[512,512]{1,0:T(8,128)(2,1)S(1)} %constant_dynamic-update-slice_fusion.7.lo_ref, bf16[512,512]{1,0:T(8,128)(2,1)S(1)} %collective-permute-done.22.hi_ref, bf16[512,512]{1,0:T(8,128)(2,1)S(1)} %get-tuple-element.113.gu_ref, ...), custom_call_target="tpu_custom_call" | custom-call | flops 1073741824 | bytes 3676320 | tf_op jit(solution)/shard_map/pallas_call | solution.py:169
  74.8 2.6 %collective-permute-done.26 = bf16[128,512]{1,0:T(8,128)(2,1)S(1)} collective-permute-done((bf16[128,512]{1,0:T(8,128)(2,1)S(1)}, bf16[128,512]{1,0:T(8,128)(2,1)S(1)}, u32[]{:S(2)}, u32[]{:S(2)}) %collective-permute-start.26) | collective-permute-done | bytes 131104 | tf_op jit(solution)/shard_map/ppermute | solution.py:203
  77.4 0.7 collective-permute-start.32
  78.1 1.0 %collective-permute-start.31 = (bf16[32,512]{1,0:T(8,128)(2,1)S(1)}, bf16[32,512]{1,0:T(8,128)(2,1)S(1)}, u32[]{:S(2)}, u32[]{:S(2)}) collective-permute-start(bf16[32,512]{1,0:T(8,128)(2,1)S(1)} %get-tuple-element.137), channel_id=1, source_target_pairs={{0,2},{1,3},{2,0},{3,1},{4,6},{5,7},{6,4},{7,5},{8,10},{9,11},{10,... | collective-permute-start | bytes 98312 | tf_op jit(solution)/shard_map/ppermute | solution.py:203
  79.1 2.8 %collective-permute-start.30 = (bf16[32,512]{1,0:T(8,128)(2,1)S(1)}, bf16[32,512]{1,0:T(8,128)(2,1)S(1)}, u32[]{:S(2)}, u32[]{:S(2)}) collective-permute-start(bf16[32,512]{1,0:T(8,128)(2,1)S(1)} %get-tuple-element.138), channel_id=1, source_target_pairs={{0,4},{1,5},{2,6},{3,7},{4,0},{5,1},{6,2},{7,3},{8,12},{9,13},{10,... | collective-permute-start | bytes 98312 | tf_op jit(solution)/shard_map/ppermute | solution.py:203
  81.9 1.7 %shard_map.145 = f32[512,512]{1,0:T(8,128)} custom-call(bf16[512,512]{1,0:T(8,128)(2,1)S(1)} %get-tuple-element.121.w_ref, bf16[512,512]{1,0:T(8,128)(2,1)S(1)} %get-tuple-element.122.u_ref, bf16[528,512]{1,0:T(8,128)(2,1)S(1)} %collective-permute-done.21.t_ref.packed_ref), custom_call_target="tpu_custom_call" | custom-call | flops 268435456 | bytes 2637824 | tf_op jit(solution)/shard_map/pallas_call | solution.py:169
  83.6 0.3 collective-permute-done.30
  83.9 0.7 divide_subtract_fusion
  (63 shorter events, 0.5 us)
Async XLA Ops:
  1.5 6.9 %collective-permute-start.2 = (bf16[32,512]{1,0:T(8,128)(2,1)S(1)}, bf16[32,512]{1,0:T(8,128)(2,1)S(1)}, u32[]{:S(2)}, u32[]{:S(2)}) collective-permute-start(bf16[32,512]{1,0:T(8,128)(2,1)S(1)} %get-tuple-element.131), channel_id=1, source_target_pairs={{0,6},{1,7},{2,4},{3,5},{4,2},{5,3},{6,0},{7,1},{8,14},{9,15},{10,... | collective-permute-start | bytes 98312 | tf_op jit(solution)/shard_map/ppermute | solution.py:203
  6.5 3.9 %collective-permute-start.1 = (bf16[32,512]{1,0:T(8,128)(2,1)S(1)}, bf16[32,512]{1,0:T(8,128)(2,1)S(1)}, u32[]{:S(2)}, u32[]{:S(2)}) collective-permute-start(bf16[32,512]{1,0:T(8,128)(2,1)S(1)} %get-tuple-element.131), channel_id=1, source_target_pairs={{0,2},{1,3},{2,0},{3,1},{4,6},{5,7},{6,4},{7,5},{8,10},{9,11},{10,... | collective-permute-start | bytes 98312 | tf_op jit(solution)/shard_map/ppermute | solution.py:203
  6.5 4.9 %collective-permute-start = (bf16[32,512]{1,0:T(8,128)(2,1)S(1)}, bf16[32,512]{1,0:T(8,128)(2,1)S(1)}, u32[]{:S(2)}, u32[]{:S(2)}) collective-permute-start(bf16[32,512]{1,0:T(8,128)(2,1)S(1)} %get-tuple-element.131), channel_id=1, source_target_pairs={{0,4},{1,5},{2,6},{3,7},{4,0},{5,1},{6,2},{7,3},{8,12},{9,13},{10,... | collective-permute-start | bytes 98312 | tf_op jit(solution)/shard_map/ppermute | solution.py:203
  11.5 7.5 %collective-permute-start.5 = (bf16[128,512]{1,0:T(8,128)(2,1)S(1)}, bf16[128,512]{1,0:T(8,128)(2,1)S(1)}, u32[]{:S(2)}, u32[]{:S(2)}) collective-permute-start(bf16[128,512]{1,0:T(8,128)(2,1)S(1)} %pad_maximum_fusion), channel_id=1, source_target_pairs={{0,17},{1,16},{2,19},{3,18},{4,21},{5,20},{6,23},{7,22},{8,25},{9,... | collective-permute-start | bytes 393224 | tf_op jit(solution)/shard_map/ppermute | solution.py:203
  14.0 5.6 %collective-permute-start.4 = (bf16[128,512]{1,0:T(8,128)(2,1)S(1)}, bf16[128,512]{1,0:T(8,128)(2,1)S(1)}, u32[]{:S(2)}, u32[]{:S(2)}) collective-permute-start(bf16[128,512]{1,0:T(8,128)(2,1)S(1)} %pad_maximum_fusion), channel_id=1, source_target_pairs={{0,16},{1,17},{2,18},{3,19},{4,20},{5,21},{6,22},{7,23},{8,24},{9,... | collective-permute-start | bytes 393224 | tf_op jit(solution)/shard_map/ppermute | solution.py:203
  14.5 5.1 %collective-permute-start.3 = (bf16[128,512]{1,0:T(8,128)(2,1)S(1)}, bf16[128,512]{1,0:T(8,128)(2,1)S(1)}, u32[]{:S(2)}, u32[]{:S(2)}) collective-permute-start(bf16[128,512]{1,0:T(8,128)(2,1)S(1)} %pad_maximum_fusion), channel_id=1, source_target_pairs={{0,1},{1,0},{2,3},{3,2},{4,5},{5,4},{6,7},{7,6},{8,9},{9,8},{10,11... | collective-permute-start | bytes 393224 | tf_op jit(solution)/shard_map/ppermute | solution.py:203
  15.0 0.7 copy-start.4
  15.0 0.7 copy-start.5
  15.0 0.7 copy-start.6
  15.0 0.7 copy-start.8
  15.1 0.7 copy-start.7
  15.8 1.2 %copy-start = (f32[512,512]{1,0:T(8,128)S(1)}, f32[512,512]{1,0:T(8,128)}, u32[]{:S(2)}) copy-start(f32[512,512]{1,0:T(8,128)} %table_ref.3) | copy-start | bytes 3145732
  17.0 1.2 %copy-start.2 = (f32[512,512]{1,0:T(8,128)S(1)}, f32[512,512]{1,0:T(8,128)}, u32[]{:S(2)}) copy-start(f32[512,512]{1,0:T(8,128)} %table_ref.2) | copy-start | bytes 3145732
  19.6 2.0 %collective-permute-start.6 = (bf16[512,512]{1,0:T(8,128)(2,1)S(1)}, bf16[512,512]{1,0:T(8,128)(2,1)S(1)}, u32[]{:S(2)}, u32[]{:S(2)}) collective-permute-start(bf16[512,512]{1,0:T(8,128)(2,1)S(1)} %constant_dynamic-update-slice_fusion.lo_ref), channel_id=1, source_target_pairs={{0,8},{1,9},{2,10},{3,11},{4,12},{5,13},{6,14},{7,15},{8,0},{9,1},... | collective-permute-start | bytes 1572872 | tf_op jit(solution)/shard_map/ppermute | solution.py:203
  19.7 0.7 copy-start.12
  20.5 0.7 copy-start.13
  21.1 0.7 copy-start.9
  21.1 3.8 %copy-start.1 = (f32[512,512]{1,0:T(8,128)S(1)}, f32[512,512]{1,0:T(8,128)}, u32[]{:S(2)}) copy-start(f32[512,512]{1,0:T(8,128)} %table_ref.3) | copy-start | bytes 3145732
  24.4 2.1 %collective-permute-start.7 = (bf16[512,512]{1,0:T(8,128)(2,1)S(1)}, bf16[512,512]{1,0:T(8,128)(2,1)S(1)}, u32[]{:S(2)}, u32[]{:S(2)}) collective-permute-start(bf16[512,512]{1,0:T(8,128)(2,1)S(1)} %get-tuple-element.85), channel_id=1, source_target_pairs={{0,8},{1,9},{2,10},{3,11},{4,12},{5,13},{6,14},{7,15},{8,0},{9,1},... | collective-permute-start | bytes 1572872 | tf_op jit(solution)/shard_map/ppermute | solution.py:203
  25.7 6.7 %copy-start.3 = (f32[512,512]{1,0:T(8,128)S(1)}, f32[512,512]{1,0:T(8,128)}, u32[]{:S(2)}) copy-start(f32[512,512]{1,0:T(8,128)} %table_ref.2) | copy-start | bytes 3145732
  25.7 15.9 %collective-permute-start.20 = (bf16[528,512]{1,0:T(8,128)(2,1)S(1)}, bf16[528,512]{1,0:T(8,128)(2,1)S(1)}, u32[]{:S(2)}, u32[]{:S(2)}) collective-permute-start(bf16[528,512]{1,0:T(8,128)(2,1)S(1)} %shard_map.142), channel_id=1, source_target_pairs={{0,0},{1,3},{2,2},{3,5},{4,4},{5,7},{6,6},{7,1},{8,8},{9,11},{10,1... | collective-permute-start | bytes 1622024 | tf_op jit(solution)/shard_map/ppermute | solution.py:278
  26.7 9.0 %collective-permute-start.10 = (bf16[128,512]{1,0:T(8,128)(2,1)S(1)}, bf16[128,512]{1,0:T(8,128)(2,1)S(1)}, u32[]{:S(2)}, u32[]{:S(2)}) collective-permute-start(bf16[128,512]{1,0:T(8,128)(2,1)S(1)} %get-tuple-element.132), channel_id=1, source_target_pairs={{0,17},{1,16},{2,19},{3,18},{4,21},{5,20},{6,23},{7,22},{8,25},{9,... | collective-permute-start | bytes 393224 | tf_op jit(solution)/shard_map/ppermute | solution.py:203
  31.7 6.2 %collective-permute-start.9 = (bf16[128,512]{1,0:T(8,128)(2,1)S(1)}, bf16[128,512]{1,0:T(8,128)(2,1)S(1)}, u32[]{:S(2)}, u32[]{:S(2)}) collective-permute-start(bf16[128,512]{1,0:T(8,128)(2,1)S(1)} %get-tuple-element.133), channel_id=1, source_target_pairs={{0,16},{1,17},{2,18},{3,19},{4,20},{5,21},{6,22},{7,23},{8,24},{9,... | collective-permute-start | bytes 393224 | tf_op jit(solution)/shard_map/ppermute | solution.py:203
  32.2 5.7 %collective-permute-start.8 = (bf16[128,512]{1,0:T(8,128)(2,1)S(1)}, bf16[128,512]{1,0:T(8,128)(2,1)S(1)}, u32[]{:S(2)}, u32[]{:S(2)}) collective-permute-start(bf16[128,512]{1,0:T(8,128)(2,1)S(1)} %get-tuple-element.134), channel_id=1, source_target_pairs={{0,1},{1,0},{2,3},{3,2},{4,5},{5,4},{6,7},{7,6},{8,9},{9,8},{10,11... | collective-permute-start | bytes 393224 | tf_op jit(solution)/shard_map/ppermute | solution.py:203
  37.9 7.8 %copy-start.10 = (f32[32,512]{1,0:T(8,128)S(1)}, f32[32,512]{1,0:T(8,128)}, u32[]{:S(2)}) copy-start(f32[32,512]{1,0:T(8,128)} %param.16) | copy-start | bytes 196612
  37.9 7.8 %copy-start.11 = (f32[32,512]{1,0:T(8,128)S(1)}, f32[32,512]{1,0:T(8,128)}, u32[]{:S(2)}) copy-start(f32[32,512]{1,0:T(8,128)} %param.17) | copy-start | bytes 196612
  38.0 7.7 %collective-permute-start.11 = (bf16[32,512]{1,0:T(8,128)(2,1)S(1)}, bf16[32,512]{1,0:T(8,128)(2,1)S(1)}, u32[]{:S(2)}, u32[]{:S(2)}) collective-permute-start(bf16[32,512]{1,0:T(8,128)(2,1)S(1)} %get-tuple-element.139), channel_id=1, source_target_pairs={{0,4},{1,5},{2,6},{3,7},{4,0},{5,1},{6,2},{7,3},{8,12},{9,13},{10,... | collective-permute-start | bytes 98312 | tf_op jit(solution)/shard_map/ppermute | solution.py:203
  38.4 7.3 %collective-permute-start.13 = (bf16[32,512]{1,0:T(8,128)(2,1)S(1)}, bf16[32,512]{1,0:T(8,128)(2,1)S(1)}, u32[]{:S(2)}, u32[]{:S(2)}) collective-permute-start(bf16[32,512]{1,0:T(8,128)(2,1)S(1)} %get-tuple-element.140), channel_id=1, source_target_pairs={{0,6},{1,7},{2,4},{3,5},{4,2},{5,3},{6,0},{7,1},{8,14},{9,15},{10,... | collective-permute-start | bytes 98312 | tf_op jit(solution)/shard_map/ppermute | solution.py:203
  40.7 5.0 %collective-permute-start.12 = (bf16[32,512]{1,0:T(8,128)(2,1)S(1)}, bf16[32,512]{1,0:T(8,128)(2,1)S(1)}, u32[]{:S(2)}, u32[]{:S(2)}) collective-permute-start(bf16[32,512]{1,0:T(8,128)(2,1)S(1)} %get-tuple-element.141), channel_id=1, source_target_pairs={{0,2},{1,3},{2,0},{3,1},{4,6},{5,7},{6,4},{7,5},{8,10},{9,11},{10,... | collective-permute-start | bytes 98312 | tf_op jit(solution)/shard_map/ppermute | solution.py:203
  41.5 20.4 %collective-permute-start.21 = (bf16[528,512]{1,0:T(8,128)(2,1)S(1)}, bf16[528,512]{1,0:T(8,128)(2,1)S(1)}, u32[]{:S(2)}, u32[]{:S(2)}) collective-permute-start(bf16[528,512]{1,0:T(8,128)(2,1)S(1)} %collective-permute-done.20), channel_id=1, source_target_pairs={{0,1},{1,0},{2,3},{3,2},{4,5},{5,4},{6,7},{7,6},{8,9},{9,8},{10,11... | collective-permute-start | bytes 1622024 | tf_op jit(solution)/shard_map/ppermute | solution.py:279
  45.8 5.8 %collective-permute-start.16 = (bf16[32,512]{1,0:T(8,128)(2,1)S(1)}, bf16[32,512]{1,0:T(8,128)(2,1)S(1)}, u32[]{:S(2)}, u32[]{:S(2)}) collective-permute-start(bf16[32,512]{1,0:T(8,128)(2,1)S(1)} %get-tuple-element.128), channel_id=1, source_target_pairs={{0,6},{1,7},{2,4},{3,5},{4,2},{5,3},{6,0},{7,1},{8,14},{9,15},{10,... | collective-permute-start | bytes 98312 | tf_op jit(solution)/shard_map/ppermute | solution.py:203
  46.6 5.0 %collective-permute-start.15 = (bf16[32,512]{1,0:T(8,128)(2,1)S(1)}, bf16[32,512]{1,0:T(8,128)(2,1)S(1)}, u32[]{:S(2)}, u32[]{:S(2)}) collective-permute-start(bf16[32,512]{1,0:T(8,128)(2,1)S(1)} %get-tuple-element.128), channel_id=1, source_target_pairs={{0,2},{1,3},{2,0},{3,1},{4,6},{5,7},{6,4},{7,5},{8,10},{9,11},{10,... | collective-permute-start | bytes 98312 | tf_op jit(solution)/shard_map/ppermute | solution.py:203
  46.7 5.5 %collective-permute-start.14 = (bf16[32,512]{1,0:T(8,128)(2,1)S(1)}, bf16[32,512]{1,0:T(8,128)(2,1)S(1)}, u32[]{:S(2)}, u32[]{:S(2)}) collective-permute-start(bf16[32,512]{1,0:T(8,128)(2,1)S(1)} %get-tuple-element.128), channel_id=1, source_target_pairs={{0,4},{1,5},{2,6},{3,7},{4,0},{5,1},{6,2},{7,3},{8,12},{9,13},{10,... | collective-permute-start | bytes 98312 | tf_op jit(solution)/shard_map/ppermute | solution.py:203
  52.2 9.2 %collective-permute-start.19 = (bf16[128,512]{1,0:T(8,128)(2,1)S(1)}, bf16[128,512]{1,0:T(8,128)(2,1)S(1)}, u32[]{:S(2)}, u32[]{:S(2)}) collective-permute-start(bf16[128,512]{1,0:T(8,128)(2,1)S(1)} %pad_maximum_fusion.1), channel_id=1, source_target_pairs={{0,17},{1,16},{2,19},{3,18},{4,21},{5,20},{6,23},{7,22},{8,25},{9,... | collective-permute-start | bytes 393224 | tf_op jit(solution)/shard_map/ppermute | solution.py:203
  54.3 7.2 %collective-permute-start.18 = (bf16[128,512]{1,0:T(8,128)(2,1)S(1)}, bf16[128,512]{1,0:T(8,128)(2,1)S(1)}, u32[]{:S(2)}, u32[]{:S(2)}) collective-permute-start(bf16[128,512]{1,0:T(8,128)(2,1)S(1)} %pad_maximum_fusion.1), channel_id=1, source_target_pairs={{0,16},{1,17},{2,18},{3,19},{4,20},{5,21},{6,22},{7,23},{8,24},{9,... | collective-permute-start | bytes 393224 | tf_op jit(solution)/shard_map/ppermute | solution.py:203
  55.1 6.9 %collective-permute-start.17 = (bf16[128,512]{1,0:T(8,128)(2,1)S(1)}, bf16[128,512]{1,0:T(8,128)(2,1)S(1)}, u32[]{:S(2)}, u32[]{:S(2)}) collective-permute-start(bf16[128,512]{1,0:T(8,128)(2,1)S(1)} %pad_maximum_fusion.1), channel_id=1, source_target_pairs={{0,1},{1,0},{2,3},{3,2},{4,5},{5,4},{6,7},{7,6},{8,9},{9,8},{10,11... | collective-permute-start | bytes 393224 | tf_op jit(solution)/shard_map/ppermute | solution.py:203
  62.0 2.0 %collective-permute-start.22 = (bf16[512,512]{1,0:T(8,128)(2,1)S(1)}, bf16[512,512]{1,0:T(8,128)(2,1)S(1)}, u32[]{:S(2)}, u32[]{:S(2)}) collective-permute-start(bf16[512,512]{1,0:T(8,128)(2,1)S(1)} %constant_dynamic-update-slice_fusion.7.lo_ref), channel_id=1, source_target_pairs={{0,8},{1,9},{2,10},{3,11},{4,12},{5,13},{6,14},{7,15},{8,0},{9,1},... | collective-permute-start | bytes 1572872 | tf_op jit(solution)/shard_map/ppermute | solution.py:203
  66.6 1.4 %collective-permute-start.23 = (bf16[128,512]{1,0:T(8,128)(2,1)S(1)}, bf16[128,512]{1,0:T(8,128)(2,1)S(1)}, u32[]{:S(2)}, u32[]{:S(2)}) collective-permute-start(bf16[128,512]{1,0:T(8,128)(2,1)S(1)} %get-tuple-element.103), channel_id=1, source_target_pairs={{0,8},{1,9},{2,10},{3,11},{4,12},{5,13},{6,14},{7,15},{8,0},{9,1},... | collective-permute-start | bytes 393224 | tf_op jit(solution)/shard_map/ppermute | solution.py:203
  66.8 4.0 %collective-permute-start.25 = (bf16[128,512]{1,0:T(8,128)(2,1)S(1)}, bf16[128,512]{1,0:T(8,128)(2,1)S(1)}, u32[]{:S(2)}, u32[]{:S(2)}) collective-permute-start(bf16[128,512]{1,0:T(8,128)(2,1)S(1)} %get-tuple-element.105), channel_id=1, source_target_pairs={{0,8},{1,9},{2,10},{3,11},{4,12},{5,13},{6,14},{7,15},{8,0},{9,1},... | collective-permute-start | bytes 393224 | tf_op jit(solution)/shard_map/ppermute | solution.py:203
  67.1 4.3 %collective-permute-start.27 = (bf16[128,512]{1,0:T(8,128)(2,1)S(1)}, bf16[128,512]{1,0:T(8,128)(2,1)S(1)}, u32[]{:S(2)}, u32[]{:S(2)}) collective-permute-start(bf16[128,512]{1,0:T(8,128)(2,1)S(1)} %get-tuple-element.107), channel_id=1, source_target_pairs={{0,8},{1,9},{2,10},{3,11},{4,12},{5,13},{6,14},{7,15},{8,0},{9,1},... | collective-permute-start | bytes 393224 | tf_op jit(solution)/shard_map/ppermute | solution.py:203
  67.3 4.5 %collective-permute-start.29 = (bf16[128,512]{1,0:T(8,128)(2,1)S(1)}, bf16[128,512]{1,0:T(8,128)(2,1)S(1)}, u32[]{:S(2)}, u32[]{:S(2)}) collective-permute-start(bf16[128,512]{1,0:T(8,128)(2,1)S(1)} %get-tuple-element.109), channel_id=1, source_target_pairs={{0,8},{1,9},{2,10},{3,11},{4,12},{5,13},{6,14},{7,15},{8,0},{9,1},... | collective-permute-start | bytes 393224 | tf_op jit(solution)/shard_map/ppermute | solution.py:203
  68.0 6.7 %collective-permute-start.24 = (bf16[128,512]{1,0:T(8,128)(2,1)S(1)}, bf16[128,512]{1,0:T(8,128)(2,1)S(1)}, u32[]{:S(2)}, u32[]{:S(2)}) collective-permute-start(bf16[128,512]{1,0:T(8,128)(2,1)S(1)} %add_convert_fusion.3), channel_id=1, source_target_pairs={{0,17},{1,16},{2,19},{3,18},{4,21},{5,20},{6,23},{7,22},{8,25},{9,... | collective-permute-start | bytes 393224 | tf_op jit(solution)/shard_map/ppermute | solution.py:203
  70.8 6.6 %collective-permute-start.26 = (bf16[128,512]{1,0:T(8,128)(2,1)S(1)}, bf16[128,512]{1,0:T(8,128)(2,1)S(1)}, u32[]{:S(2)}, u32[]{:S(2)}) collective-permute-start(bf16[128,512]{1,0:T(8,128)(2,1)S(1)} %add_convert_fusion.2), channel_id=1, source_target_pairs={{0,16},{1,17},{2,18},{3,19},{4,20},{5,21},{6,22},{7,23},{8,24},{9,... | collective-permute-start | bytes 393224 | tf_op jit(solution)/shard_map/ppermute | solution.py:203
  71.4 5.9 %collective-permute-start.28 = (bf16[128,512]{1,0:T(8,128)(2,1)S(1)}, bf16[128,512]{1,0:T(8,128)(2,1)S(1)}, u32[]{:S(2)}, u32[]{:S(2)}) collective-permute-start(bf16[128,512]{1,0:T(8,128)(2,1)S(1)} %add_convert_fusion.1), channel_id=1, source_target_pairs={{0,1},{1,0},{2,3},{3,2},{4,5},{5,4},{6,7},{7,6},{8,9},{9,8},{10,11... | collective-permute-start | bytes 393224 | tf_op jit(solution)/shard_map/ppermute | solution.py:203
  77.4 6.2 %collective-permute-start.32 = (bf16[32,512]{1,0:T(8,128)(2,1)S(1)}, bf16[32,512]{1,0:T(8,128)(2,1)S(1)}, u32[]{:S(2)}, u32[]{:S(2)}) collective-permute-start(bf16[32,512]{1,0:T(8,128)(2,1)S(1)} %get-tuple-element.136), channel_id=1, source_target_pairs={{0,6},{1,7},{2,4},{3,5},{4,2},{5,3},{6,0},{7,1},{8,14},{9,15},{10,... | collective-permute-start | bytes 98312 | tf_op jit(solution)/shard_map/ppermute | solution.py:203
  78.1 5.4 %collective-permute-start.31 = (bf16[32,512]{1,0:T(8,128)(2,1)S(1)}, bf16[32,512]{1,0:T(8,128)(2,1)S(1)}, u32[]{:S(2)}, u32[]{:S(2)}) collective-permute-start(bf16[32,512]{1,0:T(8,128)(2,1)S(1)} %get-tuple-element.137), channel_id=1, source_target_pairs={{0,2},{1,3},{2,0},{3,1},{4,6},{5,7},{6,4},{7,5},{8,10},{9,11},{10,... | collective-permute-start | bytes 98312 | tf_op jit(solution)/shard_map/ppermute | solution.py:203
  79.1 4.8 %collective-permute-start.30 = (bf16[32,512]{1,0:T(8,128)(2,1)S(1)}, bf16[32,512]{1,0:T(8,128)(2,1)S(1)}, u32[]{:S(2)}, u32[]{:S(2)}) collective-permute-start(bf16[32,512]{1,0:T(8,128)(2,1)S(1)} %get-tuple-element.138), channel_id=1, source_target_pairs={{0,4},{1,5},{2,6},{3,7},{4,0},{5,1},{6,2},{7,3},{8,12},{9,13},{10,... | collective-permute-start | bytes 98312 | tf_op jit(solution)/shard_map/ppermute | solution.py:203

commit v9 on v8

--- a/solution.py
+++ b/solution.py
@@ -60,11 +60,13 @@
 
 
 def prepare_kernel(
-    head_ref, tail_ref, hrows_ref, trows_ref, neg_ref, hstate_ref, tstate_ref,
-    h_ref, t_ref, tcol_ref, cnt_ref, hstate_out_ref, tstate_out_ref,
+    head_ref, tail_ref, hrows_ref, trows_ref, neg_ref, hstate_ref, tstate_ref, rel_ref, live_ref,
+    h_ref, t_ref, tcol_ref, cnt_ref, hstate_out_ref, tstate_out_ref, rel_out_ref, live_out_ref,
 ):
     hstate_out_ref[...] = hstate_ref[...]
     tstate_out_ref[...] = tstate_ref[...]
+    rel_out_ref[...] = rel_ref[...]
+    live_out_ref[...] = live_ref[...]
     buckets = hrows_ref.shape[0]
     blocks, nneg = neg_ref.shape[1:]
     pick = one_hot_rows(hrows_ref[0:1, :], head_ref.shape[0])
@@ -288,9 +290,11 @@
                 ((2, blocks, rows), F32),
                 (head_state.shape, F32),
                 (tail_state.shape, F32),
+                (relation_ids.shape, jnp.int32),
+                (block_counts.shape, jnp.int32),
             ],
             0, [], square,
-            head_table, tail_table, *held["indices"], head_state, tail_state,
+            head_table, tail_table, *held["indices"], head_state, tail_state, relation_ids, block_counts,
         )
         return with_("prepared")(got)
 
@@ -298,7 +302,8 @@
     for k in range(2):
         lo, hi = exchange.all_gather(relations.astype(BF16), gather_hooks)
         if k == 0:
-            head_vecs, tail_vecs, tail_col, counts, head_state, tail_state = held["prepared"]
+            head_vecs, tail_vecs, tail_col, counts, *small = held["prepared"]
+            head_state, tail_state, relation_ids, block_counts = small
         else:
             tail_vecs = held["tail"]
         cuts = 2 if k == 0 else 2 << len(exchange.stages[1])

time: 85 us -> 85.4 us (level)
  waiting for transfers between devices: 22 us -> 24.1 us
  starting transfers between devices: 41.4 us -> 40.5 us
    ppermute x31, waiting for transfers between devices: 22 us -> 24.1 us  [swap(): return lax.ppermute(x, AXES, [(i, i ^ mask) for i in range(self.devices)])]
  transfers between devices with their start and end apart: 33 -> 33, of which waited for: 15 -> 16; matrix products, arithmetic and copies ran while one was open for 1% -> 1% of each run, Pallas kernels for 10% -> 10%
where the time goes in v9:
time: 85.4 us; the launch traced here: 85.1 us
  starting transfers between devices  40.5 us (47%)
  waiting for transfers between devices  24.1 us (28%)
  Pallas kernels  13.5 us (16%)
  local copies, waits for them, and re-layouts  4.01 us (5%)
  other arithmetic  2.06 us (2%)
  between operations  0.88 us (1%)
    ppermute x31, starting transfers between devices, swap(): return lax.ppermute(x, AXES, [(i, i ^ mask) for i in range(self.devices)])  35.9 us
    ppermute x31, waiting for transfers between devices, swap(): return lax.ppermute(x, AXES, [(i, i ^ mask) for i in range(self.devices)])  24.1 us
    pallas_call x7, Pallas kernels, call(): pl.pallas_call(kernel, out_shape=outs, in_specs=[SMEM] * smem + [VMEM] *...  13.5 us
    unnamed x39, local copies, waits for them, and re-layouts  3.98 us
    ppermute x1, starting transfers between devices, rotate(): return lax.ppermute(x, 'tail', [(i, i ^ 1) for i in range(tails)])  3.8 us
  transfers between devices with their start and end apart: 33, of which 16 were waited for; matrix products, arithmetic and copies ran while one was open for 1% of the time, Pallas kernels for 10%

profile of v9, /device:TPU:0, one launch (start us, length us, event | category | flops | bytes accessed | tf_op | source)
XLA Modules:
  0.0 85.1 jit_solution(15601314678433829308)
XLA Ops:
  0.6 0.8 constant_dynamic-update-slice_fusion.6
  1.5 5.1 %collective-permute-start.2 = (bf16[32,512]{1,0:T(8,128)(2,1)S(1)}, bf16[32,512]{1,0:T(8,128)(2,1)S(1)}, u32[]{:S(2)}, u32[]{:S(2)}) collective-permute-start(bf16[32,512]{1,0:T(8,128)(2,1)S(1)} %get-tuple-element.139), channel_id=1, source_target_pairs={{0,6},{1,7},{2,4},{3,5},{4,2},{5,3},{6,0},{7,1},{8,14},{9,15},{10,... | collective-permute-start | bytes 98312 | tf_op jit(solution)/shard_map/ppermute | solution.py:205
  6.6 0.6 collective-permute-start
  7.2 0.1 copy.15.live_ref
  7.3 1.2 %collective-permute-done.2 = bf16[32,512]{1,0:T(8,128)(2,1)S(1)} collective-permute-done((bf16[32,512]{1,0:T(8,128)(2,1)S(1)}, bf16[32,512]{1,0:T(8,128)(2,1)S(1)}, u32[]{:S(2)}, u32[]{:S(2)}) %collective-permute-start.2) | collective-permute-done | bytes 32800 | tf_op jit(solution)/shard_map/ppermute | solution.py:205
  8.5 2.0 %collective-permute-done.1 = bf16[32,512]{1,0:T(8,128)(2,1)S(1)} collective-permute-done((bf16[32,512]{1,0:T(8,128)(2,1)S(1)}, bf16[32,512]{1,0:T(8,128)(2,1)S(1)}, u32[]{:S(2)}, u32[]{:S(2)}) %collective-permute-start.1) | collective-permute-done | bytes 32800 | tf_op jit(solution)/shard_map/ppermute | solution.py:205
  10.5 1.0 %collective-permute-done = bf16[32,512]{1,0:T(8,128)(2,1)S(1)} collective-permute-done((bf16[32,512]{1,0:T(8,128)(2,1)S(1)}, bf16[32,512]{1,0:T(8,128)(2,1)S(1)}, u32[]{:S(2)}, u32[]{:S(2)}) %collective-permute-start) | collective-permute-done | bytes 32800 | tf_op jit(solution)/shard_map/ppermute | solution.py:205
  11.5 2.5 %collective-permute-start.5 = (bf16[128,512]{1,0:T(8,128)(2,1)S(1)}, bf16[128,512]{1,0:T(8,128)(2,1)S(1)}, u32[]{:S(2)}, u32[]{:S(2)}) collective-permute-start(bf16[128,512]{1,0:T(8,128)(2,1)S(1)} %pad_maximum_fusion), channel_id=1, source_target_pairs={{0,17},{1,16},{2,19},{3,18},{4,21},{5,20},{6,23},{7,22},{8,25},{9,... | collective-permute-start | bytes 393224 | tf_op jit(solution)/shard_map/ppermute | solution.py:205
  14.0 0.5 collective-permute-start.4
  14.6 0.5 collective-permute-start.3
  15.2 0.6 copy-done.4
  15.9 1.2 %copy-done = f32[512,512]{1,0:T(8,128)S(1)} copy-done((f32[512,512]{1,0:T(8,128)S(1)}, f32[512,512]{1,0:T(8,128)}, u32[]{:S(2)}) %copy-start) | copy-done | bytes 1048600
  17.1 1.2 %copy-done.2 = f32[512,512]{1,0:T(8,128)S(1)} copy-done((f32[512,512]{1,0:T(8,128)S(1)}, f32[512,512]{1,0:T(8,128)}, u32[]{:S(2)}) %copy-start.2) | copy-done | bytes 1048600
  18.3 0.7 shard_map.139
  19.0 0.6 collective-permute-done.4
  19.7 0.1 collective-permute-start.6
  19.8 0.6 copy-done.13
  20.5 1.2 %collective-permute-done.6.hi_ref = bf16[512,512]{1,0:T(8,128)(2,1)S(1)} collective-permute-done((bf16[512,512]{1,0:T(8,128)(2,1)S(1)}, bf16[512,512]{1,0:T(8,128)(2,1)S(1)}, u32[]{:S(2)}, u32[]{:S(2)}) %collective-permute-start.6) | collective-permute-done | bytes 524320 | tf_op jit(solution)/shard_map/ppermute | solution.py:205
  21.7 2.6 %shard_map.140 = (bf16[512,512]{1,0:T(8,128)(2,1)S(1)}, bf16[512,512]{1,0:T(8,128)(2,1)S(1)}, bf16[512,512]{1,0:T(8,128)(2,1)S(1)}, bf16[512,512]{1,0:T(8,128)(2,1)S(1)}, bf16[512,512]{1,0:T(8,128)(2,1)S(1)}) custom-call(s32[32]{0:T(128)S(1)} %broadcast_xor_fusion.nat_ref, s32[2,1]{1,0:T(2,128)S(1)} %get-tuple-element.83.live_ref, ...), custom_call_target="tpu_custom_call" | custom-call | flops 1342177280 | bytes 5259432 | tf_op jit(solution)/shard_map/pallas_call | solution.py:171
  24.3 0.2 collective-permute-start.7
  24.5 0.7 shard_map.142
  25.2 0.8 collective-permute-start.20
  26.0 0.2 collective-permute-done.7
  26.3 0.1 add_convert_fusion.4
  26.4 4.8 %collective-permute-start.10 = (bf16[128,512]{1,0:T(8,128)(2,1)S(1)}, bf16[128,512]{1,0:T(8,128)(2,1)S(1)}, u32[]{:S(2)}, u32[]{:S(2)}) collective-permute-start(bf16[128,512]{1,0:T(8,128)(2,1)S(1)} %get-tuple-element.140), channel_id=1, source_target_pairs={{0,17},{1,16},{2,19},{3,18},{4,21},{5,20},{6,23},{7,22},{8,25},{9,... | collective-permute-start | bytes 393224 | tf_op jit(solution)/shard_map/ppermute | solution.py:205
  31.3 0.5 collective-permute-start.9
  31.8 0.1 collective-permute-start.8
  31.9 2.3 %shard_map.141 = (f32[512,512]{1,0:T(8,128)S(1)}, f32[1,512]{1,0:T(1,128)S(1)}, bf16[512,512]{1,0:T(8,128)(2,1)S(1)}) custom-call(s32[32]{0:T(128)S(1)} %broadcast_xor_fusion.nat_ref, s32[2,4]{1,0:T(2,128)S(1)} %get-tuple-element.84.rel_ref, bf16[512,512]{1,0:T(8,128)(2,1)S(1)} %constant_dynamic-update-slice_fusion.lo_ref, ...), custom_call_target="tpu_custom_call" | custom-call | flops 1073741824 | bytes 4202656 | tf_op jit(solution)/shard_map/pallas_call | solution.py:171
  34.2 1.0 %collective-permute-done.10 = bf16[128,512]{1,0:T(8,128)(2,1)S(1)} collective-permute-done((bf16[128,512]{1,0:T(8,128)(2,1)S(1)}, bf16[128,512]{1,0:T(8,128)(2,1)S(1)}, u32[]{:S(2)}, u32[]{:S(2)}) %collective-permute-start.10) | collective-permute-done | bytes 131104 | tf_op jit(solution)/shard_map/ppermute | solution.py:205
  35.2 2.6 %collective-permute-done.9 = bf16[128,512]{1,0:T(8,128)(2,1)S(1)} collective-permute-done((bf16[128,512]{1,0:T(8,128)(2,1)S(1)}, bf16[128,512]{1,0:T(8,128)(2,1)S(1)}, u32[]{:S(2)}, u32[]{:S(2)}) %collective-permute-start.9) | collective-permute-done | bytes 131104 | tf_op jit(solution)/shard_map/ppermute | solution.py:205
  37.8 0.1 add_convert_fusion.14
  37.9 0.4 collective-permute-start.11
  38.3 2.3 %collective-permute-start.13 = (bf16[32,512]{1,0:T(8,128)(2,1)S(1)}, bf16[32,512]{1,0:T(8,128)(2,1)S(1)}, u32[]{:S(2)}, u32[]{:S(2)}) collective-permute-start(bf16[32,512]{1,0:T(8,128)(2,1)S(1)} %get-tuple-element.148), channel_id=1, source_target_pairs={{0,6},{1,7},{2,4},{3,5},{4,2},{5,3},{6,0},{7,1},{8,14},{9,15},{10,... | collective-permute-start | bytes 98312 | tf_op jit(solution)/shard_map/ppermute | solution.py:205
  40.6 0.8 collective-permute-start.12
  41.4 3.8 %collective-permute-start.21 = (bf16[528,512]{1,0:T(8,128)(2,1)S(1)}, bf16[528,512]{1,0:T(8,128)(2,1)S(1)}, u32[]{:S(2)}, u32[]{:S(2)}) collective-permute-start(bf16[528,512]{1,0:T(8,128)(2,1)S(1)} %collective-permute-done.20), channel_id=1, source_target_pairs={{0,1},{1,0},{2,3},{3,2},{4,5},{5,4},{6,7},{7,6},{8,9},{9,8},{10,11... | collective-permute-start | bytes 1622024 | tf_op jit(solution)/shard_map/ppermute | solution.py:281
  45.3 0.1 constant_dynamic-update-slice_fusion.13
  45.3 1.2 %collective-permute-start.16 = (bf16[32,512]{1,0:T(8,128)(2,1)S(1)}, bf16[32,512]{1,0:T(8,128)(2,1)S(1)}, u32[]{:S(2)}, u32[]{:S(2)}) collective-permute-start(bf16[32,512]{1,0:T(8,128)(2,1)S(1)} %get-tuple-element.136), channel_id=1, source_target_pairs={{0,6},{1,7},{2,4},{3,5},{4,2},{5,3},{6,0},{7,1},{8,14},{9,15},{10,... | collective-permute-start | bytes 98312 | tf_op jit(solution)/shard_map/ppermute | solution.py:205
  46.5 3.3 %collective-permute-start.14 = (bf16[32,512]{1,0:T(8,128)(2,1)S(1)}, bf16[32,512]{1,0:T(8,128)(2,1)S(1)}, u32[]{:S(2)}, u32[]{:S(2)}) collective-permute-start(bf16[32,512]{1,0:T(8,128)(2,1)S(1)} %get-tuple-element.136), channel_id=1, source_target_pairs={{0,4},{1,5},{2,6},{3,7},{4,0},{5,1},{6,2},{7,3},{8,12},{9,13},{10,... | collective-permute-start | bytes 98312 | tf_op jit(solution)/shard_map/ppermute | solution.py:205
  49.8 1.3 %collective-permute-done.16 = bf16[32,512]{1,0:T(8,128)(2,1)S(1)} collective-permute-done((bf16[32,512]{1,0:T(8,128)(2,1)S(1)}, bf16[32,512]{1,0:T(8,128)(2,1)S(1)}, u32[]{:S(2)}, u32[]{:S(2)}) %collective-permute-start.16) | collective-permute-done | bytes 32800 | tf_op jit(solution)/shard_map/ppermute | solution.py:205
  51.1 0.6 collective-permute-done.14
  51.7 2.5 %collective-permute-start.19 = (bf16[128,512]{1,0:T(8,128)(2,1)S(1)}, bf16[128,512]{1,0:T(8,128)(2,1)S(1)}, u32[]{:S(2)}, u32[]{:S(2)}) collective-permute-start(bf16[128,512]{1,0:T(8,128)(2,1)S(1)} %pad_maximum_fusion.1), channel_id=1, source_target_pairs={{0,17},{1,16},{2,19},{3,18},{4,21},{5,20},{6,23},{7,22},{8,25},{9,... | collective-permute-start | bytes 393224 | tf_op jit(solution)/shard_map/ppermute | solution.py:205
  54.2 0.8 collective-permute-start.18
  55.0 0.3 collective-permute-start.17
  55.3 6.4 %collective-permute-done.19 = bf16[128,512]{1,0:T(8,128)(2,1)S(1)} collective-permute-done((bf16[128,512]{1,0:T(8,128)(2,1)S(1)}, bf16[128,512]{1,0:T(8,128)(2,1)S(1)}, u32[]{:S(2)}, u32[]{:S(2)}) %collective-permute-start.19) | collective-permute-done | bytes 131104 | tf_op jit(solution)/shard_map/ppermute | solution.py:205
  61.7 0.5 collective-permute-done.17
  62.2 0.1 collective-permute-start.22
  62.3 1.9 %collective-permute-done.22.hi_ref = bf16[512,512]{1,0:T(8,128)(2,1)S(1)} collective-permute-done((bf16[512,512]{1,0:T(8,128)(2,1)S(1)}, bf16[512,512]{1,0:T(8,128)(2,1)S(1)}, u32[]{:S(2)}, u32[]{:S(2)}) %collective-permute-start.22) | collective-permute-done | bytes 524320 | tf_op jit(solution)/shard_map/ppermute | solution.py:205
  64.2 2.6 %shard_map.143 = (bf16[512,512]{1,0:T(8,128)(2,1)S(1)}, bf16[512,512]{1,0:T(8,128)(2,1)S(1)}, bf16[512,512]{1,0:T(8,128)(2,1)S(1)}, bf16[128,512]{1,0:T(8,128)(2...) custom-call(s32[32]{0:T(128)S(1)} %broadcast_xor_fusion.nat_ref, ...), custom_call_target="tpu_custom_call" | custom-call | flops 1342177280 | bytes 5275816 | tf_op jit(solution)/shard_map/pallas_call | solution.py:171
  66.8 0.2 collective-permute-start.23
  67.0 0.4 collective-permute-start.25
  67.4 0.1 collective-permute-start.27
  67.5 0.4 collective-permute-start.29
  67.9 0.3 collective-permute-done.23
  68.3 2.7 %collective-permute-start.24 = (bf16[128,512]{1,0:T(8,128)(2,1)S(1)}, bf16[128,512]{1,0:T(8,128)(2,1)S(1)}, u32[]{:S(2)}, u32[]{:S(2)}) collective-permute-start(bf16[128,512]{1,0:T(8,128)(2,1)S(1)} %add_convert_fusion.3), channel_id=1, source_target_pairs={{0,17},{1,16},{2,19},{3,18},{4,21},{5,20},{6,23},{7,22},{8,25},{9,... | collective-permute-start | bytes 393224 | tf_op jit(solution)/shard_map/ppermute | solution.py:205
  71.1 0.6 collective-permute-start.26
  71.7 0.3 collective-permute-start.28
  72.1 2.9 %shard_map.144 = f32[512,512]{1,0:T(8,128)} custom-call(s32[32]{0:T(128)S(1)} %broadcast_xor_fusion.nat_ref, s32[2,4]{1,0:T(2,128)S(1)} %get-tuple-element.84.rel_ref, bf16[512,512]{1,0:T(8,128)(2,1)S(1)} %constant_dynamic-update-slice_fusion.7.lo_ref, bf16[512,512]{1,0:T(8,128)(2,1)S(1)} %collective-permute-done.22.hi_ref, ...), custom_call_target="tpu_custom_call" | custom-call | flops 1073741824 | bytes 3676320 | tf_op jit(solution)/shard_map/pallas_call | solution.py:171
  75.0 2.6 %collective-permute-done.26 = bf16[128,512]{1,0:T(8,128)(2,1)S(1)} collective-permute-done((bf16[128,512]{1,0:T(8,128)(2,1)S(1)}, bf16[128,512]{1,0:T(8,128)(2,1)S(1)}, u32[]{:S(2)}, u32[]{:S(2)}) %collective-permute-start.26) | collective-permute-done | bytes 131104 | tf_op jit(solution)/shard_map/ppermute | solution.py:205
  77.7 0.3 collective-permute-start.32
  78.0 1.0 %collective-permute-start.31 = (bf16[32,512]{1,0:T(8,128)(2,1)S(1)}, bf16[32,512]{1,0:T(8,128)(2,1)S(1)}, u32[]{:S(2)}, u32[]{:S(2)}) collective-permute-start(bf16[32,512]{1,0:T(8,128)(2,1)S(1)} %get-tuple-element.145), channel_id=1, source_target_pairs={{0,2},{1,3},{2,0},{3,1},{4,6},{5,7},{6,4},{7,5},{8,10},{9,11},{10,... | collective-permute-start | bytes 98312 | tf_op jit(solution)/shard_map/ppermute | solution.py:205
  79.0 3.2 %collective-permute-start.30 = (bf16[32,512]{1,0:T(8,128)(2,1)S(1)}, bf16[32,512]{1,0:T(8,128)(2,1)S(1)}, u32[]{:S(2)}, u32[]{:S(2)}) collective-permute-start(bf16[32,512]{1,0:T(8,128)(2,1)S(1)} %get-tuple-element.146), channel_id=1, source_target_pairs={{0,4},{1,5},{2,6},{3,7},{4,0},{5,1},{6,2},{7,3},{8,12},{9,13},{10,... | collective-permute-start | bytes 98312 | tf_op jit(solution)/shard_map/ppermute | solution.py:205
  82.2 1.7 %shard_map.145 = f32[512,512]{1,0:T(8,128)} custom-call(bf16[512,512]{1,0:T(8,128)(2,1)S(1)} %get-tuple-element.129.w_ref, bf16[512,512]{1,0:T(8,128)(2,1)S(1)} %get-tuple-element.130.u_ref, bf16[528,512]{1,0:T(8,128)(2,1)S(1)} %collective-permute-done.21.t_ref.packed_ref), custom_call_target="tpu_custom_call" | custom-call | flops 268435456 | bytes 2637824 | tf_op jit(solution)/shard_map/pallas_call | solution.py:171
  83.8 0.5 collective-permute-done.30
  84.4 0.7 divide_subtract_fusion
  (63 shorter events, 0.5 us)
Async XLA Ops:
  1.5 5.8 %copy-start.12 = (s32[2,1]{0,1:T(1,128)S(1)}, s32[2,1]{0,1:T(1,128)}, u32[]{:S(2)}) copy-start(s32[2,1]{0,1:T(1,128)} %param.22) | copy-start | bytes 28
  1.5 7.0 %collective-permute-start.2 = (bf16[32,512]{1,0:T(8,128)(2,1)S(1)}, bf16[32,512]{1,0:T(8,128)(2,1)S(1)}, u32[]{:S(2)}, u32[]{:S(2)}) collective-permute-start(bf16[32,512]{1,0:T(8,128)(2,1)S(1)} %get-tuple-element.139), channel_id=1, source_target_pairs={{0,6},{1,7},{2,4},{3,5},{4,2},{5,3},{6,0},{7,1},{8,14},{9,15},{10,... | collective-permute-start | bytes 98312 | tf_op jit(solution)/shard_map/ppermute | solution.py:205
  6.6 3.9 %collective-permute-start.1 = (bf16[32,512]{1,0:T(8,128)(2,1)S(1)}, bf16[32,512]{1,0:T(8,128)(2,1)S(1)}, u32[]{:S(2)}, u32[]{:S(2)}) collective-permute-start(bf16[32,512]{1,0:T(8,128)(2,1)S(1)} %get-tuple-element.139), channel_id=1, source_target_pairs={{0,2},{1,3},{2,0},{3,1},{4,6},{5,7},{6,4},{7,5},{8,10},{9,11},{10,... | collective-permute-start | bytes 98312 | tf_op jit(solution)/shard_map/ppermute | solution.py:205
  6.6 4.9 %collective-permute-start = (bf16[32,512]{1,0:T(8,128)(2,1)S(1)}, bf16[32,512]{1,0:T(8,128)(2,1)S(1)}, u32[]{:S(2)}, u32[]{:S(2)}) collective-permute-start(bf16[32,512]{1,0:T(8,128)(2,1)S(1)} %get-tuple-element.139), channel_id=1, source_target_pairs={{0,4},{1,5},{2,6},{3,7},{4,0},{5,1},{6,2},{7,3},{8,12},{9,13},{10,... | collective-permute-start | bytes 98312 | tf_op jit(solution)/shard_map/ppermute | solution.py:205
  11.5 7.5 %collective-permute-start.5 = (bf16[128,512]{1,0:T(8,128)(2,1)S(1)}, bf16[128,512]{1,0:T(8,128)(2,1)S(1)}, u32[]{:S(2)}, u32[]{:S(2)}) collective-permute-start(bf16[128,512]{1,0:T(8,128)(2,1)S(1)} %pad_maximum_fusion), channel_id=1, source_target_pairs={{0,17},{1,16},{2,19},{3,18},{4,21},{5,20},{6,23},{7,22},{8,25},{9,... | collective-permute-start | bytes 393224 | tf_op jit(solution)/shard_map/ppermute | solution.py:205
  14.0 5.6 %collective-permute-start.4 = (bf16[128,512]{1,0:T(8,128)(2,1)S(1)}, bf16[128,512]{1,0:T(8,128)(2,1)S(1)}, u32[]{:S(2)}, u32[]{:S(2)}) collective-permute-start(bf16[128,512]{1,0:T(8,128)(2,1)S(1)} %pad_maximum_fusion), channel_id=1, source_target_pairs={{0,16},{1,17},{2,18},{3,19},{4,20},{5,21},{6,22},{7,23},{8,24},{9,... | collective-permute-start | bytes 393224 | tf_op jit(solution)/shard_map/ppermute | solution.py:205
  14.6 5.1 %collective-permute-start.3 = (bf16[128,512]{1,0:T(8,128)(2,1)S(1)}, bf16[128,512]{1,0:T(8,128)(2,1)S(1)}, u32[]{:S(2)}, u32[]{:S(2)}) collective-permute-start(bf16[128,512]{1,0:T(8,128)(2,1)S(1)} %pad_maximum_fusion), channel_id=1, source_target_pairs={{0,1},{1,0},{2,3},{3,2},{4,5},{5,4},{6,7},{7,6},{8,9},{9,8},{10,11... | collective-permute-start | bytes 393224 | tf_op jit(solution)/shard_map/ppermute | solution.py:205
  15.1 0.7 copy-start.4
  15.1 0.7 copy-start.5
  15.1 0.7 copy-start.6
  15.1 0.7 copy-start.8
  15.1 0.7 copy-start.7
  15.1 0.7 copy-start.9
  15.9 1.2 %copy-start = (f32[512,512]{1,0:T(8,128)S(1)}, f32[512,512]{1,0:T(8,128)}, u32[]{:S(2)}) copy-start(f32[512,512]{1,0:T(8,128)} %table_ref.3) | copy-start | bytes 3145732
  17.1 1.2 %copy-start.2 = (f32[512,512]{1,0:T(8,128)S(1)}, f32[512,512]{1,0:T(8,128)}, u32[]{:S(2)}) copy-start(f32[512,512]{1,0:T(8,128)} %table_ref.2) | copy-start | bytes 3145732
  19.7 2.0 %collective-permute-start.6 = (bf16[512,512]{1,0:T(8,128)(2,1)S(1)}, bf16[512,512]{1,0:T(8,128)(2,1)S(1)}, u32[]{:S(2)}, u32[]{:S(2)}) collective-permute-start(bf16[512,512]{1,0:T(8,128)(2,1)S(1)} %constant_dynamic-update-slice_fusion.lo_ref), channel_id=1, source_target_pairs={{0,8},{1,9},{2,10},{3,11},{4,12},{5,13},{6,14},{7,15},{8,0},{9,1},... | collective-permute-start | bytes 1572872 | tf_op jit(solution)/shard_map/ppermute | solution.py:205
  19.8 0.7 copy-start.13
  20.5 4.1 %copy-start.1 = (f32[512,512]{1,0:T(8,128)S(1)}, f32[512,512]{1,0:T(8,128)}, u32[]{:S(2)}) copy-start(f32[512,512]{1,0:T(8,128)} %table_ref.3) | copy-start | bytes 3145732
  24.3 2.0 %collective-permute-start.7 = (bf16[512,512]{1,0:T(8,128)(2,1)S(1)}, bf16[512,512]{1,0:T(8,128)(2,1)S(1)}, u32[]{:S(2)}, u32[]{:S(2)}) collective-permute-start(bf16[512,512]{1,0:T(8,128)(2,1)S(1)} %get-tuple-element.93), channel_id=1, source_target_pairs={{0,8},{1,9},{2,10},{3,11},{4,12},{5,13},{6,14},{7,15},{8,0},{9,1},... | collective-permute-start | bytes 1572872 | tf_op jit(solution)/shard_map/ppermute | solution.py:205
  25.2 6.7 %copy-start.3 = (f32[512,512]{1,0:T(8,128)S(1)}, f32[512,512]{1,0:T(8,128)}, u32[]{:S(2)}) copy-start(f32[512,512]{1,0:T(8,128)} %table_ref.2) | copy-start | bytes 3145732
  25.2 16.2 %collective-permute-start.20 = (bf16[528,512]{1,0:T(8,128)(2,1)S(1)}, bf16[528,512]{1,0:T(8,128)(2,1)S(1)}, u32[]{:S(2)}, u32[]{:S(2)}) collective-permute-start(bf16[528,512]{1,0:T(8,128)(2,1)S(1)} %shard_map.142), channel_id=1, source_target_pairs={{0,0},{1,3},{2,2},{3,5},{4,4},{5,7},{6,6},{7,1},{8,8},{9,11},{10,1... | collective-permute-start | bytes 1622024 | tf_op jit(solution)/shard_map/ppermute | solution.py:280
  26.4 8.8 %collective-permute-start.10 = (bf16[128,512]{1,0:T(8,128)(2,1)S(1)}, bf16[128,512]{1,0:T(8,128)(2,1)S(1)}, u32[]{:S(2)}, u32[]{:S(2)}) collective-permute-start(bf16[128,512]{1,0:T(8,128)(2,1)S(1)} %get-tuple-element.140), channel_id=1, source_target_pairs={{0,17},{1,16},{2,19},{3,18},{4,21},{5,20},{6,23},{7,22},{8,25},{9,... | collective-permute-start | bytes 393224 | tf_op jit(solution)/shard_map/ppermute | solution.py:205
  31.3 6.5 %collective-permute-start.9 = (bf16[128,512]{1,0:T(8,128)(2,1)S(1)}, bf16[128,512]{1,0:T(8,128)(2,1)S(1)}, u32[]{:S(2)}, u32[]{:S(2)}) collective-permute-start(bf16[128,512]{1,0:T(8,128)(2,1)S(1)} %get-tuple-element.141), channel_id=1, source_target_pairs={{0,16},{1,17},{2,18},{3,19},{4,20},{5,21},{6,22},{7,23},{8,24},{9,... | collective-permute-start | bytes 393224 | tf_op jit(solution)/shard_map/ppermute | solution.py:205
  31.8 6.0 %collective-permute-start.8 = (bf16[128,512]{1,0:T(8,128)(2,1)S(1)}, bf16[128,512]{1,0:T(8,128)(2,1)S(1)}, u32[]{:S(2)}, u32[]{:S(2)}) collective-permute-start(bf16[128,512]{1,0:T(8,128)(2,1)S(1)} %get-tuple-element.142), channel_id=1, source_target_pairs={{0,1},{1,0},{2,3},{3,2},{4,5},{5,4},{6,7},{7,6},{8,9},{9,8},{10,11... | collective-permute-start | bytes 393224 | tf_op jit(solution)/shard_map/ppermute | solution.py:205
  37.8 7.4 %copy-start.10 = (f32[32,512]{1,0:T(8,128)S(1)}, f32[32,512]{1,0:T(8,128)}, u32[]{:S(2)}) copy-start(f32[32,512]{1,0:T(8,128)} %param.16) | copy-start | bytes 196612
  37.8 7.4 %copy-start.11 = (f32[32,512]{1,0:T(8,128)S(1)}, f32[32,512]{1,0:T(8,128)}, u32[]{:S(2)}) copy-start(f32[32,512]{1,0:T(8,128)} %param.17) | copy-start | bytes 196612
  37.9 7.4 %collective-permute-start.11 = (bf16[32,512]{1,0:T(8,128)(2,1)S(1)}, bf16[32,512]{1,0:T(8,128)(2,1)S(1)}, u32[]{:S(2)}, u32[]{:S(2)}) collective-permute-start(bf16[32,512]{1,0:T(8,128)(2,1)S(1)} %get-tuple-element.147), channel_id=1, source_target_pairs={{0,4},{1,5},{2,6},{3,7},{4,0},{5,1},{6,2},{7,3},{8,12},{9,13},{10,... | collective-permute-start | bytes 98312 | tf_op jit(solution)/shard_map/ppermute | solution.py:205
  38.3 6.9 %collective-permute-start.13 = (bf16[32,512]{1,0:T(8,128)(2,1)S(1)}, bf16[32,512]{1,0:T(8,128)(2,1)S(1)}, u32[]{:S(2)}, u32[]{:S(2)}) collective-permute-start(bf16[32,512]{1,0:T(8,128)(2,1)S(1)} %get-tuple-element.148), channel_id=1, source_target_pairs={{0,6},{1,7},{2,4},{3,5},{4,2},{5,3},{6,0},{7,1},{8,14},{9,15},{10,... | collective-permute-start | bytes 98312 | tf_op jit(solution)/shard_map/ppermute | solution.py:205
  40.6 4.6 %collective-permute-start.12 = (bf16[32,512]{1,0:T(8,128)(2,1)S(1)}, bf16[32,512]{1,0:T(8,128)(2,1)S(1)}, u32[]{:S(2)}, u32[]{:S(2)}) collective-permute-start(bf16[32,512]{1,0:T(8,128)(2,1)S(1)} %get-tuple-element.149), channel_id=1, source_target_pairs={{0,2},{1,3},{2,0},{3,1},{4,6},{5,7},{6,4},{7,5},{8,10},{9,11},{10,... | collective-permute-start | bytes 98312 | tf_op jit(solution)/shard_map/ppermute | solution.py:205
  41.4 20.8 %collective-permute-start.21 = (bf16[528,512]{1,0:T(8,128)(2,1)S(1)}, bf16[528,512]{1,0:T(8,128)(2,1)S(1)}, u32[]{:S(2)}, u32[]{:S(2)}) collective-permute-start(bf16[528,512]{1,0:T(8,128)(2,1)S(1)} %collective-permute-done.20), channel_id=1, source_target_pairs={{0,1},{1,0},{2,3},{3,2},{4,5},{5,4},{6,7},{7,6},{8,9},{9,8},{10,11... | collective-permute-start | bytes 1622024 | tf_op jit(solution)/shard_map/ppermute | solution.py:281
  45.3 5.8 %collective-permute-start.16 = (bf16[32,512]{1,0:T(8,128)(2,1)S(1)}, bf16[32,512]{1,0:T(8,128)(2,1)S(1)}, u32[]{:S(2)}, u32[]{:S(2)}) collective-permute-start(bf16[32,512]{1,0:T(8,128)(2,1)S(1)} %get-tuple-element.136), channel_id=1, source_target_pairs={{0,6},{1,7},{2,4},{3,5},{4,2},{5,3},{6,0},{7,1},{8,14},{9,15},{10,... | collective-permute-start | bytes 98312 | tf_op jit(solution)/shard_map/ppermute | solution.py:205
  46.5 4.6 %collective-permute-start.15 = (bf16[32,512]{1,0:T(8,128)(2,1)S(1)}, bf16[32,512]{1,0:T(8,128)(2,1)S(1)}, u32[]{:S(2)}, u32[]{:S(2)}) collective-permute-start(bf16[32,512]{1,0:T(8,128)(2,1)S(1)} %get-tuple-element.136), channel_id=1, source_target_pairs={{0,2},{1,3},{2,0},{3,1},{4,6},{5,7},{6,4},{7,5},{8,10},{9,11},{10,... | collective-permute-start | bytes 98312 | tf_op jit(solution)/shard_map/ppermute | solution.py:205
  46.5 5.1 %collective-permute-start.14 = (bf16[32,512]{1,0:T(8,128)(2,1)S(1)}, bf16[32,512]{1,0:T(8,128)(2,1)S(1)}, u32[]{:S(2)}, u32[]{:S(2)}) collective-permute-start(bf16[32,512]{1,0:T(8,128)(2,1)S(1)} %get-tuple-element.136), channel_id=1, source_target_pairs={{0,4},{1,5},{2,6},{3,7},{4,0},{5,1},{6,2},{7,3},{8,12},{9,13},{10,... | collective-permute-start | bytes 98312 | tf_op jit(solution)/shard_map/ppermute | solution.py:205
  51.7 10.0 %collective-permute-start.19 = (bf16[128,512]{1,0:T(8,128)(2,1)S(1)}, bf16[128,512]{1,0:T(8,128)(2,1)S(1)}, u32[]{:S(2)}, u32[]{:S(2)}) collective-permute-start(bf16[128,512]{1,0:T(8,128)(2,1)S(1)} %pad_maximum_fusion.1), channel_id=1, source_target_pairs={{0,17},{1,16},{2,19},{3,18},{4,21},{5,20},{6,23},{7,22},{8,25},{9,... | collective-permute-start | bytes 393224 | tf_op jit(solution)/shard_map/ppermute | solution.py:205
  54.2 7.5 %collective-permute-start.18 = (bf16[128,512]{1,0:T(8,128)(2,1)S(1)}, bf16[128,512]{1,0:T(8,128)(2,1)S(1)}, u32[]{:S(2)}, u32[]{:S(2)}) collective-permute-start(bf16[128,512]{1,0:T(8,128)(2,1)S(1)} %pad_maximum_fusion.1), channel_id=1, source_target_pairs={{0,16},{1,17},{2,18},{3,19},{4,20},{5,21},{6,22},{7,23},{8,24},{9,... | collective-permute-start | bytes 393224 | tf_op jit(solution)/shard_map/ppermute | solution.py:205
  55.0 7.2 %collective-permute-start.17 = (bf16[128,512]{1,0:T(8,128)(2,1)S(1)}, bf16[128,512]{1,0:T(8,128)(2,1)S(1)}, u32[]{:S(2)}, u32[]{:S(2)}) collective-permute-start(bf16[128,512]{1,0:T(8,128)(2,1)S(1)} %pad_maximum_fusion.1), channel_id=1, source_target_pairs={{0,1},{1,0},{2,3},{3,2},{4,5},{5,4},{6,7},{7,6},{8,9},{9,8},{10,11... | collective-permute-start | bytes 393224 | tf_op jit(solution)/shard_map/ppermute | solution.py:205
  62.2 2.0 %collective-permute-start.22 = (bf16[512,512]{1,0:T(8,128)(2,1)S(1)}, bf16[512,512]{1,0:T(8,128)(2,1)S(1)}, u32[]{:S(2)}, u32[]{:S(2)}) collective-permute-start(bf16[512,512]{1,0:T(8,128)(2,1)S(1)} %constant_dynamic-update-slice_fusion.7.lo_ref), channel_id=1, source_target_pairs={{0,8},{1,9},{2,10},{3,11},{4,12},{5,13},{6,14},{7,15},{8,0},{9,1},... | collective-permute-start | bytes 1572872 | tf_op jit(solution)/shard_map/ppermute | solution.py:205
  66.8 1.4 %collective-permute-start.23 = (bf16[128,512]{1,0:T(8,128)(2,1)S(1)}, bf16[128,512]{1,0:T(8,128)(2,1)S(1)}, u32[]{:S(2)}, u32[]{:S(2)}) collective-permute-start(bf16[128,512]{1,0:T(8,128)(2,1)S(1)} %get-tuple-element.111), channel_id=1, source_target_pairs={{0,8},{1,9},{2,10},{3,11},{4,12},{5,13},{6,14},{7,15},{8,0},{9,1},... | collective-permute-start | bytes 393224 | tf_op jit(solution)/shard_map/ppermute | solution.py:205
  67.0 4.0 %collective-permute-start.25 = (bf16[128,512]{1,0:T(8,128)(2,1)S(1)}, bf16[128,512]{1,0:T(8,128)(2,1)S(1)}, u32[]{:S(2)}, u32[]{:S(2)}) collective-permute-start(bf16[128,512]{1,0:T(8,128)(2,1)S(1)} %get-tuple-element.113), channel_id=1, source_target_pairs={{0,8},{1,9},{2,10},{3,11},{4,12},{5,13},{6,14},{7,15},{8,0},{9,1},... | collective-permute-start | bytes 393224 | tf_op jit(solution)/shard_map/ppermute | solution.py:205
  67.4 4.3 %collective-permute-start.27 = (bf16[128,512]{1,0:T(8,128)(2,1)S(1)}, bf16[128,512]{1,0:T(8,128)(2,1)S(1)}, u32[]{:S(2)}, u32[]{:S(2)}) collective-permute-start(bf16[128,512]{1,0:T(8,128)(2,1)S(1)} %get-tuple-element.115), channel_id=1, source_target_pairs={{0,8},{1,9},{2,10},{3,11},{4,12},{5,13},{6,14},{7,15},{8,0},{9,1},... | collective-permute-start | bytes 393224 | tf_op jit(solution)/shard_map/ppermute | solution.py:205
  67.5 4.5 %collective-permute-start.29 = (bf16[128,512]{1,0:T(8,128)(2,1)S(1)}, bf16[128,512]{1,0:T(8,128)(2,1)S(1)}, u32[]{:S(2)}, u32[]{:S(2)}) collective-permute-start(bf16[128,512]{1,0:T(8,128)(2,1)S(1)} %get-tuple-element.117), channel_id=1, source_target_pairs={{0,8},{1,9},{2,10},{3,11},{4,12},{5,13},{6,14},{7,15},{8,0},{9,1},... | collective-permute-start | bytes 393224 | tf_op jit(solution)/shard_map/ppermute | solution.py:205
  68.3 6.8 %collective-permute-start.24 = (bf16[128,512]{1,0:T(8,128)(2,1)S(1)}, bf16[128,512]{1,0:T(8,128)(2,1)S(1)}, u32[]{:S(2)}, u32[]{:S(2)}) collective-permute-start(bf16[128,512]{1,0:T(8,128)(2,1)S(1)} %add_convert_fusion.3), channel_id=1, source_target_pairs={{0,17},{1,16},{2,19},{3,18},{4,21},{5,20},{6,23},{7,22},{8,25},{9,... | collective-permute-start | bytes 393224 | tf_op jit(solution)/shard_map/ppermute | solution.py:205
  71.1 6.6 %collective-permute-start.26 = (bf16[128,512]{1,0:T(8,128)(2,1)S(1)}, bf16[128,512]{1,0:T(8,128)(2,1)S(1)}, u32[]{:S(2)}, u32[]{:S(2)}) collective-permute-start(bf16[128,512]{1,0:T(8,128)(2,1)S(1)} %add_convert_fusion.2), channel_id=1, source_target_pairs={{0,16},{1,17},{2,18},{3,19},{4,20},{5,21},{6,22},{7,23},{8,24},{9,... | collective-permute-start | bytes 393224 | tf_op jit(solution)/shard_map/ppermute | solution.py:205
  71.7 5.9 %collective-permute-start.28 = (bf16[128,512]{1,0:T(8,128)(2,1)S(1)}, bf16[128,512]{1,0:T(8,128)(2,1)S(1)}, u32[]{:S(2)}, u32[]{:S(2)}) collective-permute-start(bf16[128,512]{1,0:T(8,128)(2,1)S(1)} %add_convert_fusion.1), channel_id=1, source_target_pairs={{0,1},{1,0},{2,3},{3,2},{4,5},{5,4},{6,7},{7,6},{8,9},{9,8},{10,11... | collective-permute-start | bytes 393224 | tf_op jit(solution)/shard_map/ppermute | solution.py:205
  77.7 6.1 %collective-permute-start.32 = (bf16[32,512]{1,0:T(8,128)(2,1)S(1)}, bf16[32,512]{1,0:T(8,128)(2,1)S(1)}, u32[]{:S(2)}, u32[]{:S(2)}) collective-permute-start(bf16[32,512]{1,0:T(8,128)(2,1)S(1)} %get-tuple-element.144), channel_id=1, source_target_pairs={{0,6},{1,7},{2,4},{3,5},{4,2},{5,3},{6,0},{7,1},{8,14},{9,15},{10,... | collective-permute-start | bytes 98312 | tf_op jit(solution)/shard_map/ppermute | solution.py:205
  78.0 5.8 %collective-permute-start.31 = (bf16[32,512]{1,0:T(8,128)(2,1)S(1)}, bf16[32,512]{1,0:T(8,128)(2,1)S(1)}, u32[]{:S(2)}, u32[]{:S(2)}) collective-permute-start(bf16[32,512]{1,0:T(8,128)(2,1)S(1)} %get-tuple-element.145), channel_id=1, source_target_pairs={{0,2},{1,3},{2,0},{3,1},{4,6},{5,7},{6,4},{7,5},{8,10},{9,11},{10,... | collective-permute-start | bytes 98312 | tf_op jit(solution)/shard_map/ppermute | solution.py:205
  79.0 5.4 %collective-permute-start.30 = (bf16[32,512]{1,0:T(8,128)(2,1)S(1)}, bf16[32,512]{1,0:T(8,128)(2,1)S(1)}, u32[]{:S(2)}, u32[]{:S(2)}) collective-permute-start(bf16[32,512]{1,0:T(8,128)(2,1)S(1)} %get-tuple-element.146), channel_id=1, source_target_pairs={{0,4},{1,5},{2,6},{3,7},{4,0},{5,1},{6,2},{7,3},{8,12},{9,13},{10,... | collective-permute-start | bytes 98312 | tf_op jit(solution)/shard_map/ppermute | solution.py:205

commit v10 on v8

--- a/solution.py
+++ b/solution.py
@@ -324,7 +324,7 @@
             )
             held["tail"] = rotate(tail_new)
             held["head"] = update_heads(edge_grad, [(head_state.shape, F32), ((edges, width), BF16)])
-            grad = exchange.reduce_scatter(terms, {1: with_("head")})
+            grad = exchange.reduce_scatter(terms, {1: lambda got: with_("head")(got[::-1])[::-1]})
             head_table, head_state, head_vecs = held["head"]
             gather_hooks = {1: with_("tail")}
         else:

time: 85 us -> 84.9 us (level)
  no operation moved by 1% of the time
where the time goes in v10:
time: 84.9 us; the launch traced here: 84.6 us
  starting transfers between devices  40.7 us (48%)
  waiting for transfers between devices  22.7 us (27%)
  Pallas kernels  13.5 us (16%)
  local copies, waits for them, and re-layouts  4.85 us (6%)
  other arithmetic  2.07 us (2%)
  between operations  0.88 us (1%)
    ppermute x31, starting transfers between devices, swap(): return lax.ppermute(x, AXES, [(i, i ^ mask) for i in range(self.devices)])  36.3 us
    ppermute x31, waiting for transfers between devices, swap(): return lax.ppermute(x, AXES, [(i, i ^ mask) for i in range(self.devices)])  22.7 us
    pallas_call x7, Pallas kernels, call(): pl.pallas_call(kernel, out_shape=outs, in_specs=[SMEM] * smem + [VMEM] *...  13.5 us
    unnamed x39, local copies, waits for them, and re-layouts  4.83 us
    ppermute x1, starting transfers between devices, rotate(): return lax.ppermute(x, 'tail', [(i, i ^ 1) for i in range(tails)])  3.51 us
  transfers between devices with their start and end apart: 33, of which 15 were waited for; matrix products, arithmetic and copies ran while one was open for 1% of the time, Pallas kernels for 10%

profile of v10, /device:TPU:0, one launch (start us, length us, event | category | flops | bytes accessed | tf_op | source)
XLA Modules:
  0.0 84.6 jit_solution(11183966377635704399)
XLA Ops:
  0.6 0.8 %constant_dynamic-update-slice_fusion.6 = (bf16[512,512]{1,0:T(8,128)(2,1)S(1)}, bf16[32,512]{1,0:T(8,128)(2,1)S(1)}) fusion(f32[32,512]{1,0:T(8,128)} %param.16), kind=kLoop, calls=%fused_computation.28 | loop fusion | flops 16383 | bytes 131072
  1.5 5.0 %collective-permute-start.2 = (bf16[32,512]{1,0:T(8,128)(2,1)S(1)}, bf16[32,512]{1,0:T(8,128)(2,1)S(1)}, u32[]{:S(2)}, u32[]{:S(2)}) collective-permute-start(bf16[32,512]{1,0:T(8,128)(2,1)S(1)} %get-tuple-element.131), channel_id=1, source_target_pairs={{0,6},{1,7},{2,4},{3,5},{4,2},{5,3},{6,0},{7,1},{8,14},{9,15},{10,... | collective-permute-start | bytes 98312 | tf_op jit(solution)/shard_map/ppermute | solution.py:203
  6.5 0.6 collective-permute-start
  7.2 1.3 %collective-permute-done.2 = bf16[32,512]{1,0:T(8,128)(2,1)S(1)} collective-permute-done((bf16[32,512]{1,0:T(8,128)(2,1)S(1)}, bf16[32,512]{1,0:T(8,128)(2,1)S(1)}, u32[]{:S(2)}, u32[]{:S(2)}) %collective-permute-start.2) | collective-permute-done | bytes 32800 | tf_op jit(solution)/shard_map/ppermute | solution.py:203
  8.4 2.0 %collective-permute-done.1 = bf16[32,512]{1,0:T(8,128)(2,1)S(1)} collective-permute-done((bf16[32,512]{1,0:T(8,128)(2,1)S(1)}, bf16[32,512]{1,0:T(8,128)(2,1)S(1)}, u32[]{:S(2)}, u32[]{:S(2)}) %collective-permute-start.1) | collective-permute-done | bytes 32800 | tf_op jit(solution)/shard_map/ppermute | solution.py:203
  10.4 1.0 %collective-permute-done = bf16[32,512]{1,0:T(8,128)(2,1)S(1)} collective-permute-done((bf16[32,512]{1,0:T(8,128)(2,1)S(1)}, bf16[32,512]{1,0:T(8,128)(2,1)S(1)}, u32[]{:S(2)}, u32[]{:S(2)}) %collective-permute-start) | collective-permute-done | bytes 32800 | tf_op jit(solution)/shard_map/ppermute | solution.py:203
  11.5 2.5 %collective-permute-start.5 = (bf16[128,512]{1,0:T(8,128)(2,1)S(1)}, bf16[128,512]{1,0:T(8,128)(2,1)S(1)}, u32[]{:S(2)}, u32[]{:S(2)}) collective-permute-start(bf16[128,512]{1,0:T(8,128)(2,1)S(1)} %pad_maximum_fusion), channel_id=1, source_target_pairs={{0,17},{1,16},{2,19},{3,18},{4,21},{5,20},{6,23},{7,22},{8,25},{9,... | collective-permute-start | bytes 393224 | tf_op jit(solution)/shard_map/ppermute | solution.py:203
  14.0 0.5 collective-permute-start.4
  14.5 0.5 collective-permute-start.3
  15.1 0.6 copy-done.4
  15.8 1.2 %copy-done = f32[512,512]{1,0:T(8,128)S(1)} copy-done((f32[512,512]{1,0:T(8,128)S(1)}, f32[512,512]{1,0:T(8,128)}, u32[]{:S(2)}) %copy-start) | copy-done | bytes 1048600
  17.0 1.2 %copy-done.2 = f32[512,512]{1,0:T(8,128)S(1)} copy-done((f32[512,512]{1,0:T(8,128)S(1)}, f32[512,512]{1,0:T(8,128)}, u32[]{:S(2)}) %copy-start.2) | copy-done | bytes 1048600
  18.2 0.7 shard_map.139
  19.0 0.6 collective-permute-done.4
  19.6 0.1 collective-permute-start.6
  19.7 0.6 copy-done.12
  20.4 0.1 copy.16.live_ref
  20.5 0.7 copy-done.13
  21.1 0.5 collective-permute-done.6.hi_ref
  21.6 0.2 copy-done.9
  21.8 2.6 %shard_map.140 = (bf16[512,512]{1,0:T(8,128)(2,1)S(1)}, bf16[512,512]{1,0:T(8,128)(2,1)S(1)}, bf16[512,512]{1,0:T(8,128)(2,1)S(1)}, bf16[512,512]{1,0:T(8,128)(2,1)S(1)}, bf16[512,512]{1,0:T(8,128)(2,1)S(1)}) custom-call(s32[32]{0:T(128)S(1)} %broadcast_xor_fusion.nat_ref, s32[2,1]{1,0:T(2,128)S(1)} %copy.16.live_ref, s32[2,4]{1,0:T(2,128)S(1)} %copy-done.9, ...), custom_call_target="tpu_custom_call" | custom-call | flops 1342177280 | bytes 5259432 | tf_op jit(solution)/shard_map/pallas_call | solution.py:169
  24.4 0.6 collective-permute-start.7
  25.0 0.7 shard_map.142
  25.7 0.8 collective-permute-start.20
  26.5 0.1 add_convert_fusion.4
  26.7 4.1 %collective-permute-start.10 = (bf16[128,512]{1,0:T(8,128)(2,1)S(1)}, bf16[128,512]{1,0:T(8,128)(2,1)S(1)}, u32[]{:S(2)}, u32[]{:S(2)}) collective-permute-start(bf16[128,512]{1,0:T(8,128)(2,1)S(1)} %get-tuple-element.132), channel_id=1, source_target_pairs={{0,1},{1,0},{2,3},{3,2},{4,5},{5,4},{6,7},{7,6},{8,9},{9,8},{10,11... | collective-permute-start | bytes 393224 | tf_op jit(solution)/shard_map/ppermute | solution.py:203
  30.7 1.5 %collective-permute-start.9 = (bf16[128,512]{1,0:T(8,128)(2,1)S(1)}, bf16[128,512]{1,0:T(8,128)(2,1)S(1)}, u32[]{:S(2)}, u32[]{:S(2)}) collective-permute-start(bf16[128,512]{1,0:T(8,128)(2,1)S(1)} %get-tuple-element.133), channel_id=1, source_target_pairs={{0,16},{1,17},{2,18},{3,19},{4,20},{5,21},{6,22},{7,23},{8,24},{9,... | collective-permute-start | bytes 393224 | tf_op jit(solution)/shard_map/ppermute | solution.py:203
  32.3 2.2 %shard_map.141 = (f32[512,512]{1,0:T(8,128)S(1)}, f32[1,512]{1,0:T(1,128)S(1)}, bf16[512,512]{1,0:T(8,128)(2,1)S(1)}) custom-call(s32[32]{0:T(128)S(1)} %broadcast_xor_fusion.nat_ref, s32[2,4]{1,0:T(2,128)S(1)} %copy-done.9, bf16[512,512]{1,0:T(8,128)(2,1)S(1)} %constant_dynamic-update-slice_fusion.lo_ref, ...), custom_call_target="tpu_custom_call" | custom-call | flops 1073741824 | bytes 4202656 | tf_op jit(solution)/shard_map/pallas_call | solution.py:169
  34.5 0.1 collective-permute-done.10
  34.7 3.9 %collective-permute-done.9 = bf16[128,512]{1,0:T(8,128)(2,1)S(1)} collective-permute-done((bf16[128,512]{1,0:T(8,128)(2,1)S(1)}, bf16[128,512]{1,0:T(8,128)(2,1)S(1)}, u32[]{:S(2)}, u32[]{:S(2)}) %collective-permute-start.9) | collective-permute-done | bytes 131104 | tf_op jit(solution)/shard_map/ppermute | solution.py:203
  38.6 0.4 collective-permute-start.11
  39.0 2.2 %collective-permute-start.13 = (bf16[32,512]{1,0:T(8,128)(2,1)S(1)}, bf16[32,512]{1,0:T(8,128)(2,1)S(1)}, u32[]{:S(2)}, u32[]{:S(2)}) collective-permute-start(bf16[32,512]{1,0:T(8,128)(2,1)S(1)} %get-tuple-element.140), channel_id=1, source_target_pairs={{0,6},{1,7},{2,4},{3,5},{4,2},{5,3},{6,0},{7,1},{8,14},{9,15},{10,... | collective-permute-start | bytes 98312 | tf_op jit(solution)/shard_map/ppermute | solution.py:203
  41.2 0.9 %collective-permute-start.12 = (bf16[32,512]{1,0:T(8,128)(2,1)S(1)}, bf16[32,512]{1,0:T(8,128)(2,1)S(1)}, u32[]{:S(2)}, u32[]{:S(2)}) collective-permute-start(bf16[32,512]{1,0:T(8,128)(2,1)S(1)} %get-tuple-element.141), channel_id=1, source_target_pairs={{0,2},{1,3},{2,0},{3,1},{4,6},{5,7},{6,4},{7,5},{8,10},{9,11},{10,... | collective-permute-start | bytes 98312 | tf_op jit(solution)/shard_map/ppermute | solution.py:203
  42.2 3.5 %collective-permute-start.21 = (bf16[528,512]{1,0:T(8,128)(2,1)S(1)}, bf16[528,512]{1,0:T(8,128)(2,1)S(1)}, u32[]{:S(2)}, u32[]{:S(2)}) collective-permute-start(bf16[528,512]{1,0:T(8,128)(2,1)S(1)} %collective-permute-done.20), channel_id=1, source_target_pairs={{0,1},{1,0},{2,3},{3,2},{4,5},{5,4},{6,7},{7,6},{8,9},{9,8},{10,11... | collective-permute-start | bytes 1622024 | tf_op jit(solution)/shard_map/ppermute | solution.py:279
  45.7 0.1 constant_dynamic-update-slice_fusion.13
  45.8 1.5 %collective-permute-start.16 = (bf16[32,512]{1,0:T(8,128)(2,1)S(1)}, bf16[32,512]{1,0:T(8,128)(2,1)S(1)}, u32[]{:S(2)}, u32[]{:S(2)}) collective-permute-start(bf16[32,512]{1,0:T(8,128)(2,1)S(1)} %get-tuple-element.128), channel_id=1, source_target_pairs={{0,6},{1,7},{2,4},{3,5},{4,2},{5,3},{6,0},{7,1},{8,14},{9,15},{10,... | collective-permute-start | bytes 98312 | tf_op jit(solution)/shard_map/ppermute | solution.py:203
  47.2 0.1 collective-permute-start.15
  47.3 2.9 %collective-permute-start.14 = (bf16[32,512]{1,0:T(8,128)(2,1)S(1)}, bf16[32,512]{1,0:T(8,128)(2,1)S(1)}, u32[]{:S(2)}, u32[]{:S(2)}) collective-permute-start(bf16[32,512]{1,0:T(8,128)(2,1)S(1)} %get-tuple-element.128), channel_id=1, source_target_pairs={{0,4},{1,5},{2,6},{3,7},{4,0},{5,1},{6,2},{7,3},{8,12},{9,13},{10,... | collective-permute-start | bytes 98312 | tf_op jit(solution)/shard_map/ppermute | solution.py:203
  50.2 1.3 %collective-permute-done.16 = bf16[32,512]{1,0:T(8,128)(2,1)S(1)} collective-permute-done((bf16[32,512]{1,0:T(8,128)(2,1)S(1)}, bf16[32,512]{1,0:T(8,128)(2,1)S(1)}, u32[]{:S(2)}, u32[]{:S(2)}) %collective-permute-start.16) | collective-permute-done | bytes 32800 | tf_op jit(solution)/shard_map/ppermute | solution.py:203
  51.6 0.6 collective-permute-done.14
  52.1 2.1 %collective-permute-start.19 = (bf16[128,512]{1,0:T(8,128)(2,1)S(1)}, bf16[128,512]{1,0:T(8,128)(2,1)S(1)}, u32[]{:S(2)}, u32[]{:S(2)}) collective-permute-start(bf16[128,512]{1,0:T(8,128)(2,1)S(1)} %pad_maximum_fusion.1), channel_id=1, source_target_pairs={{0,17},{1,16},{2,19},{3,18},{4,21},{5,20},{6,23},{7,22},{8,25},{9,... | collective-permute-start | bytes 393224 | tf_op jit(solution)/shard_map/ppermute | solution.py:203
  54.3 0.7 collective-permute-start.18
  55.0 0.7 collective-permute-start.17
  55.7 5.7 %collective-permute-done.19 = bf16[128,512]{1,0:T(8,128)(2,1)S(1)} collective-permute-done((bf16[128,512]{1,0:T(8,128)(2,1)S(1)}, bf16[128,512]{1,0:T(8,128)(2,1)S(1)}, u32[]{:S(2)}, u32[]{:S(2)}) %collective-permute-start.19) | collective-permute-done | bytes 131104 | tf_op jit(solution)/shard_map/ppermute | solution.py:203
  61.4 0.5 collective-permute-done.17
  62.0 0.1 collective-permute-start.22
  62.1 1.9 %collective-permute-done.22.hi_ref = bf16[512,512]{1,0:T(8,128)(2,1)S(1)} collective-permute-done((bf16[512,512]{1,0:T(8,128)(2,1)S(1)}, bf16[512,512]{1,0:T(8,128)(2,1)S(1)}, u32[]{:S(2)}, u32[]{:S(2)}) %collective-permute-start.22) | collective-permute-done | bytes 524320 | tf_op jit(solution)/shard_map/ppermute | solution.py:203
  64.0 2.6 %shard_map.143 = (bf16[512,512]{1,0:T(8,128)(2,1)S(1)}, bf16[512,512]{1,0:T(8,128)(2,1)S(1)}, bf16[512,512]{1,0:T(8,128)(2,1)S(1)}, bf16[128,512]{1,0:T(8,128)(2...) custom-call(s32[32]{0:T(128)S(1)} %broadcast_xor_fusion.nat_ref, ...), custom_call_target="tpu_custom_call" | custom-call | flops 1342177280 | bytes 5275816 | tf_op jit(solution)/shard_map/pallas_call | solution.py:169
  66.6 0.2 collective-permute-start.23
  66.8 0.4 collective-permute-start.25
  67.1 0.1 collective-permute-start.27
  67.3 0.4 collective-permute-start.29
  67.7 0.3 collective-permute-done.23
  68.0 2.7 %collective-permute-start.24 = (bf16[128,512]{1,0:T(8,128)(2,1)S(1)}, bf16[128,512]{1,0:T(8,128)(2,1)S(1)}, u32[]{:S(2)}, u32[]{:S(2)}) collective-permute-start(bf16[128,512]{1,0:T(8,128)(2,1)S(1)} %add_convert_fusion.3), channel_id=1, source_target_pairs={{0,17},{1,16},{2,19},{3,18},{4,21},{5,20},{6,23},{7,22},{8,25},{9,... | collective-permute-start | bytes 393224 | tf_op jit(solution)/shard_map/ppermute | solution.py:203
  70.8 0.6 collective-permute-start.26
  71.4 0.3 collective-permute-start.28
  71.8 2.9 %shard_map.144 = f32[512,512]{1,0:T(8,128)} custom-call(s32[32]{0:T(128)S(1)} %broadcast_xor_fusion.nat_ref, s32[2,4]{1,0:T(2,128)S(1)} %copy-done.9, bf16[512,512]{1,0:T(8,128)(2,1)S(1)} %constant_dynamic-update-slice_fusion.7.lo_ref, bf16[512,512]{1,0:T(8,128)(2,1)S(1)} %collective-permute-done.22.hi_ref, bf16[512,512]{1,0:T(8,128)(2,1)S(1)} %get-tuple-element.113.gu_ref, ...), custom_call_target="tpu_custom_call" | custom-call | flops 1073741824 | bytes 3676320 | tf_op jit(solution)/shard_map/pallas_call | solution.py:169
  74.8 2.6 %collective-permute-done.26 = bf16[128,512]{1,0:T(8,128)(2,1)S(1)} collective-permute-done((bf16[128,512]{1,0:T(8,128)(2,1)S(1)}, bf16[128,512]{1,0:T(8,128)(2,1)S(1)}, u32[]{:S(2)}, u32[]{:S(2)}) %collective-permute-start.26) | collective-permute-done | bytes 131104 | tf_op jit(solution)/shard_map/ppermute | solution.py:203
  77.4 0.7 collective-permute-start.32
  78.1 0.9 %collective-permute-start.31 = (bf16[32,512]{1,0:T(8,128)(2,1)S(1)}, bf16[32,512]{1,0:T(8,128)(2,1)S(1)}, u32[]{:S(2)}, u32[]{:S(2)}) collective-permute-start(bf16[32,512]{1,0:T(8,128)(2,1)S(1)} %get-tuple-element.137), channel_id=1, source_target_pairs={{0,2},{1,3},{2,0},{3,1},{4,6},{5,7},{6,4},{7,5},{8,10},{9,11},{10,... | collective-permute-start | bytes 98312 | tf_op jit(solution)/shard_map/ppermute | solution.py:203
  79.1 2.8 %collective-permute-start.30 = (bf16[32,512]{1,0:T(8,128)(2,1)S(1)}, bf16[32,512]{1,0:T(8,128)(2,1)S(1)}, u32[]{:S(2)}, u32[]{:S(2)}) collective-permute-start(bf16[32,512]{1,0:T(8,128)(2,1)S(1)} %get-tuple-element.138), channel_id=1, source_target_pairs={{0,4},{1,5},{2,6},{3,7},{4,0},{5,1},{6,2},{7,3},{8,12},{9,13},{10,... | collective-permute-start | bytes 98312 | tf_op jit(solution)/shard_map/ppermute | solution.py:203
  81.9 1.7 %shard_map.145 = f32[512,512]{1,0:T(8,128)} custom-call(bf16[512,512]{1,0:T(8,128)(2,1)S(1)} %get-tuple-element.121.w_ref, bf16[512,512]{1,0:T(8,128)(2,1)S(1)} %get-tuple-element.122.u_ref, bf16[528,512]{1,0:T(8,128)(2,1)S(1)} %collective-permute-done.21.t_ref.packed_ref), custom_call_target="tpu_custom_call" | custom-call | flops 268435456 | bytes 2637824 | tf_op jit(solution)/shard_map/pallas_call | solution.py:169
  83.6 0.3 collective-permute-done.30
  83.9 0.7 divide_subtract_fusion
  (63 shorter events, 0.5 us)
Async XLA Ops:
  1.5 6.9 %collective-permute-start.2 = (bf16[32,512]{1,0:T(8,128)(2,1)S(1)}, bf16[32,512]{1,0:T(8,128)(2,1)S(1)}, u32[]{:S(2)}, u32[]{:S(2)}) collective-permute-start(bf16[32,512]{1,0:T(8,128)(2,1)S(1)} %get-tuple-element.131), channel_id=1, source_target_pairs={{0,6},{1,7},{2,4},{3,5},{4,2},{5,3},{6,0},{7,1},{8,14},{9,15},{10,... | collective-permute-start | bytes 98312 | tf_op jit(solution)/shard_map/ppermute | solution.py:203
  6.5 3.9 %collective-permute-start.1 = (bf16[32,512]{1,0:T(8,128)(2,1)S(1)}, bf16[32,512]{1,0:T(8,128)(2,1)S(1)}, u32[]{:S(2)}, u32[]{:S(2)}) collective-permute-start(bf16[32,512]{1,0:T(8,128)(2,1)S(1)} %get-tuple-element.131), channel_id=1, source_target_pairs={{0,2},{1,3},{2,0},{3,1},{4,6},{5,7},{6,4},{7,5},{8,10},{9,11},{10,... | collective-permute-start | bytes 98312 | tf_op jit(solution)/shard_map/ppermute | solution.py:203
  6.5 4.9 %collective-permute-start = (bf16[32,512]{1,0:T(8,128)(2,1)S(1)}, bf16[32,512]{1,0:T(8,128)(2,1)S(1)}, u32[]{:S(2)}, u32[]{:S(2)}) collective-permute-start(bf16[32,512]{1,0:T(8,128)(2,1)S(1)} %get-tuple-element.131), channel_id=1, source_target_pairs={{0,4},{1,5},{2,6},{3,7},{4,0},{5,1},{6,2},{7,3},{8,12},{9,13},{10,... | collective-permute-start | bytes 98312 | tf_op jit(solution)/shard_map/ppermute | solution.py:203
  11.5 7.5 %collective-permute-start.5 = (bf16[128,512]{1,0:T(8,128)(2,1)S(1)}, bf16[128,512]{1,0:T(8,128)(2,1)S(1)}, u32[]{:S(2)}, u32[]{:S(2)}) collective-permute-start(bf16[128,512]{1,0:T(8,128)(2,1)S(1)} %pad_maximum_fusion), channel_id=1, source_target_pairs={{0,17},{1,16},{2,19},{3,18},{4,21},{5,20},{6,23},{7,22},{8,25},{9,... | collective-permute-start | bytes 393224 | tf_op jit(solution)/shard_map/ppermute | solution.py:203
  14.0 5.6 %collective-permute-start.4 = (bf16[128,512]{1,0:T(8,128)(2,1)S(1)}, bf16[128,512]{1,0:T(8,128)(2,1)S(1)}, u32[]{:S(2)}, u32[]{:S(2)}) collective-permute-start(bf16[128,512]{1,0:T(8,128)(2,1)S(1)} %pad_maximum_fusion), channel_id=1, source_target_pairs={{0,16},{1,17},{2,18},{3,19},{4,20},{5,21},{6,22},{7,23},{8,24},{9,... | collective-permute-start | bytes 393224 | tf_op jit(solution)/shard_map/ppermute | solution.py:203
  14.5 5.1 %collective-permute-start.3 = (bf16[128,512]{1,0:T(8,128)(2,1)S(1)}, bf16[128,512]{1,0:T(8,128)(2,1)S(1)}, u32[]{:S(2)}, u32[]{:S(2)}) collective-permute-start(bf16[128,512]{1,0:T(8,128)(2,1)S(1)} %pad_maximum_fusion), channel_id=1, source_target_pairs={{0,1},{1,0},{2,3},{3,2},{4,5},{5,4},{6,7},{7,6},{8,9},{9,8},{10,11... | collective-permute-start | bytes 393224 | tf_op jit(solution)/shard_map/ppermute | solution.py:203
  15.0 0.7 copy-start.4
  15.0 0.7 copy-start.5
  15.0 0.7 copy-start.6
  15.0 0.7 copy-start.8
  15.1 0.7 copy-start.7
  15.8 1.2 %copy-start = (f32[512,512]{1,0:T(8,128)S(1)}, f32[512,512]{1,0:T(8,128)}, u32[]{:S(2)}) copy-start(f32[512,512]{1,0:T(8,128)} %table_ref.3) | copy-start | bytes 3145732
  17.0 1.2 %copy-start.2 = (f32[512,512]{1,0:T(8,128)S(1)}, f32[512,512]{1,0:T(8,128)}, u32[]{:S(2)}) copy-start(f32[512,512]{1,0:T(8,128)} %table_ref.2) | copy-start | bytes 3145732
  19.6 2.0 %collective-permute-start.6 = (bf16[512,512]{1,0:T(8,128)(2,1)S(1)}, bf16[512,512]{1,0:T(8,128)(2,1)S(1)}, u32[]{:S(2)}, u32[]{:S(2)}) collective-permute-start(bf16[512,512]{1,0:T(8,128)(2,1)S(1)} %constant_dynamic-update-slice_fusion.lo_ref), channel_id=1, source_target_pairs={{0,8},{1,9},{2,10},{3,11},{4,12},{5,13},{6,14},{7,15},{8,0},{9,1},... | collective-permute-start | bytes 1572872 | tf_op jit(solution)/shard_map/ppermute | solution.py:203
  19.7 0.7 copy-start.12
  20.5 0.7 copy-start.13
  21.1 0.7 copy-start.9
  21.1 3.8 %copy-start.1 = (f32[512,512]{1,0:T(8,128)S(1)}, f32[512,512]{1,0:T(8,128)}, u32[]{:S(2)}) copy-start(f32[512,512]{1,0:T(8,128)} %table_ref.3) | copy-start | bytes 3145732
  24.4 2.1 %collective-permute-start.7 = (bf16[512,512]{1,0:T(8,128)(2,1)S(1)}, bf16[512,512]{1,0:T(8,128)(2,1)S(1)}, u32[]{:S(2)}, u32[]{:S(2)}) collective-permute-start(bf16[512,512]{1,0:T(8,128)(2,1)S(1)} %get-tuple-element.85), channel_id=1, source_target_pairs={{0,8},{1,9},{2,10},{3,11},{4,12},{5,13},{6,14},{7,15},{8,0},{9,1},... | collective-permute-start | bytes 1572872 | tf_op jit(solution)/shard_map/ppermute | solution.py:203
  25.7 6.6 %copy-start.3 = (f32[512,512]{1,0:T(8,128)S(1)}, f32[512,512]{1,0:T(8,128)}, u32[]{:S(2)}) copy-start(f32[512,512]{1,0:T(8,128)} %table_ref.2) | copy-start | bytes 3145732
  25.7 16.5 %collective-permute-start.20 = (bf16[528,512]{1,0:T(8,128)(2,1)S(1)}, bf16[528,512]{1,0:T(8,128)(2,1)S(1)}, u32[]{:S(2)}, u32[]{:S(2)}) collective-permute-start(bf16[528,512]{1,0:T(8,128)(2,1)S(1)} %shard_map.142), channel_id=1, source_target_pairs={{0,0},{1,3},{2,2},{3,5},{4,4},{5,7},{6,6},{7,1},{8,8},{9,11},{10,1... | collective-permute-start | bytes 1622024 | tf_op jit(solution)/shard_map/ppermute | solution.py:278
  26.7 8.0 %collective-permute-start.10 = (bf16[128,512]{1,0:T(8,128)(2,1)S(1)}, bf16[128,512]{1,0:T(8,128)(2,1)S(1)}, u32[]{:S(2)}, u32[]{:S(2)}) collective-permute-start(bf16[128,512]{1,0:T(8,128)(2,1)S(1)} %get-tuple-element.132), channel_id=1, source_target_pairs={{0,1},{1,0},{2,3},{3,2},{4,5},{5,4},{6,7},{7,6},{8,9},{9,8},{10,11... | collective-permute-start | bytes 393224 | tf_op jit(solution)/shard_map/ppermute | solution.py:203
  30.7 7.8 %collective-permute-start.9 = (bf16[128,512]{1,0:T(8,128)(2,1)S(1)}, bf16[128,512]{1,0:T(8,128)(2,1)S(1)}, u32[]{:S(2)}, u32[]{:S(2)}) collective-permute-start(bf16[128,512]{1,0:T(8,128)(2,1)S(1)} %get-tuple-element.133), channel_id=1, source_target_pairs={{0,16},{1,17},{2,18},{3,19},{4,20},{5,21},{6,22},{7,23},{8,24},{9,... | collective-permute-start | bytes 393224 | tf_op jit(solution)/shard_map/ppermute | solution.py:203
  32.3 6.3 %collective-permute-start.8 = (bf16[128,512]{1,0:T(8,128)(2,1)S(1)}, bf16[128,512]{1,0:T(8,128)(2,1)S(1)}, u32[]{:S(2)}, u32[]{:S(2)}) collective-permute-start(bf16[128,512]{1,0:T(8,128)(2,1)S(1)} %get-tuple-element.134), channel_id=1, source_target_pairs={{0,17},{1,16},{2,19},{3,18},{4,21},{5,20},{6,23},{7,22},{8,25},{9,... | collective-permute-start | bytes 393224 | tf_op jit(solution)/shard_map/ppermute | solution.py:203
  38.5 7.1 %copy-start.10 = (f32[32,512]{1,0:T(8,128)S(1)}, f32[32,512]{1,0:T(8,128)}, u32[]{:S(2)}) copy-start(f32[32,512]{1,0:T(8,128)} %param.16) | copy-start | bytes 196612
  38.5 7.1 %copy-start.11 = (f32[32,512]{1,0:T(8,128)S(1)}, f32[32,512]{1,0:T(8,128)}, u32[]{:S(2)}) copy-start(f32[32,512]{1,0:T(8,128)} %param.17) | copy-start | bytes 196612
  38.6 7.1 %collective-permute-start.11 = (bf16[32,512]{1,0:T(8,128)(2,1)S(1)}, bf16[32,512]{1,0:T(8,128)(2,1)S(1)}, u32[]{:S(2)}, u32[]{:S(2)}) collective-permute-start(bf16[32,512]{1,0:T(8,128)(2,1)S(1)} %get-tuple-element.139), channel_id=1, source_target_pairs={{0,4},{1,5},{2,6},{3,7},{4,0},{5,1},{6,2},{7,3},{8,12},{9,13},{10,... | collective-permute-start | bytes 98312 | tf_op jit(solution)/shard_map/ppermute | solution.py:203
  39.0 6.7 %collective-permute-start.13 = (bf16[32,512]{1,0:T(8,128)(2,1)S(1)}, bf16[32,512]{1,0:T(8,128)(2,1)S(1)}, u32[]{:S(2)}, u32[]{:S(2)}) collective-permute-start(bf16[32,512]{1,0:T(8,128)(2,1)S(1)} %get-tuple-element.140), channel_id=1, source_target_pairs={{0,6},{1,7},{2,4},{3,5},{4,2},{5,3},{6,0},{7,1},{8,14},{9,15},{10,... | collective-permute-start | bytes 98312 | tf_op jit(solution)/shard_map/ppermute | solution.py:203
  41.2 4.5 %collective-permute-start.12 = (bf16[32,512]{1,0:T(8,128)(2,1)S(1)}, bf16[32,512]{1,0:T(8,128)(2,1)S(1)}, u32[]{:S(2)}, u32[]{:S(2)}) collective-permute-start(bf16[32,512]{1,0:T(8,128)(2,1)S(1)} %get-tuple-element.141), channel_id=1, source_target_pairs={{0,2},{1,3},{2,0},{3,1},{4,6},{5,7},{6,4},{7,5},{8,10},{9,11},{10,... | collective-permute-start | bytes 98312 | tf_op jit(solution)/shard_map/ppermute | solution.py:203
  42.2 19.8 %collective-permute-start.21 = (bf16[528,512]{1,0:T(8,128)(2,1)S(1)}, bf16[528,512]{1,0:T(8,128)(2,1)S(1)}, u32[]{:S(2)}, u32[]{:S(2)}) collective-permute-start(bf16[528,512]{1,0:T(8,128)(2,1)S(1)} %collective-permute-done.20), channel_id=1, source_target_pairs={{0,1},{1,0},{2,3},{3,2},{4,5},{5,4},{6,7},{7,6},{8,9},{9,8},{10,11... | collective-permute-start | bytes 1622024 | tf_op jit(solution)/shard_map/ppermute | solution.py:279
  45.8 5.8 %collective-permute-start.16 = (bf16[32,512]{1,0:T(8,128)(2,1)S(1)}, bf16[32,512]{1,0:T(8,128)(2,1)S(1)}, u32[]{:S(2)}, u32[]{:S(2)}) collective-permute-start(bf16[32,512]{1,0:T(8,128)(2,1)S(1)} %get-tuple-element.128), channel_id=1, source_target_pairs={{0,6},{1,7},{2,4},{3,5},{4,2},{5,3},{6,0},{7,1},{8,14},{9,15},{10,... | collective-permute-start | bytes 98312 | tf_op jit(solution)/shard_map/ppermute | solution.py:203
  47.2 4.3 %collective-permute-start.15 = (bf16[32,512]{1,0:T(8,128)(2,1)S(1)}, bf16[32,512]{1,0:T(8,128)(2,1)S(1)}, u32[]{:S(2)}, u32[]{:S(2)}) collective-permute-start(bf16[32,512]{1,0:T(8,128)(2,1)S(1)} %get-tuple-element.128), channel_id=1, source_target_pairs={{0,2},{1,3},{2,0},{3,1},{4,6},{5,7},{6,4},{7,5},{8,10},{9,11},{10,... | collective-permute-start | bytes 98312 | tf_op jit(solution)/shard_map/ppermute | solution.py:203
  47.3 4.8 %collective-permute-start.14 = (bf16[32,512]{1,0:T(8,128)(2,1)S(1)}, bf16[32,512]{1,0:T(8,128)(2,1)S(1)}, u32[]{:S(2)}, u32[]{:S(2)}) collective-permute-start(bf16[32,512]{1,0:T(8,128)(2,1)S(1)} %get-tuple-element.128), channel_id=1, source_target_pairs={{0,4},{1,5},{2,6},{3,7},{4,0},{5,1},{6,2},{7,3},{8,12},{9,13},{10,... | collective-permute-start | bytes 98312 | tf_op jit(solution)/shard_map/ppermute | solution.py:203
  52.1 9.3 %collective-permute-start.19 = (bf16[128,512]{1,0:T(8,128)(2,1)S(1)}, bf16[128,512]{1,0:T(8,128)(2,1)S(1)}, u32[]{:S(2)}, u32[]{:S(2)}) collective-permute-start(bf16[128,512]{1,0:T(8,128)(2,1)S(1)} %pad_maximum_fusion.1), channel_id=1, source_target_pairs={{0,17},{1,16},{2,19},{3,18},{4,21},{5,20},{6,23},{7,22},{8,25},{9,... | collective-permute-start | bytes 393224 | tf_op jit(solution)/shard_map/ppermute | solution.py:203
  54.3 7.2 %collective-permute-start.18 = (bf16[128,512]{1,0:T(8,128)(2,1)S(1)}, bf16[128,512]{1,0:T(8,128)(2,1)S(1)}, u32[]{:S(2)}, u32[]{:S(2)}) collective-permute-start(bf16[128,512]{1,0:T(8,128)(2,1)S(1)} %pad_maximum_fusion.1), channel_id=1, source_target_pairs={{0,16},{1,17},{2,18},{3,19},{4,20},{5,21},{6,22},{7,23},{8,24},{9,... | collective-permute-start | bytes 393224 | tf_op jit(solution)/shard_map/ppermute | solution.py:203
  55.0 7.0 %collective-permute-start.17 = (bf16[128,512]{1,0:T(8,128)(2,1)S(1)}, bf16[128,512]{1,0:T(8,128)(2,1)S(1)}, u32[]{:S(2)}, u32[]{:S(2)}) collective-permute-start(bf16[128,512]{1,0:T(8,128)(2,1)S(1)} %pad_maximum_fusion.1), channel_id=1, source_target_pairs={{0,1},{1,0},{2,3},{3,2},{4,5},{5,4},{6,7},{7,6},{8,9},{9,8},{10,11... | collective-permute-start | bytes 393224 | tf_op jit(solution)/shard_map/ppermute | solution.py:203
  62.0 2.0 %collective-permute-start.22 = (bf16[512,512]{1,0:T(8,128)(2,1)S(1)}, bf16[512,512]{1,0:T(8,128)(2,1)S(1)}, u32[]{:S(2)}, u32[]{:S(2)}) collective-permute-start(bf16[512,512]{1,0:T(8,128)(2,1)S(1)} %constant_dynamic-update-slice_fusion.7.lo_ref), channel_id=1, source_target_pairs={{0,8},{1,9},{2,10},{3,11},{4,12},{5,13},{6,14},{7,15},{8,0},{9,1},... | collective-permute-start | bytes 1572872 | tf_op jit(solution)/shard_map/ppermute | solution.py:203
  66.6 1.4 %collective-permute-start.23 = (bf16[128,512]{1,0:T(8,128)(2,1)S(1)}, bf16[128,512]{1,0:T(8,128)(2,1)S(1)}, u32[]{:S(2)}, u32[]{:S(2)}) collective-permute-start(bf16[128,512]{1,0:T(8,128)(2,1)S(1)} %get-tuple-element.103), channel_id=1, source_target_pairs={{0,8},{1,9},{2,10},{3,11},{4,12},{5,13},{6,14},{7,15},{8,0},{9,1},... | collective-permute-start | bytes 393224 | tf_op jit(solution)/shard_map/ppermute | solution.py:203
  66.8 4.0 %collective-permute-start.25 = (bf16[128,512]{1,0:T(8,128)(2,1)S(1)}, bf16[128,512]{1,0:T(8,128)(2,1)S(1)}, u32[]{:S(2)}, u32[]{:S(2)}) collective-permute-start(bf16[128,512]{1,0:T(8,128)(2,1)S(1)} %get-tuple-element.105), channel_id=1, source_target_pairs={{0,8},{1,9},{2,10},{3,11},{4,12},{5,13},{6,14},{7,15},{8,0},{9,1},... | collective-permute-start | bytes 393224 | tf_op jit(solution)/shard_map/ppermute | solution.py:203
  67.1 4.3 %collective-permute-start.27 = (bf16[128,512]{1,0:T(8,128)(2,1)S(1)}, bf16[128,512]{1,0:T(8,128)(2,1)S(1)}, u32[]{:S(2)}, u32[]{:S(2)}) collective-permute-start(bf16[128,512]{1,0:T(8,128)(2,1)S(1)} %get-tuple-element.107), channel_id=1, source_target_pairs={{0,8},{1,9},{2,10},{3,11},{4,12},{5,13},{6,14},{7,15},{8,0},{9,1},... | collective-permute-start | bytes 393224 | tf_op jit(solution)/shard_map/ppermute | solution.py:203
  67.3 4.5 %collective-permute-start.29 = (bf16[128,512]{1,0:T(8,128)(2,1)S(1)}, bf16[128,512]{1,0:T(8,128)(2,1)S(1)}, u32[]{:S(2)}, u32[]{:S(2)}) collective-permute-start(bf16[128,512]{1,0:T(8,128)(2,1)S(1)} %get-tuple-element.109), channel_id=1, source_target_pairs={{0,8},{1,9},{2,10},{3,11},{4,12},{5,13},{6,14},{7,15},{8,0},{9,1},... | collective-permute-start | bytes 393224 | tf_op jit(solution)/shard_map/ppermute | solution.py:203
  68.0 6.7 %collective-permute-start.24 = (bf16[128,512]{1,0:T(8,128)(2,1)S(1)}, bf16[128,512]{1,0:T(8,128)(2,1)S(1)}, u32[]{:S(2)}, u32[]{:S(2)}) collective-permute-start(bf16[128,512]{1,0:T(8,128)(2,1)S(1)} %add_convert_fusion.3), channel_id=1, source_target_pairs={{0,17},{1,16},{2,19},{3,18},{4,21},{5,20},{6,23},{7,22},{8,25},{9,... | collective-permute-start | bytes 393224 | tf_op jit(solution)/shard_map/ppermute | solution.py:203
  70.8 6.6 %collective-permute-start.26 = (bf16[128,512]{1,0:T(8,128)(2,1)S(1)}, bf16[128,512]{1,0:T(8,128)(2,1)S(1)}, u32[]{:S(2)}, u32[]{:S(2)}) collective-permute-start(bf16[128,512]{1,0:T(8,128)(2,1)S(1)} %add_convert_fusion.2), channel_id=1, source_target_pairs={{0,16},{1,17},{2,18},{3,19},{4,20},{5,21},{6,22},{7,23},{8,24},{9,... | collective-permute-start | bytes 393224 | tf_op jit(solution)/shard_map/ppermute | solution.py:203
  71.4 5.9 %collective-permute-start.28 = (bf16[128,512]{1,0:T(8,128)(2,1)S(1)}, bf16[128,512]{1,0:T(8,128)(2,1)S(1)}, u32[]{:S(2)}, u32[]{:S(2)}) collective-permute-start(bf16[128,512]{1,0:T(8,128)(2,1)S(1)} %add_convert_fusion.1), channel_id=1, source_target_pairs={{0,1},{1,0},{2,3},{3,2},{4,5},{5,4},{6,7},{7,6},{8,9},{9,8},{10,11... | collective-permute-start | bytes 393224 | tf_op jit(solution)/shard_map/ppermute | solution.py:203
  77.4 6.2 %collective-permute-start.32 = (bf16[32,512]{1,0:T(8,128)(2,1)S(1)}, bf16[32,512]{1,0:T(8,128)(2,1)S(1)}, u32[]{:S(2)}, u32[]{:S(2)}) collective-permute-start(bf16[32,512]{1,0:T(8,128)(2,1)S(1)} %get-tuple-element.136), channel_id=1, source_target_pairs={{0,6},{1,7},{2,4},{3,5},{4,2},{5,3},{6,0},{7,1},{8,14},{9,15},{10,... | collective-permute-start | bytes 98312 | tf_op jit(solution)/shard_map/ppermute | solution.py:203
  78.1 5.4 %collective-permute-start.31 = (bf16[32,512]{1,0:T(8,128)(2,1)S(1)}, bf16[32,512]{1,0:T(8,128)(2,1)S(1)}, u32[]{:S(2)}, u32[]{:S(2)}) collective-permute-start(bf16[32,512]{1,0:T(8,128)(2,1)S(1)} %get-tuple-element.137), channel_id=1, source_target_pairs={{0,2},{1,3},{2,0},{3,1},{4,6},{5,7},{6,4},{7,5},{8,10},{9,11},{10,... | collective-permute-start | bytes 98312 | tf_op jit(solution)/shard_map/ppermute | solution.py:203
  79.1 4.8 %collective-permute-start.30 = (bf16[32,512]{1,0:T(8,128)(2,1)S(1)}, bf16[32,512]{1,0:T(8,128)(2,1)S(1)}, u32[]{:S(2)}, u32[]{:S(2)}) collective-permute-start(bf16[32,512]{1,0:T(8,128)(2,1)S(1)} %get-tuple-element.138), channel_id=1, source_target_pairs={{0,4},{1,5},{2,6},{3,7},{4,0},{5,1},{6,2},{7,3},{8,12},{9,13},{10,... | collective-permute-start | bytes 98312 | tf_op jit(solution)/shard_map/ppermute | solution.py:203

commit v11 on v10

--- a/solution.py
+++ b/solution.py
@@ -292,7 +292,7 @@
             0, [], square,
             head_table, tail_table, *held["indices"], head_state, tail_state,
         )
-        return with_("prepared")(got)
+        return with_("prepared")(got[::-1])[::-1]
 
     gather_hooks = {2: with_("indices"), 1: prepare}
     for k in range(2):

time: 84.9 us -> 85.2 us (level)
  transfers between devices with their start and end apart: 33 -> 33, of which waited for: 15 -> 16; matrix products, arithmetic and copies ran while one was open for 1% -> 1% of each run, Pallas kernels for 10% -> 10%
where the time goes in v11:
time: 85.2 us; the launch traced here: 84.9 us
  starting transfers between devices  40.2 us (47%)
  waiting for transfers between devices  23.4 us (27%)
  Pallas kernels  13.5 us (16%)
  local copies, waits for them, and re-layouts  4.85 us (6%)
  other arithmetic  2.07 us (2%)
  between operations  0.89 us (1%)
    ppermute x31, starting transfers between devices, swap(): return lax.ppermute(x, AXES, [(i, i ^ mask) for i in range(self.devices)])  36 us
    ppermute x31, waiting for transfers between devices, swap(): return lax.ppermute(x, AXES, [(i, i ^ mask) for i in range(self.devices)])  23.4 us
    pallas_call x7, Pallas kernels, call(): pl.pallas_call(kernel, out_shape=outs, in_specs=[SMEM] * smem + [VMEM] *...  13.5 us
    unnamed x39, local copies, waits for them, and re-layouts  4.83 us
    ppermute x1, starting transfers between devices, rotate(): return lax.ppermute(x, 'tail', [(i, i ^ 1) for i in range(tails)])  3.42 us
  transfers between devices with their start and end apart: 33, of which 16 were waited for; matrix products, arithmetic and copies ran while one was open for 1% of the time, Pallas kernels for 10%

profile of v11, /device:TPU:0, one launch (start us, length us, event | category | flops | bytes accessed | tf_op | source)
XLA Modules:
  0.0 84.9 jit_solution(14402045206647773552)
XLA Ops:
  0.6 0.8 constant_dynamic-update-slice_fusion.6
  1.5 5.0 %collective-permute-start.2 = (bf16[32,512]{1,0:T(8,128)(2,1)S(1)}, bf16[32,512]{1,0:T(8,128)(2,1)S(1)}, u32[]{:S(2)}, u32[]{:S(2)}) collective-permute-start(bf16[32,512]{1,0:T(8,128)(2,1)S(1)} %get-tuple-element.131), channel_id=1, source_target_pairs={{0,6},{1,7},{2,4},{3,5},{4,2},{5,3},{6,0},{7,1},{8,14},{9,15},{10,... | collective-permute-start | bytes 98312 | tf_op jit(solution)/shard_map/ppermute | solution.py:203
  6.5 0.6 collective-permute-start
  7.2 1.3 %collective-permute-done.2 = bf16[32,512]{1,0:T(8,128)(2,1)S(1)} collective-permute-done((bf16[32,512]{1,0:T(8,128)(2,1)S(1)}, bf16[32,512]{1,0:T(8,128)(2,1)S(1)}, u32[]{:S(2)}, u32[]{:S(2)}) %collective-permute-start.2) | collective-permute-done | bytes 32800 | tf_op jit(solution)/shard_map/ppermute | solution.py:203
  8.4 2.0 %collective-permute-done.1 = bf16[32,512]{1,0:T(8,128)(2,1)S(1)} collective-permute-done((bf16[32,512]{1,0:T(8,128)(2,1)S(1)}, bf16[32,512]{1,0:T(8,128)(2,1)S(1)}, u32[]{:S(2)}, u32[]{:S(2)}) %collective-permute-start.1) | collective-permute-done | bytes 32800 | tf_op jit(solution)/shard_map/ppermute | solution.py:203
  10.4 1.0 %collective-permute-done = bf16[32,512]{1,0:T(8,128)(2,1)S(1)} collective-permute-done((bf16[32,512]{1,0:T(8,128)(2,1)S(1)}, bf16[32,512]{1,0:T(8,128)(2,1)S(1)}, u32[]{:S(2)}, u32[]{:S(2)}) %collective-permute-start) | collective-permute-done | bytes 32800 | tf_op jit(solution)/shard_map/ppermute | solution.py:203
  11.5 1.6 %collective-permute-start.5 = (bf16[128,512]{1,0:T(8,128)(2,1)S(1)}, bf16[128,512]{1,0:T(8,128)(2,1)S(1)}, u32[]{:S(2)}, u32[]{:S(2)}) collective-permute-start(bf16[128,512]{1,0:T(8,128)(2,1)S(1)} %pad_maximum_fusion), channel_id=1, source_target_pairs={{0,1},{1,0},{2,3},{3,2},{4,5},{5,4},{6,7},{7,6},{8,9},{9,8},{10,11... | collective-permute-start | bytes 393224 | tf_op jit(solution)/shard_map/ppermute | solution.py:203
  13.0 1.5 %collective-permute-start.4 = (bf16[128,512]{1,0:T(8,128)(2,1)S(1)}, bf16[128,512]{1,0:T(8,128)(2,1)S(1)}, u32[]{:S(2)}, u32[]{:S(2)}) collective-permute-start(bf16[128,512]{1,0:T(8,128)(2,1)S(1)} %pad_maximum_fusion), channel_id=1, source_target_pairs={{0,16},{1,17},{2,18},{3,19},{4,20},{5,21},{6,22},{7,23},{8,24},{9,... | collective-permute-start | bytes 393224 | tf_op jit(solution)/shard_map/ppermute | solution.py:203
  14.6 0.5 collective-permute-start.3
  15.1 0.6 copy-done.4
  15.8 1.2 %copy-done = f32[512,512]{1,0:T(8,128)S(1)} copy-done((f32[512,512]{1,0:T(8,128)S(1)}, f32[512,512]{1,0:T(8,128)}, u32[]{:S(2)}) %copy-start) | copy-done | bytes 1048600
  17.0 1.2 %copy-done.2 = f32[512,512]{1,0:T(8,128)S(1)} copy-done((f32[512,512]{1,0:T(8,128)S(1)}, f32[512,512]{1,0:T(8,128)}, u32[]{:S(2)}) %copy-start.2) | copy-done | bytes 1048600
  18.2 0.7 shard_map.139
  19.0 1.4 %collective-permute-done.3 = bf16[128,512]{1,0:T(8,128)(2,1)S(1)} collective-permute-done((bf16[128,512]{1,0:T(8,128)(2,1)S(1)}, bf16[128,512]{1,0:T(8,128)(2,1)S(1)}, u32[]{:S(2)}, u32[]{:S(2)}) %collective-permute-start.3) | collective-permute-done | bytes 131104 | tf_op jit(solution)/shard_map/ppermute | solution.py:203
  20.5 0.1 collective-permute-start.6
  20.6 0.6 copy-done.12
  21.2 0.1 copy.16.live_ref
  21.3 0.7 copy-done.13
  22.0 0.5 collective-permute-done.6.hi_ref
  22.4 0.2 copy-done.9
  22.6 2.6 %shard_map.140 = (bf16[512,512]{1,0:T(8,128)(2,1)S(1)}, bf16[512,512]{1,0:T(8,128)(2,1)S(1)}, bf16[512,512]{1,0:T(8,128)(2,1)S(1)}, bf16[512,512]{1,0:T(8,128)(2,1)S(1)}, bf16[512,512]{1,0:T(8,128)(2,1)S(1)}) custom-call(s32[32]{0:T(128)S(1)} %broadcast_xor_fusion.nat_ref, s32[2,1]{1,0:T(2,128)S(1)} %copy.16.live_ref, s32[2,4]{1,0:T(2,128)S(1)} %copy-done.9, ...), custom_call_target="tpu_custom_call" | custom-call | flops 1342177280 | bytes 5259432 | tf_op jit(solution)/shard_map/pallas_call | solution.py:169
  25.2 0.6 collective-permute-start.7
  25.8 0.7 shard_map.142
  26.5 0.8 collective-permute-start.20
  27.3 0.1 add_convert_fusion.4
  27.5 3.7 %collective-permute-start.10 = (bf16[128,512]{1,0:T(8,128)(2,1)S(1)}, bf16[128,512]{1,0:T(8,128)(2,1)S(1)}, u32[]{:S(2)}, u32[]{:S(2)}) collective-permute-start(bf16[128,512]{1,0:T(8,128)(2,1)S(1)} %get-tuple-element.132), channel_id=1, source_target_pairs={{0,1},{1,0},{2,3},{3,2},{4,5},{5,4},{6,7},{7,6},{8,9},{9,8},{10,11... | collective-permute-start | bytes 393224 | tf_op jit(solution)/shard_map/ppermute | solution.py:203
  31.2 1.0 %collective-permute-start.9 = (bf16[128,512]{1,0:T(8,128)(2,1)S(1)}, bf16[128,512]{1,0:T(8,128)(2,1)S(1)}, u32[]{:S(2)}, u32[]{:S(2)}) collective-permute-start(bf16[128,512]{1,0:T(8,128)(2,1)S(1)} %get-tuple-element.133), channel_id=1, source_target_pairs={{0,16},{1,17},{2,18},{3,19},{4,20},{5,21},{6,22},{7,23},{8,24},{9,... | collective-permute-start | bytes 393224 | tf_op jit(solution)/shard_map/ppermute | solution.py:203
  32.3 0.5 collective-permute-start.8
  32.8 2.2 %shard_map.141 = (f32[512,512]{1,0:T(8,128)S(1)}, f32[1,512]{1,0:T(1,128)S(1)}, bf16[512,512]{1,0:T(8,128)(2,1)S(1)}) custom-call(s32[32]{0:T(128)S(1)} %broadcast_xor_fusion.nat_ref, s32[2,4]{1,0:T(2,128)S(1)} %copy-done.9, bf16[512,512]{1,0:T(8,128)(2,1)S(1)} %constant_dynamic-update-slice_fusion.lo_ref, ...), custom_call_target="tpu_custom_call" | custom-call | flops 1073741824 | bytes 4202656 | tf_op jit(solution)/shard_map/pallas_call | solution.py:169
  35.0 0.1 collective-permute-done.10
  35.1 3.9 %collective-permute-done.9 = bf16[128,512]{1,0:T(8,128)(2,1)S(1)} collective-permute-done((bf16[128,512]{1,0:T(8,128)(2,1)S(1)}, bf16[128,512]{1,0:T(8,128)(2,1)S(1)}, u32[]{:S(2)}, u32[]{:S(2)}) %collective-permute-start.9) | collective-permute-done | bytes 131104 | tf_op jit(solution)/shard_map/ppermute | solution.py:203
  39.1 0.4 collective-permute-start.11
  39.5 2.2 %collective-permute-start.13 = (bf16[32,512]{1,0:T(8,128)(2,1)S(1)}, bf16[32,512]{1,0:T(8,128)(2,1)S(1)}, u32[]{:S(2)}, u32[]{:S(2)}) collective-permute-start(bf16[32,512]{1,0:T(8,128)(2,1)S(1)} %get-tuple-element.140), channel_id=1, source_target_pairs={{0,6},{1,7},{2,4},{3,5},{4,2},{5,3},{6,0},{7,1},{8,14},{9,15},{10,... | collective-permute-start | bytes 98312 | tf_op jit(solution)/shard_map/ppermute | solution.py:203
  41.7 0.9 %collective-permute-start.12 = (bf16[32,512]{1,0:T(8,128)(2,1)S(1)}, bf16[32,512]{1,0:T(8,128)(2,1)S(1)}, u32[]{:S(2)}, u32[]{:S(2)}) collective-permute-start(bf16[32,512]{1,0:T(8,128)(2,1)S(1)} %get-tuple-element.141), channel_id=1, source_target_pairs={{0,2},{1,3},{2,0},{3,1},{4,6},{5,7},{6,4},{7,5},{8,10},{9,11},{10,... | collective-permute-start | bytes 98312 | tf_op jit(solution)/shard_map/ppermute | solution.py:203
  42.6 3.4 %collective-permute-start.21 = (bf16[528,512]{1,0:T(8,128)(2,1)S(1)}, bf16[528,512]{1,0:T(8,128)(2,1)S(1)}, u32[]{:S(2)}, u32[]{:S(2)}) collective-permute-start(bf16[528,512]{1,0:T(8,128)(2,1)S(1)} %collective-permute-done.20), channel_id=1, source_target_pairs={{0,1},{1,0},{2,3},{3,2},{4,5},{5,4},{6,7},{7,6},{8,9},{9,8},{10,11... | collective-permute-start | bytes 1622024 | tf_op jit(solution)/shard_map/ppermute | solution.py:279
  46.1 0.1 constant_dynamic-update-slice_fusion.13
  46.1 1.6 %collective-permute-start.16 = (bf16[32,512]{1,0:T(8,128)(2,1)S(1)}, bf16[32,512]{1,0:T(8,128)(2,1)S(1)}, u32[]{:S(2)}, u32[]{:S(2)}) collective-permute-start(bf16[32,512]{1,0:T(8,128)(2,1)S(1)} %get-tuple-element.128), channel_id=1, source_target_pairs={{0,6},{1,7},{2,4},{3,5},{4,2},{5,3},{6,0},{7,1},{8,14},{9,15},{10,... | collective-permute-start | bytes 98312 | tf_op jit(solution)/shard_map/ppermute | solution.py:203
  47.7 2.9 %collective-permute-start.14 = (bf16[32,512]{1,0:T(8,128)(2,1)S(1)}, bf16[32,512]{1,0:T(8,128)(2,1)S(1)}, u32[]{:S(2)}, u32[]{:S(2)}) collective-permute-start(bf16[32,512]{1,0:T(8,128)(2,1)S(1)} %get-tuple-element.128), channel_id=1, source_target_pairs={{0,4},{1,5},{2,6},{3,7},{4,0},{5,1},{6,2},{7,3},{8,12},{9,13},{10,... | collective-permute-start | bytes 98312 | tf_op jit(solution)/shard_map/ppermute | solution.py:203
  50.6 1.4 %collective-permute-done.16 = bf16[32,512]{1,0:T(8,128)(2,1)S(1)} collective-permute-done((bf16[32,512]{1,0:T(8,128)(2,1)S(1)}, bf16[32,512]{1,0:T(8,128)(2,1)S(1)}, u32[]{:S(2)}, u32[]{:S(2)}) %collective-permute-start.16) | collective-permute-done | bytes 32800 | tf_op jit(solution)/shard_map/ppermute | solution.py:203
  52.0 0.5 collective-permute-done.14
  52.5 1.7 %collective-permute-start.19 = (bf16[128,512]{1,0:T(8,128)(2,1)S(1)}, bf16[128,512]{1,0:T(8,128)(2,1)S(1)}, u32[]{:S(2)}, u32[]{:S(2)}) collective-permute-start(bf16[128,512]{1,0:T(8,128)(2,1)S(1)} %pad_maximum_fusion.1), channel_id=1, source_target_pairs={{0,17},{1,16},{2,19},{3,18},{4,21},{5,20},{6,23},{7,22},{8,25},{9,... | collective-permute-start | bytes 393224 | tf_op jit(solution)/shard_map/ppermute | solution.py:203
  54.3 1.0 %collective-permute-start.18 = (bf16[128,512]{1,0:T(8,128)(2,1)S(1)}, bf16[128,512]{1,0:T(8,128)(2,1)S(1)}, u32[]{:S(2)}, u32[]{:S(2)}) collective-permute-start(bf16[128,512]{1,0:T(8,128)(2,1)S(1)} %pad_maximum_fusion.1), channel_id=1, source_target_pairs={{0,16},{1,17},{2,18},{3,19},{4,20},{5,21},{6,22},{7,23},{8,24},{9,... | collective-permute-start | bytes 393224 | tf_op jit(solution)/shard_map/ppermute | solution.py:203
  55.3 0.8 collective-permute-start.17
  56.1 5.3 %collective-permute-done.19 = bf16[128,512]{1,0:T(8,128)(2,1)S(1)} collective-permute-done((bf16[128,512]{1,0:T(8,128)(2,1)S(1)}, bf16[128,512]{1,0:T(8,128)(2,1)S(1)}, u32[]{:S(2)}, u32[]{:S(2)}) %collective-permute-start.19) | collective-permute-done | bytes 131104 | tf_op jit(solution)/shard_map/ppermute | solution.py:203
  61.4 0.9 %collective-permute-done.17 = bf16[128,512]{1,0:T(8,128)(2,1)S(1)} collective-permute-done((bf16[128,512]{1,0:T(8,128)(2,1)S(1)}, bf16[128,512]{1,0:T(8,128)(2,1)S(1)}, u32[]{:S(2)}, u32[]{:S(2)}) %collective-permute-start.17) | collective-permute-done | bytes 131104 | tf_op jit(solution)/shard_map/ppermute | solution.py:203
  62.4 0.1 collective-permute-start.22
  62.5 1.9 %collective-permute-done.22.hi_ref = bf16[512,512]{1,0:T(8,128)(2,1)S(1)} collective-permute-done((bf16[512,512]{1,0:T(8,128)(2,1)S(1)}, bf16[512,512]{1,0:T(8,128)(2,1)S(1)}, u32[]{:S(2)}, u32[]{:S(2)}) %collective-permute-start.22) | collective-permute-done | bytes 524320 | tf_op jit(solution)/shard_map/ppermute | solution.py:203
  64.4 2.6 %shard_map.143 = (bf16[512,512]{1,0:T(8,128)(2,1)S(1)}, bf16[512,512]{1,0:T(8,128)(2,1)S(1)}, bf16[512,512]{1,0:T(8,128)(2,1)S(1)}, bf16[128,512]{1,0:T(8,128)(2...) custom-call(s32[32]{0:T(128)S(1)} %broadcast_xor_fusion.nat_ref, ...), custom_call_target="tpu_custom_call" | custom-call | flops 1342177280 | bytes 5275816 | tf_op jit(solution)/shard_map/pallas_call | solution.py:169
  67.0 0.2 collective-permute-start.23
  67.2 0.4 collective-permute-start.25
  67.6 0.1 collective-permute-start.27
  67.7 0.4 collective-permute-start.29
  68.1 0.3 collective-permute-done.23
  68.4 2.3 %collective-permute-start.24 = (bf16[128,512]{1,0:T(8,128)(2,1)S(1)}, bf16[128,512]{1,0:T(8,128)(2,1)S(1)}, u32[]{:S(2)}, u32[]{:S(2)}) collective-permute-start(bf16[128,512]{1,0:T(8,128)(2,1)S(1)} %add_convert_fusion.3), channel_id=1, source_target_pairs={{0,17},{1,16},{2,19},{3,18},{4,21},{5,20},{6,23},{7,22},{8,25},{9,... | collective-permute-start | bytes 393224 | tf_op jit(solution)/shard_map/ppermute | solution.py:203
  70.8 1.0 %collective-permute-start.26 = (bf16[128,512]{1,0:T(8,128)(2,1)S(1)}, bf16[128,512]{1,0:T(8,128)(2,1)S(1)}, u32[]{:S(2)}, u32[]{:S(2)}) collective-permute-start(bf16[128,512]{1,0:T(8,128)(2,1)S(1)} %add_convert_fusion.2), channel_id=1, source_target_pairs={{0,16},{1,17},{2,18},{3,19},{4,20},{5,21},{6,22},{7,23},{8,24},{9,... | collective-permute-start | bytes 393224 | tf_op jit(solution)/shard_map/ppermute | solution.py:203
  71.9 0.4 collective-permute-start.28
  72.3 2.9 %shard_map.144 = f32[512,512]{1,0:T(8,128)} custom-call(s32[32]{0:T(128)S(1)} %broadcast_xor_fusion.nat_ref, s32[2,4]{1,0:T(2,128)S(1)} %copy-done.9, bf16[512,512]{1,0:T(8,128)(2,1)S(1)} %constant_dynamic-update-slice_fusion.7.lo_ref, bf16[512,512]{1,0:T(8,128)(2,1)S(1)} %collective-permute-done.22.hi_ref, bf16[512,512]{1,0:T(8,128)(2,1)S(1)} %get-tuple-element.113.gu_ref, ...), custom_call_target="tpu_custom_call" | custom-call | flops 1073741824 | bytes 3676320 | tf_op jit(solution)/shard_map/pallas_call | solution.py:169
  75.3 2.5 %collective-permute-done.26 = bf16[128,512]{1,0:T(8,128)(2,1)S(1)} collective-permute-done((bf16[128,512]{1,0:T(8,128)(2,1)S(1)}, bf16[128,512]{1,0:T(8,128)(2,1)S(1)}, u32[]{:S(2)}, u32[]{:S(2)}) %collective-permute-start.26) | collective-permute-done | bytes 131104 | tf_op jit(solution)/shard_map/ppermute | solution.py:203
  77.8 0.6 collective-permute-start.32
  78.4 0.9 %collective-permute-start.31 = (bf16[32,512]{1,0:T(8,128)(2,1)S(1)}, bf16[32,512]{1,0:T(8,128)(2,1)S(1)}, u32[]{:S(2)}, u32[]{:S(2)}) collective-permute-start(bf16[32,512]{1,0:T(8,128)(2,1)S(1)} %get-tuple-element.137), channel_id=1, source_target_pairs={{0,2},{1,3},{2,0},{3,1},{4,6},{5,7},{6,4},{7,5},{8,10},{9,11},{10,... | collective-permute-start | bytes 98312 | tf_op jit(solution)/shard_map/ppermute | solution.py:203
  79.3 3.0 %collective-permute-start.30 = (bf16[32,512]{1,0:T(8,128)(2,1)S(1)}, bf16[32,512]{1,0:T(8,128)(2,1)S(1)}, u32[]{:S(2)}, u32[]{:S(2)}) collective-permute-start(bf16[32,512]{1,0:T(8,128)(2,1)S(1)} %get-tuple-element.138), channel_id=1, source_target_pairs={{0,4},{1,5},{2,6},{3,7},{4,0},{5,1},{6,2},{7,3},{8,12},{9,13},{10,... | collective-permute-start | bytes 98312 | tf_op jit(solution)/shard_map/ppermute | solution.py:203
  82.3 1.7 %shard_map.145 = f32[512,512]{1,0:T(8,128)} custom-call(bf16[512,512]{1,0:T(8,128)(2,1)S(1)} %get-tuple-element.121.w_ref, bf16[512,512]{1,0:T(8,128)(2,1)S(1)} %get-tuple-element.122.u_ref, bf16[528,512]{1,0:T(8,128)(2,1)S(1)} %collective-permute-done.21.t_ref.packed_ref), custom_call_target="tpu_custom_call" | custom-call | flops 268435456 | bytes 2637824 | tf_op jit(solution)/shard_map/pallas_call | solution.py:169
  84.0 0.2 collective-permute-done.30
  84.2 0.7 divide_subtract_fusion
  (63 shorter events, 0.6 us)
Async XLA Ops:
  1.5 6.9 %collective-permute-start.2 = (bf16[32,512]{1,0:T(8,128)(2,1)S(1)}, bf16[32,512]{1,0:T(8,128)(2,1)S(1)}, u32[]{:S(2)}, u32[]{:S(2)}) collective-permute-start(bf16[32,512]{1,0:T(8,128)(2,1)S(1)} %get-tuple-element.131), channel_id=1, source_target_pairs={{0,6},{1,7},{2,4},{3,5},{4,2},{5,3},{6,0},{7,1},{8,14},{9,15},{10,... | collective-permute-start | bytes 98312 | tf_op jit(solution)/shard_map/ppermute | solution.py:203
  6.5 3.9 %collective-permute-start.1 = (bf16[32,512]{1,0:T(8,128)(2,1)S(1)}, bf16[32,512]{1,0:T(8,128)(2,1)S(1)}, u32[]{:S(2)}, u32[]{:S(2)}) collective-permute-start(bf16[32,512]{1,0:T(8,128)(2,1)S(1)} %get-tuple-element.131), channel_id=1, source_target_pairs={{0,2},{1,3},{2,0},{3,1},{4,6},{5,7},{6,4},{7,5},{8,10},{9,11},{10,... | collective-permute-start | bytes 98312 | tf_op jit(solution)/shard_map/ppermute | solution.py:203
  6.5 4.9 %collective-permute-start = (bf16[32,512]{1,0:T(8,128)(2,1)S(1)}, bf16[32,512]{1,0:T(8,128)(2,1)S(1)}, u32[]{:S(2)}, u32[]{:S(2)}) collective-permute-start(bf16[32,512]{1,0:T(8,128)(2,1)S(1)} %get-tuple-element.131), channel_id=1, source_target_pairs={{0,4},{1,5},{2,6},{3,7},{4,0},{5,1},{6,2},{7,3},{8,12},{9,13},{10,... | collective-permute-start | bytes 98312 | tf_op jit(solution)/shard_map/ppermute | solution.py:203
  11.5 7.5 %collective-permute-start.5 = (bf16[128,512]{1,0:T(8,128)(2,1)S(1)}, bf16[128,512]{1,0:T(8,128)(2,1)S(1)}, u32[]{:S(2)}, u32[]{:S(2)}) collective-permute-start(bf16[128,512]{1,0:T(8,128)(2,1)S(1)} %pad_maximum_fusion), channel_id=1, source_target_pairs={{0,1},{1,0},{2,3},{3,2},{4,5},{5,4},{6,7},{7,6},{8,9},{9,8},{10,11... | collective-permute-start | bytes 393224 | tf_op jit(solution)/shard_map/ppermute | solution.py:203
  13.0 5.9 %collective-permute-start.4 = (bf16[128,512]{1,0:T(8,128)(2,1)S(1)}, bf16[128,512]{1,0:T(8,128)(2,1)S(1)}, u32[]{:S(2)}, u32[]{:S(2)}) collective-permute-start(bf16[128,512]{1,0:T(8,128)(2,1)S(1)} %pad_maximum_fusion), channel_id=1, source_target_pairs={{0,16},{1,17},{2,18},{3,19},{4,20},{5,21},{6,22},{7,23},{8,24},{9,... | collective-permute-start | bytes 393224 | tf_op jit(solution)/shard_map/ppermute | solution.py:203
  14.6 5.9 %collective-permute-start.3 = (bf16[128,512]{1,0:T(8,128)(2,1)S(1)}, bf16[128,512]{1,0:T(8,128)(2,1)S(1)}, u32[]{:S(2)}, u32[]{:S(2)}) collective-permute-start(bf16[128,512]{1,0:T(8,128)(2,1)S(1)} %pad_maximum_fusion), channel_id=1, source_target_pairs={{0,17},{1,16},{2,19},{3,18},{4,21},{5,20},{6,23},{7,22},{8,25},{9,... | collective-permute-start | bytes 393224 | tf_op jit(solution)/shard_map/ppermute | solution.py:203
  15.0 0.7 copy-start.4
  15.0 0.7 copy-start.5
  15.0 0.7 copy-start.6
  15.0 0.7 copy-start.8
  15.1 0.7 copy-start.7
  15.8 1.2 %copy-start = (f32[512,512]{1,0:T(8,128)S(1)}, f32[512,512]{1,0:T(8,128)}, u32[]{:S(2)}) copy-start(f32[512,512]{1,0:T(8,128)} %table_ref.3) | copy-start | bytes 3145732
  17.0 1.2 %copy-start.2 = (f32[512,512]{1,0:T(8,128)S(1)}, f32[512,512]{1,0:T(8,128)}, u32[]{:S(2)}) copy-start(f32[512,512]{1,0:T(8,128)} %table_ref.2) | copy-start | bytes 3145732
  20.5 2.0 %collective-permute-start.6 = (bf16[512,512]{1,0:T(8,128)(2,1)S(1)}, bf16[512,512]{1,0:T(8,128)(2,1)S(1)}, u32[]{:S(2)}, u32[]{:S(2)}) collective-permute-start(bf16[512,512]{1,0:T(8,128)(2,1)S(1)} %constant_dynamic-update-slice_fusion.lo_ref), channel_id=1, source_target_pairs={{0,8},{1,9},{2,10},{3,11},{4,12},{5,13},{6,14},{7,15},{8,0},{9,1},... | collective-permute-start | bytes 1572872 | tf_op jit(solution)/shard_map/ppermute | solution.py:203
  20.6 0.7 copy-start.12
  21.3 0.7 copy-start.13
  22.0 0.7 copy-start.9
  22.0 3.8 %copy-start.1 = (f32[512,512]{1,0:T(8,128)S(1)}, f32[512,512]{1,0:T(8,128)}, u32[]{:S(2)}) copy-start(f32[512,512]{1,0:T(8,128)} %table_ref.3) | copy-start | bytes 3145732
  25.2 2.1 %collective-permute-start.7 = (bf16[512,512]{1,0:T(8,128)(2,1)S(1)}, bf16[512,512]{1,0:T(8,128)(2,1)S(1)}, u32[]{:S(2)}, u32[]{:S(2)}) collective-permute-start(bf16[512,512]{1,0:T(8,128)(2,1)S(1)} %get-tuple-element.85), channel_id=1, source_target_pairs={{0,8},{1,9},{2,10},{3,11},{4,12},{5,13},{6,14},{7,15},{8,0},{9,1},... | collective-permute-start | bytes 1572872 | tf_op jit(solution)/shard_map/ppermute | solution.py:203
  26.5 6.3 %copy-start.3 = (f32[512,512]{1,0:T(8,128)S(1)}, f32[512,512]{1,0:T(8,128)}, u32[]{:S(2)}) copy-start(f32[512,512]{1,0:T(8,128)} %table_ref.2) | copy-start | bytes 3145732
  26.5 16.1 %collective-permute-start.20 = (bf16[528,512]{1,0:T(8,128)(2,1)S(1)}, bf16[528,512]{1,0:T(8,128)(2,1)S(1)}, u32[]{:S(2)}, u32[]{:S(2)}) collective-permute-start(bf16[528,512]{1,0:T(8,128)(2,1)S(1)} %shard_map.142), channel_id=1, source_target_pairs={{0,0},{1,3},{2,2},{3,5},{4,4},{5,7},{6,6},{7,1},{8,8},{9,11},{10,1... | collective-permute-start | bytes 1622024 | tf_op jit(solution)/shard_map/ppermute | solution.py:278
  27.5 7.6 %collective-permute-start.10 = (bf16[128,512]{1,0:T(8,128)(2,1)S(1)}, bf16[128,512]{1,0:T(8,128)(2,1)S(1)}, u32[]{:S(2)}, u32[]{:S(2)}) collective-permute-start(bf16[128,512]{1,0:T(8,128)(2,1)S(1)} %get-tuple-element.132), channel_id=1, source_target_pairs={{0,1},{1,0},{2,3},{3,2},{4,5},{5,4},{6,7},{7,6},{8,9},{9,8},{10,11... | collective-permute-start | bytes 393224 | tf_op jit(solution)/shard_map/ppermute | solution.py:203
  31.2 7.8 %collective-permute-start.9 = (bf16[128,512]{1,0:T(8,128)(2,1)S(1)}, bf16[128,512]{1,0:T(8,128)(2,1)S(1)}, u32[]{:S(2)}, u32[]{:S(2)}) collective-permute-start(bf16[128,512]{1,0:T(8,128)(2,1)S(1)} %get-tuple-element.133), channel_id=1, source_target_pairs={{0,16},{1,17},{2,18},{3,19},{4,20},{5,21},{6,22},{7,23},{8,24},{9,... | collective-permute-start | bytes 393224 | tf_op jit(solution)/shard_map/ppermute | solution.py:203
  32.3 6.7 %collective-permute-start.8 = (bf16[128,512]{1,0:T(8,128)(2,1)S(1)}, bf16[128,512]{1,0:T(8,128)(2,1)S(1)}, u32[]{:S(2)}, u32[]{:S(2)}) collective-permute-start(bf16[128,512]{1,0:T(8,128)(2,1)S(1)} %get-tuple-element.134), channel_id=1, source_target_pairs={{0,17},{1,16},{2,19},{3,18},{4,21},{5,20},{6,23},{7,22},{8,25},{9,... | collective-permute-start | bytes 393224 | tf_op jit(solution)/shard_map/ppermute | solution.py:203
  39.0 7.1 %copy-start.10 = (f32[32,512]{1,0:T(8,128)S(1)}, f32[32,512]{1,0:T(8,128)}, u32[]{:S(2)}) copy-start(f32[32,512]{1,0:T(8,128)} %param.16) | copy-start | bytes 196612
  39.0 7.1 %copy-start.11 = (f32[32,512]{1,0:T(8,128)S(1)}, f32[32,512]{1,0:T(8,128)}, u32[]{:S(2)}) copy-start(f32[32,512]{1,0:T(8,128)} %param.17) | copy-start | bytes 196612
  39.1 7.0 %collective-permute-start.11 = (bf16[32,512]{1,0:T(8,128)(2,1)S(1)}, bf16[32,512]{1,0:T(8,128)(2,1)S(1)}, u32[]{:S(2)}, u32[]{:S(2)}) collective-permute-start(bf16[32,512]{1,0:T(8,128)(2,1)S(1)} %get-tuple-element.139), channel_id=1, source_target_pairs={{0,4},{1,5},{2,6},{3,7},{4,0},{5,1},{6,2},{7,3},{8,12},{9,13},{10,... | collective-permute-start | bytes 98312 | tf_op jit(solution)/shard_map/ppermute | solution.py:203
  39.5 6.6 %collective-permute-start.13 = (bf16[32,512]{1,0:T(8,128)(2,1)S(1)}, bf16[32,512]{1,0:T(8,128)(2,1)S(1)}, u32[]{:S(2)}, u32[]{:S(2)}) collective-permute-start(bf16[32,512]{1,0:T(8,128)(2,1)S(1)} %get-tuple-element.140), channel_id=1, source_target_pairs={{0,6},{1,7},{2,4},{3,5},{4,2},{5,3},{6,0},{7,1},{8,14},{9,15},{10,... | collective-permute-start | bytes 98312 | tf_op jit(solution)/shard_map/ppermute | solution.py:203
  41.7 4.4 %collective-permute-start.12 = (bf16[32,512]{1,0:T(8,128)(2,1)S(1)}, bf16[32,512]{1,0:T(8,128)(2,1)S(1)}, u32[]{:S(2)}, u32[]{:S(2)}) collective-permute-start(bf16[32,512]{1,0:T(8,128)(2,1)S(1)} %get-tuple-element.141), channel_id=1, source_target_pairs={{0,2},{1,3},{2,0},{3,1},{4,6},{5,7},{6,4},{7,5},{8,10},{9,11},{10,... | collective-permute-start | bytes 98312 | tf_op jit(solution)/shard_map/ppermute | solution.py:203
  42.6 19.7 %collective-permute-start.21 = (bf16[528,512]{1,0:T(8,128)(2,1)S(1)}, bf16[528,512]{1,0:T(8,128)(2,1)S(1)}, u32[]{:S(2)}, u32[]{:S(2)}) collective-permute-start(bf16[528,512]{1,0:T(8,128)(2,1)S(1)} %collective-permute-done.20), channel_id=1, source_target_pairs={{0,1},{1,0},{2,3},{3,2},{4,5},{5,4},{6,7},{7,6},{8,9},{9,8},{10,11... | collective-permute-start | bytes 1622024 | tf_op jit(solution)/shard_map/ppermute | solution.py:279
  46.1 5.8 %collective-permute-start.16 = (bf16[32,512]{1,0:T(8,128)(2,1)S(1)}, bf16[32,512]{1,0:T(8,128)(2,1)S(1)}, u32[]{:S(2)}, u32[]{:S(2)}) collective-permute-start(bf16[32,512]{1,0:T(8,128)(2,1)S(1)} %get-tuple-element.128), channel_id=1, source_target_pairs={{0,6},{1,7},{2,4},{3,5},{4,2},{5,3},{6,0},{7,1},{8,14},{9,15},{10,... | collective-permute-start | bytes 98312 | tf_op jit(solution)/shard_map/ppermute | solution.py:203
  47.7 4.3 %collective-permute-start.15 = (bf16[32,512]{1,0:T(8,128)(2,1)S(1)}, bf16[32,512]{1,0:T(8,128)(2,1)S(1)}, u32[]{:S(2)}, u32[]{:S(2)}) collective-permute-start(bf16[32,512]{1,0:T(8,128)(2,1)S(1)} %get-tuple-element.128), channel_id=1, source_target_pairs={{0,2},{1,3},{2,0},{3,1},{4,6},{5,7},{6,4},{7,5},{8,10},{9,11},{10,... | collective-permute-start | bytes 98312 | tf_op jit(solution)/shard_map/ppermute | solution.py:203
  47.7 4.8 %collective-permute-start.14 = (bf16[32,512]{1,0:T(8,128)(2,1)S(1)}, bf16[32,512]{1,0:T(8,128)(2,1)S(1)}, u32[]{:S(2)}, u32[]{:S(2)}) collective-permute-start(bf16[32,512]{1,0:T(8,128)(2,1)S(1)} %get-tuple-element.128), channel_id=1, source_target_pairs={{0,4},{1,5},{2,6},{3,7},{4,0},{5,1},{6,2},{7,3},{8,12},{9,13},{10,... | collective-permute-start | bytes 98312 | tf_op jit(solution)/shard_map/ppermute | solution.py:203
  52.5 8.9 %collective-permute-start.19 = (bf16[128,512]{1,0:T(8,128)(2,1)S(1)}, bf16[128,512]{1,0:T(8,128)(2,1)S(1)}, u32[]{:S(2)}, u32[]{:S(2)}) collective-permute-start(bf16[128,512]{1,0:T(8,128)(2,1)S(1)} %pad_maximum_fusion.1), channel_id=1, source_target_pairs={{0,17},{1,16},{2,19},{3,18},{4,21},{5,20},{6,23},{7,22},{8,25},{9,... | collective-permute-start | bytes 393224 | tf_op jit(solution)/shard_map/ppermute | solution.py:203
  54.3 7.1 %collective-permute-start.18 = (bf16[128,512]{1,0:T(8,128)(2,1)S(1)}, bf16[128,512]{1,0:T(8,128)(2,1)S(1)}, u32[]{:S(2)}, u32[]{:S(2)}) collective-permute-start(bf16[128,512]{1,0:T(8,128)(2,1)S(1)} %pad_maximum_fusion.1), channel_id=1, source_target_pairs={{0,16},{1,17},{2,18},{3,19},{4,20},{5,21},{6,22},{7,23},{8,24},{9,... | collective-permute-start | bytes 393224 | tf_op jit(solution)/shard_map/ppermute | solution.py:203
  55.3 7.1 %collective-permute-start.17 = (bf16[128,512]{1,0:T(8,128)(2,1)S(1)}, bf16[128,512]{1,0:T(8,128)(2,1)S(1)}, u32[]{:S(2)}, u32[]{:S(2)}) collective-permute-start(bf16[128,512]{1,0:T(8,128)(2,1)S(1)} %pad_maximum_fusion.1), channel_id=1, source_target_pairs={{0,1},{1,0},{2,3},{3,2},{4,5},{5,4},{6,7},{7,6},{8,9},{9,8},{10,11... | collective-permute-start | bytes 393224 | tf_op jit(solution)/shard_map/ppermute | solution.py:203
  62.4 2.0 %collective-permute-start.22 = (bf16[512,512]{1,0:T(8,128)(2,1)S(1)}, bf16[512,512]{1,0:T(8,128)(2,1)S(1)}, u32[]{:S(2)}, u32[]{:S(2)}) collective-permute-start(bf16[512,512]{1,0:T(8,128)(2,1)S(1)} %constant_dynamic-update-slice_fusion.7.lo_ref), channel_id=1, source_target_pairs={{0,8},{1,9},{2,10},{3,11},{4,12},{5,13},{6,14},{7,15},{8,0},{9,1},... | collective-permute-start | bytes 1572872 | tf_op jit(solution)/shard_map/ppermute | solution.py:203
  67.0 1.4 %collective-permute-start.23 = (bf16[128,512]{1,0:T(8,128)(2,1)S(1)}, bf16[128,512]{1,0:T(8,128)(2,1)S(1)}, u32[]{:S(2)}, u32[]{:S(2)}) collective-permute-start(bf16[128,512]{1,0:T(8,128)(2,1)S(1)} %get-tuple-element.103), channel_id=1, source_target_pairs={{0,8},{1,9},{2,10},{3,11},{4,12},{5,13},{6,14},{7,15},{8,0},{9,1},... | collective-permute-start | bytes 393224 | tf_op jit(solution)/shard_map/ppermute | solution.py:203
  67.2 3.5 %collective-permute-start.25 = (bf16[128,512]{1,0:T(8,128)(2,1)S(1)}, bf16[128,512]{1,0:T(8,128)(2,1)S(1)}, u32[]{:S(2)}, u32[]{:S(2)}) collective-permute-start(bf16[128,512]{1,0:T(8,128)(2,1)S(1)} %get-tuple-element.105), channel_id=1, source_target_pairs={{0,8},{1,9},{2,10},{3,11},{4,12},{5,13},{6,14},{7,15},{8,0},{9,1},... | collective-permute-start | bytes 393224 | tf_op jit(solution)/shard_map/ppermute | solution.py:203
  67.6 4.3 %collective-permute-start.27 = (bf16[128,512]{1,0:T(8,128)(2,1)S(1)}, bf16[128,512]{1,0:T(8,128)(2,1)S(1)}, u32[]{:S(2)}, u32[]{:S(2)}) collective-permute-start(bf16[128,512]{1,0:T(8,128)(2,1)S(1)} %get-tuple-element.107), channel_id=1, source_target_pairs={{0,8},{1,9},{2,10},{3,11},{4,12},{5,13},{6,14},{7,15},{8,0},{9,1},... | collective-permute-start | bytes 393224 | tf_op jit(solution)/shard_map/ppermute | solution.py:203
  67.7 4.5 %collective-permute-start.29 = (bf16[128,512]{1,0:T(8,128)(2,1)S(1)}, bf16[128,512]{1,0:T(8,128)(2,1)S(1)}, u32[]{:S(2)}, u32[]{:S(2)}) collective-permute-start(bf16[128,512]{1,0:T(8,128)(2,1)S(1)} %get-tuple-element.109), channel_id=1, source_target_pairs={{0,8},{1,9},{2,10},{3,11},{4,12},{5,13},{6,14},{7,15},{8,0},{9,1},... | collective-permute-start | bytes 393224 | tf_op jit(solution)/shard_map/ppermute | solution.py:203
  68.4 6.8 %collective-permute-start.24 = (bf16[128,512]{1,0:T(8,128)(2,1)S(1)}, bf16[128,512]{1,0:T(8,128)(2,1)S(1)}, u32[]{:S(2)}, u32[]{:S(2)}) collective-permute-start(bf16[128,512]{1,0:T(8,128)(2,1)S(1)} %add_convert_fusion.3), channel_id=1, source_target_pairs={{0,17},{1,16},{2,19},{3,18},{4,21},{5,20},{6,23},{7,22},{8,25},{9,... | collective-permute-start | bytes 393224 | tf_op jit(solution)/shard_map/ppermute | solution.py:203
  70.8 7.0 %collective-permute-start.26 = (bf16[128,512]{1,0:T(8,128)(2,1)S(1)}, bf16[128,512]{1,0:T(8,128)(2,1)S(1)}, u32[]{:S(2)}, u32[]{:S(2)}) collective-permute-start(bf16[128,512]{1,0:T(8,128)(2,1)S(1)} %add_convert_fusion.2), channel_id=1, source_target_pairs={{0,16},{1,17},{2,18},{3,19},{4,20},{5,21},{6,22},{7,23},{8,24},{9,... | collective-permute-start | bytes 393224 | tf_op jit(solution)/shard_map/ppermute | solution.py:203
  71.9 5.9 %collective-permute-start.28 = (bf16[128,512]{1,0:T(8,128)(2,1)S(1)}, bf16[128,512]{1,0:T(8,128)(2,1)S(1)}, u32[]{:S(2)}, u32[]{:S(2)}) collective-permute-start(bf16[128,512]{1,0:T(8,128)(2,1)S(1)} %add_convert_fusion.1), channel_id=1, source_target_pairs={{0,1},{1,0},{2,3},{3,2},{4,5},{5,4},{6,7},{7,6},{8,9},{9,8},{10,11... | collective-permute-start | bytes 393224 | tf_op jit(solution)/shard_map/ppermute | solution.py:203
  77.8 6.1 %collective-permute-start.32 = (bf16[32,512]{1,0:T(8,128)(2,1)S(1)}, bf16[32,512]{1,0:T(8,128)(2,1)S(1)}, u32[]{:S(2)}, u32[]{:S(2)}) collective-permute-start(bf16[32,512]{1,0:T(8,128)(2,1)S(1)} %get-tuple-element.136), channel_id=1, source_target_pairs={{0,6},{1,7},{2,4},{3,5},{4,2},{5,3},{6,0},{7,1},{8,14},{9,15},{10,... | collective-permute-start | bytes 98312 | tf_op jit(solution)/shard_map/ppermute | solution.py:203
  78.4 5.6 %collective-permute-start.31 = (bf16[32,512]{1,0:T(8,128)(2,1)S(1)}, bf16[32,512]{1,0:T(8,128)(2,1)S(1)}, u32[]{:S(2)}, u32[]{:S(2)}) collective-permute-start(bf16[32,512]{1,0:T(8,128)(2,1)S(1)} %get-tuple-element.137), channel_id=1, source_target_pairs={{0,2},{1,3},{2,0},{3,1},{4,6},{5,7},{6,4},{7,5},{8,10},{9,11},{10,... | collective-permute-start | bytes 98312 | tf_op jit(solution)/shard_map/ppermute | solution.py:203
  79.3 4.9 %collective-permute-start.30 = (bf16[32,512]{1,0:T(8,128)(2,1)S(1)}, bf16[32,512]{1,0:T(8,128)(2,1)S(1)}, u32[]{:S(2)}, u32[]{:S(2)}) collective-permute-start(bf16[32,512]{1,0:T(8,128)(2,1)S(1)} %get-tuple-element.138), channel_id=1, source_target_pairs={{0,4},{1,5},{2,6},{3,7},{4,0},{5,1},{6,2},{7,3},{8,12},{9,13},{10,... | collective-permute-start | bytes 98312 | tf_op jit(solution)/shard_map/ppermute | solution.py:203
